TPU v7x, 32 devices: a whole 2x2x4 slice. The times are simulated.
32 devices in a mesh: groups: 2 (over x), sample: 16 (over z, y, core).
Axes of the slice: x: 2, y: 2, z: 4, core: 2. Of those that a mesh axis runs over, the one named last changes fastest.
Arguments:
- prompt_kv: bfloat16 [64, 16, 32, 2048], P('groups', 'sample'), parts along dimension 0, may hold values from -16 to 16
- prompt_blocks: int32 [16], P('groups'), parts along dimension 0, may hold values from 1 to 128, 512 in all
- slot_prompt: int32 [32], P('groups'), parts along dimension 0, may hold values from 0 to 7, as said below
- queries: bfloat16 [256, 4, 8192], P(('groups', 'sample')), parts along dimension 0, may hold values from -24 to 24
- new_kv: bfloat16 [256, 4, 2048], P(('groups', 'sample')), parts along dimension 0, may hold values from -16 to 16
Outputs:
- attention: bfloat16 [256, 4, 8192], P(('groups', 'sample')), parts along dimension 0
- deviation: bfloat16 [256, 4, 8192], P(('groups', 'sample')), parts along dimension 0
There are 2 independent parts, one for each index of `groups`. A program takes and returns all parts, laid end to end along the dimension named above; each array names one. Nothing has to cross between parts.
Inputs may be any that keep to these rules, and one draw needn't show every extreme that they name: `slot_prompt`: slots 2s and 2s + 1 decode the same prompt, and each prompt is decoded by exactly one such pair of slots. `prompt_blocks`: counts of whole blocks of 32 tokens; they sum to 512.
All inputs are finite; a program needn't handle non-finite values.
Results may differ from a plain program's by a relative error of at most 0.0055.
Values may be sent and summed in bfloat16 or wider, within the bound.
No kernel may reach another device: no remote copies, remote signals or barrier semaphores. Data moves between devices by JAX's collectives and lax.ppermute only.
A program may use at most 128 MiB of HBM per device.

v0:
```python
import math

import jax
import jax.numpy as jnp
from jax import lax
from jax.sharding import PartitionSpec as P

HEADS = 64
KVH = 8
HD = 128
BLK = 32
MAXB = 128


NEG_FILL = -1e30


def swapped(array, axis, apart):
    return lax.ppermute(array, axis, [(i, i ^ 1 << apart) for i in range(lax.axis_size(axis))])


def causal_table(step_count):
    step_order = jnp.arange(step_count)
    return step_order[:, None] >= step_order[None, :]


def prompt_scores(head_query, head_keys, usable):
    scores = jnp.einsum(
        "msrd,ld->msrl", head_query, head_keys, preferred_element_type=jnp.float32
    ) * (1.0 / math.sqrt(HD))
    return jnp.where(usable[None, None, None, :], scores, NEG_FILL)


def fresh_scores(head_query, head_keys):
    scores = jnp.einsum(
        "msrd,mud->msru", head_query, head_keys, preferred_element_type=jnp.float32
    ) * (1.0 / math.sqrt(HD))
    allowed = causal_table(head_query.shape[1])
    return jnp.where(allowed[None, :, None, :], scores, NEG_FILL)


def shards(prompt_kv, prompt_blocks, slot_prompt, queries, new_kv):
    nsample = lax.axis_size("sample")
    my_index = lax.axis_index("sample")
    capacity = (MAXB + nsample - 1) // nsample
    sample_count, step_count, feature_width = queries.shape
    group_size = HEADS // KVH
    row_width = 2 * KVH * HD
    local_blocks = prompt_kv.reshape(prompt_kv.shape[0], BLK, row_width)
    prompt_ids = jnp.arange(prompt_blocks.shape[0], dtype=jnp.int32)
    block_starts = jnp.cumsum(prompt_blocks) - prompt_blocks
    selection = (slot_prompt[:, None] == prompt_ids[None, :]).astype(jnp.int32)
    dest_first = jnp.sum(selection * block_starts[None, :], axis=1)
    dest_count = jnp.sum(selection * prompt_blocks[None, :], axis=1)
    layer_steps = jnp.arange(capacity, dtype=jnp.int32)
    target_block = (
        dest_first[:, None]
        + jnp.mod(my_index - dest_first, nsample)[:, None]
        + nsample * layer_steps[None, :]
    )
    sending = target_block < (dest_first + dest_count)[:, None]
    local_index = jnp.where(sending, target_block // nsample, 0)
    slot_ids = jnp.arange(nsample, dtype=jnp.int32)
    is_mine = slot_ids == my_index
    my_first = jnp.sum(jnp.where(is_mine, dest_first, 0))
    my_count = jnp.sum(jnp.where(is_mine, dest_count, 0))
    arrived = (
        my_first + jnp.mod(slot_ids - my_first, nsample)[:, None] + nsample * layer_steps[None, :]
    )
    present = arrived < my_first + my_count
    own_query = queries.reshape(sample_count, step_count, KVH, group_size, HD)
    fresh_kv = new_kv.reshape(sample_count, step_count, 2, KVH, HD)
    outgoing = local_blocks[local_index]
    outgoing = jnp.where(sending[:, :, None, None], outgoing, jnp.zeros((), outgoing.dtype))
    incoming = lax.all_to_all(outgoing, "sample", split_axis=0, concat_axis=0, tiled=True)
    prompt_keys = incoming.reshape(-1, 2, KVH, HD)
    usable = jnp.repeat(present.reshape(-1), BLK)
    head_outputs = []
    for kv_head in range(KVH):
        head_query = own_query[:, :, kv_head]
        prompt_part = prompt_scores(head_query, prompt_keys[:, 0, kv_head], usable)
        fresh_part = fresh_scores(head_query, fresh_kv[:, :, 0, kv_head])
        row_peak = jnp.maximum(jnp.max(prompt_part, axis=-1), jnp.max(fresh_part, axis=-1))
        prompt_raised = jnp.exp(prompt_part - row_peak[..., None])
        fresh_raised = jnp.exp(fresh_part - row_peak[..., None])
        weight_sum = jnp.sum(prompt_raised, axis=-1) + jnp.sum(fresh_raised, axis=-1)
        weighted = jnp.einsum(
            "msrl,ld->msrd",
            prompt_raised.astype(jnp.bfloat16),
            prompt_keys[:, 1, kv_head],
            preferred_element_type=jnp.float32,
        )
        weighted = weighted + jnp.einsum(
            "msru,mud->msrd",
            fresh_raised.astype(jnp.bfloat16),
            fresh_kv[:, :, 1, kv_head],
            preferred_element_type=jnp.float32,
        )
        head_outputs.append(weighted / weight_sum[..., None])
    attention_full = jnp.stack(head_outputs, axis=2)
    attention_full = attention_full.reshape(sample_count, step_count, feature_width)
    own_sum = jnp.sum(attention_full, axis=0)
    partner_total = swapped(own_sum.astype(jnp.bfloat16), "sample", 0).astype(own_sum.dtype)
    centroid = (own_sum + partner_total) / (2 * sample_count)
    deviation = attention_full - centroid[None]
    return (attention_full.astype(jnp.bfloat16), deviation.astype(jnp.bfloat16))


def solution(mesh):
    placed = (
        P("groups", "sample", None, None),
        P("groups"),
        P("groups"),
        P(("groups", "sample"), None, None),
        P(("groups", "sample"), None, None),
    )
    return jax.shard_map(
        shards,
        mesh=mesh,
        in_specs=placed,
        out_specs=(P(("groups", "sample"), None, None), P(("groups", "sample"), None, None)),
        check_vma=False,
    )
```

profile of v0, /device:TPU:19, one launch (start us, length us, event | category | flops | bytes accessed | tf_op | source)
XLA Modules:
  0.0 504.8 jit_solution(4605883932843901821)
XLA Ops:
  5.7 10.3 %gather_fusion = bf16[128,32,2048]{2,1,0:T(8,128)(2,1)} fusion(bf16[32,32,2048]{2,1,0:T(8,128)(2,1)} %bitcast.411, s32[1024]{0:T(1024)S(1)} %pad_clamp_fusion), kind=kCustom, calls=%fused_computation | custom fusion | bytes 33554944 | tf_op jit(solution)/shard_map/gather | solution.py:73
  16.1 14.0 %broadcast_select_fusion = bf16[16,8,32,2048]{3,2,1,0:T(8,128)(2,1)} fusion(bf16[16,8,32,2048]{3,2,1,0:T(8,128)(2,1)} %bitcast.412, pred[16,8]{1,0:T(8,128)(4,1)S(1)} %get-tuple-element.46), kind=kLoop, calls=%fused_computation.1 | loop fusion | flops 8388608 | bytes 33554560 | tf_op jit(solution)/shard_map/jit(_where)/select_n | solution.py:74
  30.0 6.7 %all-to-all-start = ((bf16[16,8,32,2048]{3,2,1,0:T(8,128)(2,1)}), bf16[16,8,32,2048]{3,2,1,0:T(8,128)(2,1)}, u32[]{:S(2)}, u32[]{:S(2)}) async-start(bf16[16,8,32,2048]{3,2,1,0:T(8,128)(2,1)} %broadcast_select_fusion), calls=%async_computation | async-start | bytes 33554432 | tf_op jit(solution)/shard_map/all_to_all | solution.py:75
  38.2 0.9 fusion.214
  39.1 1.0 fusion.216
  40.1 1.0 fusion.218
  41.2 1.0 fusion.220
  42.2 1.0 fusion.222
  43.2 1.0 fusion.224
  44.2 1.0 fusion.226
  45.2 1.0 fusion.228
  46.3 1.0 fusion.230
  47.3 351.2 %all-to-all-done = bf16[16,8,32,2048]{3,2,1,0:T(8,128)(2,1)} async-done(((bf16[16,8,32,2048]{3,2,1,0:T(8,128)(2,1)}), bf16[16,8,32,2048]{3,2,1,0:T(8,128)(2,1)}, u32[]{:S(2)}, u32[]{:S(2)}) %all-to-all-start) | async-done | bytes 16777248 | tf_op jit(solution)/shard_map/all_to_all | solution.py:75
  398.5 15.1 %copy.287 = bf16[512,8,16,128]{3,2,1,0:T(8,128)(2,1)} copy(bf16[512,8,16,128]{3,1,2,0:T(8,128)(2,1)} %bitcast.207) | data formatting | bytes 33554432
  413.6 55.8 %fusion.213 = (bf16[4096,1,1,128]{3,2,1,0:T(2,128)(2,1)S(1)}, bf16[4096,1,1,128]{3,2,1,0:T(2,128)(2,1)}, bf16[4096,1,1,128]{3,2,1,0:T(2,128)(2,1)}, bf16[4096,1,...) fusion(bf16[4096,2,8,128]{3,2,1,0:T(8,128)(2,1)} %bitcast.410), kind=kLoop, calls=%fused_computation.237 | loop fusion | bytes 33554432 | tf_op jit(solution)/shard_map/slice | solution.py:90
  469.5 2.5 fusion.215
  473.6 0.9 fusion.217
  476.1 0.9 fusion.219
  478.6 0.9 fusion.221
  481.1 0.9 fusion.223
  483.6 0.9 fusion.225
  486.1 0.9 fusion.227
  488.6 1.1 fusion.229
  492.1 2.6 fusion.77
  494.8 0.9 fusion.89
  495.7 0.9 fusion.101
  496.6 0.9 fusion.113
  497.5 0.9 fusion.125
  499.2 0.9 fusion.149
  500.3 0.9 collective-permute-start
  502.4 1.2 copy.187
  503.6 1.2 copy.188
  (132 shorter events, 20.8 us)
Async XLA Ops:
  30.0 6.7 %copy-start.16 = (bf16[8,4,2048]{2,1,0:T(4,128)(2,1)S(1)}, bf16[8,4,2048]{2,1,0:T(4,128)(2,1)}, u32[]{:S(2)}) copy-start(bf16[8,4,2048]{2,1,0:T(4,128)(2,1)} %param.9) | copy-start | bytes 393220
  30.0 6.8 %copy-start.13 = (bf16[8,4,8192]{2,1,0:T(4,128)(2,1)S(1)}, bf16[8,4,8192]{2,1,0:T(4,128)(2,1)}, u32[]{:S(2)}) copy-start(bf16[8,4,8192]{2,1,0:T(4,128)(2,1)} %param.8) | copy-start | bytes 1572868
  30.0 368.5 %all-to-all-start = ((bf16[16,8,32,2048]{3,2,1,0:T(8,128)(2,1)}), bf16[16,8,32,2048]{3,2,1,0:T(8,128)(2,1)}, u32[]{:S(2)}, u32[]{:S(2)}) async-start(bf16[16,8,32,2048]{3,2,1,0:T(8,128)(2,1)} %broadcast_select_fusion), calls=%async_computation | async-start | bytes 33554432 | tf_op jit(solution)/shard_map/all_to_all | solution.py:75
  37.3 376.3 %copy-start.14 = (bf16[8,4,8,8,128]{4,3,2,1,0:T(8,128)(2,1)}, bf16[8,4,8,8,128]{4,3,2,1,0:T(8,128)(2,1)S(1)}, u32[]{:S(2)}) copy-start(bf16[8,4,8,8,128]{4,3,2,1,0:T(8,128)(2,1)S(1)} %reshape.406) | copy-start | bytes 1572868
  413.6 55.9 %copy-start.15 = (bf16[8,4,8,8,128]{4,3,2,1,0:T(8,128)(2,1)S(1)}, bf16[8,4,8,8,128]{4,3,2,1,0:T(8,128)(2,1)}, u32[]{:S(2)}) copy-start(bf16[8,4,8,8,128]{4,3,2,1,0:T(8,128)(2,1)} %copy-done.14) | copy-start | bytes 1572868
  413.6 55.9 %copy-start.32 = (pred[4096]{0:T(1024)(128)(4,1)S(1)}, pred[4096]{0:T(1024)(128)(4,1)}, u32[]{:S(2)}) copy-start(pred[4096]{0:T(1024)(128)(4,1)} %broadcast_in_dim.181) | copy-start | bytes 12292
  469.5 2.5 copy-start.31
  469.5 2.6 copy-start.23
  472.0 1.6 copy-start.12
  473.6 1.0 copy-start.22
  474.5 1.6 copy-start.11
  476.1 1.0 copy-start.21
  477.0 1.6 copy-start.10
  478.6 0.9 copy-start.28
  478.6 1.0 copy-start.20
  479.5 1.6 copy-start.9
  481.1 0.9 copy-start.27
  481.1 1.0 copy-start.19
  482.0 1.6 copy-start.8
  483.6 0.9 copy-start.26
  483.6 1.0 copy-start.18
  484.5 1.6 copy-start.7
  486.1 1.0 copy-start.17
  487.0 1.6 copy-start.6
  488.6 1.1 copy-start.24
  489.7 1.6 copy-start.5
  491.3 3.5 copy-start.4
  492.1 3.5 copy-start.3
  494.8 1.8 copy-start.2
  495.7 1.8 copy-start.1
  496.6 1.8 copy-start
  500.3 1.8 collective-permute-start
  (3 other events, 2.7 us)
where the time goes:
time: 506 us; the launch traced here: 505 us
  waiting for transfers between devices  352 us (70%)
  local copies, waits for them, and re-layouts  90.8 us (18%)
  matrix products  27.5 us (5%)
  other arithmetic  24.5 us (5%)
  starting transfers between devices  7.58 us (1%)
    all_to_all x1, waiting for transfers between devices, shards(): lax.all_to_all(outgoing, 'sample', split_axis=0, concat_axis=0, tiled=True)  351 us
    slice x1, local copies, waits for them, and re-layouts, shards(): prompt_keys[:, 1, kv_head]  55.8 us
    unnamed x70, local copies, waits for them, and re-layouts  21.9 us
    select_n x1, other arithmetic, shards(): jnp.where(sending[:, :, None, None], outgoing, jnp.zeros((), outgoing.dty...  14 us
    gather x1, local copies, waits for them, and re-layouts, shards(): outgoing = local_blocks[local_index]  10.3 us
  transfers between devices with their start and end apart: 2, of which 2 were waited for; matrix products, arithmetic and copies ran while one was open for 2% of the time, Pallas kernels for 0%

commit v1 on v0

v1 whole, which is shorter than its diff:
```python
import functools
import math

import jax
import jax.numpy as jnp
from jax import lax
from jax.experimental import pallas as pl
from jax.experimental.pallas import tpu as pltpu
from jax.sharding import PartitionSpec as P

HEADS = 64
KVH = 8
HD = 128
BLK = 32
QUAD = 4
HPD = KVH // QUAD
GROUP = HEADS // KVH
TILE_BLOCKS = 8
TILE = TILE_BLOCKS * BLK
NEG = -1e30
EXP_SCALE = math.log2(math.e) / math.sqrt(HD)
F32 = jnp.float32
BF16 = jnp.bfloat16
ANY = pl.BlockSpec(memory_space=pl.ANY)
VMEM = pl.BlockSpec(memory_space=pltpu.VMEM)
SMEM = pl.BlockSpec(memory_space=pltpu.SMEM)


def lanes(start, size):
    return pl.ds(pl.multiple_of(start, 128), size)


def params(mib):
    return pltpu.CompilerParams(vmem_limit_bytes=mib << 20)


def cost(flops, nbytes, trans=0):
    return pl.CostEstimate(flops=flops, bytes_accessed=nbytes, transcendentals=trans)


def pack_queries_kernel(q_ref, new_ref, *outs):
    mine = lax.rem(lax.axis_index("sample"), QUAD)
    rows = q_ref.shape[0]
    for k, out in enumerate(outs):
        peer = jnp.bitwise_xor(mine, k)
        for h in range(HPD):
            head = peer * HPD + h
            for g in range(GROUP):
                out[h, g * rows:(g + 1) * rows] = q_ref[:, lanes((head * GROUP + g) * HD, HD)]
            base = GROUP * rows
            out[h, base:base + rows] = new_ref[:, lanes(head * HD, HD)]
            out[h, base + rows:base + 2 * rows] = new_ref[:, lanes((KVH + head) * HD, HD)]


def pack_queries(q2, new2):
    rows = q2.shape[0]
    shape = jax.ShapeDtypeStruct((HPD, (GROUP + 2) * rows, HD), BF16)
    return pl.pallas_call(
        pack_queries_kernel,
        out_shape=[shape] * QUAD,
        in_specs=[VMEM, VMEM],
        out_specs=[VMEM] * QUAD,
        compiler_params=params(32),
        cost_estimate=cost(0, 2 << 20),
        name="pack_queries",
    )(q2, new2)


def pack_kv_kernel(kv_ref, *refs):
    outs, sem = refs[:-1], refs[-1]
    mine = lax.rem(lax.axis_index("sample"), QUAD)
    copies = []
    for h in range(HPD):
        for k in range(1, QUAD):
            head = jnp.bitwise_xor(mine, k) * HPD + h
            out = outs[h * (QUAD - 1) + k - 1]
            for part in range(2):
                copies.append(
                    pltpu.make_async_copy(
                        kv_ref.at[:, lanes((part * KVH + head) * HD, HD)],
                        out.at[:, part * HD:(part + 1) * HD],
                        sem.at[len(copies)],
                    )
                )
    for copy in copies:
        copy.start()
    for copy in copies:
        copy.wait()


def pack_kv(kv2):
    count = HPD * (QUAD - 1)
    shape = jax.ShapeDtypeStruct((kv2.shape[0], 2 * HD), BF16)
    return pl.pallas_call(
        pack_kv_kernel,
        out_shape=[shape] * count,
        in_specs=[ANY],
        out_specs=[ANY] * count,
        scratch_shapes=[pltpu.SemaphoreType.DMA((2 * count,))],
        compiler_params=params(16),
        cost_estimate=cost(0, 6 << 20),
        name="pack_kv",
    )(kv2)


def as_rows(column):
    size = column.shape[0]
    out = []
    for i in range(size // 128):
        block = jnp.broadcast_to(column[i * 128:(i + 1) * 128], (128, 128))
        out.append(block.T[0:1])
    return jnp.concatenate(out, axis=0)


def as_columns(rows):
    out = []
    for i in range(rows.shape[0]):
        out.append(jnp.broadcast_to(rows[i:i + 1], (128, 128)).T)
    return jnp.concatenate(out, axis=0)


def dot_t(a, b):
    return lax.dot_general(a, b, (((1,), (1,)), ((), ())), preferred_element_type=F32)


def attend_kernel(h, offsets, fresh, counts_ref, slots_ref, kv_ref, *refs):
    nsample = lax.axis_size("sample")
    quads = nsample // QUAD
    index = lax.axis_index("sample")
    quad, mine = lax.div(index, QUAD), lax.rem(index, QUAD)
    arrived = refs[:QUAD - 1]
    refs = refs[QUAD - 1:]
    nq = QUAD if fresh else len(offsets)
    queries, refs = refs[:nq], refs[nq:]
    outs, (held, sem) = refs[:-2], refs[-2:]
    blocks = kv_ref.shape[0]

    copies = []
    for part in range(2):
        copies.append(
            pltpu.make_async_copy(
                kv_ref.at[:, :, lanes((part * KVH + mine * HPD + h) * HD, HD)],
                held.at[0:blocks, mine, :, part * HD:(part + 1) * HD],
                sem.at[part],
            )
        )
    for k in range(1, QUAD):
        copies.append(
            pltpu.make_async_copy(
                arrived[k - 1], held.at[0:blocks, jnp.bitwise_xor(mine, k)], sem.at[k + 1]
            )
        )
    for copy in copies:
        copy.start()
    held[blocks:] = jnp.zeros_like(held[blocks:])
    for copy in copies:
        copy.wait()
    flat = held.reshape(held.shape[0] * QUAD * BLK, 2 * HD)

    def local_count(block):
        inside = jnp.clip(lax.rem(block, nsample) - QUAD * quad, 0, QUAD)
        return QUAD * lax.div(block, nsample) + inside

    for n, offset in enumerate(offsets):
        home = lax.rem(quad + offset, quads)
        for pair in range(2):
            slot_pair = jnp.bitwise_xor(lax.div(mine, 2), pair)
            prompt = slots_ref[QUAD * home + 2 * slot_pair]
            start = lax.fori_loop(0, prompt, lambda p, total: total + counts_ref[p], jnp.int32(0))
            low, high = local_count(start), local_count(start + counts_ref[prompt])
            if fresh:
                parts = []
                for half in range(2):
                    msg = queries[2 * pair + half]
                    rows = msg.shape[1] // (GROUP + 2)
                    query = msg[h, 0:GROUP * rows]
                    new_k = msg[h, GROUP * rows:(GROUP + 1) * rows]
                    new_v = msg[h, (GROUP + 1) * rows:]
                    s = dot_t(query, new_k)
                    row = lax.rem(lax.broadcasted_iota(jnp.int32, s.shape, 0), rows)
                    col = lax.broadcasted_iota(jnp.int32, s.shape, 1)
                    steps = fresh
                    seen = (lax.div(row, steps) == lax.div(col, steps)) & (
                        lax.rem(row, steps) >= lax.rem(col, steps)
                    )
                    s = jnp.where(seen, s, NEG)
                    m = jnp.max(s, axis=1, keepdims=True)
                    p = jnp.exp2((s - m) * EXP_SCALE)
                    l = jnp.sum(p, axis=1, keepdims=True)
                    acc = jnp.dot(p.astype(BF16), new_v, preferred_element_type=F32)
                    parts.append((query, m, l, acc))
                query, m, l, acc = (jnp.concatenate(x, axis=0) for x in zip(*parts))
            else:
                query = jnp.concatenate([queries[n][2 * pair], queries[n][2 * pair + 1]], axis=0)
                size = query.shape[0]
                m = jnp.full((size, 1), NEG, F32)
                l = jnp.zeros((size, 1), F32)
                acc = jnp.zeros((size, HD), F32)

            def body(t, carry, query=query, low=low, high=high):
                m, l, acc = carry
                first = low + t * TILE_BLOCKS
                row = pl.multiple_of(first * BLK, BLK)
                k = flat[pl.ds(row, TILE), 0:HD]
                v = flat[pl.ds(row, TILE), HD:2 * HD]
                s = dot_t(query, k)
                col = lax.broadcasted_iota(jnp.int32, s.shape, 1)
                s = jnp.where(col < (high - first) * BLK, s, NEG)
                m_new = jnp.maximum(m, jnp.max(s, axis=1, keepdims=True))
                p = jnp.exp2((s - m_new) * EXP_SCALE)
                alpha = jnp.exp2((m - m_new) * EXP_SCALE)
                l = l * alpha + jnp.sum(p, axis=1, keepdims=True)
                acc = acc * alpha + jnp.dot(p.astype(BF16), v, preferred_element_type=F32)
                return m_new, l, acc

            tiles = lax.div(high - low + TILE_BLOCKS - 1, TILE_BLOCKS)
            m, l, acc = lax.fori_loop(0, tiles, body, (m, l, acc))
            some = l > 0.0
            out = acc / jnp.where(some, l, 1.0)
            lse = jnp.where(some, m * EXP_SCALE + jnp.log(jnp.where(some, l, 1.0)) * math.log2(math.e), NEG)
            if fresh:
                outs[0][pair] = out
                outs[1][pair] = jnp.broadcast_to(lse, out.shape)
            else:
                size = out.shape[0]
                stat = as_rows(lse)
                high_part = stat.astype(BF16)
                rest = stat - high_part.astype(F32)
                mid_part = rest.astype(BF16)
                low_part = (rest - mid_part.astype(F32)).astype(BF16)
                pad = jnp.zeros((16 - 3 * stat.shape[0], HD), F32)
                tail = jnp.concatenate(
                    [high_part.astype(F32), mid_part.astype(F32), low_part.astype(F32), pad], axis=0
                )
                outs[n][pair, 0:size] = out.astype(BF16)
                outs[n][pair, size:size + 16] = tail.astype(BF16)


def attend(h, offsets, fresh, counts, slots, kv3, arrived, queries):
    size = 2 * (queries[0].shape[1] * GROUP // (GROUP + 2) if fresh else queries[0].shape[1])
    if fresh:
        out_shape = [jax.ShapeDtypeStruct((2, size, HD), F32)] * 2
    else:
        out_shape = [jax.ShapeDtypeStruct((2, size + 16, HD), BF16)] * len(offsets)
    blocks = kv3.shape[0]
    work = len(offsets) * 2 * size * blocks * BLK // 2
    return pl.pallas_call(
        functools.partial(attend_kernel, h, offsets, fresh),
        out_shape=out_shape,
        in_specs=[SMEM, SMEM, ANY] + [ANY] * len(arrived) + [VMEM] * len(queries),
        out_specs=[VMEM] * len(out_shape),
        scratch_shapes=[
            pltpu.VMEM((blocks + 2, QUAD, BLK, 2 * HD), BF16),
            pltpu.SemaphoreType.DMA((QUAD + 1,)),
        ],
        compiler_params=params(48),
        cost_estimate=cost(4 * work * HD, 4 << 20, work),
        name="attend_own" if fresh else "attend_others",
    )(counts, slots, kv3, *arrived, *queries)


def finish_kernel(steps, own_ref, own_lse_ref, *refs):
    parts, outs = refs[:-QUAD], refs[-QUAD:]
    size = own_ref.shape[1]
    stats = size // 128
    for pair in range(2):
        values, lses = [own_ref[pair]], [own_lse_ref[pair]]
        for ref in parts:
            values.append(ref[pair, 0:size].astype(F32))
            tail = ref[pair, size:size + 16].astype(F32)
            lses.append(
                as_columns(tail[0:stats] + tail[stats:2 * stats] + tail[2 * stats:3 * stats])
            )
        top = functools.reduce(jnp.maximum, lses)
        total, weight = None, None
        for value, lse in zip(values, lses):
            w = jnp.exp2(lse - top)
            total = value * w if total is None else total + value * w
            weight = w if weight is None else weight + w
        full = total / weight
        rows = size // (2 * GROUP)
        wide = full.reshape(2, GROUP, rows // 8, 8, HD)
        mean = jnp.sum(wide, axis=(0, 2)) * (steps / (2.0 * rows))
        if steps == 4:
            flat = mean.reshape(GROUP * 8, HD)
            lane_row = lax.rem(lax.broadcasted_iota(jnp.int32, flat.shape, 0), 8)
            up, down = pltpu.roll(flat, 4, 0), pltpu.roll(flat, GROUP * 8 - 4, 0)
            flat = flat + jnp.where(lane_row < 4, down, up)
            mean = flat.reshape(GROUP, 8, HD)
        dev = wide - mean[None, :, None]
        flat = mean.reshape(GROUP * 8, HD)
        coarse = flat.astype(BF16).astype(F32)
        lane_row = lax.rem(lax.broadcasted_iota(jnp.int32, flat.shape, 0), 8)
        carried = jnp.where(lane_row < 4, coarse, flat - coarse).astype(BF16)
        dev = dev.reshape(2, size // 2, HD).astype(BF16)
        for half in range(2):
            out = outs[2 * pair + half]
            out[0:size // 2] = dev[half]
            out[size // 2:] = carried


def finish(steps, own, own_lse, parts):
    size = own.shape[1]
    shape = jax.ShapeDtypeStruct((size // 2 + GROUP * 8, HD), BF16)
    return pl.pallas_call(
        functools.partial(finish_kernel, steps),
        out_shape=[shape] * QUAD,
        in_specs=[VMEM] * (2 + len(parts)),
        out_specs=[VMEM] * QUAD,
        compiler_params=params(48),
        cost_estimate=cost(1 << 24, 3 << 20),
        name="finish",
    )(own, own_lse, *parts)


def emit_kernel(*refs):
    msgs, (att_ref, dev_ref) = refs[:-2], refs[-2:]
    mine = lax.rem(lax.axis_index("sample"), QUAD)
    rows = att_ref.shape[0]
    for h in range(HPD):
        for k in range(QUAD):
            msg = msgs[h * QUAD + k]
            head = jnp.bitwise_xor(mine, k) * HPD + h
            for g in range(GROUP):
                dev = msg[g * rows:(g + 1) * rows]
                base = GROUP * rows
                pair = msg[base:].astype(F32)[g * 8:(g + 1) * 8]
                mean = pair + pltpu.roll(pair, 4, 0)
                att = dev.astype(F32).reshape(rows // 8, 8, HD) + mean[None]
                cols = lanes((head * GROUP + g) * HD, HD)
                att_ref[:, cols] = att.reshape(rows, HD).astype(BF16)
                dev_ref[:, cols] = dev


def emit(msgs):
    rows = (msgs[0].shape[0] - GROUP * 8) // GROUP
    shape = jax.ShapeDtypeStruct((rows, HEADS * HD), BF16)
    return pl.pallas_call(
        emit_kernel,
        out_shape=[shape] * 2,
        in_specs=[VMEM] * len(msgs),
        out_specs=[VMEM] * 2,
        compiler_params=params(32),
        cost_estimate=cost(1 << 20, 2 << 20),
        name="emit",
    )(*msgs)


def shards(prompt_kv, prompt_blocks, slot_prompt, queries, new_kv):
    nsample = lax.axis_size("sample")
    quads = nsample // QUAD
    samples, steps, width = queries.shape
    rows = samples * steps

    def across(array, k):
        return lax.ppermute(array, "sample", [(i, i ^ k) for i in range(nsample)])

    def along(array, shift):
        return lax.ppermute(
            array, "sample", [(i, (i + shift * QUAD) % nsample) for i in range(nsample)]
        )

    kv3 = prompt_kv.reshape(prompt_kv.shape[0], BLK, prompt_kv.shape[-1])
    kv2 = kv3.reshape(-1, kv3.shape[-1])
    msgs = pack_queries(queries.reshape(rows, width), new_kv.reshape(rows, new_kv.shape[-1]))
    msgs = [msgs[0]] + [across(msgs[k], k) for k in range(1, QUAD)]
    cut = pack_kv(kv2)
    arrived = [
        [
            across(cut[h * (QUAD - 1) + k - 1], k).reshape(kv3.shape[0], BLK, 2 * HD)
            for k in range(1, QUAD)
        ]
        for h in range(HPD)
    ]
    final = []
    for h in range(HPD):
        own = jnp.stack([m[h, :GROUP * rows] for m in msgs])
        ahead = (quads - 1 + (1 - h % 2)) // 2
        held = {}
        block = own
        for s in range(1, ahead + 1):
            block = along(block, -1)
            held[s] = block
        block = own
        for s in range(1, quads - ahead):
            block = along(block, 1)
            held[quads - s] = block
        offsets = tuple(sorted(held))
        partial = attend(
            h, offsets, 0, prompt_blocks, slot_prompt, kv3, arrived[h], [held[o] for o in offsets]
        )
        back = [along(p, o) for o, p in zip(offsets, partial)]
        mine, mine_lse = attend(
            h, (0,), steps, prompt_blocks, slot_prompt, kv3, arrived[h], msgs
        )
        done = finish(steps, mine, mine_lse, back)
        final.append([done[0]] + [across(done[k], k) for k in range(1, QUAD)])
    attention, deviation = emit([m for per_head in final for m in per_head])
    return attention.reshape(queries.shape), deviation.reshape(queries.shape)


def solution(mesh):
    placed = (
        P("groups", "sample", None, None),
        P("groups"),
        P("groups"),
        P(("groups", "sample"), None, None),
        P(("groups", "sample"), None, None),
    )
    return jax.shard_map(
        shards,
        mesh=mesh,
        in_specs=placed,
        out_specs=(P(("groups", "sample"), None, None), P(("groups", "sample"), None, None)),
        check_vma=False,
    )
```

time: 506 us -> 122 us (0.24)
  the two profiles are of different devices: /device:TPU:19 before, /device:TPU:25 now
where the time goes in v1:
time: 122 us
  Pallas kernels  47.9 us (39%)
  waiting for transfers between devices  36.4 us (30%)
  starting transfers between devices  30.2 us (25%)
  local copies, waits for them, and re-layouts  6.32 us (5%)
    pallas_call x4, Pallas kernels, attend(): pl.pallas_call(functools.partial(attend_kernel, h, offsets, fresh), out_s...  44.8 us
    ppermute x15, waiting for transfers between devices, across(): return lax.ppermute(array, 'sample', [(i, i ^ k) for i in range(nsample)])  23.6 us
    ppermute x12, starting transfers between devices, along(): lax.ppermute(array, 'sample', [(i, (i + shift * QUAD) % nsample) for i in...  15.4 us
    ppermute x15, starting transfers between devices, across(): return lax.ppermute(array, 'sample', [(i, i ^ k) for i in range(nsample)])  14.7 us
    ppermute x12, waiting for transfers between devices, along(): lax.ppermute(array, 'sample', [(i, (i + shift * QUAD) % nsample) for i in...  12.8 us
  transfers between devices with their start and end apart: 27, of which 10 were waited for; matrix products, arithmetic and copies ran while one was open for 0% of the time, Pallas kernels for 39%

profile of v1, /device:TPU:25, one launch (start us, length us, event | category | flops | bytes accessed | tf_op | source)
XLA Modules:
  0.0 121.7 jit_solution(571353905203581502)
XLA Ops:
  0.7 1.2 reshape.41.q_ref
  1.8 0.9 reshape.42.new_ref
  3.7 1.3 %collective-permute-start.4 = (bf16[2,320,128]{2,1,0:T(8,128)(2,1)S(1)}, bf16[2,320,128]{2,1,0:T(8,128)(2,1)S(1)}, u32[]{:S(2)}, u32[]{:S(2)}) collective-permute-start(bf16[2,320,128]{2,1,0:T(8,128)(2,1)S(1)} %get-tuple-element.37), channel_id=1, source_target_pairs={{0,2},{1,3},{2,0},{3,1},{4,6},{5,7},{6,4},{7,5},{8,10},{9,11},{10,... | collective-permute-start | bytes 491528 | tf_op jit(solution)/shard_map/ppermute | solution.py:356
  5.5 4.0 %collective-permute-done.4.refs_5_ = bf16[2,320,128]{2,1,0:T(8,128)(2,1)S(1)} collective-permute-done((bf16[2,320,128]{2,1,0:T(8,128)(2,1)S(1)}, bf16[2,320,128]{2,1,0:T(8,128)(2,1)S(1)}, u32[]{:S(2)}, u32[]{:S(2)}) %collective-permute-start.4) | collective-permute-done | bytes 163872 | tf_op jit(solution)/shard_map/ppermute | solution.py:356
  9.5 3.7 %collective-permute-done.5.refs_6_ = bf16[2,320,128]{2,1,0:T(8,128)(2,1)S(1)} collective-permute-done((bf16[2,320,128]{2,1,0:T(8,128)(2,1)S(1)}, bf16[2,320,128]{2,1,0:T(8,128)(2,1)S(1)}, u32[]{:S(2)}, u32[]{:S(2)}) %collective-permute-start.5) | collective-permute-done | bytes 163872 | tf_op jit(solution)/shard_map/ppermute | solution.py:356
  13.3 2.2 %copy-done = bf16[32,1,32,2048]{3,2,1,0:T(8,128)(2,1)S(1)} copy-done((bf16[32,1,32,2048]{3,2,1,0:T(8,128)(2,1)S(1)}, bf16[32,1,32,2048]{3,2,1,0:T(8,128)(2,1)}, u32[]{:S(2)}) %copy-start) | copy-done | bytes 4194328
  15.5 1.0 pack_kv.1
  16.9 1.3 %collective-permute-start.16 = (bf16[1024,256]{1,0:T(8,128)(2,1)S(1)}, bf16[1024,256]{1,0:T(8,128)(2,1)S(1)}, u32[]{:S(2)}, u32[]{:S(2)}) collective-permute-start(bf16[1024,256]{1,0:T(8,128)(2,1)S(1)} %get-tuple-element.49), channel_id=1, source_target_pairs={{0,2},{1,3},{2,0},{3,1},{4,6},{5,7},{6,4},{7,5},{8,10},{9,11},{10,... | collective-permute-start | bytes 1572872 | tf_op jit(solution)/shard_map/ppermute | solution.py:356
  18.7 1.5 %collective-permute-start.18 = (bf16[4,256,128]{2,1,0:T(8,128)(2,1)S(1)}, bf16[4,256,128]{2,1,0:T(8,128)(2,1)S(1)}, u32[]{:S(2)}, u32[]{:S(2)}) collective-permute-start(bf16[4,256,128]{2,1,0:T(8,128)(2,1)S(1)} %pad_maximum_fusion.1), channel_id=1, source_target_pairs={{0,12},{1,13},{2,14},{3,15},{4,0},{5,1},{6,2},{7,3},{8,4},{9,5},{1... | collective-permute-start | bytes 786440 | tf_op jit(solution)/shard_map/ppermute | solution.py:359
  21.1 7.1 %collective-permute-done.18.refs_3_ = bf16[4,256,128]{2,1,0:T(8,128)(2,1)S(1)} collective-permute-done((bf16[4,256,128]{2,1,0:T(8,128)(2,1)S(1)}, bf16[4,256,128]{2,1,0:T(8,128)(2,1)S(1)}, u32[]{:S(2)}, u32[]{:S(2)}) %collective-permute-start.18) | collective-permute-done | bytes 262176 | tf_op jit(solution)/shard_map/ppermute | solution.py:359
  29.0 4.9 %collective-permute-done.6.refs_3_ = bf16[4,256,128]{2,1,0:T(8,128)(2,1)S(1)} collective-permute-done((bf16[4,256,128]{2,1,0:T(8,128)(2,1)S(1)}, bf16[4,256,128]{2,1,0:T(8,128)(2,1)S(1)}, u32[]{:S(2)}, u32[]{:S(2)}) %collective-permute-start.6) | collective-permute-done | bytes 262176 | tf_op jit(solution)/shard_map/ppermute | solution.py:359
  33.9 1.5 %collective-permute-start = (bf16[1024,256]{1,0:T(8,128)(2,1)S(1)}, bf16[1024,256]{1,0:T(8,128)(2,1)S(1)}, u32[]{:S(2)}, u32[]{:S(2)}) collective-permute-start(bf16[1024,256]{1,0:T(8,128)(2,1)S(1)} %get-tuple-element.32), channel_id=1, source_target_pairs={{0,1},{1,0},{2,3},{3,2},{4,5},{5,4},{6,7},{7,6},{8,9},{9,8},{10,11... | collective-permute-start | bytes 1572872 | tf_op jit(solution)/shard_map/ppermute | solution.py:356
  35.4 1.3 %collective-permute-start.1 = (bf16[1024,256]{1,0:T(8,128)(2,1)S(1)}, bf16[1024,256]{1,0:T(8,128)(2,1)S(1)}, u32[]{:S(2)}, u32[]{:S(2)}) collective-permute-start(bf16[1024,256]{1,0:T(8,128)(2,1)S(1)} %get-tuple-element.33), channel_id=1, source_target_pairs={{0,2},{1,3},{2,0},{3,1},{4,6},{5,7},{6,4},{7,5},{8,10},{9,11},{10,... | collective-permute-start | bytes 1572872 | tf_op jit(solution)/shard_map/ppermute | solution.py:356
  37.1 5.3 %collective-permute-done.17 = bf16[1024,256]{1,0:T(8,128)(2,1)S(1)} collective-permute-done((bf16[1024,256]{1,0:T(8,128)(2,1)S(1)}, bf16[1024,256]{1,0:T(8,128)(2,1)S(1)}, u32[]{:S(2)}, u32[]{:S(2)}) %collective-permute-start.17) | collective-permute-done | bytes 524320 | tf_op jit(solution)/shard_map/ppermute | solution.py:356
  42.3 1.3 %collective-permute-start.8 = (bf16[4,256,128]{2,1,0:T(8,128)(2,1)S(1)}, bf16[4,256,128]{2,1,0:T(8,128)(2,1)S(1)}, u32[]{:S(2)}, u32[]{:S(2)}) collective-permute-start(bf16[4,256,128]{2,1,0:T(8,128)(2,1)S(1)} %pad_maximum_fusion), channel_id=1, source_target_pairs={{0,4},{1,5},{2,6},{3,7},{4,8},{5,9},{6,10},{7,11},{8,12},{9,13},{1... | collective-permute-start | bytes 786440 | tf_op jit(solution)/shard_map/ppermute | solution.py:359
  43.9 9.6 %attend_others.3 = (bf16[2,528,128]{2,1,0:T(8,128)(2,1)S(1)}, bf16[2,528,128]{2,1,0:T(8,128)(2,1)S(1)}, bf16[2,528,128]{2,1,0:T(8,128)(2,1)S(1)}) custom-call(s32[8]{0:T(128)S(1)} %copy-done.1, s32[16]{0:T(128)S(1)} %copy-done.2, bf16[32,32,2048]{2,1,0:T(8,128)(2,1)} %bitcast.8, bf16[32,32,256]{2,1,0:T(8,128)(2,1)S(1)} %bitcast.13, ...), custom_call_target="tpu_custom_call" | custom-call | flops 805306368 | bytes 4194304 | tf_op jit(solution)/shard_map/attend_others/pallas_call | solution.py:247
  53.4 4.8 %collective-permute-start.21 = (bf16[2,528,128]{2,1,0:T(8,128)(2,1)S(1)}, bf16[2,528,128]{2,1,0:T(8,128)(2,1)S(1)}, u32[]{:S(2)}, u32[]{:S(2)}) collective-permute-start(bf16[2,528,128]{2,1,0:T(8,128)(2,1)S(1)} %get-tuple-element.53), channel_id=1, source_target_pairs={{0,4},{1,5},{2,6},{3,7},{4,8},{5,9},{6,10},{7,11},{8,12},{9,13},{1... | collective-permute-start | bytes 811016 | tf_op jit(solution)/shard_map/ppermute | solution.py:359
  58.6 6.0 %collective-permute-done.2 = bf16[1024,256]{1,0:T(8,128)(2,1)S(1)} collective-permute-done((bf16[1024,256]{1,0:T(8,128)(2,1)S(1)}, bf16[1024,256]{1,0:T(8,128)(2,1)S(1)}, u32[]{:S(2)}, u32[]{:S(2)}) %collective-permute-start.2) | collective-permute-done | bytes 524320 | tf_op jit(solution)/shard_map/ppermute | solution.py:356
  64.6 9.7 %attend_others.2 = (bf16[2,528,128]{2,1,0:T(8,128)(2,1)S(1)}, bf16[2,528,128]{2,1,0:T(8,128)(2,1)S(1)}, bf16[2,528,128]{2,1,0:T(8,128)(2,1)S(1)}) custom-call(s32[8]{0:T(128)S(1)} %copy-done.1, s32[16]{0:T(128)S(1)} %copy-done.2, bf16[32,32,2048]{2,1,0:T(8,128)(2,1)} %bitcast.9, bf16[32,32,256]{2,1,0:T(8,128)(2,1)S(1)} %bitcast.19, ...), custom_call_target="tpu_custom_call" | custom-call | flops 805306368 | bytes 4194304 | tf_op jit(solution)/shard_map/attend_others/pallas_call | solution.py:247
  74.3 3.0 %collective-permute-start.10 = (bf16[2,528,128]{2,1,0:T(8,128)(2,1)S(1)}, bf16[2,528,128]{2,1,0:T(8,128)(2,1)S(1)}, u32[]{:S(2)}, u32[]{:S(2)}) collective-permute-start(bf16[2,528,128]{2,1,0:T(8,128)(2,1)S(1)} %get-tuple-element.42), channel_id=1, source_target_pairs={{0,8},{1,9},{2,10},{3,11},{4,12},{5,13},{6,14},{7,15},{8,0},{9,1},... | collective-permute-start | bytes 811016 | tf_op jit(solution)/shard_map/ppermute | solution.py:359
  77.7 2.9 %collective-permute-start.9 = (bf16[2,528,128]{2,1,0:T(8,128)(2,1)S(1)}, bf16[2,528,128]{2,1,0:T(8,128)(2,1)S(1)}, u32[]{:S(2)}, u32[]{:S(2)}) collective-permute-start(bf16[2,528,128]{2,1,0:T(8,128)(2,1)S(1)} %get-tuple-element.41), channel_id=1, source_target_pairs={{0,4},{1,5},{2,6},{3,7},{4,8},{5,9},{6,10},{7,11},{8,12},{9,13},{1... | collective-permute-start | bytes 811016 | tf_op jit(solution)/shard_map/ppermute | solution.py:359
  80.6 12.7 %attend_own.3 = (f32[2,512,128]{2,1,0:T(8,128)S(1)}, f32[2,512,128]{2,1,0:T(8,128)S(1)}) custom-call(s32[8]{0:T(128)S(1)} %copy-done.1, s32[16]{0:T(128)S(1)} %copy-done.2, bf16[32,32,2048]{2,1,0:T(8,128)(2,1)} %bitcast.10, bf16[32,32,256]{2,1,0:T(8,128)(2,1)S(1)} %bitcast.14, bf16[32,32,256]{2,1,0:T(8,128)(2,1)S(1)} %bitcast.16, ...), custom_call_target="tpu_custom_call" | custom-call | flops 268435456 | bytes 4194304 | tf_op jit(solution)/shard_map/attend_own/pallas_call | solution.py:247
  94.3 3.0 %collective-permute-start.24 = (bf16[320,128]{1,0:T(8,128)(2,1)S(1)}, bf16[320,128]{1,0:T(8,128)(2,1)S(1)}, u32[]{:S(2)}, u32[]{:S(2)}) collective-permute-start(bf16[320,128]{1,0:T(8,128)(2,1)S(1)} %get-tuple-element.57), channel_id=1, source_target_pairs={{0,1},{1,0},{2,3},{3,2},{4,5},{5,4},{6,7},{7,6},{8,9},{9,8},{10,11... | collective-permute-start | bytes 245768 | tf_op jit(solution)/shard_map/ppermute | solution.py:356
  97.3 12.7 %attend_own.2 = (f32[2,512,128]{2,1,0:T(8,128)S(1)}, f32[2,512,128]{2,1,0:T(8,128)S(1)}) custom-call(s32[8]{0:T(128)S(1)} %copy-done.1, s32[16]{0:T(128)S(1)} %copy-done.2, bf16[32,32,2048]{2,1,0:T(8,128)(2,1)} %bitcast.11, bf16[32,32,256]{2,1,0:T(8,128)(2,1)S(1)} %bitcast.20, bf16[32,32,256]{2,1,0:T(8,128)(2,1)S(1)} %bitcast.22, ...), custom_call_target="tpu_custom_call" | custom-call | flops 268435456 | bytes 4194304 | tf_op jit(solution)/shard_map/attend_own/pallas_call | solution.py:247
  110.0 1.3 %collective-permute-start.25 = (bf16[320,128]{1,0:T(8,128)(2,1)S(1)}, bf16[320,128]{1,0:T(8,128)(2,1)S(1)}, u32[]{:S(2)}, u32[]{:S(2)}) collective-permute-start(bf16[320,128]{1,0:T(8,128)(2,1)S(1)} %get-tuple-element.58), channel_id=1, source_target_pairs={{0,2},{1,3},{2,0},{3,1},{4,6},{5,7},{6,4},{7,5},{8,10},{9,11},{10,... | collective-permute-start | bytes 245768 | tf_op jit(solution)/shard_map/ppermute | solution.py:356
  111.7 0.9 finish.2
  112.9 1.2 %collective-permute-start.13 = (bf16[320,128]{1,0:T(8,128)(2,1)S(1)}, bf16[320,128]{1,0:T(8,128)(2,1)S(1)}, u32[]{:S(2)}, u32[]{:S(2)}) collective-permute-start(bf16[320,128]{1,0:T(8,128)(2,1)S(1)} %get-tuple-element.46), channel_id=1, source_target_pairs={{0,2},{1,3},{2,0},{3,1},{4,6},{5,7},{6,4},{7,5},{8,10},{9,11},{10,... | collective-permute-start | bytes 245768 | tf_op jit(solution)/shard_map/ppermute | solution.py:356
  114.8 1.5 %collective-permute-done.26.refs_7_ = bf16[320,128]{1,0:T(8,128)(2,1)S(1)} collective-permute-done((bf16[320,128]{1,0:T(8,128)(2,1)S(1)}, bf16[320,128]{1,0:T(8,128)(2,1)S(1)}, u32[]{:S(2)}, u32[]{:S(2)}) %collective-permute-start.26) | collective-permute-done | bytes 81952 | tf_op jit(solution)/shard_map/ppermute | solution.py:356
  116.3 1.3 %collective-permute-done.13.refs_2_ = bf16[320,128]{1,0:T(8,128)(2,1)S(1)} collective-permute-done((bf16[320,128]{1,0:T(8,128)(2,1)S(1)}, bf16[320,128]{1,0:T(8,128)(2,1)S(1)}, u32[]{:S(2)}, u32[]{:S(2)}) %collective-permute-start.13) | collective-permute-done | bytes 81952 | tf_op jit(solution)/shard_map/ppermute | solution.py:356
  117.7 1.8 %collective-permute-done.14.refs_3_ = bf16[320,128]{1,0:T(8,128)(2,1)S(1)} collective-permute-done((bf16[320,128]{1,0:T(8,128)(2,1)S(1)}, bf16[320,128]{1,0:T(8,128)(2,1)S(1)}, u32[]{:S(2)}, u32[]{:S(2)}) %collective-permute-start.14) | collective-permute-done | bytes 81952 | tf_op jit(solution)/shard_map/ppermute | solution.py:356
  119.7 1.0 reshape.46
  120.7 1.0 reshape.47
  (47 shorter events, 8.0 us)
Async XLA Ops:
  0.6 43.2 %copy-start.1 = (s32[8]{0:T(128)S(1)}, s32[8]{0:T(128)}, u32[]{:S(2)}) copy-start(s32[8]{0:T(128)} %counts_ref.7) | copy-start | bytes 100
  0.6 43.2 %copy-start.2 = (s32[16]{0:T(128)S(1)}, s32[16]{0:T(128)}, u32[]{:S(2)}) copy-start(s32[16]{0:T(128)} %slots_ref.7) | copy-start | bytes 196
  3.0 2.5 %collective-permute-start.3 = (bf16[2,320,128]{2,1,0:T(8,128)(2,1)S(1)}, bf16[2,320,128]{2,1,0:T(8,128)(2,1)S(1)}, u32[]{:S(2)}, u32[]{:S(2)}) collective-permute-start(bf16[2,320,128]{2,1,0:T(8,128)(2,1)S(1)} %get-tuple-element.36), channel_id=1, source_target_pairs={{0,1},{1,0},{2,3},{3,2},{4,5},{5,4},{6,7},{7,6},{8,9},{9,8},{10,11... | collective-permute-start | bytes 491528 | tf_op jit(solution)/shard_map/ppermute | solution.py:356
  3.7 5.8 %collective-permute-start.4 = (bf16[2,320,128]{2,1,0:T(8,128)(2,1)S(1)}, bf16[2,320,128]{2,1,0:T(8,128)(2,1)S(1)}, u32[]{:S(2)}, u32[]{:S(2)}) collective-permute-start(bf16[2,320,128]{2,1,0:T(8,128)(2,1)S(1)} %get-tuple-element.37), channel_id=1, source_target_pairs={{0,2},{1,3},{2,0},{3,1},{4,6},{5,7},{6,4},{7,5},{8,10},{9,11},{10,... | collective-permute-start | bytes 491528 | tf_op jit(solution)/shard_map/ppermute | solution.py:356
  5.0 8.2 %collective-permute-start.5 = (bf16[2,320,128]{2,1,0:T(8,128)(2,1)S(1)}, bf16[2,320,128]{2,1,0:T(8,128)(2,1)S(1)}, u32[]{:S(2)}, u32[]{:S(2)}) collective-permute-start(bf16[2,320,128]{2,1,0:T(8,128)(2,1)S(1)} %get-tuple-element.38), channel_id=1, source_target_pairs={{0,3},{1,2},{2,1},{3,0},{4,7},{5,6},{6,5},{7,4},{8,11},{9,10},{10,... | collective-permute-start | bytes 491528 | tf_op jit(solution)/shard_map/ppermute | solution.py:356
  13.2 7.7 %collective-permute-start.19 = (bf16[4,256,128]{2,1,0:T(8,128)(2,1)S(1)}, bf16[4,256,128]{2,1,0:T(8,128)(2,1)S(1)}, u32[]{:S(2)}, u32[]{:S(2)}) collective-permute-start(bf16[4,256,128]{2,1,0:T(8,128)(2,1)S(1)} %pad_maximum_fusion.1), channel_id=1, source_target_pairs={{0,4},{1,5},{2,6},{3,7},{4,8},{5,9},{6,10},{7,11},{8,12},{9,13},{1... | collective-permute-start | bytes 786440 | tf_op jit(solution)/shard_map/ppermute | solution.py:359
  13.3 2.2 %copy-start = (bf16[32,1,32,2048]{3,2,1,0:T(8,128)(2,1)S(1)}, bf16[32,1,32,2048]{3,2,1,0:T(8,128)(2,1)}, u32[]{:S(2)}) copy-start(bf16[32,1,32,2048]{3,2,1,0:T(8,128)(2,1)} %param.5) | copy-start | bytes 12582916
  16.5 19.0 %collective-permute-start.15 = (bf16[1024,256]{1,0:T(8,128)(2,1)S(1)}, bf16[1024,256]{1,0:T(8,128)(2,1)S(1)}, u32[]{:S(2)}, u32[]{:S(2)}) collective-permute-start(bf16[1024,256]{1,0:T(8,128)(2,1)S(1)} %get-tuple-element.48), channel_id=1, source_target_pairs={{0,1},{1,0},{2,3},{3,2},{4,5},{5,4},{6,7},{7,6},{8,9},{9,8},{10,11... | collective-permute-start | bytes 1572872 | tf_op jit(solution)/shard_map/ppermute | solution.py:356
  16.9 19.8 %collective-permute-start.16 = (bf16[1024,256]{1,0:T(8,128)(2,1)S(1)}, bf16[1024,256]{1,0:T(8,128)(2,1)S(1)}, u32[]{:S(2)}, u32[]{:S(2)}) collective-permute-start(bf16[1024,256]{1,0:T(8,128)(2,1)S(1)} %get-tuple-element.49), channel_id=1, source_target_pairs={{0,2},{1,3},{2,0},{3,1},{4,6},{5,7},{6,4},{7,5},{8,10},{9,11},{10,... | collective-permute-start | bytes 1572872 | tf_op jit(solution)/shard_map/ppermute | solution.py:356
  18.2 24.1 %collective-permute-start.17 = (bf16[1024,256]{1,0:T(8,128)(2,1)S(1)}, bf16[1024,256]{1,0:T(8,128)(2,1)S(1)}, u32[]{:S(2)}, u32[]{:S(2)}) collective-permute-start(bf16[1024,256]{1,0:T(8,128)(2,1)S(1)} %get-tuple-element.50), channel_id=1, source_target_pairs={{0,3},{1,2},{2,1},{3,0},{4,7},{5,6},{6,5},{7,4},{8,11},{9,10},{10,... | collective-permute-start | bytes 1572872 | tf_op jit(solution)/shard_map/ppermute | solution.py:356
  18.7 9.6 %collective-permute-start.18 = (bf16[4,256,128]{2,1,0:T(8,128)(2,1)S(1)}, bf16[4,256,128]{2,1,0:T(8,128)(2,1)S(1)}, u32[]{:S(2)}, u32[]{:S(2)}) collective-permute-start(bf16[4,256,128]{2,1,0:T(8,128)(2,1)S(1)} %pad_maximum_fusion.1), channel_id=1, source_target_pairs={{0,12},{1,13},{2,14},{3,15},{4,0},{5,1},{6,2},{7,3},{8,4},{9,5},{1... | collective-permute-start | bytes 786440 | tf_op jit(solution)/shard_map/ppermute | solution.py:359
  20.9 12.9 %collective-permute-start.6 = (bf16[4,256,128]{2,1,0:T(8,128)(2,1)S(1)}, bf16[4,256,128]{2,1,0:T(8,128)(2,1)S(1)}, u32[]{:S(2)}, u32[]{:S(2)}) collective-permute-start(bf16[4,256,128]{2,1,0:T(8,128)(2,1)S(1)} %pad_maximum_fusion), channel_id=1, source_target_pairs={{0,12},{1,13},{2,14},{3,15},{4,0},{5,1},{6,2},{7,3},{8,4},{9,5},{1... | collective-permute-start | bytes 786440 | tf_op jit(solution)/shard_map/ppermute | solution.py:359
  28.2 15.4 %collective-permute-start.20 = (bf16[4,256,128]{2,1,0:T(8,128)(2,1)S(1)}, bf16[4,256,128]{2,1,0:T(8,128)(2,1)S(1)}, u32[]{:S(2)}, u32[]{:S(2)}) collective-permute-start(bf16[4,256,128]{2,1,0:T(8,128)(2,1)S(1)} %collective-permute-done.19.refs_5_), channel_id=1, source_target_pairs={{0,4},{1,5},{2,6},{3,7},{4,8},{5,9},{6,10},{7,11},{8,12},{9,13},{1... | collective-permute-start | bytes 786440 | tf_op jit(solution)/shard_map/ppermute | solution.py:359
  33.9 24.3 %collective-permute-start = (bf16[1024,256]{1,0:T(8,128)(2,1)S(1)}, bf16[1024,256]{1,0:T(8,128)(2,1)S(1)}, u32[]{:S(2)}, u32[]{:S(2)}) collective-permute-start(bf16[1024,256]{1,0:T(8,128)(2,1)S(1)} %get-tuple-element.32), channel_id=1, source_target_pairs={{0,1},{1,0},{2,3},{3,2},{4,5},{5,4},{6,7},{7,6},{8,9},{9,8},{10,11... | collective-permute-start | bytes 1572872 | tf_op jit(solution)/shard_map/ppermute | solution.py:356
  35.4 22.8 %collective-permute-start.1 = (bf16[1024,256]{1,0:T(8,128)(2,1)S(1)}, bf16[1024,256]{1,0:T(8,128)(2,1)S(1)}, u32[]{:S(2)}, u32[]{:S(2)}) collective-permute-start(bf16[1024,256]{1,0:T(8,128)(2,1)S(1)} %get-tuple-element.33), channel_id=1, source_target_pairs={{0,2},{1,3},{2,0},{3,1},{4,6},{5,7},{6,4},{7,5},{8,10},{9,11},{10,... | collective-permute-start | bytes 1572872 | tf_op jit(solution)/shard_map/ppermute | solution.py:356
  36.7 27.9 %collective-permute-start.2 = (bf16[1024,256]{1,0:T(8,128)(2,1)S(1)}, bf16[1024,256]{1,0:T(8,128)(2,1)S(1)}, u32[]{:S(2)}, u32[]{:S(2)}) collective-permute-start(bf16[1024,256]{1,0:T(8,128)(2,1)S(1)} %get-tuple-element.34), channel_id=1, source_target_pairs={{0,3},{1,2},{2,1},{3,0},{4,7},{5,6},{6,5},{7,4},{8,11},{9,10},{10,... | collective-permute-start | bytes 1572872 | tf_op jit(solution)/shard_map/ppermute | solution.py:356
  42.3 11.1 %collective-permute-start.8 = (bf16[4,256,128]{2,1,0:T(8,128)(2,1)S(1)}, bf16[4,256,128]{2,1,0:T(8,128)(2,1)S(1)}, u32[]{:S(2)}, u32[]{:S(2)}) collective-permute-start(bf16[4,256,128]{2,1,0:T(8,128)(2,1)S(1)} %pad_maximum_fusion), channel_id=1, source_target_pairs={{0,4},{1,5},{2,6},{3,7},{4,8},{5,9},{6,10},{7,11},{8,12},{9,13},{1... | collective-permute-start | bytes 786440 | tf_op jit(solution)/shard_map/ppermute | solution.py:359
  43.6 21.0 %collective-permute-start.7 = (bf16[4,256,128]{2,1,0:T(8,128)(2,1)S(1)}, bf16[4,256,128]{2,1,0:T(8,128)(2,1)S(1)}, u32[]{:S(2)}, u32[]{:S(2)}) collective-permute-start(bf16[4,256,128]{2,1,0:T(8,128)(2,1)S(1)} %collective-permute-done.6.refs_3_), channel_id=1, source_target_pairs={{0,12},{1,13},{2,14},{3,15},{4,0},{5,1},{6,2},{7,3},{8,4},{9,5},{1... | collective-permute-start | bytes 786440 | tf_op jit(solution)/shard_map/ppermute | solution.py:359
  53.4 24.3 %collective-permute-start.21 = (bf16[2,528,128]{2,1,0:T(8,128)(2,1)S(1)}, bf16[2,528,128]{2,1,0:T(8,128)(2,1)S(1)}, u32[]{:S(2)}, u32[]{:S(2)}) collective-permute-start(bf16[2,528,128]{2,1,0:T(8,128)(2,1)S(1)} %get-tuple-element.53), channel_id=1, source_target_pairs={{0,4},{1,5},{2,6},{3,7},{4,8},{5,9},{6,10},{7,11},{8,12},{9,13},{1... | collective-permute-start | bytes 811016 | tf_op jit(solution)/shard_map/ppermute | solution.py:359
  58.2 35.2 %collective-permute-start.22 = (bf16[2,528,128]{2,1,0:T(8,128)(2,1)S(1)}, bf16[2,528,128]{2,1,0:T(8,128)(2,1)S(1)}, u32[]{:S(2)}, u32[]{:S(2)}) collective-permute-start(bf16[2,528,128]{2,1,0:T(8,128)(2,1)S(1)} %get-tuple-element.54), channel_id=1, source_target_pairs={{0,8},{1,9},{2,10},{3,11},{4,12},{5,13},{6,14},{7,15},{8,0},{9,1},... | collective-permute-start | bytes 811016 | tf_op jit(solution)/shard_map/ppermute | solution.py:359
  58.2 35.2 %collective-permute-start.23 = (bf16[2,528,128]{2,1,0:T(8,128)(2,1)S(1)}, bf16[2,528,128]{2,1,0:T(8,128)(2,1)S(1)}, u32[]{:S(2)}, u32[]{:S(2)}) collective-permute-start(bf16[2,528,128]{2,1,0:T(8,128)(2,1)S(1)} %get-tuple-element.55), channel_id=1, source_target_pairs={{0,12},{1,13},{2,14},{3,15},{4,0},{5,1},{6,2},{7,3},{8,4},{9,5},{1... | collective-permute-start | bytes 811016 | tf_op jit(solution)/shard_map/ppermute | solution.py:359
  74.3 37.0 %collective-permute-start.10 = (bf16[2,528,128]{2,1,0:T(8,128)(2,1)S(1)}, bf16[2,528,128]{2,1,0:T(8,128)(2,1)S(1)}, u32[]{:S(2)}, u32[]{:S(2)}) collective-permute-start(bf16[2,528,128]{2,1,0:T(8,128)(2,1)S(1)} %get-tuple-element.42), channel_id=1, source_target_pairs={{0,8},{1,9},{2,10},{3,11},{4,12},{5,13},{6,14},{7,15},{8,0},{9,1},... | collective-permute-start | bytes 811016 | tf_op jit(solution)/shard_map/ppermute | solution.py:359
  77.3 34.4 %collective-permute-start.11 = (bf16[2,528,128]{2,1,0:T(8,128)(2,1)S(1)}, bf16[2,528,128]{2,1,0:T(8,128)(2,1)S(1)}, u32[]{:S(2)}, u32[]{:S(2)}) collective-permute-start(bf16[2,528,128]{2,1,0:T(8,128)(2,1)S(1)} %get-tuple-element.43), channel_id=1, source_target_pairs={{0,12},{1,13},{2,14},{3,15},{4,0},{5,1},{6,2},{7,3},{8,4},{9,5},{1... | collective-permute-start | bytes 811016 | tf_op jit(solution)/shard_map/ppermute | solution.py:359
  77.7 34.0 %collective-permute-start.9 = (bf16[2,528,128]{2,1,0:T(8,128)(2,1)S(1)}, bf16[2,528,128]{2,1,0:T(8,128)(2,1)S(1)}, u32[]{:S(2)}, u32[]{:S(2)}) collective-permute-start(bf16[2,528,128]{2,1,0:T(8,128)(2,1)S(1)} %get-tuple-element.41), channel_id=1, source_target_pairs={{0,4},{1,5},{2,6},{3,7},{4,8},{5,9},{6,10},{7,11},{8,12},{9,13},{1... | collective-permute-start | bytes 811016 | tf_op jit(solution)/shard_map/ppermute | solution.py:359
  94.3 19.9 %collective-permute-start.24 = (bf16[320,128]{1,0:T(8,128)(2,1)S(1)}, bf16[320,128]{1,0:T(8,128)(2,1)S(1)}, u32[]{:S(2)}, u32[]{:S(2)}) collective-permute-start(bf16[320,128]{1,0:T(8,128)(2,1)S(1)} %get-tuple-element.57), channel_id=1, source_target_pairs={{0,1},{1,0},{2,3},{3,2},{4,5},{5,4},{6,7},{7,6},{8,9},{9,8},{10,11... | collective-permute-start | bytes 245768 | tf_op jit(solution)/shard_map/ppermute | solution.py:356
  110.0 4.8 %collective-permute-start.25 = (bf16[320,128]{1,0:T(8,128)(2,1)S(1)}, bf16[320,128]{1,0:T(8,128)(2,1)S(1)}, u32[]{:S(2)}, u32[]{:S(2)}) collective-permute-start(bf16[320,128]{1,0:T(8,128)(2,1)S(1)} %get-tuple-element.58), channel_id=1, source_target_pairs={{0,2},{1,3},{2,0},{3,1},{4,6},{5,7},{6,4},{7,5},{8,10},{9,11},{10,... | collective-permute-start | bytes 245768 | tf_op jit(solution)/shard_map/ppermute | solution.py:356
  111.3 5.1 %collective-permute-start.26 = (bf16[320,128]{1,0:T(8,128)(2,1)S(1)}, bf16[320,128]{1,0:T(8,128)(2,1)S(1)}, u32[]{:S(2)}, u32[]{:S(2)}) collective-permute-start(bf16[320,128]{1,0:T(8,128)(2,1)S(1)} %get-tuple-element.59), channel_id=1, source_target_pairs={{0,3},{1,2},{2,1},{3,0},{4,7},{5,6},{6,5},{7,4},{8,11},{9,10},{10,... | collective-permute-start | bytes 245768 | tf_op jit(solution)/shard_map/ppermute | solution.py:356
  112.6 3.7 %collective-permute-start.12 = (bf16[320,128]{1,0:T(8,128)(2,1)S(1)}, bf16[320,128]{1,0:T(8,128)(2,1)S(1)}, u32[]{:S(2)}, u32[]{:S(2)}) collective-permute-start(bf16[320,128]{1,0:T(8,128)(2,1)S(1)} %get-tuple-element.45), channel_id=1, source_target_pairs={{0,1},{1,0},{2,3},{3,2},{4,5},{5,4},{6,7},{7,6},{8,9},{9,8},{10,11... | collective-permute-start | bytes 245768 | tf_op jit(solution)/shard_map/ppermute | solution.py:356
  112.9 4.8 %collective-permute-start.13 = (bf16[320,128]{1,0:T(8,128)(2,1)S(1)}, bf16[320,128]{1,0:T(8,128)(2,1)S(1)}, u32[]{:S(2)}, u32[]{:S(2)}) collective-permute-start(bf16[320,128]{1,0:T(8,128)(2,1)S(1)} %get-tuple-element.46), channel_id=1, source_target_pairs={{0,2},{1,3},{2,0},{3,1},{4,6},{5,7},{6,4},{7,5},{8,10},{9,11},{10,... | collective-permute-start | bytes 245768 | tf_op jit(solution)/shard_map/ppermute | solution.py:356
  114.1 5.4 %collective-permute-start.14 = (bf16[320,128]{1,0:T(8,128)(2,1)S(1)}, bf16[320,128]{1,0:T(8,128)(2,1)S(1)}, u32[]{:S(2)}, u32[]{:S(2)}) collective-permute-start(bf16[320,128]{1,0:T(8,128)(2,1)S(1)} %get-tuple-element.47), channel_id=1, source_target_pairs={{0,3},{1,2},{2,1},{3,0},{4,7},{5,6},{6,5},{7,4},{8,11},{9,10},{10,... | collective-permute-start | bytes 245768 | tf_op jit(solution)/shard_map/ppermute | solution.py:356

commit v2 on v0

v2 whole, which is shorter than its diff:
```python
import functools
import math

import jax
import jax.numpy as jnp
from jax import lax
from jax.experimental import pallas as pl
from jax.experimental.pallas import tpu as pltpu
from jax.sharding import PartitionSpec as P

HEADS = 64
KVH = 8
HD = 128
BLK = 32
QUAD = 4
HPD = KVH // QUAD
GROUP = HEADS // KVH
TILE_BLOCKS = 8
TILE = TILE_BLOCKS * BLK
STAT_ROWS = 16
NEG = -1e30
LOG2E = math.log2(math.e)
EXP_SCALE = LOG2E / math.sqrt(HD)
F32 = jnp.float32
BF16 = jnp.bfloat16
ANY = pl.BlockSpec(memory_space=pl.ANY)
VMEM = pl.BlockSpec(memory_space=pltpu.VMEM)
SMEM = pl.BlockSpec(memory_space=pltpu.SMEM)


def params(mib):
    return pltpu.CompilerParams(vmem_limit_bytes=mib << 20)


def cost(flops, nbytes, trans=0):
    return pl.CostEstimate(flops=flops, bytes_accessed=nbytes, transcendentals=trans)


def pack_queries_kernel(q_ref, new_ref, out):
    rows = q_ref.shape[0] * q_ref.shape[1]

    def column(ref, head):
        return ref[:, :, head * HD:(head + 1) * HD].astype(F32).reshape(rows, HD).astype(BF16)

    for p in range(QUAD):
        for h in range(HPD):
            head = p * HPD + h
            for g in range(GROUP):
                out[p, h, g * rows:(g + 1) * rows] = column(q_ref, head * GROUP + g)
            base = GROUP * rows
            out[p, h, base:base + rows] = column(new_ref, head)
            out[p, h, base + rows:base + 2 * rows] = column(new_ref, KVH + head)


def pack_queries(queries, new_kv):
    rows = queries.shape[0] * queries.shape[1]
    return pl.pallas_call(
        pack_queries_kernel,
        out_shape=jax.ShapeDtypeStruct((QUAD, HPD, (GROUP + 2) * rows, HD), BF16),
        in_specs=[VMEM, VMEM],
        out_specs=VMEM,
        compiler_params=params(32),
        cost_estimate=cost(0, 2 << 20),
        name="pack_queries",
    )(queries, new_kv)


def pack_kv_kernel(kv_ref, *refs):
    outs, sem = refs[:-1], refs[-1]
    copies = []
    for h in range(HPD):
        for p in range(QUAD):
            for part in range(2):
                first = (part * KVH + p * HPD + h) * HD
                copies.append(
                    pltpu.make_async_copy(
                        kv_ref.at[:, first:first + HD],
                        outs[h].at[p, :, part * HD:(part + 1) * HD],
                        sem.at[len(copies)],
                    )
                )
    for copy in copies:
        copy.start()
    for copy in copies:
        copy.wait()


def pack_kv(kv2):
    return pl.pallas_call(
        pack_kv_kernel,
        out_shape=[jax.ShapeDtypeStruct((QUAD, kv2.shape[0], 2 * HD), BF16)] * HPD,
        in_specs=[ANY],
        out_specs=[ANY] * HPD,
        scratch_shapes=[pltpu.SemaphoreType.DMA((2 * QUAD * HPD,))],
        compiler_params=params(56),
        cost_estimate=cost(0, 8 << 20),
        name="pack_kv",
    )(kv2)


def scores_of(keys, query):
    return lax.dot_general(keys, query, (((1,), (1,)), ((), ())), preferred_element_type=F32)


def values_by(values, weights):
    return lax.dot_general(values, weights, (((0,), (0,)), ((), ())), preferred_element_type=F32)


def attend_kernel(h, steps, counts_ref, slots_ref, kv_ref, fresh_ref, q_ref, out_ref, held, sem):
    nsample = lax.axis_size("sample")
    quads = nsample // QUAD
    quad = lax.div(lax.axis_index("sample"), QUAD)
    blocks = kv_ref.shape[1]
    size = q_ref.shape[2]
    rows = size // GROUP

    copies = [
        pltpu.make_async_copy(kv_ref.at[b], held.at[0:blocks, b], sem.at[b]) for b in range(QUAD)
    ]
    for copy in copies:
        copy.start()
    held[blocks:] = jnp.zeros_like(held[blocks:])
    for copy in copies:
        copy.wait()
    flat = held.reshape(held.shape[0] * QUAD * BLK, 2 * HD)

    def local_count(block):
        inside = jnp.clip(lax.rem(block, nsample) - QUAD * quad, 0, QUAD)
        return QUAD * lax.div(block, nsample) + inside

    def over_prompt(home, pair, query, state):
        prompt = slots_ref[QUAD * home + 2 * pair]
        start = lax.fori_loop(0, prompt, lambda p, total: total + counts_ref[p], jnp.int32(0))
        low, high = local_count(start), local_count(start + counts_ref[prompt])

        def body(t, carry):
            m, l, acc = carry
            first = low + t * TILE_BLOCKS
            row = pl.multiple_of(first * BLK, BLK)
            s = scores_of(flat[pl.ds(row, TILE), 0:HD], query)
            token = lax.broadcasted_iota(jnp.int32, s.shape, 0)
            s = jnp.where(token < (high - first) * BLK, s, NEG)
            m_new = jnp.maximum(m, jnp.max(s, axis=0, keepdims=True))
            p = jnp.exp2((s - m_new) * EXP_SCALE)
            alpha = jnp.exp2((m - m_new) * EXP_SCALE)
            l = l * alpha + jnp.sum(p, axis=0, keepdims=True)
            v = flat[pl.ds(row, TILE), HD:2 * HD]
            return m_new, l, acc * alpha + values_by(v, p.astype(BF16))

        tiles = lax.div(high - low + TILE_BLOCKS - 1, TILE_BLOCKS)
        m, l, acc = lax.fori_loop(0, tiles, body, state)
        some = l > 0.0
        safe = jnp.where(some, l, 1.0)
        lse = jnp.where(some, m * EXP_SCALE + jnp.log(safe) * LOG2E, NEG)
        coarse = lse.astype(BF16).astype(F32)
        middle = (lse - coarse).astype(BF16).astype(F32)
        rest = lse - coarse - middle
        index = lax.broadcasted_iota(jnp.int32, (STAT_ROWS, lse.shape[1]), 0)
        stats = jnp.where(index == 0, coarse, jnp.where(index == 1, middle, jnp.where(index == 2, rest, 0.0)))
        out_ref[home, pair, 0:HD] = (acc * (1.0 / safe)).astype(BF16)
        out_ref[home, pair, HD:] = stats.astype(BF16)

    def others(s, _):
        home = lax.rem(quad + s, quads)
        for pair in range(2):
            query = jnp.concatenate([q_ref[home, 2 * pair], q_ref[home, 2 * pair + 1]], axis=0)
            wide = query.shape[0]
            empty = (
                jnp.full((1, wide), NEG, F32),
                jnp.zeros((1, wide), F32),
                jnp.zeros((HD, wide), F32),
            )
            over_prompt(home, pair, query, empty)
        return 0

    lax.fori_loop(1, quads, others, 0)
    for pair in range(2):
        states, parts = [], []
        for half in range(2):
            msg = fresh_ref.at[2 * pair + half, h]
            query = msg[0:size]
            new_k, new_v = msg[size:size + rows], msg[size + rows:]
            s = scores_of(new_k, query)
            key = lax.broadcasted_iota(jnp.int32, s.shape, 0)
            row = lax.broadcasted_iota(jnp.int32, s.shape, 1) & (rows - 1)
            shift = steps.bit_length() - 1
            seen = ((row >> shift) == (key >> shift)) & ((row & (steps - 1)) >= (key & (steps - 1)))
            s = jnp.where(seen, s, NEG)
            m = jnp.max(s, axis=0, keepdims=True)
            p = jnp.exp2((s - m) * EXP_SCALE)
            l = jnp.sum(p, axis=0, keepdims=True)
            states.append((m, l, values_by(new_v, p.astype(BF16))))
            parts.append(query)
        state = tuple(jnp.concatenate(x, axis=1) for x in zip(*states))
        over_prompt(quad, pair, jnp.concatenate(parts, axis=0), state)


def attend(h, steps, counts, slots, arrived, fresh, queries):
    quads, _, size, _ = queries.shape
    blocks = arrived.shape[1]
    work = quads * 4 * size * blocks * BLK // 2
    return pl.pallas_call(
        functools.partial(attend_kernel, h, steps),
        out_shape=jax.ShapeDtypeStruct((quads, 2, HD + STAT_ROWS, 2 * size), BF16),
        in_specs=[SMEM, SMEM, ANY, VMEM, VMEM],
        out_specs=VMEM,
        scratch_shapes=[
            pltpu.VMEM((blocks + 2, QUAD, BLK, 2 * HD), BF16),
            pltpu.SemaphoreType.DMA((QUAD,)),
        ],
        compiler_params=params(48),
        cost_estimate=cost(4 * work * HD, 4 << 20, work),
        name="attend",
    )(counts, slots, arrived, fresh, queries)


def finish_kernel(steps, part_ref, out_ref):
    quads, _, _, size = part_ref.shape
    rows = size // (2 * GROUP)
    for pair in range(2):
        def lse_of(i):
            tail = part_ref[i, pair, HD:HD + STAT_ROWS].astype(F32)
            return tail[0:1] + tail[1:2] + tail[2:3]

        top = lax.fori_loop(1, quads, lambda i, t: jnp.maximum(t, lse_of(i)), lse_of(0))

        def add(i, carry):
            total, weight = carry
            w = jnp.exp2(lse_of(i) - top)
            return total + part_ref[i, pair, 0:HD].astype(F32) * w, weight + w

        total, weight = lax.fori_loop(
            0, quads, add, (jnp.zeros((HD, size), F32), jnp.zeros((1, size), F32))
        )
        full = (total * (1.0 / weight)).T
        wide = full.reshape(2, GROUP, rows // 8, 8, HD)
        mean = jnp.sum(wide, axis=(0, 2)) * (steps / (2.0 * rows))
        flat = mean.reshape(GROUP * 8, HD)
        place = lax.broadcasted_iota(jnp.int32, flat.shape, 0) & 7
        if steps == 4:
            up, down = pltpu.roll(flat, 4, 0), pltpu.roll(flat, GROUP * 8 - 4, 0)
            flat = flat + jnp.where(place < 4, down, up)
        dev = wide - flat.reshape(GROUP, 8, HD)[None, :, None]
        coarse = flat.astype(BF16).astype(F32)
        carried = jnp.where(place < 4, coarse, flat - coarse).astype(BF16)
        dev = dev.reshape(2, size // 2, HD).astype(BF16)
        for half in range(2):
            out_ref[2 * pair + half, 0:size // 2] = dev[half]
            out_ref[2 * pair + half, size // 2:] = carried


def finish(steps, parts):
    size = parts.shape[-1]
    return pl.pallas_call(
        functools.partial(finish_kernel, steps),
        out_shape=jax.ShapeDtypeStruct((QUAD, size // 2 + GROUP * 8, HD), BF16),
        in_specs=[VMEM],
        out_specs=VMEM,
        compiler_params=params(48),
        cost_estimate=cost(1 << 24, 3 << 20),
        name="finish",
    )(parts)


def emit_kernel(*refs):
    msgs, (att_ref, dev_ref) = refs[:-2], refs[-2:]
    samples, steps, _ = att_ref.shape
    rows = samples * steps
    for h in range(HPD):
        for p in range(QUAD):
            msg = msgs[h].at[p]
            head = p * HPD + h
            means = msg[GROUP * rows:].astype(F32)
            for g in range(GROUP):
                dev = msg[g * rows:(g + 1) * rows].astype(F32)
                pair = means[g * 8:(g + 1) * 8]
                mean = pair + pltpu.roll(pair, 4, 0)
                att = (dev.reshape(rows // 8, 8, HD) + mean[None]).reshape(samples, steps, HD)
                first = (head * GROUP + g) * HD
                att_ref[:, :, first:first + HD] = att.astype(BF16)
                dev_ref[:, :, first:first + HD] = dev.reshape(samples, steps, HD).astype(BF16)


def emit(msgs, shape):
    return pl.pallas_call(
        emit_kernel,
        out_shape=[jax.ShapeDtypeStruct(shape, BF16)] * 2,
        in_specs=[VMEM] * len(msgs),
        out_specs=[VMEM] * 2,
        compiler_params=params(32),
        cost_estimate=cost(1 << 20, 2 << 20),
        name="emit",
    )(*msgs)


def shards(prompt_kv, prompt_blocks, slot_prompt, queries, new_kv):
    nsample = lax.axis_size("sample")
    quads = nsample // QUAD
    samples, steps, width = queries.shape
    rows = samples * steps
    same_quad = [[q * QUAD + j for j in range(QUAD)] for q in range(quads)]
    same_heads = [[q * QUAD + j for q in range(quads)] for j in range(QUAD)]

    def inside(array):
        return lax.all_to_all(array, "sample", 0, 0, axis_index_groups=same_quad, tiled=True)

    def along(array):
        return lax.all_to_all(array, "sample", 0, 0, axis_index_groups=same_heads, tiled=True)

    def gathered(array):
        return lax.all_gather(array, "sample", axis_index_groups=same_heads)

    kv2 = prompt_kv.reshape(-1, prompt_kv.shape[-1])
    fresh = inside(pack_queries(queries, new_kv))
    cut = pack_kv(kv2)
    final = []
    for h in range(HPD):
        asked = gathered(fresh[:, h, :GROUP * rows])
        arrived = inside(cut[h]).reshape(QUAD, -1, BLK, 2 * HD)
        partial = attend(h, steps, prompt_blocks, slot_prompt, arrived, fresh, asked)
        final.append(inside(finish(steps, along(partial))))
    return tuple(emit(final, queries.shape))


def solution(mesh):
    placed = (
        P("groups", "sample", None, None),
        P("groups"),
        P("groups"),
        P(("groups", "sample"), None, None),
        P(("groups", "sample"), None, None),
    )
    return jax.shard_map(
        shards,
        mesh=mesh,
        in_specs=placed,
        out_specs=(P(("groups", "sample"), None, None), P(("groups", "sample"), None, None)),
        check_vma=False,
    )
```

time: 506 us -> 329 us (0.65)
  the two profiles are of different devices: /device:TPU:19 before, /device:TPU:0 now
where the time goes in v2:
time: 329 us; the launch traced here: 328 us
  Pallas kernels  158 us (48%)
  waiting for transfers between devices  112 us (34%)
  starting transfers between devices  24.2 us (7%)
  between operations  14.1 us (4%)
  local copies, waits for them, and re-layouts  10.2 us (3%)
  blocking collectives  9.1 us (3%)
    pallas_call x1, Pallas kernels, pack_kv(): pl.pallas_call(pack_kv_kernel, out_shape=[jax.ShapeDtypeStruct((QUAD, kv2...  128 us
    all_gather x2, waiting for transfers between devices, gathered(): return lax.all_gather(array, 'sample', axis_index_groups=same_heads)  47.5 us
    all_to_all x4, waiting for transfers between devices, inside(): lax.all_to_all(array, 'sample', 0, 0, axis_index_groups=same_quad, tiled=...  38 us
    all_to_all x2, waiting for transfers between devices, along(): lax.all_to_all(array, 'sample', 0, 0, axis_index_groups=same_heads, tiled...  26 us
    pallas_call x2, Pallas kernels, attend(): pl.pallas_call(functools.partial(attend_kernel, h, steps), out_shape=jax....  23.3 us
    all_to_all x4, starting transfers between devices, inside(): lax.all_to_all(array, 'sample', 0, 0, axis_index_groups=same_quad, tiled=...  15 us
    unnamed x20, local copies, waits for them, and re-layouts  9.34 us
    all_to_all x2, starting transfers between devices, along(): lax.all_to_all(array, 'sample', 0, 0, axis_index_groups=same_heads, tiled...  9.1 us
  transfers between devices with their start and end apart: 8, of which 6 were waited for; matrix products, arithmetic and copies ran while one was open for 0% of the time, Pallas kernels for 47%

profile of v2, /device:TPU:0, one launch (start us, length us, event | category | flops | bytes accessed | tf_op | source)
XLA Modules:
  0.0 327.8 jit_solution(4139848932798400819)
XLA Ops:
  7.2 1.0 copy-done.6
  8.2 0.9 copy-done.7
  9.1 1.0 pack_queries.1
  10.1 4.2 %all-to-all-start.1 = ((bf16[4,2,320,128]{3,2,1,0:T(8,128)(2,1)}), bf16[4,2,320,128]{3,2,1,0:T(8,128)(2,1)S(1)}, u32[]{:S(2)}, u32[]{:S(2)}) async-start(bf16[4,2,320,128]{3,2,1,0:T(8,128)(2,1)} %pack_queries.1), calls=%async_computation.1 | async-start | bytes 1310720 | tf_op jit(solution)/shard_map/all_to_all | solution.py:305
  14.3 128.3 %pack_kv.1 = (bf16[4,1024,256]{2,1,0:T(8,128)(2,1)}, bf16[4,1024,256]{2,1,0:T(8,128)(2,1)}) custom-call(bf16[1024,2048]{1,0:T(8,128)(2,1)} %bitcast.9), custom_call_target="tpu_custom_call" | custom-call | bytes 8388608 | tf_op jit(solution)/shard_map/pack_kv/pallas_call | solution.py:89
  142.7 3.6 %all-to-all-start = ((bf16[4,1024,256]{2,1,0:T(8,128)(2,1)}), bf16[4,1024,256]{2,1,0:T(8,128)(2,1)S(1)}, u32[]{:S(2)}, u32[]{:S(2)}) async-start(bf16[4,1024,256]{2,1,0:T(8,128)(2,1)} %get-tuple-element.4), calls=%async_computation | async-start | bytes 4194304 | tf_op jit(solution)/shard_map/all_to_all | solution.py:305
  146.3 0.0 all-gather.5.cloned.1.call-start
  146.3 0.8 fusion
  147.2 0.0 all-gather.5.cloned.1.call-update
  147.2 24.8 %all-to-all-done = bf16[4,1024,256]{2,1,0:T(8,128)(2,1)S(1)} async-done(((bf16[4,1024,256]{2,1,0:T(8,128)(2,1)}), bf16[4,1024,256]{2,1,0:T(8,128)(2,1)S(1)}, u32[]{:S(2)}, u32[]{:S(2)}) %all-to-all-start) | async-done | bytes 2097184 | tf_op jit(solution)/shard_map/all_to_all | solution.py:305
  172.0 1.3 copy-done
  173.3 3.7 %all-to-all-start.4 = ((bf16[4,1024,256]{2,1,0:T(8,128)(2,1)}), bf16[4,1024,256]{2,1,0:T(8,128)(2,1)S(1)}, u32[]{:S(2)}, u32[]{:S(2)}) async-start(bf16[4,1024,256]{2,1,0:T(8,128)(2,1)} %get-tuple-element.5), calls=%async_computation.4 | async-start | bytes 4194304 | tf_op jit(solution)/shard_map/all_to_all | solution.py:305
  177.0 2.6 all-gather.5.cloned.1.call-done
  179.7 1.6 copy-done.1
  181.2 1.2 copy-done.4
  182.5 11.7 %attend.2 = bf16[4,2,144,512]{3,2,1,0:T(8,128)(2,1)S(1)} custom-call(s32[8]{0:T(128)S(1)} %copy-done.8, s32[16]{0:T(128)S(1)} %copy-done.9, bf16[4,32,32,256]{3,2,1,0:T(8,128)(2,1)S(1)} %bitcast.6, bf16[4,2,320,128]{3,2,1,0:T(8,128)(2,1)S(1)} %all-to-all-done.1.fresh_ref, bf16[4,4,256,128]{3,2,1,0:T(8,128)(2,1)S(1)} %bitcast.7), custom_call_target="tpu_custom_call" | custom-call | flops 1073741824 | bytes 4194304 | tf_op jit(solution)/shard_map/attend/pallas_call | solution.py:202
  194.1 1.0 copy-done.2
  195.2 7.5 %all-to-all-done.4 = bf16[4,1024,256]{2,1,0:T(8,128)(2,1)S(1)} async-done(((bf16[4,1024,256]{2,1,0:T(8,128)(2,1)}), bf16[4,1024,256]{2,1,0:T(8,128)(2,1)S(1)}, u32[]{:S(2)}, u32[]{:S(2)}) %all-to-all-start.4) | async-done | bytes 2097184 | tf_op jit(solution)/shard_map/all_to_all | solution.py:305
  202.7 5.6 %all-to-all-start.2 = ((bf16[4,2,144,512]{3,2,1,0:T(8,128)(2,1)}), bf16[4,2,144,512]{3,2,1,0:T(8,128)(2,1)}, u32[]{:S(2)}, u32[]{:S(2)}) async-start(bf16[4,2,144,512]{3,2,1,0:T(8,128)(2,1)} %copy-done.2), calls=%async_computation.2 | async-start | bytes 2359296 | tf_op jit(solution)/shard_map/all_to_all | solution.py:308
  208.2 0.7 all-gather.7.cloned.1.call-update
  209.0 44.9 %all-gather.7.cloned.1.call-done = bf16[16,1,256,128]{3,2,1,0:T(8,128)(2,1)} async-done(((bf16[4,1,256,128]{3,2,1,0:T(8,128)(2,1)}), bf16[16,1,256,128]{3,2,1,0:T(8,128)(2,1)}) %all-gather.7.cloned.1.call-update) | async-done | bytes 1048592 | tf_op jit(solution)/shard_map/all_gather | solution.py:311
  253.9 1.2 copy-done.5
  255.1 11.6 %attend.3 = bf16[4,2,144,512]{3,2,1,0:T(8,128)(2,1)S(1)} custom-call(s32[8]{0:T(128)S(1)} %copy-done.8, s32[16]{0:T(128)S(1)} %copy-done.9, bf16[4,32,32,256]{3,2,1,0:T(8,128)(2,1)S(1)} %bitcast.5, bf16[4,2,320,128]{3,2,1,0:T(8,128)(2,1)S(1)} %all-to-all-done.1.fresh_ref, bf16[4,4,256,128]{3,2,1,0:T(8,128)(2,1)S(1)} %bitcast.8), custom_call_target="tpu_custom_call" | custom-call | flops 1073741824 | bytes 4194304 | tf_op jit(solution)/shard_map/attend/pallas_call | solution.py:202
  266.7 1.0 copy-done.3
  267.8 3.5 %all-to-all-start.5 = ((bf16[4,2,144,512]{3,2,1,0:T(8,128)(2,1)}), bf16[4,2,144,512]{3,2,1,0:T(8,128)(2,1)S(1)}, u32[]{:S(2)}, u32[]{:S(2)}) async-start(bf16[4,2,144,512]{3,2,1,0:T(8,128)(2,1)} %copy-done.3), calls=%async_computation.5 | async-start | bytes 2359296 | tf_op jit(solution)/shard_map/all_to_all | solution.py:308
  271.3 2.9 finish.2
  274.2 26.0 %all-to-all-done.5.part_ref = bf16[4,2,144,512]{3,2,1,0:T(8,128)(2,1)S(1)} async-done(((bf16[4,2,144,512]{3,2,1,0:T(8,128)(2,1)}), bf16[4,2,144,512]{3,2,1,0:T(8,128)(2,1)S(1)}, u32[]{:S(2)}, u32[]{:S(2)}) %all-to-all-start.5) | async-done | bytes 1179680 | tf_op jit(solution)/shard_map/all_to_all | solution.py:308
  300.2 3.5 %all-to-all-start.3 = ((bf16[4,320,128]{2,1,0:T(8,128)(2,1)}), bf16[4,320,128]{2,1,0:T(8,128)(2,1)S(1)}, u32[]{:S(2)}, u32[]{:S(2)}) async-start(bf16[4,320,128]{2,1,0:T(8,128)(2,1)} %finish.2), calls=%async_computation.3 | async-start | bytes 655360 | tf_op jit(solution)/shard_map/all_to_all | solution.py:305
  303.7 0.9 finish.3
  304.6 5.8 %all-to-all-done.3.refs_0_ = bf16[4,320,128]{2,1,0:T(8,128)(2,1)S(1)} async-done(((bf16[4,320,128]{2,1,0:T(8,128)(2,1)}), bf16[4,320,128]{2,1,0:T(8,128)(2,1)S(1)}, u32[]{:S(2)}, u32[]{:S(2)}) %all-to-all-start.3) | async-done | bytes 327712 | tf_op jit(solution)/shard_map/all_to_all | solution.py:305
  310.4 9.1 %all_to_all.35.refs_1_ = bf16[4,320,128]{2,1,0:T(8,128)(2,1)S(1)} all-to-all(bf16[4,320,128]{2,1,0:T(8,128)(2,1)S(1)} %finish.3), channel_id=1, replica_groups={{0,1,2,3},{4,5,6,7},{8,9,10,11},{12,13,14,15},{16,17,18,19},{20,21,22,2..., dimensions={0} | all-to-all | bytes 655360 | tf_op jit(solution)/shard_map/all_to_all | solution.py:305
  319.5 1.4 emit.1
  (15 shorter events, 0.0 us)
Async XLA Ops:
  7.2 1.0 copy-start.6
  8.2 0.9 copy-start.7
  10.1 132.5 %all-to-all-start.1 = ((bf16[4,2,320,128]{3,2,1,0:T(8,128)(2,1)}), bf16[4,2,320,128]{3,2,1,0:T(8,128)(2,1)S(1)}, u32[]{:S(2)}, u32[]{:S(2)}) async-start(bf16[4,2,320,128]{3,2,1,0:T(8,128)(2,1)} %pack_queries.1), calls=%async_computation.1 | async-start | bytes 1310720 | tf_op jit(solution)/shard_map/all_to_all | solution.py:305
  142.7 29.3 %all-to-all-start = ((bf16[4,1024,256]{2,1,0:T(8,128)(2,1)}), bf16[4,1024,256]{2,1,0:T(8,128)(2,1)S(1)}, u32[]{:S(2)}, u32[]{:S(2)}) async-start(bf16[4,1024,256]{2,1,0:T(8,128)(2,1)} %get-tuple-element.4), calls=%async_computation | async-start | bytes 4194304 | tf_op jit(solution)/shard_map/all_to_all | solution.py:305
  146.3 33.4 %all-gather.5.cloned.1.call-start = ((), (), s32[]{:S(2)}) async-start(), calls=%async_computation.7 | async-start | bytes 1310720 | tf_op jit(solution)/shard_map/all_gather | solution.py:311
  172.0 1.3 copy-start
  173.3 6.4 %copy-start.8 = (s32[8]{0:T(128)S(1)}, s32[8]{0:T(128)}, u32[]{:S(2)}) copy-start(s32[8]{0:T(128)} %counts_ref.3) | copy-start | bytes 100
  173.3 6.4 %copy-start.9 = (s32[16]{0:T(128)S(1)}, s32[16]{0:T(128)}, u32[]{:S(2)}) copy-start(s32[16]{0:T(128)} %slots_ref.3) | copy-start | bytes 196
  173.3 29.4 %all-to-all-start.4 = ((bf16[4,1024,256]{2,1,0:T(8,128)(2,1)}), bf16[4,1024,256]{2,1,0:T(8,128)(2,1)S(1)}, u32[]{:S(2)}, u32[]{:S(2)}) async-start(bf16[4,1024,256]{2,1,0:T(8,128)(2,1)} %get-tuple-element.5), calls=%async_computation.4 | async-start | bytes 4194304 | tf_op jit(solution)/shard_map/all_to_all | solution.py:305
  179.6 1.6 copy-start.1
  181.2 1.2 copy-start.4
  194.1 1.0 copy-start.2
  202.7 65.1 %all-to-all-start.2 = ((bf16[4,2,144,512]{3,2,1,0:T(8,128)(2,1)}), bf16[4,2,144,512]{3,2,1,0:T(8,128)(2,1)}, u32[]{:S(2)}, u32[]{:S(2)}) async-start(bf16[4,2,144,512]{3,2,1,0:T(8,128)(2,1)} %copy-done.2), calls=%async_computation.2 | async-start | bytes 2359296 | tf_op jit(solution)/shard_map/all_to_all | solution.py:308
  208.2 45.6 %all-gather.7.cloned.1.call-start = ((), (), s32[]{:S(2)}) async-start(), calls=%async_computation.8 | async-start | bytes 1310720 | tf_op jit(solution)/shard_map/all_gather | solution.py:311
  253.9 1.2 copy-start.5
  266.7 1.0 copy-start.3
  267.8 32.5 %all-to-all-start.5 = ((bf16[4,2,144,512]{3,2,1,0:T(8,128)(2,1)}), bf16[4,2,144,512]{3,2,1,0:T(8,128)(2,1)S(1)}, u32[]{:S(2)}, u32[]{:S(2)}) async-start(bf16[4,2,144,512]{3,2,1,0:T(8,128)(2,1)} %copy-done.3), calls=%async_computation.5 | async-start | bytes 2359296 | tf_op jit(solution)/shard_map/all_to_all | solution.py:308
  300.2 10.2 %all-to-all-start.3 = ((bf16[4,320,128]{2,1,0:T(8,128)(2,1)}), bf16[4,320,128]{2,1,0:T(8,128)(2,1)S(1)}, u32[]{:S(2)}, u32[]{:S(2)}) async-start(bf16[4,320,128]{2,1,0:T(8,128)(2,1)} %finish.2), calls=%async_computation.3 | async-start | bytes 655360 | tf_op jit(solution)/shard_map/all_to_all | solution.py:305
Sparse Core Ops, SparseCore 0:
  149.3 30.3 all-gather.4
  211.2 42.5 all-gather.6

commit v3 on v2

v3 whole, which is shorter than its diff:
```python
import functools
import math

import jax
import jax.numpy as jnp
from jax import lax
from jax.experimental import pallas as pl
from jax.experimental.pallas import tpu as pltpu
from jax.sharding import PartitionSpec as P

HEADS = 64
KVH = 8
HD = 128
BLK = 32
QUAD = 4
HPD = KVH // QUAD
GROUP = HEADS // KVH
TILE_BLOCKS = 8
TILE = TILE_BLOCKS * BLK
STAT_ROWS = 16
NEG = -1e30
LOG2E = math.log2(math.e)
EXP_SCALE = LOG2E / math.sqrt(HD)
F32 = jnp.float32
BF16 = jnp.bfloat16
ANY = pl.BlockSpec(memory_space=pl.ANY)
VMEM = pl.BlockSpec(memory_space=pltpu.VMEM)
SMEM = pl.BlockSpec(memory_space=pltpu.SMEM)


def lanes(start, size):
    return pl.ds(pl.multiple_of(start, 128), size)


def params(mib):
    return pltpu.CompilerParams(vmem_limit_bytes=mib << 20)


def cost(flops, nbytes, trans=0):
    return pl.CostEstimate(flops=flops, bytes_accessed=nbytes, transcendentals=trans)


def pack_queries_kernel(q_hbm, new_hbm, *refs):
    outs, (q_ref, new_ref, sem) = refs[:-3], refs[-3:]
    copies = [
        pltpu.make_async_copy(q_hbm, q_ref, sem.at[0]),
        pltpu.make_async_copy(new_hbm, new_ref, sem.at[1]),
    ]
    for copy in copies:
        copy.start()
    for copy in copies:
        copy.wait()
    mine = lax.rem(lax.axis_index("sample"), QUAD)
    rows = q_ref.shape[0] * q_ref.shape[1]

    def column(ref, head):
        return ref[:, :, lanes(head * HD, HD)].astype(F32).reshape(rows, HD).astype(BF16)

    for k in range(QUAD):
        for h in range(HPD):
            head = jnp.bitwise_xor(mine, k) * HPD + h
            for g in range(GROUP):
                outs[k][h, g * rows:(g + 1) * rows] = column(q_ref, head * GROUP + g)
            base = GROUP * rows
            outs[k][h, base:base + rows] = column(new_ref, head)
            outs[k][h, base + rows:base + 2 * rows] = column(new_ref, KVH + head)


def pack_queries(queries, new_kv):
    rows = queries.shape[0] * queries.shape[1]
    return pl.pallas_call(
        pack_queries_kernel,
        out_shape=[jax.ShapeDtypeStruct((HPD, (GROUP + 2) * rows, HD), BF16)] * QUAD,
        in_specs=[ANY, ANY],
        out_specs=[VMEM] * QUAD,
        scratch_shapes=[
            pltpu.VMEM(queries.shape, BF16),
            pltpu.VMEM(new_kv.shape, BF16),
            pltpu.SemaphoreType.DMA((2,)),
        ],
        compiler_params=params(56),
        cost_estimate=cost(0, 2 << 20),
        name="pack_queries",
    )(queries, new_kv)


def pack_kv_kernel(kv_ref, *refs):
    near, far, sem = refs[0], refs[1:-1], refs[-1]
    mine = lax.rem(lax.axis_index("sample"), QUAD)
    copies = []
    for h in range(HPD):
        for k in range(1, QUAD):
            head = jnp.bitwise_xor(mine, k) * HPD + h
            out = near.at[h] if k == 1 else far[h * (QUAD - 2) + k - 2]
            for part in range(2):
                copies.append(
                    pltpu.make_async_copy(
                        kv_ref.at[:, lanes((part * KVH + head) * HD, HD)],
                        out.at[:, part * HD:(part + 1) * HD],
                        sem.at[len(copies)],
                    )
                )
    for copy in copies:
        copy.start()
    for copy in copies:
        copy.wait()


def pack_kv(kv2):
    count = HPD * (QUAD - 2)
    tokens = kv2.shape[0]
    return pl.pallas_call(
        pack_kv_kernel,
        out_shape=[jax.ShapeDtypeStruct((HPD, tokens, 2 * HD), BF16)]
        + [jax.ShapeDtypeStruct((tokens, 2 * HD), BF16)] * count,
        in_specs=[ANY],
        out_specs=[ANY] * (count + 1),
        scratch_shapes=[pltpu.SemaphoreType.DMA((2 * HPD * (QUAD - 1),))],
        compiler_params=params(16),
        cost_estimate=cost(0, 6 << 20),
        name="pack_kv",
    )(kv2)


def scores_of(keys, query):
    return lax.dot_general(keys, query, (((1,), (1,)), ((), ())), preferred_element_type=F32)


def values_by(values, weights):
    return lax.dot_general(values, weights, (((0,), (0,)), ((), ())), preferred_element_type=F32)


def attend_kernel(h, offsets, steps, counts_ref, slots_ref, kv_ref, near, *refs):
    far, refs = refs[:QUAD - 2], refs[QUAD - 2:]
    nq = QUAD if steps else len(offsets)
    queries, refs = refs[:nq], refs[nq:]
    outs, (held, sem) = refs[:-2], refs[-2:]
    nsample = lax.axis_size("sample")
    quads = nsample // QUAD
    index = lax.axis_index("sample")
    quad, mine = lax.div(index, QUAD), lax.rem(index, QUAD)
    blocks = kv_ref.shape[0]

    copies = []
    for part in range(2):
        copies.append(
            pltpu.make_async_copy(
                kv_ref.at[:, :, lanes((part * KVH + mine * HPD + h) * HD, HD)],
                held.at[0:blocks, mine, :, part * HD:(part + 1) * HD],
                sem.at[part],
            )
        )
    for k in range(1, QUAD):
        source = near.at[h] if k == 1 else far[k - 2]
        copies.append(
            pltpu.make_async_copy(source, held.at[0:blocks, jnp.bitwise_xor(mine, k)], sem.at[k + 1])
        )
    for copy in copies:
        copy.start()
    held[blocks:] = jnp.zeros_like(held[blocks:])

    def fresh_state(pair):
        states, parts = [], []
        for half in range(2):
            msg = queries[2 * pair + half].at[h]
            rows = msg.shape[0] // (GROUP + 2)
            size = rows * GROUP
            query = msg[0:size]
            s = scores_of(msg[size:size + rows], query)
            key = lax.broadcasted_iota(jnp.int32, s.shape, 0)
            row = lax.broadcasted_iota(jnp.int32, s.shape, 1) & (rows - 1)
            shift = steps.bit_length() - 1
            seen = ((row >> shift) == (key >> shift)) & ((row & (steps - 1)) >= (key & (steps - 1)))
            s = jnp.where(seen, s, NEG)
            m = jnp.max(s, axis=0, keepdims=True)
            p = jnp.exp2((s - m) * EXP_SCALE)
            l = jnp.sum(p, axis=0, keepdims=True)
            states.append((m, l, values_by(msg[size + rows:], p.astype(BF16))))
            parts.append(query)
        return jnp.concatenate(parts, axis=0), tuple(jnp.concatenate(x, axis=1) for x in zip(*states))

    begun = [fresh_state(pair) for pair in range(2)] if steps else None
    for copy in copies:
        copy.wait()
    flat = held.reshape(held.shape[0] * QUAD * BLK, 2 * HD)

    def local_count(block):
        inside = jnp.clip(lax.rem(block, nsample) - QUAD * quad, 0, QUAD)
        return QUAD * lax.div(block, nsample) + inside

    def over_prompt(home, pair, query, state):
        prompt = slots_ref[QUAD * home + 2 * jnp.bitwise_xor(lax.div(mine, 2), pair)]
        start = lax.fori_loop(0, prompt, lambda p, total: total + counts_ref[p], jnp.int32(0))
        low, high = local_count(start), local_count(start + counts_ref[prompt])

        def body(t, carry):
            m, l, acc = carry
            first = low + t * TILE_BLOCKS
            row = pl.multiple_of(first * BLK, BLK)
            s = scores_of(flat[pl.ds(row, TILE), 0:HD], query)
            token = lax.broadcasted_iota(jnp.int32, s.shape, 0)
            s = jnp.where(token < (high - first) * BLK, s, NEG)
            m_new = jnp.maximum(m, jnp.max(s, axis=0, keepdims=True))
            p = jnp.exp2((s - m_new) * EXP_SCALE)
            alpha = jnp.exp2((m - m_new) * EXP_SCALE)
            l = l * alpha + jnp.sum(p, axis=0, keepdims=True)
            v = flat[pl.ds(row, TILE), HD:2 * HD]
            return m_new, l, acc * alpha + values_by(v, p.astype(BF16))

        tiles = lax.div(high - low + TILE_BLOCKS - 1, TILE_BLOCKS)
        m, l, acc = lax.fori_loop(0, tiles, body, state)
        some = l > 0.0
        safe = jnp.where(some, l, 1.0)
        lse = jnp.where(some, m * EXP_SCALE + jnp.log(safe) * LOG2E, NEG)
        return acc * (1.0 / safe), lse

    for n, offset in enumerate(offsets):
        home = lax.rem(quad + offset, quads)
        for pair in range(2):
            if steps:
                query, state = begun[pair]
                out, lse = over_prompt(home, pair, query, state)
                outs[0][pair] = out
                outs[1][pair] = jnp.broadcast_to(lse, (8, lse.shape[1]))
                continue
            query = jnp.concatenate([queries[n][2 * pair], queries[n][2 * pair + 1]], axis=0)
            wide = query.shape[0]
            empty = (
                jnp.full((1, wide), NEG, F32),
                jnp.zeros((1, wide), F32),
                jnp.zeros((HD, wide), F32),
            )
            out, lse = over_prompt(home, pair, query, empty)
            coarse = lse.astype(BF16).astype(F32)
            middle = (lse - coarse).astype(BF16).astype(F32)
            rest = lse - coarse - middle
            place = lax.broadcasted_iota(jnp.int32, (STAT_ROWS, wide), 0)
            stats = jnp.where(place == 1, middle, jnp.where(place == 2, rest, 0.0))
            outs[n][pair, 0:HD] = out.astype(BF16)
            outs[n][pair, HD:] = jnp.where(place == 0, coarse, stats).astype(BF16)


def attend(h, offsets, steps, counts, slots, kv3, arrived, queries):
    if steps:
        size = queries[0].shape[1] * GROUP // (GROUP + 2)
        out_shape = [
            jax.ShapeDtypeStruct((2, HD, 2 * size), F32),
            jax.ShapeDtypeStruct((2, 8, 2 * size), F32),
        ]
    else:
        size = queries[0].shape[1]
        out_shape = [jax.ShapeDtypeStruct((2, HD + STAT_ROWS, 2 * size), BF16)] * len(offsets)
    blocks = kv3.shape[0]
    work = len(offsets) * 2 * size * blocks * BLK
    return pl.pallas_call(
        functools.partial(attend_kernel, h, offsets, steps),
        out_shape=out_shape,
        in_specs=[SMEM, SMEM, ANY] + [ANY] * len(arrived) + [VMEM] * len(queries),
        out_specs=[VMEM] * len(out_shape),
        scratch_shapes=[
            pltpu.VMEM((blocks + 2, QUAD, BLK, 2 * HD), BF16),
            pltpu.SemaphoreType.DMA((QUAD + 1,)),
        ],
        compiler_params=params(48),
        cost_estimate=cost(4 * work * HD, 4 << 20, work),
        name="attend_own" if steps else "attend_others",
    )(counts, slots, kv3, *arrived, *queries)


def finish_kernel(steps, own_ref, own_lse_ref, *refs):
    parts, outs = refs[:-QUAD], refs[-QUAD:]
    size = own_ref.shape[2]
    rows = size // (2 * GROUP)
    for pair in range(2):
        lses = [own_lse_ref[pair, 0:1]]
        for ref in parts:
            tail = ref[pair, HD:HD + STAT_ROWS].astype(F32)
            lses.append(tail[0:1] + tail[1:2] + tail[2:3])
        top = functools.reduce(jnp.maximum, lses)
        shares = [jnp.exp2(lse - top) for lse in lses]
        scale = 1.0 / functools.reduce(jnp.add, shares)
        total = own_ref[pair] * (shares[0] * scale)
        for ref, share in zip(parts, shares[1:]):
            total = total + ref[pair, 0:HD].astype(F32) * (share * scale)
        wide = total.T.reshape(2, GROUP, rows // 8, 8, HD)
        mean = jnp.sum(wide, axis=(0, 2)) * (steps / (2.0 * rows))
        flat = mean.reshape(GROUP * 8, HD)
        place = lax.broadcasted_iota(jnp.int32, flat.shape, 0) & 7
        up, down = pltpu.roll(flat, 4, 0), pltpu.roll(flat, GROUP * 8 - 4, 0)
        flat = flat + jnp.where(place < 4, down, up)
        dev = wide - flat.reshape(GROUP, 8, HD)[None, :, None]
        coarse = flat.astype(BF16).astype(F32)
        carried = jnp.where(place < 4, coarse, flat - coarse).astype(BF16)
        dev = dev.reshape(2, size // 2, HD).astype(BF16)
        for half in range(2):
            out = outs[2 * pair + half]
            out[0:size // 2] = dev[half]
            out[size // 2:] = carried


def finish(steps, own, own_lse, parts):
    size = own.shape[2]
    return pl.pallas_call(
        functools.partial(finish_kernel, steps),
        out_shape=[jax.ShapeDtypeStruct((size // 2 + GROUP * 8, HD), BF16)] * QUAD,
        in_specs=[VMEM] * (2 + len(parts)),
        out_specs=[VMEM] * QUAD,
        compiler_params=params(48),
        cost_estimate=cost(1 << 24, 3 << 20),
        name="finish",
    )(own, own_lse, *parts)


def emit_kernel(*refs):
    msgs, (att_ref, dev_ref) = refs[:-2], refs[-2:]
    samples, steps, _ = att_ref.shape
    rows = samples * steps
    mine = lax.rem(lax.axis_index("sample"), QUAD)
    for h in range(HPD):
        for k in range(QUAD):
            msg = msgs[h * QUAD + k]
            head = jnp.bitwise_xor(mine, k) * HPD + h
            means = msg[GROUP * rows:].astype(F32)
            for g in range(GROUP):
                dev = msg[g * rows:(g + 1) * rows].astype(F32)
                pair = means[g * 8:(g + 1) * 8]
                mean = pair + pltpu.roll(pair, 4, 0)
                att = (dev.reshape(rows // 8, 8, HD) + mean[None]).reshape(samples, steps, HD)
                cols = lanes((head * GROUP + g) * HD, HD)
                att_ref[:, :, cols] = att.astype(BF16)
                dev_ref[:, :, cols] = dev.reshape(samples, steps, HD).astype(BF16)


def emit(msgs, shape):
    return pl.pallas_call(
        emit_kernel,
        out_shape=[jax.ShapeDtypeStruct(shape, BF16)] * 2,
        in_specs=[VMEM] * len(msgs),
        out_specs=[VMEM] * 2,
        compiler_params=params(32),
        cost_estimate=cost(1 << 20, 2 << 20),
        name="emit",
    )(*msgs)


def shards(prompt_kv, prompt_blocks, slot_prompt, queries, new_kv):
    nsample = lax.axis_size("sample")
    quads = nsample // QUAD
    samples, steps, width = queries.shape
    rows = samples * steps

    def across(array, k):
        return lax.ppermute(array, "sample", [(i, i ^ k) for i in range(nsample)])

    def along(array, shift):
        return lax.ppermute(
            array, "sample", [(i, (i + shift * QUAD) % nsample) for i in range(nsample)]
        )

    kv3 = prompt_kv.reshape(prompt_kv.shape[0], BLK, prompt_kv.shape[-1])
    msgs = pack_queries(queries, new_kv)
    near, *far = pack_kv(kv3.reshape(-1, kv3.shape[-1]))
    msgs = [msgs[0]] + [across(msgs[k], k) for k in range(1, QUAD)]
    near, msgs = lax.optimization_barrier((near, msgs))
    near = across(near, 1).reshape(HPD, -1, BLK, 2 * HD)
    far = [
        across(block, 2 + i % (QUAD - 2)).reshape(-1, BLK, 2 * HD) for i, block in enumerate(far)
    ]
    final = []
    for h in range(HPD):
        arrived = [near] + far[h * (QUAD - 2):(h + 1) * (QUAD - 2)]
        own = jnp.stack([m[h, :GROUP * rows] for m in msgs])
        ahead = (quads - 1 + (1 - h % 2)) // 2
        held = {}
        block = own
        for s in range(1, ahead + 1):
            block = along(block, -1)
            held[s] = block
        block = own
        for s in range(1, quads - ahead):
            block = along(block, 1)
            held[quads - s] = block
        offsets = tuple(sorted(held))
        partial = attend(
            h, offsets, 0, prompt_blocks, slot_prompt, kv3, arrived, [held[o] for o in offsets]
        )
        back = [along(p, o) for o, p in zip(offsets, partial)]
        mine = attend(h, (0,), steps, prompt_blocks, slot_prompt, kv3, arrived, msgs)
        done = finish(steps, *mine, back)
        final.append([done[0]] + [across(done[k], k) for k in range(1, QUAD)])
    return tuple(emit([m for per_head in final for m in per_head], queries.shape))


def solution(mesh):
    placed = (
        P("groups", "sample", None, None),
        P("groups"),
        P("groups"),
        P(("groups", "sample"), None, None),
        P(("groups", "sample"), None, None),
    )
    return jax.shard_map(
        shards,
        mesh=mesh,
        in_specs=placed,
        out_specs=(P(("groups", "sample"), None, None), P(("groups", "sample"), None, None)),
        check_vma=False,
    )
```

time: 329 us -> 116 us (0.35)
  the two profiles are of different devices: /device:TPU:0 before, /device:TPU:9 now
where the time goes in v3:
time: 116 us
  waiting for transfers between devices  52.9 us (46%)
  Pallas kernels  31.9 us (28%)
  starting transfers between devices  27.9 us (24%)
  local copies, waits for them, and re-layouts  2.24 us (2%)
    ppermute x12, waiting for transfers between devices, along(): lax.ppermute(array, 'sample', [(i, (i + shift * QUAD) % nsample) for i in...  37.4 us
    pallas_call x4, Pallas kernels, attend(): pl.pallas_call(functools.partial(attend_kernel, h, offsets, steps), out_s...  26.5 us
    ppermute x14, starting transfers between devices, across(): return lax.ppermute(array, 'sample', [(i, i ^ k) for i in range(nsample)])  15.5 us
    ppermute x14, waiting for transfers between devices, across(): return lax.ppermute(array, 'sample', [(i, i ^ k) for i in range(nsample)])  15.4 us
    ppermute x12, starting transfers between devices, along(): lax.ppermute(array, 'sample', [(i, (i + shift * QUAD) % nsample) for i in...  12.4 us
  transfers between devices with their start and end apart: 26, of which 12 were waited for; matrix products, arithmetic and copies ran while one was open for 0% of the time, Pallas kernels for 24%

profile of v3, /device:TPU:9, one launch (start us, length us, event | category | flops | bytes accessed | tf_op | source)
XLA Modules:
  0.0 115.8 jit_solution(8798764340398810237)
XLA Ops:
  0.7 2.3 %pack_queries.1 = (bf16[2,320,128]{2,1,0:T(8,128)(2,1)}, bf16[2,320,128]{2,1,0:T(8,128)(2,1)}, bf16[2,320,128]{2,1,0:T(8,128)(2,1)}, bf16[2,320,128]{2,1,0:T(8,128)(2,1)}) custom-call(bf16[8,4,8192]{2,1,0:T(4,128)(2,1)} %q_hbm.1, bf16[8,4,2048]{2,1,0:T(4,128)(2,1)} %new_hbm.1), custom_call_target="tpu_custom_call" | custom-call | bytes 2097152 | tf_op jit(solution)/shard_map/pack_queries/pallas_call | solution.py:71
  3.7 1.3 %collective-permute-start.1 = (bf16[2,320,128]{2,1,0:T(8,128)(2,1)}, bf16[2,320,128]{2,1,0:T(8,128)(2,1)S(1)}, u32[]{:S(2)}, u32[]{:S(2)}) collective-permute-start(bf16[2,320,128]{2,1,0:T(8,128)(2,1)} %get-tuple-element.37), channel_id=1, source_target_pairs={{0,2},{1,3},{2,0},{3,1},{4,6},{5,7},{6,4},{7,5},{8,10},{9,11},{10,... | collective-permute-start | bytes 491528 | tf_op jit(solution)/shard_map/ppermute | solution.py:353
  5.4 2.2 %copy-done = bf16[32,1,32,2048]{3,2,1,0:T(8,128)(2,1)S(1)} copy-done((bf16[32,1,32,2048]{3,2,1,0:T(8,128)(2,1)S(1)}, bf16[32,1,32,2048]{3,2,1,0:T(8,128)(2,1)}, u32[]{:S(2)}) %copy-start) | copy-done | bytes 4194328
  7.6 1.0 pack_kv.1
  8.6 1.1 collective-permute-done.1.refs_4_
  9.6 3.7 %collective-permute-done.2.refs_5_ = bf16[2,320,128]{2,1,0:T(8,128)(2,1)S(1)} collective-permute-done((bf16[2,320,128]{2,1,0:T(8,128)(2,1)}, bf16[2,320,128]{2,1,0:T(8,128)(2,1)S(1)}, u32[]{:S(2)}, u32[]{:S(2)}) %collective-permute-start.2) | collective-permute-done | bytes 163872 | tf_op jit(solution)/shard_map/ppermute | solution.py:353
  13.6 1.3 %collective-permute-start.18 = (bf16[4,256,128]{2,1,0:T(8,128)(2,1)S(1)}, bf16[4,256,128]{2,1,0:T(8,128)(2,1)S(1)}, u32[]{:S(2)}, u32[]{:S(2)}) collective-permute-start(bf16[4,256,128]{2,1,0:T(8,128)(2,1)S(1)} %pad_maximum_fusion.1), channel_id=1, source_target_pairs={{0,4},{1,5},{2,6},{3,7},{4,8},{5,9},{6,10},{7,11},{8,12},{9,13},{1... | collective-permute-start | bytes 786440 | tf_op jit(solution)/shard_map/ppermute | solution.py:356
  15.0 1.2 %collective-permute-start.15 = (bf16[1024,256]{1,0:T(8,128)(2,1)S(1)}, bf16[1024,256]{1,0:T(8,128)(2,1)S(1)}, u32[]{:S(2)}, u32[]{:S(2)}) collective-permute-start(bf16[1024,256]{1,0:T(8,128)(2,1)S(1)} %get-tuple-element.55), channel_id=1, source_target_pairs={{0,2},{1,3},{2,0},{3,1},{4,6},{5,7},{6,4},{7,5},{8,10},{9,11},{10,... | collective-permute-start | bytes 1572872 | tf_op jit(solution)/shard_map/ppermute | solution.py:353
  16.2 0.9 collective-permute-start.16
  17.4 3.9 %collective-permute-done.18.refs_4_ = bf16[4,256,128]{2,1,0:T(8,128)(2,1)S(1)} collective-permute-done((bf16[4,256,128]{2,1,0:T(8,128)(2,1)S(1)}, bf16[4,256,128]{2,1,0:T(8,128)(2,1)S(1)}, u32[]{:S(2)}, u32[]{:S(2)}) %collective-permute-start.18) | collective-permute-done | bytes 262176 | tf_op jit(solution)/shard_map/ppermute | solution.py:356
  21.3 2.3 %collective-permute-start.6 = (bf16[4,256,128]{2,1,0:T(8,128)(2,1)S(1)}, bf16[4,256,128]{2,1,0:T(8,128)(2,1)S(1)}, u32[]{:S(2)}, u32[]{:S(2)}) collective-permute-start(bf16[4,256,128]{2,1,0:T(8,128)(2,1)S(1)} %pad_maximum_fusion), channel_id=1, source_target_pairs={{0,12},{1,13},{2,14},{3,15},{4,0},{5,1},{6,2},{7,3},{8,4},{9,5},{1... | collective-permute-start | bytes 786440 | tf_op jit(solution)/shard_map/ppermute | solution.py:356
  23.7 4.8 %collective-permute-done.17.refs_2_ = bf16[4,256,128]{2,1,0:T(8,128)(2,1)S(1)} collective-permute-done((bf16[4,256,128]{2,1,0:T(8,128)(2,1)S(1)}, bf16[4,256,128]{2,1,0:T(8,128)(2,1)S(1)}, u32[]{:S(2)}, u32[]{:S(2)}) %collective-permute-start.17) | collective-permute-done | bytes 262176 | tf_op jit(solution)/shard_map/ppermute | solution.py:356
  28.5 7.3 %collective-permute-done.6.refs_2_ = bf16[4,256,128]{2,1,0:T(8,128)(2,1)S(1)} collective-permute-done((bf16[4,256,128]{2,1,0:T(8,128)(2,1)S(1)}, bf16[4,256,128]{2,1,0:T(8,128)(2,1)S(1)}, u32[]{:S(2)}, u32[]{:S(2)}) %collective-permute-start.6) | collective-permute-done | bytes 262176 | tf_op jit(solution)/shard_map/ppermute | solution.py:356
  35.7 1.3 %collective-permute-start.4 = (bf16[1024,256]{1,0:T(8,128)(2,1)S(1)}, bf16[1024,256]{1,0:T(8,128)(2,1)S(1)}, u32[]{:S(2)}, u32[]{:S(2)}) collective-permute-start(bf16[1024,256]{1,0:T(8,128)(2,1)S(1)} %get-tuple-element.40), channel_id=1, source_target_pairs={{0,2},{1,3},{2,0},{3,1},{4,6},{5,7},{6,4},{7,5},{8,10},{9,11},{10,... | collective-permute-start | bytes 1572872 | tf_op jit(solution)/shard_map/ppermute | solution.py:353
  37.0 3.6 %collective-permute-start.5 = (bf16[1024,256]{1,0:T(8,128)(2,1)S(1)}, bf16[1024,256]{1,0:T(8,128)(2,1)S(1)}, u32[]{:S(2)}, u32[]{:S(2)}) collective-permute-start(bf16[1024,256]{1,0:T(8,128)(2,1)S(1)} %get-tuple-element.41), channel_id=1, source_target_pairs={{0,3},{1,2},{2,1},{3,0},{4,7},{5,6},{6,5},{7,4},{8,11},{9,10},{10,... | collective-permute-start | bytes 1572872 | tf_op jit(solution)/shard_map/ppermute | solution.py:353
  41.2 1.0 collective-permute-start.8
  42.7 9.4 %attend_others.3 = (bf16[2,144,512]{2,1,0:T(8,128)(2,1)S(1)}, bf16[2,144,512]{2,1,0:T(8,128)(2,1)S(1)}, bf16[2,144,512]{2,1,0:T(8,128)(2,1)S(1)}) custom-call(s32[8]{0:T(128)S(1)} %copy-done.2, s32[16]{0:T(128)S(1)} %copy-done.3, bf16[32,32,2048]{2,1,0:T(8,128)(2,1)} %bitcast.7, bf16[2,32,32,256]{3,2,1,0:T(8,128)(2,1)S(1)} %bitcast.12, ...), custom_call_target="tpu_custom_call" | custom-call | flops 805306368 | bytes 4194304 | tf_op jit(solution)/shard_map/attend_others/pallas_call | solution.py:255
  52.6 3.9 %collective-permute-start.21 = (bf16[2,144,512]{2,1,0:T(8,128)(2,1)S(1)}, bf16[2,144,512]{2,1,0:T(8,128)(2,1)S(1)}, u32[]{:S(2)}, u32[]{:S(2)}) collective-permute-start(bf16[2,144,512]{2,1,0:T(8,128)(2,1)S(1)} %get-tuple-element.60), channel_id=1, source_target_pairs={{0,8},{1,9},{2,10},{3,11},{4,12},{5,13},{6,14},{7,15},{8,0},{9,1},... | collective-permute-start | bytes 884744 | tf_op jit(solution)/shard_map/ppermute | solution.py:356
  56.5 5.9 %collective-permute-done.5 = bf16[1024,256]{1,0:T(8,128)(2,1)S(1)} collective-permute-done((bf16[1024,256]{1,0:T(8,128)(2,1)S(1)}, bf16[1024,256]{1,0:T(8,128)(2,1)S(1)}, u32[]{:S(2)}, u32[]{:S(2)}) %collective-permute-start.5) | collective-permute-done | bytes 524320 | tf_op jit(solution)/shard_map/ppermute | solution.py:353
  62.4 9.4 %attend_others.2 = (bf16[2,144,512]{2,1,0:T(8,128)(2,1)S(1)}, bf16[2,144,512]{2,1,0:T(8,128)(2,1)S(1)}, bf16[2,144,512]{2,1,0:T(8,128)(2,1)S(1)}) custom-call(s32[8]{0:T(128)S(1)} %copy-done.2, s32[16]{0:T(128)S(1)} %copy-done.3, bf16[32,32,2048]{2,1,0:T(8,128)(2,1)} %bitcast.8, bf16[2,32,32,256]{3,2,1,0:T(8,128)(2,1)S(1)} %bitcast.13, ...), custom_call_target="tpu_custom_call" | custom-call | flops 805306368 | bytes 4194304 | tf_op jit(solution)/shard_map/attend_others/pallas_call | solution.py:255
  72.2 1.9 %collective-permute-start.11 = (bf16[2,144,512]{2,1,0:T(8,128)(2,1)S(1)}, bf16[2,144,512]{2,1,0:T(8,128)(2,1)S(1)}, u32[]{:S(2)}, u32[]{:S(2)}) collective-permute-start(bf16[2,144,512]{2,1,0:T(8,128)(2,1)S(1)} %get-tuple-element.50), channel_id=1, source_target_pairs={{0,12},{1,13},{2,14},{3,15},{4,0},{5,1},{6,2},{7,3},{8,4},{9,5},{1... | collective-permute-start | bytes 884744 | tf_op jit(solution)/shard_map/ppermute | solution.py:356
  74.5 3.8 %attend_own.3 = (f32[2,128,512]{2,1,0:T(8,128)S(1)}, f32[2,8,512]{2,1,0:T(8,128)S(1)}) custom-call(s32[8]{0:T(128)S(1)} %copy-done.2, s32[16]{0:T(128)S(1)} %copy-done.3, bf16[32,32,2048]{2,1,0:T(8,128)(2,1)} %bitcast.9, bf16[2,32,32,256]{3,2,1,0:T(8,128)(2,1)S(1)} %bitcast.14, bf16[32,32,256]{2,1,0:T(8,128)(2,1)S(1)} %bitcast.17, ...), custom_call_target="tpu_custom_call" | custom-call | flops 268435456 | bytes 4194304 | tf_op jit(solution)/shard_map/attend_own/pallas_call | solution.py:255
  78.3 13.6 %collective-permute-done.21.refs_1_ = bf16[2,144,512]{2,1,0:T(8,128)(2,1)S(1)} collective-permute-done((bf16[2,144,512]{2,1,0:T(8,128)(2,1)S(1)}, bf16[2,144,512]{2,1,0:T(8,128)(2,1)S(1)}, u32[]{:S(2)}, u32[]{:S(2)}) %collective-permute-start.21) | collective-permute-done | bytes 294944 | tf_op jit(solution)/shard_map/ppermute | solution.py:356
  92.9 3.8 %attend_own.2 = (f32[2,128,512]{2,1,0:T(8,128)S(1)}, f32[2,8,512]{2,1,0:T(8,128)S(1)}) custom-call(s32[8]{0:T(128)S(1)} %copy-done.2, s32[16]{0:T(128)S(1)} %copy-done.3, bf16[32,32,2048]{2,1,0:T(8,128)(2,1)} %bitcast.10, bf16[2,32,32,256]{3,2,1,0:T(8,128)(2,1)S(1)} %bitcast.15, bf16[32,32,256]{2,1,0:T(8,128)(2,1)S(1)} %bitcast.21, ...), custom_call_target="tpu_custom_call" | custom-call | flops 268435456 | bytes 4194304 | tf_op jit(solution)/shard_map/attend_own/pallas_call | solution.py:255
  96.7 1.0 collective-permute-start.24
  98.2 1.3 %collective-permute-start.25 = (bf16[320,128]{1,0:T(8,128)(2,1)S(1)}, bf16[320,128]{1,0:T(8,128)(2,1)S(1)}, u32[]{:S(2)}, u32[]{:S(2)}) collective-permute-start(bf16[320,128]{1,0:T(8,128)(2,1)S(1)} %get-tuple-element.65), channel_id=1, source_target_pairs={{0,3},{1,2},{2,1},{3,0},{4,7},{5,6},{6,5},{7,4},{8,11},{9,10},{10,... | collective-permute-start | bytes 245768 | tf_op jit(solution)/shard_map/ppermute | solution.py:353
  99.5 7.3 %collective-permute-done.11.refs_2_ = bf16[2,144,512]{2,1,0:T(8,128)(2,1)S(1)} collective-permute-done((bf16[2,144,512]{2,1,0:T(8,128)(2,1)S(1)}, bf16[2,144,512]{2,1,0:T(8,128)(2,1)S(1)}, u32[]{:S(2)}, u32[]{:S(2)}) %collective-permute-start.11) | collective-permute-done | bytes 294944 | tf_op jit(solution)/shard_map/ppermute | solution.py:356
  107.3 1.1 collective-permute-start.12
  108.4 1.3 %collective-permute-start.13 = (bf16[320,128]{1,0:T(8,128)(2,1)S(1)}, bf16[320,128]{1,0:T(8,128)(2,1)S(1)}, u32[]{:S(2)}, u32[]{:S(2)}) collective-permute-start(bf16[320,128]{1,0:T(8,128)(2,1)S(1)} %get-tuple-element.53), channel_id=1, source_target_pairs={{0,2},{1,3},{2,0},{3,1},{4,6},{5,7},{6,4},{7,5},{8,10},{9,11},{10,... | collective-permute-start | bytes 245768 | tf_op jit(solution)/shard_map/ppermute | solution.py:353
  110.1 2.3 %collective-permute-done.13.refs_2_ = bf16[320,128]{1,0:T(8,128)(2,1)S(1)} collective-permute-done((bf16[320,128]{1,0:T(8,128)(2,1)S(1)}, bf16[320,128]{1,0:T(8,128)(2,1)S(1)}, u32[]{:S(2)}, u32[]{:S(2)}) %collective-permute-start.13) | collective-permute-done | bytes 81952 | tf_op jit(solution)/shard_map/ppermute | solution.py:353
  112.4 1.9 %collective-permute-done.14.refs_3_ = bf16[320,128]{1,0:T(8,128)(2,1)S(1)} collective-permute-done((bf16[320,128]{1,0:T(8,128)(2,1)S(1)}, bf16[320,128]{1,0:T(8,128)(2,1)S(1)}, u32[]{:S(2)}, u32[]{:S(2)}) %collective-permute-start.14) | collective-permute-done | bytes 81952 | tf_op jit(solution)/shard_map/ppermute | solution.py:353
  114.3 1.5 %emit.1 = (bf16[8,4,8192]{2,1,0:T(4,128)(2,1)}, bf16[8,4,8192]{2,1,0:T(4,128)(2,1)}) custom-call(bf16[320,128]{1,0:T(8,128)(2,1)S(1)} %get-tuple-element.51.refs_0_, bf16[320,128]{1,0:T(8,128)(2,1)S(1)} %collective-permute-done.12.refs_1_, bf16[320,128]{1,0:T(8,128)(2,1)S(1)} %collective-permute-done.13.refs_2_, ...), custom_call_target="tpu_custom_call" | custom-call | flops 1048576 | bytes 2097152 | tf_op jit(solution)/shard_map/emit/pallas_call | solution.py:335
  (41 shorter events, 6.5 us)
Async XLA Ops:
  0.6 42.0 %copy-start.2 = (s32[8]{0:T(128)S(1)}, s32[8]{0:T(128)}, u32[]{:S(2)}) copy-start(s32[8]{0:T(128)} %counts_ref.7) | copy-start | bytes 100
  0.6 42.0 %copy-start.3 = (s32[16]{0:T(128)S(1)}, s32[16]{0:T(128)}, u32[]{:S(2)}) copy-start(s32[16]{0:T(128)} %slots_ref.7) | copy-start | bytes 196
  2.9 5.6 %collective-permute-start = (bf16[2,320,128]{2,1,0:T(8,128)(2,1)}, bf16[2,320,128]{2,1,0:T(8,128)(2,1)S(1)}, u32[]{:S(2)}, u32[]{:S(2)}) collective-permute-start(bf16[2,320,128]{2,1,0:T(8,128)(2,1)} %get-tuple-element.36), channel_id=1, source_target_pairs={{0,1},{1,0},{2,3},{3,2},{4,5},{5,4},{6,7},{7,6},{8,9},{9,8},{10,11... | collective-permute-start | bytes 491528 | tf_op jit(solution)/shard_map/ppermute | solution.py:353
  3.7 6.0 %collective-permute-start.1 = (bf16[2,320,128]{2,1,0:T(8,128)(2,1)}, bf16[2,320,128]{2,1,0:T(8,128)(2,1)S(1)}, u32[]{:S(2)}, u32[]{:S(2)}) collective-permute-start(bf16[2,320,128]{2,1,0:T(8,128)(2,1)} %get-tuple-element.37), channel_id=1, source_target_pairs={{0,2},{1,3},{2,0},{3,1},{4,6},{5,7},{6,4},{7,5},{8,10},{9,11},{10,... | collective-permute-start | bytes 491528 | tf_op jit(solution)/shard_map/ppermute | solution.py:353
  4.9 8.4 %collective-permute-start.2 = (bf16[2,320,128]{2,1,0:T(8,128)(2,1)}, bf16[2,320,128]{2,1,0:T(8,128)(2,1)S(1)}, u32[]{:S(2)}, u32[]{:S(2)}) collective-permute-start(bf16[2,320,128]{2,1,0:T(8,128)(2,1)} %get-tuple-element.38), channel_id=1, source_target_pairs={{0,3},{1,2},{2,1},{3,0},{4,7},{5,6},{6,5},{7,4},{8,11},{9,10},{10,... | collective-permute-start | bytes 491528 | tf_op jit(solution)/shard_map/ppermute | solution.py:353
  5.4 2.2 %copy-start = (bf16[32,1,32,2048]{3,2,1,0:T(8,128)(2,1)S(1)}, bf16[32,1,32,2048]{3,2,1,0:T(8,128)(2,1)}, u32[]{:S(2)}) copy-start(bf16[32,1,32,2048]{3,2,1,0:T(8,128)(2,1)} %param.5) | copy-start | bytes 12582916
  7.6 6.0 %copy-start.1 = (bf16[2,320,128]{2,1,0:T(8,128)(2,1)S(1)}, bf16[2,320,128]{2,1,0:T(8,128)(2,1)}, u32[]{:S(2)}) copy-start(bf16[2,320,128]{2,1,0:T(8,128)(2,1)} %get-tuple-element.42.refs_2_) | copy-start | bytes 491524
  13.3 29.3 %collective-permute-start.3 = (bf16[2,1024,256]{2,1,0:T(8,128)(2,1)S(1)}, bf16[2,1024,256]{2,1,0:T(8,128)(2,1)S(1)}, u32[]{:S(2)}, u32[]{:S(2)}) collective-permute-start(bf16[2,1024,256]{2,1,0:T(8,128)(2,1)S(1)} %get-tuple-element.39), channel_id=1, source_target_pairs={{0,1},{1,0},{2,3},{3,2},{4,5},{5,4},{6,7},{7,6},{8,9},{9,8},{10,11... | collective-permute-start | bytes 3145736 | tf_op jit(solution)/shard_map/ppermute | solution.py:353
  13.6 7.7 %collective-permute-start.18 = (bf16[4,256,128]{2,1,0:T(8,128)(2,1)S(1)}, bf16[4,256,128]{2,1,0:T(8,128)(2,1)S(1)}, u32[]{:S(2)}, u32[]{:S(2)}) collective-permute-start(bf16[4,256,128]{2,1,0:T(8,128)(2,1)S(1)} %pad_maximum_fusion.1), channel_id=1, source_target_pairs={{0,4},{1,5},{2,6},{3,7},{4,8},{5,9},{6,10},{7,11},{8,12},{9,13},{1... | collective-permute-start | bytes 786440 | tf_op jit(solution)/shard_map/ppermute | solution.py:356
  15.0 22.0 %collective-permute-start.15 = (bf16[1024,256]{1,0:T(8,128)(2,1)S(1)}, bf16[1024,256]{1,0:T(8,128)(2,1)S(1)}, u32[]{:S(2)}, u32[]{:S(2)}) collective-permute-start(bf16[1024,256]{1,0:T(8,128)(2,1)S(1)} %get-tuple-element.55), channel_id=1, source_target_pairs={{0,2},{1,3},{2,0},{3,1},{4,6},{5,7},{6,4},{7,5},{8,10},{9,11},{10,... | collective-permute-start | bytes 1572872 | tf_op jit(solution)/shard_map/ppermute | solution.py:353
  16.2 25.0 %collective-permute-start.16 = (bf16[1024,256]{1,0:T(8,128)(2,1)S(1)}, bf16[1024,256]{1,0:T(8,128)(2,1)S(1)}, u32[]{:S(2)}, u32[]{:S(2)}) collective-permute-start(bf16[1024,256]{1,0:T(8,128)(2,1)S(1)} %get-tuple-element.56), channel_id=1, source_target_pairs={{0,3},{1,2},{2,1},{3,0},{4,7},{5,6},{6,5},{7,4},{8,11},{9,10},{10,... | collective-permute-start | bytes 1572872 | tf_op jit(solution)/shard_map/ppermute | solution.py:353
  17.2 11.3 %collective-permute-start.17 = (bf16[4,256,128]{2,1,0:T(8,128)(2,1)S(1)}, bf16[4,256,128]{2,1,0:T(8,128)(2,1)S(1)}, u32[]{:S(2)}, u32[]{:S(2)}) collective-permute-start(bf16[4,256,128]{2,1,0:T(8,128)(2,1)S(1)} %pad_maximum_fusion.1), channel_id=1, source_target_pairs={{0,12},{1,13},{2,14},{3,15},{4,0},{5,1},{6,2},{7,3},{8,4},{9,5},{1... | collective-permute-start | bytes 786440 | tf_op jit(solution)/shard_map/ppermute | solution.py:356
  21.3 14.4 %collective-permute-start.6 = (bf16[4,256,128]{2,1,0:T(8,128)(2,1)S(1)}, bf16[4,256,128]{2,1,0:T(8,128)(2,1)S(1)}, u32[]{:S(2)}, u32[]{:S(2)}) collective-permute-start(bf16[4,256,128]{2,1,0:T(8,128)(2,1)S(1)} %pad_maximum_fusion), channel_id=1, source_target_pairs={{0,12},{1,13},{2,14},{3,15},{4,0},{5,1},{6,2},{7,3},{8,4},{9,5},{1... | collective-permute-start | bytes 786440 | tf_op jit(solution)/shard_map/ppermute | solution.py:356
  28.5 13.7 %collective-permute-start.19 = (bf16[4,256,128]{2,1,0:T(8,128)(2,1)S(1)}, bf16[4,256,128]{2,1,0:T(8,128)(2,1)S(1)}, u32[]{:S(2)}, u32[]{:S(2)}) collective-permute-start(bf16[4,256,128]{2,1,0:T(8,128)(2,1)S(1)} %collective-permute-done.18.refs_4_), channel_id=1, source_target_pairs={{0,4},{1,5},{2,6},{3,7},{4,8},{5,9},{6,10},{7,11},{8,12},{9,13},{1... | collective-permute-start | bytes 786440 | tf_op jit(solution)/shard_map/ppermute | solution.py:356
  35.7 20.8 %collective-permute-start.4 = (bf16[1024,256]{1,0:T(8,128)(2,1)S(1)}, bf16[1024,256]{1,0:T(8,128)(2,1)S(1)}, u32[]{:S(2)}, u32[]{:S(2)}) collective-permute-start(bf16[1024,256]{1,0:T(8,128)(2,1)S(1)} %get-tuple-element.40), channel_id=1, source_target_pairs={{0,2},{1,3},{2,0},{3,1},{4,6},{5,7},{6,4},{7,5},{8,10},{9,11},{10,... | collective-permute-start | bytes 1572872 | tf_op jit(solution)/shard_map/ppermute | solution.py:353
  37.0 25.4 %collective-permute-start.5 = (bf16[1024,256]{1,0:T(8,128)(2,1)S(1)}, bf16[1024,256]{1,0:T(8,128)(2,1)S(1)}, u32[]{:S(2)}, u32[]{:S(2)}) collective-permute-start(bf16[1024,256]{1,0:T(8,128)(2,1)S(1)} %get-tuple-element.41), channel_id=1, source_target_pairs={{0,3},{1,2},{2,1},{3,0},{4,7},{5,6},{6,5},{7,4},{8,11},{9,10},{10,... | collective-permute-start | bytes 1572872 | tf_op jit(solution)/shard_map/ppermute | solution.py:353
  41.2 11.4 %collective-permute-start.8 = (bf16[4,256,128]{2,1,0:T(8,128)(2,1)S(1)}, bf16[4,256,128]{2,1,0:T(8,128)(2,1)S(1)}, u32[]{:S(2)}, u32[]{:S(2)}) collective-permute-start(bf16[4,256,128]{2,1,0:T(8,128)(2,1)S(1)} %pad_maximum_fusion), channel_id=1, source_target_pairs={{0,4},{1,5},{2,6},{3,7},{4,8},{5,9},{6,10},{7,11},{8,12},{9,13},{1... | collective-permute-start | bytes 786440 | tf_op jit(solution)/shard_map/ppermute | solution.py:356
  42.2 20.2 %collective-permute-start.7 = (bf16[4,256,128]{2,1,0:T(8,128)(2,1)S(1)}, bf16[4,256,128]{2,1,0:T(8,128)(2,1)S(1)}, u32[]{:S(2)}, u32[]{:S(2)}) collective-permute-start(bf16[4,256,128]{2,1,0:T(8,128)(2,1)S(1)} %collective-permute-done.6.refs_2_), channel_id=1, source_target_pairs={{0,12},{1,13},{2,14},{3,15},{4,0},{5,1},{6,2},{7,3},{8,4},{9,5},{1... | collective-permute-start | bytes 786440 | tf_op jit(solution)/shard_map/ppermute | solution.py:356
  52.1 22.0 %collective-permute-start.20 = (bf16[2,144,512]{2,1,0:T(8,128)(2,1)S(1)}, bf16[2,144,512]{2,1,0:T(8,128)(2,1)S(1)}, u32[]{:S(2)}, u32[]{:S(2)}) collective-permute-start(bf16[2,144,512]{2,1,0:T(8,128)(2,1)S(1)} %get-tuple-element.59), channel_id=1, source_target_pairs={{0,4},{1,5},{2,6},{3,7},{4,8},{5,9},{6,10},{7,11},{8,12},{9,13},{1... | collective-permute-start | bytes 884744 | tf_op jit(solution)/shard_map/ppermute | solution.py:356
  52.6 39.3 %collective-permute-start.21 = (bf16[2,144,512]{2,1,0:T(8,128)(2,1)S(1)}, bf16[2,144,512]{2,1,0:T(8,128)(2,1)S(1)}, u32[]{:S(2)}, u32[]{:S(2)}) collective-permute-start(bf16[2,144,512]{2,1,0:T(8,128)(2,1)S(1)} %get-tuple-element.60), channel_id=1, source_target_pairs={{0,8},{1,9},{2,10},{3,11},{4,12},{5,13},{6,14},{7,15},{8,0},{9,1},... | collective-permute-start | bytes 884744 | tf_op jit(solution)/shard_map/ppermute | solution.py:356
  56.5 35.4 %collective-permute-start.22 = (bf16[2,144,512]{2,1,0:T(8,128)(2,1)S(1)}, bf16[2,144,512]{2,1,0:T(8,128)(2,1)S(1)}, u32[]{:S(2)}, u32[]{:S(2)}) collective-permute-start(bf16[2,144,512]{2,1,0:T(8,128)(2,1)S(1)} %get-tuple-element.61), channel_id=1, source_target_pairs={{0,12},{1,13},{2,14},{3,15},{4,0},{5,1},{6,2},{7,3},{8,4},{9,5},{1... | collective-permute-start | bytes 884744 | tf_op jit(solution)/shard_map/ppermute | solution.py:356
  71.8 26.5 %collective-permute-start.10 = (bf16[2,144,512]{2,1,0:T(8,128)(2,1)S(1)}, bf16[2,144,512]{2,1,0:T(8,128)(2,1)S(1)}, u32[]{:S(2)}, u32[]{:S(2)}) collective-permute-start(bf16[2,144,512]{2,1,0:T(8,128)(2,1)S(1)} %get-tuple-element.49), channel_id=1, source_target_pairs={{0,8},{1,9},{2,10},{3,11},{4,12},{5,13},{6,14},{7,15},{8,0},{9,1},... | collective-permute-start | bytes 884744 | tf_op jit(solution)/shard_map/ppermute | solution.py:356
  72.2 34.7 %collective-permute-start.11 = (bf16[2,144,512]{2,1,0:T(8,128)(2,1)S(1)}, bf16[2,144,512]{2,1,0:T(8,128)(2,1)S(1)}, u32[]{:S(2)}, u32[]{:S(2)}) collective-permute-start(bf16[2,144,512]{2,1,0:T(8,128)(2,1)S(1)} %get-tuple-element.50), channel_id=1, source_target_pairs={{0,12},{1,13},{2,14},{3,15},{4,0},{5,1},{6,2},{7,3},{8,4},{9,5},{1... | collective-permute-start | bytes 884744 | tf_op jit(solution)/shard_map/ppermute | solution.py:356
  74.1 32.8 %collective-permute-start.9 = (bf16[2,144,512]{2,1,0:T(8,128)(2,1)S(1)}, bf16[2,144,512]{2,1,0:T(8,128)(2,1)S(1)}, u32[]{:S(2)}, u32[]{:S(2)}) collective-permute-start(bf16[2,144,512]{2,1,0:T(8,128)(2,1)S(1)} %get-tuple-element.48), channel_id=1, source_target_pairs={{0,4},{1,5},{2,6},{3,7},{4,8},{5,9},{6,10},{7,11},{8,12},{9,13},{1... | collective-permute-start | bytes 884744 | tf_op jit(solution)/shard_map/ppermute | solution.py:356
  92.3 17.3 %collective-permute-start.23 = (bf16[320,128]{1,0:T(8,128)(2,1)S(1)}, bf16[320,128]{1,0:T(8,128)(2,1)S(1)}, u32[]{:S(2)}, u32[]{:S(2)}) collective-permute-start(bf16[320,128]{1,0:T(8,128)(2,1)S(1)} %get-tuple-element.63), channel_id=1, source_target_pairs={{0,1},{1,0},{2,3},{3,2},{4,5},{5,4},{6,7},{7,6},{8,9},{9,8},{10,11... | collective-permute-start | bytes 245768 | tf_op jit(solution)/shard_map/ppermute | solution.py:353
  96.7 13.4 %collective-permute-start.24 = (bf16[320,128]{1,0:T(8,128)(2,1)S(1)}, bf16[320,128]{1,0:T(8,128)(2,1)S(1)}, u32[]{:S(2)}, u32[]{:S(2)}) collective-permute-start(bf16[320,128]{1,0:T(8,128)(2,1)S(1)} %get-tuple-element.64), channel_id=1, source_target_pairs={{0,2},{1,3},{2,0},{3,1},{4,6},{5,7},{6,4},{7,5},{8,10},{9,11},{10,... | collective-permute-start | bytes 245768 | tf_op jit(solution)/shard_map/ppermute | solution.py:353
  98.2 11.9 %collective-permute-start.25 = (bf16[320,128]{1,0:T(8,128)(2,1)S(1)}, bf16[320,128]{1,0:T(8,128)(2,1)S(1)}, u32[]{:S(2)}, u32[]{:S(2)}) collective-permute-start(bf16[320,128]{1,0:T(8,128)(2,1)S(1)} %get-tuple-element.65), channel_id=1, source_target_pairs={{0,3},{1,2},{2,1},{3,0},{4,7},{5,6},{6,5},{7,4},{8,11},{9,10},{10,... | collective-permute-start | bytes 245768 | tf_op jit(solution)/shard_map/ppermute | solution.py:353
  107.3 2.8 %collective-permute-start.12 = (bf16[320,128]{1,0:T(8,128)(2,1)S(1)}, bf16[320,128]{1,0:T(8,128)(2,1)S(1)}, u32[]{:S(2)}, u32[]{:S(2)}) collective-permute-start(bf16[320,128]{1,0:T(8,128)(2,1)S(1)} %get-tuple-element.52), channel_id=1, source_target_pairs={{0,1},{1,0},{2,3},{3,2},{4,5},{5,4},{6,7},{7,6},{8,9},{9,8},{10,11... | collective-permute-start | bytes 245768 | tf_op jit(solution)/shard_map/ppermute | solution.py:353
  108.4 4.0 %collective-permute-start.13 = (bf16[320,128]{1,0:T(8,128)(2,1)S(1)}, bf16[320,128]{1,0:T(8,128)(2,1)S(1)}, u32[]{:S(2)}, u32[]{:S(2)}) collective-permute-start(bf16[320,128]{1,0:T(8,128)(2,1)S(1)} %get-tuple-element.53), channel_id=1, source_target_pairs={{0,2},{1,3},{2,0},{3,1},{4,6},{5,7},{6,4},{7,5},{8,10},{9,11},{10,... | collective-permute-start | bytes 245768 | tf_op jit(solution)/shard_map/ppermute | solution.py:353
  109.6 4.7 %collective-permute-start.14 = (bf16[320,128]{1,0:T(8,128)(2,1)S(1)}, bf16[320,128]{1,0:T(8,128)(2,1)S(1)}, u32[]{:S(2)}, u32[]{:S(2)}) collective-permute-start(bf16[320,128]{1,0:T(8,128)(2,1)S(1)} %get-tuple-element.54), channel_id=1, source_target_pairs={{0,3},{1,2},{2,1},{3,0},{4,7},{5,6},{6,5},{7,4},{8,11},{9,10},{10,... | collective-permute-start | bytes 245768 | tf_op jit(solution)/shard_map/ppermute | solution.py:353

commit v4 on v3

v4 whole, which is shorter than its diff:
```python
import functools
import math

import jax
import jax.numpy as jnp
from jax import lax
from jax.experimental import pallas as pl
from jax.experimental.pallas import tpu as pltpu
from jax.sharding import PartitionSpec as P

HEADS = 64
KVH = 8
HD = 128
BLK = 32
MAXB = 128
QUAD = 4
HPD = KVH // QUAD
GROUP = HEADS // KVH
TILE_BLOCKS = 8
TILE = TILE_BLOCKS * BLK
STAT_ROWS = 16
NEG = -1e30
LOG2E = math.log2(math.e)
EXP_SCALE = LOG2E / math.sqrt(HD)
F32 = jnp.float32
BF16 = jnp.bfloat16
ANY = pl.BlockSpec(memory_space=pl.ANY)
VMEM = pl.BlockSpec(memory_space=pltpu.VMEM)
SMEM = pl.BlockSpec(memory_space=pltpu.SMEM)


def lanes(start, size):
    return pl.ds(pl.multiple_of(start, 128), size)


def params(mib):
    return pltpu.CompilerParams(vmem_limit_bytes=mib << 20)


def cost(flops, nbytes, trans=0):
    return pl.CostEstimate(flops=flops, bytes_accessed=nbytes, transcendentals=trans)


def pack_queries_kernel(q_hbm, new_hbm, *refs):
    outs, (q_ref, new_ref, sem) = refs[:-3], refs[-3:]
    copies = [
        pltpu.make_async_copy(q_hbm, q_ref, sem.at[0]),
        pltpu.make_async_copy(new_hbm, new_ref, sem.at[1]),
    ]
    for copy in copies:
        copy.start()
    for copy in copies:
        copy.wait()
    mine = lax.rem(lax.axis_index("sample"), QUAD)
    rows = q_ref.shape[0] * q_ref.shape[1]

    def column(ref, head):
        return ref[:, :, lanes(head * HD, HD)].astype(F32).reshape(rows, HD).astype(BF16)

    for k in range(QUAD):
        for h in range(HPD):
            head = jnp.bitwise_xor(mine, k) * HPD + h
            for g in range(GROUP):
                outs[k][h, g * rows:(g + 1) * rows] = column(q_ref, head * GROUP + g)
            base = GROUP * rows
            outs[k][h, base:base + rows] = column(new_ref, head)
            outs[k][h, base + rows:base + 2 * rows] = column(new_ref, KVH + head)


def pack_queries(queries, new_kv):
    rows = queries.shape[0] * queries.shape[1]
    return pl.pallas_call(
        pack_queries_kernel,
        out_shape=[jax.ShapeDtypeStruct((HPD, (GROUP + 2) * rows, HD), BF16)] * QUAD,
        in_specs=[ANY, ANY],
        out_specs=[VMEM] * QUAD,
        scratch_shapes=[
            pltpu.VMEM(queries.shape, BF16),
            pltpu.VMEM(new_kv.shape, BF16),
            pltpu.SemaphoreType.DMA((2,)),
        ],
        compiler_params=params(56),
        cost_estimate=cost(0, 2 << 20),
        name="pack_queries",
    )(queries, new_kv)


def pack_kv_kernel(kv_ref, near, *refs):
    far, sem = refs[:-1], refs[-1]
    mine = lax.rem(lax.axis_index("sample"), QUAD)
    copies = []
    for h in range(HPD):
        for k in range(1, QUAD):
            head = jnp.bitwise_xor(mine, k) * HPD + h
            out = near.at[h] if k == 1 else far[h].at[k - 2]
            for part in range(2):
                copies.append(
                    pltpu.make_async_copy(
                        kv_ref.at[:, lanes((part * KVH + head) * HD, HD)],
                        out.at[:, part * HD:(part + 1) * HD],
                        sem.at[len(copies)],
                    )
                )
    for copy in copies:
        copy.start()
    for copy in copies:
        copy.wait()


def pack_kv(kv2):
    shape = jax.ShapeDtypeStruct((2, kv2.shape[0], 2 * HD), BF16)
    return pl.pallas_call(
        pack_kv_kernel,
        out_shape=[shape] * (1 + HPD),
        in_specs=[ANY],
        out_specs=[ANY] * (1 + HPD),
        scratch_shapes=[pltpu.SemaphoreType.DMA((2 * HPD * (QUAD - 1),))],
        compiler_params=params(16),
        cost_estimate=cost(0, 6 << 20),
        name="pack_kv",
    )(kv2)


def scores_of(keys, query):
    return lax.dot_general(keys, query, (((1,), (1,)), ((), ())), preferred_element_type=F32)


def values_by(values, weights):
    return lax.dot_general(values, weights, (((0,), (0,)), ((), ())), preferred_element_type=F32)


def attend_kernel(h, offsets, steps, max_tiles, counts_ref, slots_ref, kv_ref, near, same, passed, *refs):
    count = len(offsets)
    nq = QUAD if steps else count
    queries, refs = refs[:nq], refs[nq:]
    nout = 2 if steps else count
    outs, refs = refs[:nout], refs[nout:]
    held, asked, fresh, state, acc, stage, sem = refs
    nsample = lax.axis_size("sample")
    quads = nsample // QUAD
    index = lax.axis_index("sample")
    quad, mine = lax.div(index, QUAD), lax.rem(index, QUAD)
    blocks = kv_ref.shape[0]
    size = asked.shape[2]

    first_copies = []

    def copied(copies, source, target):
        copies.append(pltpu.make_async_copy(source, target, sem.at[len(first_copies) + len(later)]))
        copies[-1].start()

    later = []
    for n in range(nq):
        if steps:
            copied(first_copies, queries[n].at[h, 0:size], asked.at[0, n])
            copied(first_copies, queries[n].at[h, size:], fresh.at[n])
        else:
            copied(first_copies, queries[n], asked.at[n])
    for part in range(2):
        copied(
            later,
            kv_ref.at[:, :, lanes((part * KVH + mine * HPD + h) * HD, HD)],
            held.at[0:blocks, mine, :, part * HD:(part + 1) * HD],
        )
    for k, source in ((1, near.at[h]), (2, same.at[0]), (3, passed)):
        copied(later, source, held.at[0:blocks, jnp.bitwise_xor(mine, k)])
    held[blocks:] = jnp.zeros_like(held[blocks:])
    for copy in first_copies:
        copy.wait()

    def fresh_state(pair):
        parts = []
        for half in range(2):
            slot = 2 * pair + half
            rows = size // GROUP
            s = scores_of(fresh[slot, 0:rows], asked[0, slot])
            key = lax.broadcasted_iota(jnp.int32, s.shape, 0)
            row = lax.broadcasted_iota(jnp.int32, s.shape, 1) & (rows - 1)
            shift = steps.bit_length() - 1
            seen = ((row >> shift) == (key >> shift)) & ((row & (steps - 1)) >= (key & (steps - 1)))
            s = jnp.where(seen, s, NEG)
            m = jnp.max(s, axis=0, keepdims=True)
            p = jnp.exp2((s - m) * EXP_SCALE)
            l = jnp.sum(p, axis=0, keepdims=True)
            parts.append((m, l, values_by(fresh[slot, rows:], p.astype(BF16))))
        m, l, out = (jnp.concatenate(x, axis=1) for x in zip(*parts))
        state[pair, 0:1] = m
        state[pair, 1:2] = l
        acc[pair] = out

    if steps:
        for pair in range(2):
            fresh_state(pair)
    for copy in later:
        copy.wait()
    flat = held.reshape(held.shape[0] * QUAD * BLK, 2 * HD)

    def local_count(block):
        inside = jnp.clip(lax.rem(block, nsample) - QUAD * quad, 0, QUAD)
        return QUAD * lax.div(block, nsample) + inside

    def one_pass(n, pair, low, high, tiles):
        tokens = tiles * TILE
        query = asked[n, pl.ds(2 * pair, 2)].reshape(2 * size, HD)
        row = pl.multiple_of(low * BLK, BLK)
        s = scores_of(flat[pl.ds(row, tokens), 0:HD], query)
        last = s[tokens - TILE:]
        token = lax.broadcasted_iota(jnp.int32, last.shape, 0)
        last = jnp.where(token < (high - low) * BLK - (tokens - TILE), last, NEG)
        s = last if tiles == 1 else jnp.concatenate([s[:tokens - TILE], last], axis=0)
        m = jnp.max(s, axis=0, keepdims=True)
        if steps:
            before = state[pair, 0:1]
            m = jnp.maximum(m, before)
        p = jnp.exp2((s - m) * EXP_SCALE)
        l = jnp.sum(p, axis=0, keepdims=True)
        out = values_by(flat[pl.ds(row, tokens), HD:2 * HD], p.astype(BF16))
        if steps:
            alpha = jnp.exp2((before - m) * EXP_SCALE)
            l = l + alpha * state[pair, 1:2]
            out = out + alpha * acc[pair]
        state[pair, 0:1] = m
        state[pair, 1:2] = l
        acc[pair] = out

    def chunk(n, _):
        offset = jnp.int32(0) if steps else offset_of(n)
        home = lax.rem(quad + offset, quads)

        def prompt_of(pair, _):
            prompt = slots_ref[QUAD * home + 2 * jnp.bitwise_xor(lax.div(mine, 2), pair)]
            start = lax.fori_loop(0, prompt, lambda p, total: total + counts_ref[p], jnp.int32(0))
            low, high = local_count(start), local_count(start + counts_ref[prompt])
            tiles = lax.div(high - low + TILE_BLOCKS - 1, TILE_BLOCKS)
            if not steps:
                @pl.when(tiles == 0)
                def _():
                    state[pair, 0:1] = jnp.full((1, 2 * size), NEG, F32)
                    state[pair, 1:2] = jnp.zeros((1, 2 * size), F32)
                    acc[pair] = jnp.zeros((HD, 2 * size), F32)

            for t in range(1, max_tiles + 1):
                @pl.when(tiles == t)
                def _(t=t):
                    one_pass(n, pair, low, high, t)

            return 0

        lax.fori_loop(0, 2, prompt_of, 0)
        lses = []
        for pair in range(2):
            m, l = state[pair, 0:1], state[pair, 1:2]
            some = l > 0.0
            safe = jnp.where(some, l, 1.0)
            lses.append(jnp.where(some, m * EXP_SCALE + jnp.log(safe) * LOG2E, NEG))
            out = acc[pair] * (1.0 / safe)
            if steps:
                outs[0][pair] = out
                outs[1][pair] = jnp.broadcast_to(lses[pair], (8, 2 * size))
            else:
                stage[n, pair * HD:(pair + 1) * HD] = out.astype(BF16)
        if not steps:
            stage[n, 2 * HD:] = stat_tile(lses)
        return 0

    def offset_of(n):
        offset = jnp.int32(offsets[0])
        for i in range(1, count):
            offset = jnp.where(n == i, offsets[i], offset)
        return offset

    lax.fori_loop(0, count, chunk, 0)
    if not steps:
        copies = []
        for n in range(count):
            copied(copies, stage.at[n], outs[n])
            later.append(copies[-1])
        for copy in copies:
            copy.wait()


def attend(h, offsets, steps, counts, slots, kv3, arrived, queries):
    count = len(offsets)
    if steps:
        size = queries[0].shape[1] * GROUP // (GROUP + 2)
        out_shape = [
            jax.ShapeDtypeStruct((2, HD, 2 * size), F32),
            jax.ShapeDtypeStruct((2, 8, 2 * size), F32),
        ]
    else:
        size = queries[0].shape[1]
        out_shape = [jax.ShapeDtypeStruct((2 * HD + STAT_ROWS, 2 * size), BF16)] * count
    blocks = kv3.shape[0]
    max_tiles = -(-(-(-MAXB // lax.axis_size("sample")) * QUAD) // TILE_BLOCKS)
    work = count * 2 * size * blocks * BLK
    return pl.pallas_call(
        functools.partial(attend_kernel, h, offsets, steps, max_tiles),
        out_shape=out_shape,
        in_specs=[SMEM, SMEM, ANY] + [ANY] * len(arrived) + [ANY] * len(queries),
        out_specs=[VMEM if steps else ANY] * len(out_shape),
        scratch_shapes=[
            pltpu.VMEM((blocks + max_tiles * TILE_BLOCKS // QUAD, QUAD, BLK, 2 * HD), BF16),
            pltpu.VMEM((count, QUAD, size, HD), BF16),
            pltpu.VMEM((QUAD, 2 * size // GROUP, HD), BF16),
            pltpu.VMEM((2, 8, 2 * size), F32),
            pltpu.VMEM((2, HD, 2 * size), F32),
            pltpu.VMEM((1 if steps else count, 2 * HD + STAT_ROWS, 2 * size), BF16),
            pltpu.SemaphoreType.DMA((2 * QUAD + 2 * count + 8,)),
        ],
        compiler_params=params(48),
        cost_estimate=cost(0, 1024),
        name="attend_own" if steps else "attend_others",
    )(counts, slots, kv3, *arrived, *queries)


def lse_of(ref, pair):
    tail = ref[2 * HD:2 * HD + STAT_ROWS].astype(F32)[3 * pair:3 * pair + 3]
    return tail[0:1] + tail[1:2] + tail[2:3]


def stat_tile(lses):
    place = lax.broadcasted_iota(jnp.int32, (STAT_ROWS, lses[0].shape[1]), 0)
    stats = jnp.zeros(place.shape, F32)
    for pair, lse in enumerate(lses):
        coarse = lse.astype(BF16).astype(F32)
        middle = (lse - coarse).astype(BF16).astype(F32)
        for i, piece in enumerate((coarse, middle, lse - coarse - middle)):
            stats = jnp.where(place == 3 * pair + i, piece, stats)
    return stats.astype(BF16)


def merge_kernel(one_ref, two_ref, out_ref):
    lses = []
    for pair in range(2):
        one, two = lse_of(one_ref, pair), lse_of(two_ref, pair)
        top = jnp.maximum(one, two)
        w1, w2 = jnp.exp2(one - top), jnp.exp2(two - top)
        total = w1 + w2
        scale = 1.0 / total
        rows = slice(pair * HD, (pair + 1) * HD)
        merged = one_ref[rows].astype(F32) * (w1 * scale) + two_ref[rows].astype(F32) * (w2 * scale)
        out_ref[rows] = merged.astype(BF16)
        lses.append(top + jnp.log(total) * LOG2E)
    out_ref[2 * HD:] = stat_tile(lses)


def merge(one, two):
    return pl.pallas_call(
        merge_kernel,
        out_shape=jax.ShapeDtypeStruct(one.shape, BF16),
        in_specs=[VMEM, VMEM],
        out_specs=VMEM,
        compiler_params=params(16),
        cost_estimate=cost(0, 1024),
        name="merge",
    )(one, two)


def finish_kernel(steps, own_ref, own_lse_ref, *refs):
    parts, outs = refs[:-QUAD], refs[-QUAD:]
    size = own_ref.shape[2]
    rows = size // (2 * GROUP)
    for pair in range(2):
        lses = [own_lse_ref[pair, 0:1]]
        for ref in parts:
            lses.append(lse_of(ref, pair))
        top = functools.reduce(jnp.maximum, lses)
        shares = [jnp.exp2(lse - top) for lse in lses]
        scale = 1.0 / functools.reduce(jnp.add, shares)
        total = own_ref[pair] * (shares[0] * scale)
        for ref, share in zip(parts, shares[1:]):
            total = total + ref[pair * HD:(pair + 1) * HD].astype(F32) * (share * scale)
        wide = total.T.reshape(2, GROUP, rows // 8, 8, HD)
        mean = jnp.sum(wide, axis=(0, 2)) * (steps / (2.0 * rows))
        flat = mean.reshape(GROUP * 8, HD)
        place = lax.broadcasted_iota(jnp.int32, flat.shape, 0) & 7
        up, down = pltpu.roll(flat, 4, 0), pltpu.roll(flat, GROUP * 8 - 4, 0)
        flat = flat + jnp.where(place < 4, down, up)
        dev = wide - flat.reshape(GROUP, 8, HD)[None, :, None]
        coarse = flat.astype(BF16).astype(F32)
        carried = jnp.where(place < 4, coarse, flat - coarse).astype(BF16)
        dev = dev.reshape(2, size // 2, HD).astype(BF16)
        for half in range(2):
            out = outs[2 * pair + half]
            out[0:size // 2] = dev[half]
            out[size // 2:] = carried


def finish(steps, own, own_lse, parts):
    size = own.shape[2]
    return pl.pallas_call(
        functools.partial(finish_kernel, steps),
        out_shape=[jax.ShapeDtypeStruct((size // 2 + GROUP * 8, HD), BF16)] * QUAD,
        in_specs=[VMEM] * (2 + len(parts)),
        out_specs=[VMEM] * QUAD,
        compiler_params=params(48),
        cost_estimate=cost(0, 1024),
        name="finish",
    )(own, own_lse, *parts)


def emit_kernel(*refs):
    msgs, (att_ref, dev_ref) = refs[:-2], refs[-2:]
    samples, steps, _ = att_ref.shape
    rows = samples * steps
    mine = lax.rem(lax.axis_index("sample"), QUAD)
    for h in range(HPD):
        for k in range(QUAD):
            msg = msgs[h * QUAD + k]
            head = jnp.bitwise_xor(mine, k) * HPD + h
            means = msg[GROUP * rows:].astype(F32)
            for g in range(GROUP):
                dev = msg[g * rows:(g + 1) * rows].astype(F32)
                pair = means[g * 8:(g + 1) * 8]
                mean = pair + pltpu.roll(pair, 4, 0)
                att = (dev.reshape(rows // 8, 8, HD) + mean[None]).reshape(samples, steps, HD)
                cols = lanes((head * GROUP + g) * HD, HD)
                att_ref[:, :, cols] = att.astype(BF16)
                dev_ref[:, :, cols] = dev.reshape(samples, steps, HD).astype(BF16)


def emit(msgs, shape):
    return pl.pallas_call(
        emit_kernel,
        out_shape=[jax.ShapeDtypeStruct(shape, BF16)] * 2,
        in_specs=[VMEM] * len(msgs),
        out_specs=[VMEM] * 2,
        compiler_params=params(32),
        cost_estimate=cost(1 << 20, 2 << 20),
        name="emit",
    )(*msgs)


def shards(prompt_kv, prompt_blocks, slot_prompt, queries, new_kv):
    nsample = lax.axis_size("sample")
    quads = nsample // QUAD
    samples, steps, width = queries.shape
    rows = samples * steps

    def across(array, k):
        return lax.ppermute(array, "sample", [(i, i ^ k) for i in range(nsample)])

    def along(array, shift):
        return lax.ppermute(
            array, "sample", [(i, (i + shift * QUAD) % nsample) for i in range(nsample)]
        )

    kv3 = prompt_kv.reshape(prompt_kv.shape[0], BLK, prompt_kv.shape[-1])
    msgs = pack_queries(queries, new_kv)
    near, *far = pack_kv(kv3.reshape(-1, kv3.shape[-1]))
    msgs = [msgs[0]] + [across(msgs[k], k) for k in range(1, QUAD)]
    near, msgs = lax.optimization_barrier((near, msgs))
    near = across(near, 1).reshape(HPD, -1, BLK, 2 * HD)

    def gather(h):
        own = jnp.stack([m[h, :GROUP * rows] for m in msgs])
        ahead = (quads - 1 + (1 - h % 2)) // 2
        held = {}
        for shift, hops in ((-1, ahead), (1, quads - 1 - ahead)):
            block = own
            for s in range(1, hops + 1):
                block = along(block, shift)
                held[-shift * s % quads] = block
        return held

    asked = [gather(h) for h in range(HPD)]
    arrived, handed = [], []
    for h in range(HPD):
        source = far[h]
        if h:
            source, arrived[-1], asked[h - 1], near = lax.optimization_barrier(
                (source, arrived[-1], asked[h - 1], near)
            )
        arrived.append(across(source, 2))
        handed.append(arrived[h][1])
    final = []
    for h in range(HPD):
        if h:
            handed[h], asked[h] = lax.optimization_barrier((handed[h], asked[h]))
        passed = across(handed[h], 1).reshape(-1, BLK, 2 * HD)
        blocks = [near, arrived[h].reshape(2, -1, BLK, 2 * HD), passed]
        offsets = tuple(sorted(asked[h]))
        partial = attend(
            h, offsets, 0, prompt_blocks, slot_prompt, kv3, blocks, [asked[h][o] for o in offsets]
        )
        if h:
            back, partial = lax.optimization_barrier((back, partial))
            done = finish(steps, *mine, back)
            final.append([done[0]] + [across(done[k], k) for k in range(1, QUAD)])
            partial, _ = lax.optimization_barrier((partial, done[0]))
        parts = dict(zip(offsets, partial))
        far_right = (quads - 1 + (1 - h % 2)) // 2
        back = []
        for shift, hops in sorted(((1, far_right), (-1, quads - 1 - far_right)), key=lambda x: x[1]):
            for s in range(hops, 0, -1):
                block = parts[shift * s % quads]
                if s < hops:
                    if s == 1:
                        moved, back = lax.optimization_barrier((moved, back))
                    block = merge(block, moved)
                moved = along(block, shift)
            if hops:
                back.append(moved)
        mine = attend(h, (0,), steps, prompt_blocks, slot_prompt, kv3, blocks, msgs)
    done = finish(steps, *mine, back)
    final.append([done[0]] + [across(done[k], k) for k in range(1, QUAD)])
    return tuple(emit([m for per_head in final for m in per_head], queries.shape))


def solution(mesh):
    placed = (
        P("groups", "sample", None, None),
        P("groups"),
        P("groups"),
        P(("groups", "sample"), None, None),
        P(("groups", "sample"), None, None),
    )
    return jax.shard_map(
        shards,
        mesh=mesh,
        in_specs=placed,
        out_specs=(P(("groups", "sample"), None, None), P(("groups", "sample"), None, None)),
        check_vma=False,
    )
```

time: 116 us -> 116 us (level)
  the two profiles are of different devices: /device:TPU:9 before, /device:TPU:0 now
where the time goes in v4:
time: 116 us
  waiting for transfers between devices  50 us (43%)
  starting transfers between devices  35.8 us (31%)
  Pallas kernels  27.2 us (23%)
  local copies, waits for them, and re-layouts  2.31 us (2%)
    ppermute x12, waiting for transfers between devices, along(): lax.ppermute(array, 'sample', [(i, (i + shift * QUAD) % nsample) for i in...  40.7 us
    ppermute x12, starting transfers between devices, along(): lax.ppermute(array, 'sample', [(i, (i + shift * QUAD) % nsample) for i in...  24.8 us
    pallas_call x4, Pallas kernels, attend(): pl.pallas_call(functools.partial(attend_kernel, h, offsets, steps, max_ti...  21.5 us
    ppermute x14, starting transfers between devices, across(): return lax.ppermute(array, 'sample', [(i, i ^ k) for i in range(nsample)])  11 us
    ppermute x14, waiting for transfers between devices, across(): return lax.ppermute(array, 'sample', [(i, i ^ k) for i in range(nsample)])  9.29 us
  transfers between devices with their start and end apart: 26, of which 15 were waited for; matrix products, arithmetic and copies ran while one was open for 0% of the time, Pallas kernels for 20%

profile of v4, /device:TPU:0, one launch (start us, length us, event | category | flops | bytes accessed | tf_op | source)
XLA Modules:
  0.0 116.2 jit_solution(17617565912230776686)
XLA Ops:
  0.7 2.3 %pack_queries.1 = (bf16[2,320,128]{2,1,0:T(8,128)(2,1)}, bf16[2,320,128]{2,1,0:T(8,128)(2,1)}, bf16[2,320,128]{2,1,0:T(8,128)(2,1)}, bf16[2,320,128]{2,1,0:T(8,128)(2,1)}) custom-call(bf16[8,4,8192]{2,1,0:T(4,128)(2,1)} %q_hbm.1, bf16[8,4,2048]{2,1,0:T(4,128)(2,1)} %new_hbm.1), custom_call_target="tpu_custom_call" | custom-call | bytes 2097152 | tf_op jit(solution)/shard_map/pack_queries/pallas_call | solution.py:72
  3.4 2.6 %collective-permute-start.2 = (bf16[2,320,128]{2,1,0:T(8,128)(2,1)}, bf16[2,320,128]{2,1,0:T(8,128)(2,1)S(1)}, u32[]{:S(2)}, u32[]{:S(2)}) collective-permute-start(bf16[2,320,128]{2,1,0:T(8,128)(2,1)} %get-tuple-element.59), channel_id=1, source_target_pairs={{0,2},{1,3},{2,0},{3,1},{4,6},{5,7},{6,4},{7,5},{8,10},{9,11},{10,... | collective-permute-start | bytes 491528 | tf_op jit(solution)/shard_map/ppermute | solution.py:441
  6.1 2.2 %copy-done = bf16[32,1,32,2048]{3,2,1,0:T(8,128)(2,1)S(1)} copy-done((bf16[32,1,32,2048]{3,2,1,0:T(8,128)(2,1)S(1)}, bf16[32,1,32,2048]{3,2,1,0:T(8,128)(2,1)}, u32[]{:S(2)}) %copy-start) | copy-done | bytes 4194328
  8.3 1.0 pack_kv.1
  9.3 1.8 %collective-permute-start = (bf16[2,1024,256]{2,1,0:T(8,128)(2,1)S(1)}, bf16[2,1024,256]{2,1,0:T(8,128)(2,1)S(1)}, u32[]{:S(2)}, u32[]{:S(2)}) collective-permute-start(bf16[2,1024,256]{2,1,0:T(8,128)(2,1)S(1)} %get-tuple-element.55), channel_id=1, source_target_pairs={{0,2},{1,3},{2,0},{3,1},{4,6},{5,7},{6,4},{7,5},{8,10},{9,11},{10,... | collective-permute-start | bytes 3145736 | tf_op jit(solution)/shard_map/ppermute | solution.py:441
  11.3 3.1 %collective-permute-done.3.refs_3_ = bf16[2,320,128]{2,1,0:T(8,128)(2,1)S(1)} collective-permute-done((bf16[2,320,128]{2,1,0:T(8,128)(2,1)}, bf16[2,320,128]{2,1,0:T(8,128)(2,1)S(1)}, u32[]{:S(2)}, u32[]{:S(2)}) %collective-permute-start.3) | collective-permute-done | bytes 163872 | tf_op jit(solution)/shard_map/ppermute | solution.py:441
  14.7 4.1 %collective-permute-start.4 = (bf16[4,256,128]{2,1,0:T(8,128)(2,1)S(1)}, bf16[4,256,128]{2,1,0:T(8,128)(2,1)S(1)}, u32[]{:S(2)}, u32[]{:S(2)}) collective-permute-start(bf16[4,256,128]{2,1,0:T(8,128)(2,1)S(1)} %pad_maximum_fusion), channel_id=1, source_target_pairs={{0,12},{1,13},{2,14},{3,15},{4,0},{5,1},{6,2},{7,3},{8,4},{9,5},{1... | collective-permute-start | bytes 786440 | tf_op jit(solution)/shard_map/ppermute | solution.py:444
  18.8 6.7 %collective-permute-done.4.refs_0_ = bf16[4,256,128]{2,1,0:T(8,128)(2,1)S(1)} collective-permute-done((bf16[4,256,128]{2,1,0:T(8,128)(2,1)S(1)}, bf16[4,256,128]{2,1,0:T(8,128)(2,1)S(1)}, u32[]{:S(2)}, u32[]{:S(2)}) %collective-permute-start.4) | collective-permute-done | bytes 262176 | tf_op jit(solution)/shard_map/ppermute | solution.py:444
  25.5 4.3 %collective-permute-start.5 = (bf16[4,256,128]{2,1,0:T(8,128)(2,1)S(1)}, bf16[4,256,128]{2,1,0:T(8,128)(2,1)S(1)}, u32[]{:S(2)}, u32[]{:S(2)}) collective-permute-start(bf16[4,256,128]{2,1,0:T(8,128)(2,1)S(1)} %collective-permute-done.4.refs_0_), channel_id=1, source_target_pairs={{0,12},{1,13},{2,14},{3,15},{4,0},{5,1},{6,2},{7,3},{8,4},{9,5},{1... | collective-permute-start | bytes 786440 | tf_op jit(solution)/shard_map/ppermute | solution.py:444
  29.8 2.2 %collective-permute-done.6.refs_2_ = bf16[4,256,128]{2,1,0:T(8,128)(2,1)S(1)} collective-permute-done((bf16[4,256,128]{2,1,0:T(8,128)(2,1)S(1)}, bf16[4,256,128]{2,1,0:T(8,128)(2,1)S(1)}, u32[]{:S(2)}, u32[]{:S(2)}) %collective-permute-start.6) | collective-permute-done | bytes 262176 | tf_op jit(solution)/shard_map/ppermute | solution.py:444
  32.1 4.6 %collective-permute-done.5.refs_1_ = bf16[4,256,128]{2,1,0:T(8,128)(2,1)S(1)} collective-permute-done((bf16[4,256,128]{2,1,0:T(8,128)(2,1)S(1)}, bf16[4,256,128]{2,1,0:T(8,128)(2,1)S(1)}, u32[]{:S(2)}, u32[]{:S(2)}) %collective-permute-start.5) | collective-permute-done | bytes 262176 | tf_op jit(solution)/shard_map/ppermute | solution.py:444
  37.0 1.8 %collective-permute-start.12 = (bf16[2,1024,256]{2,1,0:T(8,128)(2,1)S(1)}, bf16[2,1024,256]{2,1,0:T(8,128)(2,1)S(1)}, u32[]{:S(2)}, u32[]{:S(2)}) collective-permute-start(bf16[2,1024,256]{2,1,0:T(8,128)(2,1)S(1)} %get-tuple-element.78), channel_id=1, source_target_pairs={{0,2},{1,3},{2,0},{3,1},{4,6},{5,7},{6,4},{7,5},{8,10},{9,11},{10,... | collective-permute-start | bytes 3145736 | tf_op jit(solution)/shard_map/ppermute | solution.py:441
  38.9 1.6 %collective-permute-start.14 = (bf16[4,256,128]{2,1,0:T(8,128)(2,1)S(1)}, bf16[4,256,128]{2,1,0:T(8,128)(2,1)S(1)}, u32[]{:S(2)}, u32[]{:S(2)}) collective-permute-start(bf16[4,256,128]{2,1,0:T(8,128)(2,1)S(1)} %pad_maximum_fusion.1), channel_id=1, source_target_pairs={{0,4},{1,5},{2,6},{3,7},{4,8},{5,9},{6,10},{7,11},{8,12},{9,13},{1... | collective-permute-start | bytes 786440 | tf_op jit(solution)/shard_map/ppermute | solution.py:444
  40.6 2.2 %collective-permute-start.13 = (bf16[4,256,128]{2,1,0:T(8,128)(2,1)S(1)}, bf16[4,256,128]{2,1,0:T(8,128)(2,1)S(1)}, u32[]{:S(2)}, u32[]{:S(2)}) collective-permute-start(bf16[4,256,128]{2,1,0:T(8,128)(2,1)S(1)} %pad_maximum_fusion.1), channel_id=1, source_target_pairs={{0,12},{1,13},{2,14},{3,15},{4,0},{5,1},{6,2},{7,3},{8,4},{9,5},{1... | collective-permute-start | bytes 786440 | tf_op jit(solution)/shard_map/ppermute | solution.py:444
  42.8 7.1 %collective-permute-done.14.refs_2_ = bf16[4,256,128]{2,1,0:T(8,128)(2,1)S(1)} collective-permute-done((bf16[4,256,128]{2,1,0:T(8,128)(2,1)S(1)}, bf16[4,256,128]{2,1,0:T(8,128)(2,1)S(1)}, u32[]{:S(2)}, u32[]{:S(2)}) %collective-permute-start.14) | collective-permute-done | bytes 262176 | tf_op jit(solution)/shard_map/ppermute | solution.py:444
  49.9 6.8 %attend_others.2 = (bf16[272,512]{1,0:T(8,128)(2,1)S(1)}, bf16[272,512]{1,0:T(8,128)(2,1)S(1)}, bf16[272,512]{1,0:T(8,128)(2,1)S(1)}) custom-call(s32[8]{0:T(128)S(1)} %copy-done.2, s32[16]{0:T(128)S(1)} %copy-done.3, bf16[32,32,2048]{2,1,0:T(8,128)(2,1)} %bitcast.11, bf16[2,32,32,256]{3,2,1,0:T(8,128)(2,1)S(1)} %bitcast.16, ...), custom_call_target="tpu_custom_call" | custom-call | bytes 1024 | tf_op jit(solution)/shard_map/attend_others/pallas_call | solution.py:296
  56.8 6.1 %collective-permute-start.9 = (bf16[272,512]{1,0:T(8,128)(2,1)S(1)}, bf16[272,512]{1,0:T(8,128)(2,1)S(1)}, u32[]{:S(2)}, u32[]{:S(2)}) collective-permute-start(bf16[272,512]{1,0:T(8,128)(2,1)S(1)} %get-tuple-element.73), channel_id=1, source_target_pairs={{0,4},{1,5},{2,6},{3,7},{4,8},{5,9},{6,10},{7,11},{8,12},{9,13},{1... | collective-permute-start | bytes 835592 | tf_op jit(solution)/shard_map/ppermute | solution.py:444
  63.8 6.4 %collective-permute-done.9.two_ref = bf16[272,512]{1,0:T(8,128)(2,1)S(1)} collective-permute-done((bf16[272,512]{1,0:T(8,128)(2,1)S(1)}, bf16[272,512]{1,0:T(8,128)(2,1)S(1)}, u32[]{:S(2)}, u32[]{:S(2)}) %collective-permute-start.9) | collective-permute-done | bytes 278560 | tf_op jit(solution)/shard_map/ppermute | solution.py:444
  70.2 2.8 %collective-permute-done.10.refs_0_ = bf16[272,512]{1,0:T(8,128)(2,1)S(1)} collective-permute-done((bf16[272,512]{1,0:T(8,128)(2,1)S(1)}, bf16[272,512]{1,0:T(8,128)(2,1)S(1)}, u32[]{:S(2)}, u32[]{:S(2)}) %collective-permute-start.10) | collective-permute-done | bytes 278560 | tf_op jit(solution)/shard_map/ppermute | solution.py:444
  73.9 4.0 %attend_own.2 = (f32[2,128,512]{2,1,0:T(8,128)S(1)}, f32[2,8,512]{2,1,0:T(8,128)S(1)}) custom-call(s32[8]{0:T(128)S(1)} %copy-done.2, s32[16]{0:T(128)S(1)} %copy-done.3, bf16[32,32,2048]{2,1,0:T(8,128)(2,1)} %bitcast.12, bf16[2,32,32,256]{3,2,1,0:T(8,128)(2,1)S(1)} %bitcast.17, bf16[2,32,32,256]{3,2,1,0:T(8,128)(2,1)S(1)} %bitcast.21, ...), custom_call_target="tpu_custom_call" | custom-call | bytes 1024 | tf_op jit(solution)/shard_map/attend_own/pallas_call | solution.py:296
  77.9 6.8 %attend_others.3 = (bf16[272,512]{1,0:T(8,128)(2,1)S(1)}, bf16[272,512]{1,0:T(8,128)(2,1)S(1)}, bf16[272,512]{1,0:T(8,128)(2,1)S(1)}) custom-call(s32[8]{0:T(128)S(1)} %copy-done.2, s32[16]{0:T(128)S(1)} %copy-done.3, bf16[32,32,2048]{2,1,0:T(8,128)(2,1)} %bitcast.13, bf16[2,32,32,256]{3,2,1,0:T(8,128)(2,1)S(1)} %bitcast.18, ...), custom_call_target="tpu_custom_call" | custom-call | bytes 1024 | tf_op jit(solution)/shard_map/attend_others/pallas_call | solution.py:296
  85.1 3.3 %collective-permute-start.20 = (bf16[272,512]{1,0:T(8,128)(2,1)S(1)}, bf16[272,512]{1,0:T(8,128)(2,1)S(1)}, u32[]{:S(2)}, u32[]{:S(2)}) collective-permute-start(bf16[272,512]{1,0:T(8,128)(2,1)S(1)} %get-tuple-element.97), channel_id=1, source_target_pairs={{0,12},{1,13},{2,14},{3,15},{4,0},{5,1},{6,2},{7,3},{8,4},{9,5},{1... | collective-permute-start | bytes 835592 | tf_op jit(solution)/shard_map/ppermute | solution.py:444
  88.4 6.8 %collective-permute-done.20.two_ref = bf16[272,512]{1,0:T(8,128)(2,1)S(1)} collective-permute-done((bf16[272,512]{1,0:T(8,128)(2,1)S(1)}, bf16[272,512]{1,0:T(8,128)(2,1)S(1)}, u32[]{:S(2)}, u32[]{:S(2)}) %collective-permute-start.20) | collective-permute-done | bytes 278560 | tf_op jit(solution)/shard_map/ppermute | solution.py:444
  95.2 4.1 %collective-permute-done.21.refs_0_ = bf16[272,512]{1,0:T(8,128)(2,1)S(1)} collective-permute-done((bf16[272,512]{1,0:T(8,128)(2,1)S(1)}, bf16[272,512]{1,0:T(8,128)(2,1)S(1)}, u32[]{:S(2)}, u32[]{:S(2)}) %collective-permute-start.21) | collective-permute-done | bytes 278560 | tf_op jit(solution)/shard_map/ppermute | solution.py:444
  99.4 1.5 %collective-permute-start.22 = (bf16[272,512]{1,0:T(8,128)(2,1)S(1)}, bf16[272,512]{1,0:T(8,128)(2,1)S(1)}, u32[]{:S(2)}, u32[]{:S(2)}) collective-permute-start(bf16[272,512]{1,0:T(8,128)(2,1)S(1)} %merge.3), channel_id=1, source_target_pairs={{0,12},{1,13},{2,14},{3,15},{4,0},{5,1},{6,2},{7,3},{8,4},{9,5},{1... | collective-permute-start | bytes 835592 | tf_op jit(solution)/shard_map/ppermute | solution.py:444
  100.9 4.0 %attend_own.3 = (f32[2,128,512]{2,1,0:T(8,128)S(1)}, f32[2,8,512]{2,1,0:T(8,128)S(1)}) custom-call(s32[8]{0:T(128)S(1)} %copy-done.2, s32[16]{0:T(128)S(1)} %copy-done.3, bf16[32,32,2048]{2,1,0:T(8,128)(2,1)} %bitcast.14, bf16[2,32,32,256]{3,2,1,0:T(8,128)(2,1)S(1)} %bitcast.19, bf16[2,32,32,256]{3,2,1,0:T(8,128)(2,1)S(1)} %bitcast.23, ...), custom_call_target="tpu_custom_call" | custom-call | bytes 1024 | tf_op jit(solution)/shard_map/attend_own/pallas_call | solution.py:296
  105.5 1.4 %collective-permute-start.19 = (bf16[320,128]{1,0:T(8,128)(2,1)S(1)}, bf16[320,128]{1,0:T(8,128)(2,1)S(1)}, u32[]{:S(2)}, u32[]{:S(2)}) collective-permute-start(bf16[320,128]{1,0:T(8,128)(2,1)S(1)} %get-tuple-element.91), channel_id=1, source_target_pairs={{0,3},{1,2},{2,1},{3,0},{4,7},{5,6},{6,5},{7,4},{8,11},{9,10},{10,... | collective-permute-start | bytes 245768 | tf_op jit(solution)/shard_map/ppermute | solution.py:441
  108.0 1.1 collective-permute-start.25
  109.1 1.1 collective-permute-done.18.refs_2_
  110.2 1.0 collective-permute-done.19.refs_3_
  111.2 2.5 %collective-permute-done.24.refs_6_ = bf16[320,128]{1,0:T(8,128)(2,1)S(1)} collective-permute-done((bf16[320,128]{1,0:T(8,128)(2,1)S(1)}, bf16[320,128]{1,0:T(8,128)(2,1)S(1)}, u32[]{:S(2)}, u32[]{:S(2)}) %collective-permute-start.24) | collective-permute-done | bytes 81952 | tf_op jit(solution)/shard_map/ppermute | solution.py:441
  114.7 1.5 %emit.1 = (bf16[8,4,8192]{2,1,0:T(4,128)(2,1)}, bf16[8,4,8192]{2,1,0:T(4,128)(2,1)}) custom-call(bf16[320,128]{1,0:T(8,128)(2,1)S(1)} %get-tuple-element.88.refs_0_, bf16[320,128]{1,0:T(8,128)(2,1)S(1)} %collective-permute-done.17.refs_1_, bf16[320,128]{1,0:T(8,128)(2,1)S(1)} %collective-permute-done.18.refs_2_, ...), custom_call_target="tpu_custom_call" | custom-call | flops 1048576 | bytes 2097152 | tf_op jit(solution)/shard_map/emit/pallas_call | solution.py:423
  (45 shorter events, 6.7 us)
Async XLA Ops:
  0.6 49.3 %copy-start.3 = (s32[16]{0:T(128)S(1)}, s32[16]{0:T(128)}, u32[]{:S(2)}) copy-start(s32[16]{0:T(128)} %slots_ref.7) | copy-start | bytes 196
  0.6 49.3 %copy-start.2 = (s32[8]{0:T(128)S(1)}, s32[8]{0:T(128)}, u32[]{:S(2)}) copy-start(s32[8]{0:T(128)} %counts_ref.7) | copy-start | bytes 100
  2.9 8.2 %collective-permute-start.1 = (bf16[2,320,128]{2,1,0:T(8,128)(2,1)}, bf16[2,320,128]{2,1,0:T(8,128)(2,1)S(1)}, u32[]{:S(2)}, u32[]{:S(2)}) collective-permute-start(bf16[2,320,128]{2,1,0:T(8,128)(2,1)} %get-tuple-element.58), channel_id=1, source_target_pairs={{0,1},{1,0},{2,3},{3,2},{4,5},{5,4},{6,7},{7,6},{8,9},{9,8},{10,11... | collective-permute-start | bytes 491528 | tf_op jit(solution)/shard_map/ppermute | solution.py:441
  3.4 7.9 %collective-permute-start.2 = (bf16[2,320,128]{2,1,0:T(8,128)(2,1)}, bf16[2,320,128]{2,1,0:T(8,128)(2,1)S(1)}, u32[]{:S(2)}, u32[]{:S(2)}) collective-permute-start(bf16[2,320,128]{2,1,0:T(8,128)(2,1)} %get-tuple-element.59), channel_id=1, source_target_pairs={{0,2},{1,3},{2,0},{3,1},{4,6},{5,7},{6,4},{7,5},{8,10},{9,11},{10,... | collective-permute-start | bytes 491528 | tf_op jit(solution)/shard_map/ppermute | solution.py:441
  6.0 8.3 %collective-permute-start.3 = (bf16[2,320,128]{2,1,0:T(8,128)(2,1)}, bf16[2,320,128]{2,1,0:T(8,128)(2,1)S(1)}, u32[]{:S(2)}, u32[]{:S(2)}) collective-permute-start(bf16[2,320,128]{2,1,0:T(8,128)(2,1)} %get-tuple-element.60), channel_id=1, source_target_pairs={{0,3},{1,2},{2,1},{3,0},{4,7},{5,6},{6,5},{7,4},{8,11},{9,10},{10,... | collective-permute-start | bytes 491528 | tf_op jit(solution)/shard_map/ppermute | solution.py:441
  6.1 2.2 %copy-start = (bf16[32,1,32,2048]{3,2,1,0:T(8,128)(2,1)S(1)}, bf16[32,1,32,2048]{3,2,1,0:T(8,128)(2,1)}, u32[]{:S(2)}) copy-start(bf16[32,1,32,2048]{3,2,1,0:T(8,128)(2,1)} %param.5) | copy-start | bytes 12582916
  8.3 6.3 %copy-start.1 = (bf16[2,320,128]{2,1,0:T(8,128)(2,1)S(1)}, bf16[2,320,128]{2,1,0:T(8,128)(2,1)}, u32[]{:S(2)}) copy-start(bf16[2,320,128]{2,1,0:T(8,128)(2,1)} %get-tuple-element.61.refs_0_) | copy-start | bytes 491524
  9.3 27.7 %collective-permute-start = (bf16[2,1024,256]{2,1,0:T(8,128)(2,1)S(1)}, bf16[2,1024,256]{2,1,0:T(8,128)(2,1)S(1)}, u32[]{:S(2)}, u32[]{:S(2)}) collective-permute-start(bf16[2,1024,256]{2,1,0:T(8,128)(2,1)S(1)} %get-tuple-element.55), channel_id=1, source_target_pairs={{0,2},{1,3},{2,0},{3,1},{4,6},{5,7},{6,4},{7,5},{8,10},{9,11},{10,... | collective-permute-start | bytes 3145736 | tf_op jit(solution)/shard_map/ppermute | solution.py:441
  14.4 22.6 %collective-permute-start.7 = (bf16[2,1024,256]{2,1,0:T(8,128)(2,1)S(1)}, bf16[2,1024,256]{2,1,0:T(8,128)(2,1)S(1)}, u32[]{:S(2)}, u32[]{:S(2)}) collective-permute-start(bf16[2,1024,256]{2,1,0:T(8,128)(2,1)S(1)} %get-tuple-element.65), channel_id=1, source_target_pairs={{0,1},{1,0},{2,3},{3,2},{4,5},{5,4},{6,7},{7,6},{8,9},{9,8},{10,11... | collective-permute-start | bytes 3145736 | tf_op jit(solution)/shard_map/ppermute | solution.py:441
  14.7 10.8 %collective-permute-start.4 = (bf16[4,256,128]{2,1,0:T(8,128)(2,1)S(1)}, bf16[4,256,128]{2,1,0:T(8,128)(2,1)S(1)}, u32[]{:S(2)}, u32[]{:S(2)}) collective-permute-start(bf16[4,256,128]{2,1,0:T(8,128)(2,1)S(1)} %pad_maximum_fusion), channel_id=1, source_target_pairs={{0,12},{1,13},{2,14},{3,15},{4,0},{5,1},{6,2},{7,3},{8,4},{9,5},{1... | collective-permute-start | bytes 786440 | tf_op jit(solution)/shard_map/ppermute | solution.py:444
  18.8 13.3 %collective-permute-start.6 = (bf16[4,256,128]{2,1,0:T(8,128)(2,1)S(1)}, bf16[4,256,128]{2,1,0:T(8,128)(2,1)S(1)}, u32[]{:S(2)}, u32[]{:S(2)}) collective-permute-start(bf16[4,256,128]{2,1,0:T(8,128)(2,1)S(1)} %pad_maximum_fusion), channel_id=1, source_target_pairs={{0,4},{1,5},{2,6},{3,7},{4,8},{5,9},{6,10},{7,11},{8,12},{9,13},{1... | collective-permute-start | bytes 786440 | tf_op jit(solution)/shard_map/ppermute | solution.py:444
  25.5 11.1 %collective-permute-start.5 = (bf16[4,256,128]{2,1,0:T(8,128)(2,1)S(1)}, bf16[4,256,128]{2,1,0:T(8,128)(2,1)S(1)}, u32[]{:S(2)}, u32[]{:S(2)}) collective-permute-start(bf16[4,256,128]{2,1,0:T(8,128)(2,1)S(1)} %collective-permute-done.4.refs_0_), channel_id=1, source_target_pairs={{0,12},{1,13},{2,14},{3,15},{4,0},{5,1},{6,2},{7,3},{8,4},{9,5},{1... | collective-permute-start | bytes 786440 | tf_op jit(solution)/shard_map/ppermute | solution.py:444
  37.0 26.7 %collective-permute-start.12 = (bf16[2,1024,256]{2,1,0:T(8,128)(2,1)S(1)}, bf16[2,1024,256]{2,1,0:T(8,128)(2,1)S(1)}, u32[]{:S(2)}, u32[]{:S(2)}) collective-permute-start(bf16[2,1024,256]{2,1,0:T(8,128)(2,1)S(1)} %get-tuple-element.78), channel_id=1, source_target_pairs={{0,2},{1,3},{2,0},{3,1},{4,6},{5,7},{6,4},{7,5},{8,10},{9,11},{10,... | collective-permute-start | bytes 3145736 | tf_op jit(solution)/shard_map/ppermute | solution.py:441
  38.8 11.1 %collective-permute-start.8 = (bf16[1024,256]{1,0:T(8,128)(2,1)S(1)}, bf16[1024,256]{1,0:T(8,128)(2,1)S(1)}, u32[]{:S(2)}, u32[]{:S(2)}) collective-permute-start(bf16[1024,256]{1,0:T(8,128)(2,1)S(1)} %slice_bitcast_fusion.1), channel_id=1, source_target_pairs={{0,1},{1,0},{2,3},{3,2},{4,5},{5,4},{6,7},{7,6},{8,9},{9,8},{10,11... | collective-permute-start | bytes 1572872 | tf_op jit(solution)/shard_map/ppermute | solution.py:441
  38.9 11.0 %collective-permute-start.14 = (bf16[4,256,128]{2,1,0:T(8,128)(2,1)S(1)}, bf16[4,256,128]{2,1,0:T(8,128)(2,1)S(1)}, u32[]{:S(2)}, u32[]{:S(2)}) collective-permute-start(bf16[4,256,128]{2,1,0:T(8,128)(2,1)S(1)} %pad_maximum_fusion.1), channel_id=1, source_target_pairs={{0,4},{1,5},{2,6},{3,7},{4,8},{5,9},{6,10},{7,11},{8,12},{9,13},{1... | collective-permute-start | bytes 786440 | tf_op jit(solution)/shard_map/ppermute | solution.py:444
  40.6 23.2 %collective-permute-start.13 = (bf16[4,256,128]{2,1,0:T(8,128)(2,1)S(1)}, bf16[4,256,128]{2,1,0:T(8,128)(2,1)S(1)}, u32[]{:S(2)}, u32[]{:S(2)}) collective-permute-start(bf16[4,256,128]{2,1,0:T(8,128)(2,1)S(1)} %pad_maximum_fusion.1), channel_id=1, source_target_pairs={{0,12},{1,13},{2,14},{3,15},{4,0},{5,1},{6,2},{7,3},{8,4},{9,5},{1... | collective-permute-start | bytes 786440 | tf_op jit(solution)/shard_map/ppermute | solution.py:444
  49.9 13.8 %collective-permute-start.15 = (bf16[4,256,128]{2,1,0:T(8,128)(2,1)S(1)}, bf16[4,256,128]{2,1,0:T(8,128)(2,1)S(1)}, u32[]{:S(2)}, u32[]{:S(2)}) collective-permute-start(bf16[4,256,128]{2,1,0:T(8,128)(2,1)S(1)} %collective-permute-done.14.refs_2_), channel_id=1, source_target_pairs={{0,4},{1,5},{2,6},{3,7},{4,8},{5,9},{6,10},{7,11},{8,12},{9,13},{1... | collective-permute-start | bytes 786440 | tf_op jit(solution)/shard_map/ppermute | solution.py:444
  56.8 13.4 %collective-permute-start.9 = (bf16[272,512]{1,0:T(8,128)(2,1)S(1)}, bf16[272,512]{1,0:T(8,128)(2,1)S(1)}, u32[]{:S(2)}, u32[]{:S(2)}) collective-permute-start(bf16[272,512]{1,0:T(8,128)(2,1)S(1)} %get-tuple-element.73), channel_id=1, source_target_pairs={{0,4},{1,5},{2,6},{3,7},{4,8},{5,9},{6,10},{7,11},{8,12},{9,13},{1... | collective-permute-start | bytes 835592 | tf_op jit(solution)/shard_map/ppermute | solution.py:444
  62.9 10.1 %collective-permute-start.10 = (bf16[272,512]{1,0:T(8,128)(2,1)S(1)}, bf16[272,512]{1,0:T(8,128)(2,1)S(1)}, u32[]{:S(2)}, u32[]{:S(2)}) collective-permute-start(bf16[272,512]{1,0:T(8,128)(2,1)S(1)} %get-tuple-element.74), channel_id=1, source_target_pairs={{0,12},{1,13},{2,14},{3,15},{4,0},{5,1},{6,2},{7,3},{8,4},{9,5},{1... | collective-permute-start | bytes 835592 | tf_op jit(solution)/shard_map/ppermute | solution.py:444
  63.8 14.2 %collective-permute-start.16 = (bf16[1024,256]{1,0:T(8,128)(2,1)S(1)}, bf16[1024,256]{1,0:T(8,128)(2,1)S(1)}, u32[]{:S(2)}, u32[]{:S(2)}) collective-permute-start(bf16[1024,256]{1,0:T(8,128)(2,1)S(1)} %slice_bitcast_fusion), channel_id=1, source_target_pairs={{0,1},{1,0},{2,3},{3,2},{4,5},{5,4},{6,7},{7,6},{8,9},{9,8},{10,11... | collective-permute-start | bytes 1572872 | tf_op jit(solution)/shard_map/ppermute | solution.py:441
  73.1 11.6 %collective-permute-start.11 = (bf16[272,512]{1,0:T(8,128)(2,1)S(1)}, bf16[272,512]{1,0:T(8,128)(2,1)S(1)}, u32[]{:S(2)}, u32[]{:S(2)}) collective-permute-start(bf16[272,512]{1,0:T(8,128)(2,1)S(1)} %merge.2), channel_id=1, source_target_pairs={{0,4},{1,5},{2,6},{3,7},{4,8},{5,9},{6,10},{7,11},{8,12},{9,13},{1... | collective-permute-start | bytes 835592 | tf_op jit(solution)/shard_map/ppermute | solution.py:444
  85.1 10.1 %collective-permute-start.20 = (bf16[272,512]{1,0:T(8,128)(2,1)S(1)}, bf16[272,512]{1,0:T(8,128)(2,1)S(1)}, u32[]{:S(2)}, u32[]{:S(2)}) collective-permute-start(bf16[272,512]{1,0:T(8,128)(2,1)S(1)} %get-tuple-element.97), channel_id=1, source_target_pairs={{0,12},{1,13},{2,14},{3,15},{4,0},{5,1},{6,2},{7,3},{8,4},{9,5},{1... | collective-permute-start | bytes 835592 | tf_op jit(solution)/shard_map/ppermute | solution.py:444
  88.4 10.9 %collective-permute-start.21 = (bf16[272,512]{1,0:T(8,128)(2,1)S(1)}, bf16[272,512]{1,0:T(8,128)(2,1)S(1)}, u32[]{:S(2)}, u32[]{:S(2)}) collective-permute-start(bf16[272,512]{1,0:T(8,128)(2,1)S(1)} %get-tuple-element.98), channel_id=1, source_target_pairs={{0,4},{1,5},{2,6},{3,7},{4,8},{5,9},{6,10},{7,11},{8,12},{9,13},{1... | collective-permute-start | bytes 835592 | tf_op jit(solution)/shard_map/ppermute | solution.py:444
  99.4 7.4 %collective-permute-start.22 = (bf16[272,512]{1,0:T(8,128)(2,1)S(1)}, bf16[272,512]{1,0:T(8,128)(2,1)S(1)}, u32[]{:S(2)}, u32[]{:S(2)}) collective-permute-start(bf16[272,512]{1,0:T(8,128)(2,1)S(1)} %merge.3), channel_id=1, source_target_pairs={{0,12},{1,13},{2,14},{3,15},{4,0},{5,1},{6,2},{7,3},{8,4},{9,5},{1... | collective-permute-start | bytes 835592 | tf_op jit(solution)/shard_map/ppermute | solution.py:444
  100.9 7.1 %collective-permute-start.17 = (bf16[320,128]{1,0:T(8,128)(2,1)S(1)}, bf16[320,128]{1,0:T(8,128)(2,1)S(1)}, u32[]{:S(2)}, u32[]{:S(2)}) collective-permute-start(bf16[320,128]{1,0:T(8,128)(2,1)S(1)} %get-tuple-element.89), channel_id=1, source_target_pairs={{0,1},{1,0},{2,3},{3,2},{4,5},{5,4},{6,7},{7,6},{8,9},{9,8},{10,11... | collective-permute-start | bytes 245768 | tf_op jit(solution)/shard_map/ppermute | solution.py:441
  104.9 5.3 %collective-permute-start.18 = (bf16[320,128]{1,0:T(8,128)(2,1)S(1)}, bf16[320,128]{1,0:T(8,128)(2,1)S(1)}, u32[]{:S(2)}, u32[]{:S(2)}) collective-permute-start(bf16[320,128]{1,0:T(8,128)(2,1)S(1)} %get-tuple-element.90), channel_id=1, source_target_pairs={{0,2},{1,3},{2,0},{3,1},{4,6},{5,7},{6,4},{7,5},{8,10},{9,11},{10,... | collective-permute-start | bytes 245768 | tf_op jit(solution)/shard_map/ppermute | solution.py:441
  105.5 5.7 %collective-permute-start.19 = (bf16[320,128]{1,0:T(8,128)(2,1)S(1)}, bf16[320,128]{1,0:T(8,128)(2,1)S(1)}, u32[]{:S(2)}, u32[]{:S(2)}) collective-permute-start(bf16[320,128]{1,0:T(8,128)(2,1)S(1)} %get-tuple-element.91), channel_id=1, source_target_pairs={{0,3},{1,2},{2,1},{3,0},{4,7},{5,6},{6,5},{7,4},{8,11},{9,10},{10,... | collective-permute-start | bytes 245768 | tf_op jit(solution)/shard_map/ppermute | solution.py:441
  107.2 4.0 %collective-permute-start.23 = (bf16[320,128]{1,0:T(8,128)(2,1)S(1)}, bf16[320,128]{1,0:T(8,128)(2,1)S(1)}, u32[]{:S(2)}, u32[]{:S(2)}) collective-permute-start(bf16[320,128]{1,0:T(8,128)(2,1)S(1)} %get-tuple-element.103), channel_id=1, source_target_pairs={{0,1},{1,0},{2,3},{3,2},{4,5},{5,4},{6,7},{7,6},{8,9},{9,8},{10,11... | collective-permute-start | bytes 245768 | tf_op jit(solution)/shard_map/ppermute | solution.py:441
  107.5 6.2 %collective-permute-start.24 = (bf16[320,128]{1,0:T(8,128)(2,1)S(1)}, bf16[320,128]{1,0:T(8,128)(2,1)S(1)}, u32[]{:S(2)}, u32[]{:S(2)}) collective-permute-start(bf16[320,128]{1,0:T(8,128)(2,1)S(1)} %get-tuple-element.104), channel_id=1, source_target_pairs={{0,2},{1,3},{2,0},{3,1},{4,6},{5,7},{6,4},{7,5},{8,10},{9,11},{10,... | collective-permute-start | bytes 245768 | tf_op jit(solution)/shard_map/ppermute | solution.py:441
  108.0 6.7 %collective-permute-start.25 = (bf16[320,128]{1,0:T(8,128)(2,1)S(1)}, bf16[320,128]{1,0:T(8,128)(2,1)S(1)}, u32[]{:S(2)}, u32[]{:S(2)}) collective-permute-start(bf16[320,128]{1,0:T(8,128)(2,1)S(1)} %get-tuple-element.105), channel_id=1, source_target_pairs={{0,3},{1,2},{2,1},{3,0},{4,7},{5,6},{6,5},{7,4},{8,11},{9,10},{10,... | collective-permute-start | bytes 245768 | tf_op jit(solution)/shard_map/ppermute | solution.py:441

commit v5 on v4

--- a/solution.py
+++ b/solution.py
@@ -129,13 +129,13 @@
     return lax.dot_general(values, weights, (((0,), (0,)), ((), ())), preferred_element_type=F32)
 
 
-def attend_kernel(h, offsets, steps, max_tiles, counts_ref, slots_ref, kv_ref, near, same, passed, *refs):
+def attend_kernel(h, offsets, steps, counts_ref, slots_ref, kv_ref, near, same, passed, *refs):
     count = len(offsets)
     nq = QUAD if steps else count
     queries, refs = refs[:nq], refs[nq:]
     nout = 2 if steps else count
     outs, refs = refs[:nout], refs[nout:]
-    held, asked, fresh, state, acc, stage, sem = refs
+    held, asked, fresh, state, acc, stage, scores, weights, sem = refs
     nsample = lax.axis_size("sample")
     quads = nsample // QUAD
     index = lax.axis_index("sample")
@@ -199,29 +199,52 @@
         inside = jnp.clip(lax.rem(block, nsample) - QUAD * quad, 0, QUAD)
         return QUAD * lax.div(block, nsample) + inside
 
-    def one_pass(n, pair, low, high, tiles):
-        tokens = tiles * TILE
+    def one_prompt(n, pair, low, high):
+        tiles = lax.div(high - low + TILE_BLOCKS - 1, TILE_BLOCKS)
         query = asked[n, pl.ds(2 * pair, 2)].reshape(2 * size, HD)
-        row = pl.multiple_of(low * BLK, BLK)
-        s = scores_of(flat[pl.ds(row, tokens), 0:HD], query)
-        last = s[tokens - TILE:]
-        token = lax.broadcasted_iota(jnp.int32, last.shape, 0)
-        last = jnp.where(token < (high - low) * BLK - (tokens - TILE), last, NEG)
-        s = last if tiles == 1 else jnp.concatenate([s[:tokens - TILE], last], axis=0)
-        m = jnp.max(s, axis=0, keepdims=True)
+
+        def score(t, top):
+            row = pl.multiple_of((low + t * TILE_BLOCKS) * BLK, BLK)
+            s = scores_of(flat[pl.ds(row, TILE), 0:HD], query)
+            token = lax.broadcasted_iota(jnp.int32, s.shape, 0)
+            s = jnp.where(token < (high - low - t * TILE_BLOCKS) * BLK, s, NEG)
+            scores[pl.ds(pl.multiple_of(t * TILE, TILE), TILE)] = s
+            return jnp.maximum(top, jnp.max(s.reshape(TILE // 8, 8, 2 * size), axis=0))
+
+        before = state[pair, 0:1] if steps else jnp.full((1, 2 * size), NEG, F32)
+        top = lax.fori_loop(0, tiles, score, jnp.broadcast_to(before, (8, 2 * size)))
+        m = jnp.max(top, axis=0, keepdims=True)
+        shift = m * EXP_SCALE
+
+        def raise_block(b, total):
+            rows = pl.ds(pl.multiple_of(b * BLK, BLK), BLK)
+            p = jnp.exp2(scores[rows] * EXP_SCALE - shift)
+            weights[rows] = p.astype(BF16)
+            return total + jnp.sum(p.reshape(BLK // 8, 8, 2 * size), axis=0)
+
+        def clear_block(b, _):
+            weights[pl.ds(pl.multiple_of(b * BLK, BLK), BLK)] = jnp.zeros((BLK, 2 * size), BF16)
+            return 0
+
+        total = lax.fori_loop(0, high - low, raise_block, jnp.zeros((8, 2 * size), F32))
+        lax.fori_loop(high - low, tiles * TILE_BLOCKS, clear_block, 0)
+        l = jnp.sum(total, axis=0, keepdims=True)
         if steps:
-            before = state[pair, 0:1]
-            m = jnp.maximum(m, before)
-        p = jnp.exp2((s - m) * EXP_SCALE)
-        l = jnp.sum(p, axis=0, keepdims=True)
-        out = values_by(flat[pl.ds(row, tokens), HD:2 * HD], p.astype(BF16))
-        if steps:
-            alpha = jnp.exp2((before - m) * EXP_SCALE)
+            alpha = jnp.exp2(before * EXP_SCALE - shift)
             l = l + alpha * state[pair, 1:2]
-            out = out + alpha * acc[pair]
+            acc[pair] = alpha * acc[pair]
+        else:
+            acc[pair] = jnp.zeros((HD, 2 * size), F32)
         state[pair, 0:1] = m
         state[pair, 1:2] = l
-        acc[pair] = out
+
+        def add(t, _):
+            row = pl.multiple_of((low + t * TILE_BLOCKS) * BLK, BLK)
+            p = weights[pl.ds(pl.multiple_of(t * TILE, TILE), TILE)]
+            acc[pair] += values_by(flat[pl.ds(row, TILE), HD:2 * HD], p)
+            return 0
+
+        lax.fori_loop(0, tiles, add, 0)
 
     def chunk(n, _):
         offset = jnp.int32(0) if steps else offset_of(n)
@@ -231,19 +254,7 @@
             prompt = slots_ref[QUAD * home + 2 * jnp.bitwise_xor(lax.div(mine, 2), pair)]
             start = lax.fori_loop(0, prompt, lambda p, total: total + counts_ref[p], jnp.int32(0))
             low, high = local_count(start), local_count(start + counts_ref[prompt])
-            tiles = lax.div(high - low + TILE_BLOCKS - 1, TILE_BLOCKS)
-            if not steps:
-                @pl.when(tiles == 0)
-                def _():
-                    state[pair, 0:1] = jnp.full((1, 2 * size), NEG, F32)
-                    state[pair, 1:2] = jnp.zeros((1, 2 * size), F32)
-                    acc[pair] = jnp.zeros((HD, 2 * size), F32)
-
-            for t in range(1, max_tiles + 1):
-                @pl.when(tiles == t)
-                def _(t=t):
-                    one_pass(n, pair, low, high, t)
-
+            one_prompt(n, pair, low, high)
             return 0
 
         lax.fori_loop(0, 2, prompt_of, 0)
@@ -294,7 +305,7 @@
     max_tiles = -(-(-(-MAXB // lax.axis_size("sample")) * QUAD) // TILE_BLOCKS)
     work = count * 2 * size * blocks * BLK
     return pl.pallas_call(
-        functools.partial(attend_kernel, h, offsets, steps, max_tiles),
+        functools.partial(attend_kernel, h, offsets, steps),
         out_shape=out_shape,
         in_specs=[SMEM, SMEM, ANY] + [ANY] * len(arrived) + [ANY] * len(queries),
         out_specs=[VMEM if steps else ANY] * len(out_shape),
@@ -305,6 +316,8 @@
             pltpu.VMEM((2, 8, 2 * size), F32),
             pltpu.VMEM((2, HD, 2 * size), F32),
             pltpu.VMEM((1 if steps else count, 2 * HD + STAT_ROWS, 2 * size), BF16),
+            pltpu.VMEM((max_tiles * TILE, 2 * size), F32),
+            pltpu.VMEM((max_tiles * TILE, 2 * size), BF16),
             pltpu.SemaphoreType.DMA((2 * QUAD + 2 * count + 8,)),
         ],
         compiler_params=params(48),
@@ -452,24 +465,23 @@
     near, msgs = lax.optimization_barrier((near, msgs))
     near = across(near, 1).reshape(HPD, -1, BLK, 2 * HD)
 
-    def gather(h):
-        own = jnp.stack([m[h, :GROUP * rows] for m in msgs])
-        ahead = (quads - 1 + (1 - h % 2)) // 2
+    own = jnp.stack([jnp.stack([m[h, :GROUP * rows] for m in msgs]) for h in range(HPD)])
+    first_hop = {shift: along(own, shift) for shift in ((-1, 1) if quads > 2 else (-1,))}
+    asked = []
+    for h in range(HPD):
+        ahead = (quads - 1 + (1 - h % 2)) // 2 if quads > 2 else quads - 1
         held = {}
         for shift, hops in ((-1, ahead), (1, quads - 1 - ahead)):
-            block = own
             for s in range(1, hops + 1):
-                block = along(block, shift)
+                block = first_hop[shift][h] if s == 1 else along(block, shift)
                 held[-shift * s % quads] = block
-        return held
-
-    asked = [gather(h) for h in range(HPD)]
+        asked.append(held)
     arrived, handed = [], []
     for h in range(HPD):
         source = far[h]
         if h:
-            source, arrived[-1], asked[h - 1], near = lax.optimization_barrier(
-                (source, arrived[-1], asked[h - 1], near)
+            source, arrived[-1], first_hop, near = lax.optimization_barrier(
+                (source, arrived[-1], first_hop, near)
             )
         arrived.append(across(source, 2))
         handed.append(arrived[h][1])

time: 116 us -> 135 us (1.16)
  waiting for transfers between devices: 50 us -> 63.4 us
  Pallas kernels: 27.2 us -> 38.1 us
  starting transfers between devices: 35.8 us -> 29 us
    ppermute x12 -> x10, waiting for transfers between devices: 40.7 us -> 54.5 us  [along(): lax.ppermute(array, 'sample', [(i, (i + shift * QUAD) % nsample) for i in...]
    pallas_call x4, Pallas kernels: 21.5 us -> 32.5 us  [attend(): pl.pallas_call(functools.partial(attend_kernel, h, offsets, steps), out_s...]
    ppermute x12 -> x10, starting transfers between devices: 24.8 us -> 18.3 us  [along(): lax.ppermute(array, 'sample', [(i, (i + shift * QUAD) % nsample) for i in...]
  transfers between devices with their start and end apart: 26 -> 24, of which waited for: 15 -> 13; matrix products, arithmetic and copies ran while one was open for 0% -> 0% of each run, Pallas kernels for 20% -> 25%
where the time goes in v5:
time: 135 us; the launch traced here: 134 us
  waiting for transfers between devices  63.4 us (47%)
  Pallas kernels  38.1 us (28%)
  starting transfers between devices  29 us (21%)
  local copies, waits for them, and re-layouts  2.38 us (2%)
    ppermute x10, waiting for transfers between devices, along(): lax.ppermute(array, 'sample', [(i, (i + shift * QUAD) % nsample) for i in...  54.5 us
    pallas_call x4, Pallas kernels, attend(): pl.pallas_call(functools.partial(attend_kernel, h, offsets, steps), out_s...  32.5 us
    ppermute x10, starting transfers between devices, along(): lax.ppermute(array, 'sample', [(i, (i + shift * QUAD) % nsample) for i in...  18.3 us
    ppermute x14, starting transfers between devices, across(): return lax.ppermute(array, 'sample', [(i, i ^ k) for i in range(nsample)])  10.7 us
    ppermute x14, waiting for transfers between devices, across(): return lax.ppermute(array, 'sample', [(i, i ^ k) for i in range(nsample)])  8.91 us
  transfers between devices with their start and end apart: 24, of which 13 were waited for; matrix products, arithmetic and copies ran while one was open for 0% of the time, Pallas kernels for 25%

profile of v5, /device:TPU:0, one launch (start us, length us, event | category | flops | bytes accessed | tf_op | source)
XLA Modules:
  0.0 134.0 jit_solution(2200183536368321593)
XLA Ops:
  0.6 2.2 %pack_queries.1 = (bf16[2,320,128]{2,1,0:T(8,128)(2,1)}, bf16[2,320,128]{2,1,0:T(8,128)(2,1)}, bf16[2,320,128]{2,1,0:T(8,128)(2,1)}, bf16[2,320,128]{2,1,0:T(8,128)(2,1)}) custom-call(bf16[8,4,8192]{2,1,0:T(4,128)(2,1)} %q_hbm.1, bf16[8,4,2048]{2,1,0:T(4,128)(2,1)} %new_hbm.1), custom_call_target="tpu_custom_call" | custom-call | bytes 2097152 | tf_op jit(solution)/shard_map/pack_queries/pallas_call | solution.py:72
  2.9 0.5 collective-permute-start.1
  3.4 2.6 %collective-permute-start.2 = (bf16[2,320,128]{2,1,0:T(8,128)(2,1)}, bf16[2,320,128]{2,1,0:T(8,128)(2,1)S(1)}, u32[]{:S(2)}, u32[]{:S(2)}) collective-permute-start(bf16[2,320,128]{2,1,0:T(8,128)(2,1)} %get-tuple-element.56), channel_id=1, source_target_pairs={{0,2},{1,3},{2,0},{3,1},{4,6},{5,7},{6,4},{7,5},{8,10},{9,11},{10,... | collective-permute-start | bytes 491528 | tf_op jit(solution)/shard_map/ppermute | solution.py:454
  6.1 2.2 %copy-done = bf16[32,1,32,2048]{3,2,1,0:T(8,128)(2,1)S(1)} copy-done((bf16[32,1,32,2048]{3,2,1,0:T(8,128)(2,1)S(1)}, bf16[32,1,32,2048]{3,2,1,0:T(8,128)(2,1)}, u32[]{:S(2)}) %copy-start) | copy-done | bytes 4194328
  8.3 1.0 pack_kv.1
  9.3 1.8 %collective-permute-start = (bf16[2,1024,256]{2,1,0:T(8,128)(2,1)S(1)}, bf16[2,1024,256]{2,1,0:T(8,128)(2,1)S(1)}, u32[]{:S(2)}, u32[]{:S(2)}) collective-permute-start(bf16[2,1024,256]{2,1,0:T(8,128)(2,1)S(1)} %get-tuple-element.52), channel_id=1, source_target_pairs={{0,2},{1,3},{2,0},{3,1},{4,6},{5,7},{6,4},{7,5},{8,10},{9,11},{10,... | collective-permute-start | bytes 3145736 | tf_op jit(solution)/shard_map/ppermute | solution.py:454
  11.3 3.1 %collective-permute-done.3.refs_3_ = bf16[2,320,128]{2,1,0:T(8,128)(2,1)S(1)} collective-permute-done((bf16[2,320,128]{2,1,0:T(8,128)(2,1)}, bf16[2,320,128]{2,1,0:T(8,128)(2,1)S(1)}, u32[]{:S(2)}, u32[]{:S(2)}) %collective-permute-start.3) | collective-permute-done | bytes 163872 | tf_op jit(solution)/shard_map/ppermute | solution.py:454
  14.8 4.1 %collective-permute-start.4 = (bf16[2,4,256,128]{3,2,1,0:T(8,128)(2,1)S(1)}, bf16[2,4,256,128]{3,2,1,0:T(8,128)(2,1)S(1)}, u32[]{:S(2)}, u32[]{:S(2)}) collective-permute-start(bf16[2,4,256,128]{3,2,1,0:T(8,128)(2,1)S(1)} %pad_maximum_fusion), channel_id=1, source_target_pairs={{0,12},{1,13},{2,14},{3,15},{4,0},{5,1},{6,2},{7,3},{8,4},{9,5},{1... | collective-permute-start | bytes 1572872 | tf_op jit(solution)/shard_map/ppermute | solution.py:457
  18.9 12.3 %collective-permute-done.4 = bf16[2,4,256,128]{3,2,1,0:T(8,128)(2,1)S(1)} collective-permute-done((bf16[2,4,256,128]{3,2,1,0:T(8,128)(2,1)S(1)}, bf16[2,4,256,128]{3,2,1,0:T(8,128)(2,1)S(1)}, u32[]{:S(2)}, u32[]{:S(2)}) %collective-permute-start.4) | collective-permute-done | bytes 524320 | tf_op jit(solution)/shard_map/ppermute | solution.py:457
  31.2 11.1 %collective-permute-done.5 = bf16[2,4,256,128]{3,2,1,0:T(8,128)(2,1)S(1)} collective-permute-done((bf16[2,4,256,128]{3,2,1,0:T(8,128)(2,1)S(1)}, bf16[2,4,256,128]{3,2,1,0:T(8,128)(2,1)S(1)}, u32[]{:S(2)}, u32[]{:S(2)}) %collective-permute-start.5) | collective-permute-done | bytes 524320 | tf_op jit(solution)/shard_map/ppermute | solution.py:457
  42.4 1.5 %collective-permute-start.12 = (bf16[2,1024,256]{2,1,0:T(8,128)(2,1)S(1)}, bf16[2,1024,256]{2,1,0:T(8,128)(2,1)S(1)}, u32[]{:S(2)}, u32[]{:S(2)}) collective-permute-start(bf16[2,1024,256]{2,1,0:T(8,128)(2,1)S(1)} %get-tuple-element.72), channel_id=1, source_target_pairs={{0,2},{1,3},{2,0},{3,1},{4,6},{5,7},{6,4},{7,5},{8,10},{9,11},{10,... | collective-permute-start | bytes 3145736 | tf_op jit(solution)/shard_map/ppermute | solution.py:454
  44.1 1.8 %collective-permute-start.8 = (bf16[4,256,128]{2,1,0:T(8,128)(2,1)S(1)}, bf16[4,256,128]{2,1,0:T(8,128)(2,1)S(1)}, u32[]{:S(2)}, u32[]{:S(2)}) collective-permute-start(bf16[4,256,128]{2,1,0:T(8,128)(2,1)S(1)} %get-tuple-element.103.refs_0_), channel_id=1, source_target_pairs={{0,12},{1,13},{2,14},{3,15},{4,0},{5,1},{6,2},{7,3},{8,4},{9,5},{1... | collective-permute-start | bytes 786440 | tf_op jit(solution)/shard_map/ppermute | solution.py:457
  46.2 6.8 %collective-permute-done.8.refs_1_ = bf16[4,256,128]{2,1,0:T(8,128)(2,1)S(1)} collective-permute-done((bf16[4,256,128]{2,1,0:T(8,128)(2,1)S(1)}, bf16[4,256,128]{2,1,0:T(8,128)(2,1)S(1)}, u32[]{:S(2)}, u32[]{:S(2)}) %collective-permute-start.8) | collective-permute-done | bytes 262176 | tf_op jit(solution)/shard_map/ppermute | solution.py:457
  53.0 11.6 %attend_others.2 = (bf16[272,512]{1,0:T(8,128)(2,1)S(1)}, bf16[272,512]{1,0:T(8,128)(2,1)S(1)}, bf16[272,512]{1,0:T(8,128)(2,1)S(1)}) custom-call(s32[8]{0:T(128)S(1)} %copy-done.2, s32[16]{0:T(128)S(1)} %copy-done.3, bf16[32,32,2048]{2,1,0:T(8,128)(2,1)} %bitcast.23, bf16[2,32,32,256]{3,2,1,0:T(8,128)(2,1)S(1)} %bitcast.28, ...), custom_call_target="tpu_custom_call" | custom-call | bytes 1024 | tf_op jit(solution)/shard_map/attend_others/pallas_call | solution.py:307
  64.6 5.9 %collective-permute-start.9 = (bf16[272,512]{1,0:T(8,128)(2,1)S(1)}, bf16[272,512]{1,0:T(8,128)(2,1)S(1)}, u32[]{:S(2)}, u32[]{:S(2)}) collective-permute-start(bf16[272,512]{1,0:T(8,128)(2,1)S(1)} %get-tuple-element.67), channel_id=1, source_target_pairs={{0,4},{1,5},{2,6},{3,7},{4,8},{5,9},{6,10},{7,11},{8,12},{9,13},{1... | collective-permute-start | bytes 835592 | tf_op jit(solution)/shard_map/ppermute | solution.py:457
  70.7 6.9 %collective-permute-done.9.two_ref = bf16[272,512]{1,0:T(8,128)(2,1)S(1)} collective-permute-done((bf16[272,512]{1,0:T(8,128)(2,1)S(1)}, bf16[272,512]{1,0:T(8,128)(2,1)S(1)}, u32[]{:S(2)}, u32[]{:S(2)}) %collective-permute-start.9) | collective-permute-done | bytes 278560 | tf_op jit(solution)/shard_map/ppermute | solution.py:457
  77.6 5.0 %collective-permute-done.10.refs_0_ = bf16[272,512]{1,0:T(8,128)(2,1)S(1)} collective-permute-done((bf16[272,512]{1,0:T(8,128)(2,1)S(1)}, bf16[272,512]{1,0:T(8,128)(2,1)S(1)}, u32[]{:S(2)}, u32[]{:S(2)}) %collective-permute-start.10) | collective-permute-done | bytes 278560 | tf_op jit(solution)/shard_map/ppermute | solution.py:457
  82.8 4.7 %attend_own.2 = (f32[2,128,512]{2,1,0:T(8,128)S(1)}, f32[2,8,512]{2,1,0:T(8,128)S(1)}) custom-call(s32[8]{0:T(128)S(1)} %copy-done.2, s32[16]{0:T(128)S(1)} %copy-done.3, bf16[32,32,2048]{2,1,0:T(8,128)(2,1)} %bitcast.24, bf16[2,32,32,256]{3,2,1,0:T(8,128)(2,1)S(1)} %bitcast.29, bf16[2,32,32,256]{3,2,1,0:T(8,128)(2,1)S(1)} %bitcast.33, ...), custom_call_target="tpu_custom_call" | custom-call | bytes 1024 | tf_op jit(solution)/shard_map/attend_own/pallas_call | solution.py:307
  87.5 11.6 %attend_others.3 = (bf16[272,512]{1,0:T(8,128)(2,1)S(1)}, bf16[272,512]{1,0:T(8,128)(2,1)S(1)}, bf16[272,512]{1,0:T(8,128)(2,1)S(1)}) custom-call(s32[8]{0:T(128)S(1)} %copy-done.2, s32[16]{0:T(128)S(1)} %copy-done.3, bf16[32,32,2048]{2,1,0:T(8,128)(2,1)} %bitcast.25, bf16[2,32,32,256]{3,2,1,0:T(8,128)(2,1)S(1)} %bitcast.30, ...), custom_call_target="tpu_custom_call" | custom-call | bytes 1024 | tf_op jit(solution)/shard_map/attend_others/pallas_call | solution.py:307
  99.4 4.3 %collective-permute-start.18 = (bf16[272,512]{1,0:T(8,128)(2,1)S(1)}, bf16[272,512]{1,0:T(8,128)(2,1)S(1)}, u32[]{:S(2)}, u32[]{:S(2)}) collective-permute-start(bf16[272,512]{1,0:T(8,128)(2,1)S(1)} %get-tuple-element.91), channel_id=1, source_target_pairs={{0,12},{1,13},{2,14},{3,15},{4,0},{5,1},{6,2},{7,3},{8,4},{9,5},{1... | collective-permute-start | bytes 835592 | tf_op jit(solution)/shard_map/ppermute | solution.py:457
  103.7 7.1 %collective-permute-done.18.two_ref = bf16[272,512]{1,0:T(8,128)(2,1)S(1)} collective-permute-done((bf16[272,512]{1,0:T(8,128)(2,1)S(1)}, bf16[272,512]{1,0:T(8,128)(2,1)S(1)}, u32[]{:S(2)}, u32[]{:S(2)}) %collective-permute-start.18) | collective-permute-done | bytes 278560 | tf_op jit(solution)/shard_map/ppermute | solution.py:457
  110.8 5.2 %collective-permute-done.19.refs_0_ = bf16[272,512]{1,0:T(8,128)(2,1)S(1)} collective-permute-done((bf16[272,512]{1,0:T(8,128)(2,1)S(1)}, bf16[272,512]{1,0:T(8,128)(2,1)S(1)}, u32[]{:S(2)}, u32[]{:S(2)}) %collective-permute-start.19) | collective-permute-done | bytes 278560 | tf_op jit(solution)/shard_map/ppermute | solution.py:457
  116.2 1.8 %collective-permute-start.20 = (bf16[272,512]{1,0:T(8,128)(2,1)S(1)}, bf16[272,512]{1,0:T(8,128)(2,1)S(1)}, u32[]{:S(2)}, u32[]{:S(2)}) collective-permute-start(bf16[272,512]{1,0:T(8,128)(2,1)S(1)} %merge.3), channel_id=1, source_target_pairs={{0,12},{1,13},{2,14},{3,15},{4,0},{5,1},{6,2},{7,3},{8,4},{9,5},{1... | collective-permute-start | bytes 835592 | tf_op jit(solution)/shard_map/ppermute | solution.py:457
  118.0 4.7 %attend_own.3 = (f32[2,128,512]{2,1,0:T(8,128)S(1)}, f32[2,8,512]{2,1,0:T(8,128)S(1)}) custom-call(s32[8]{0:T(128)S(1)} %copy-done.2, s32[16]{0:T(128)S(1)} %copy-done.3, bf16[32,32,2048]{2,1,0:T(8,128)(2,1)} %bitcast.26, bf16[2,32,32,256]{3,2,1,0:T(8,128)(2,1)S(1)} %bitcast.31, bf16[2,32,32,256]{3,2,1,0:T(8,128)(2,1)S(1)} %bitcast.35, ...), custom_call_target="tpu_custom_call" | custom-call | bytes 1024 | tf_op jit(solution)/shard_map/attend_own/pallas_call | solution.py:307
  122.7 0.6 collective-permute-start.16
  123.3 1.4 %collective-permute-start.17 = (bf16[320,128]{1,0:T(8,128)(2,1)S(1)}, bf16[320,128]{1,0:T(8,128)(2,1)S(1)}, u32[]{:S(2)}, u32[]{:S(2)}) collective-permute-start(bf16[320,128]{1,0:T(8,128)(2,1)S(1)} %get-tuple-element.85), channel_id=1, source_target_pairs={{0,3},{1,2},{2,1},{3,0},{4,7},{5,6},{6,5},{7,4},{8,11},{9,10},{10,... | collective-permute-start | bytes 245768 | tf_op jit(solution)/shard_map/ppermute | solution.py:454
  125.8 1.1 collective-permute-start.23
  126.9 1.1 collective-permute-done.16.refs_2_
  128.0 1.0 collective-permute-done.17.refs_3_
  129.0 2.5 %collective-permute-done.22.refs_6_ = bf16[320,128]{1,0:T(8,128)(2,1)S(1)} collective-permute-done((bf16[320,128]{1,0:T(8,128)(2,1)S(1)}, bf16[320,128]{1,0:T(8,128)(2,1)S(1)}, u32[]{:S(2)}, u32[]{:S(2)}) %collective-permute-start.22) | collective-permute-done | bytes 81952 | tf_op jit(solution)/shard_map/ppermute | solution.py:454
  131.5 1.0 collective-permute-done.23.refs_7_
  132.5 1.5 %emit.1 = (bf16[8,4,8192]{2,1,0:T(4,128)(2,1)}, bf16[8,4,8192]{2,1,0:T(4,128)(2,1)}) custom-call(bf16[320,128]{1,0:T(8,128)(2,1)S(1)} %get-tuple-element.82.refs_0_, bf16[320,128]{1,0:T(8,128)(2,1)S(1)} %collective-permute-done.15.refs_1_, bf16[320,128]{1,0:T(8,128)(2,1)S(1)} %collective-permute-done.16.refs_2_, ...), custom_call_target="tpu_custom_call" | custom-call | flops 1048576 | bytes 2097152 | tf_op jit(solution)/shard_map/emit/pallas_call | solution.py:436
  (44 shorter events, 3.2 us)
Async XLA Ops:
  2.9 8.2 %collective-permute-start.1 = (bf16[2,320,128]{2,1,0:T(8,128)(2,1)}, bf16[2,320,128]{2,1,0:T(8,128)(2,1)S(1)}, u32[]{:S(2)}, u32[]{:S(2)}) collective-permute-start(bf16[2,320,128]{2,1,0:T(8,128)(2,1)} %get-tuple-element.55), channel_id=1, source_target_pairs={{0,1},{1,0},{2,3},{3,2},{4,5},{5,4},{6,7},{7,6},{8,9},{9,8},{10,11... | collective-permute-start | bytes 491528 | tf_op jit(solution)/shard_map/ppermute | solution.py:454
  3.4 7.9 %collective-permute-start.2 = (bf16[2,320,128]{2,1,0:T(8,128)(2,1)}, bf16[2,320,128]{2,1,0:T(8,128)(2,1)S(1)}, u32[]{:S(2)}, u32[]{:S(2)}) collective-permute-start(bf16[2,320,128]{2,1,0:T(8,128)(2,1)} %get-tuple-element.56), channel_id=1, source_target_pairs={{0,2},{1,3},{2,0},{3,1},{4,6},{5,7},{6,4},{7,5},{8,10},{9,11},{10,... | collective-permute-start | bytes 491528 | tf_op jit(solution)/shard_map/ppermute | solution.py:454
  6.0 8.3 %collective-permute-start.3 = (bf16[2,320,128]{2,1,0:T(8,128)(2,1)}, bf16[2,320,128]{2,1,0:T(8,128)(2,1)S(1)}, u32[]{:S(2)}, u32[]{:S(2)}) collective-permute-start(bf16[2,320,128]{2,1,0:T(8,128)(2,1)} %get-tuple-element.57), channel_id=1, source_target_pairs={{0,3},{1,2},{2,1},{3,0},{4,7},{5,6},{6,5},{7,4},{8,11},{9,10},{10,... | collective-permute-start | bytes 491528 | tf_op jit(solution)/shard_map/ppermute | solution.py:454
  6.1 2.2 %copy-start = (bf16[32,1,32,2048]{3,2,1,0:T(8,128)(2,1)S(1)}, bf16[32,1,32,2048]{3,2,1,0:T(8,128)(2,1)}, u32[]{:S(2)}) copy-start(bf16[32,1,32,2048]{3,2,1,0:T(8,128)(2,1)} %param.5) | copy-start | bytes 12582916
  8.3 6.4 %copy-start.1 = (bf16[2,320,128]{2,1,0:T(8,128)(2,1)S(1)}, bf16[2,320,128]{2,1,0:T(8,128)(2,1)}, u32[]{:S(2)}) copy-start(bf16[2,320,128]{2,1,0:T(8,128)(2,1)} %get-tuple-element.58.refs_0_) | copy-start | bytes 491524
  9.2 43.8 %copy-start.2 = (s32[8]{0:T(128)S(1)}, s32[8]{0:T(128)}, u32[]{:S(2)}) copy-start(s32[8]{0:T(128)} %counts_ref.7) | copy-start | bytes 100
  9.3 43.8 %copy-start.3 = (s32[16]{0:T(128)S(1)}, s32[16]{0:T(128)}, u32[]{:S(2)}) copy-start(s32[16]{0:T(128)} %slots_ref.7) | copy-start | bytes 196
  9.3 33.1 %collective-permute-start = (bf16[2,1024,256]{2,1,0:T(8,128)(2,1)S(1)}, bf16[2,1024,256]{2,1,0:T(8,128)(2,1)S(1)}, u32[]{:S(2)}, u32[]{:S(2)}) collective-permute-start(bf16[2,1024,256]{2,1,0:T(8,128)(2,1)S(1)} %get-tuple-element.52), channel_id=1, source_target_pairs={{0,2},{1,3},{2,0},{3,1},{4,6},{5,7},{6,4},{7,5},{8,10},{9,11},{10,... | collective-permute-start | bytes 3145736 | tf_op jit(solution)/shard_map/ppermute | solution.py:454
  14.3 28.0 %collective-permute-start.6 = (bf16[2,1024,256]{2,1,0:T(8,128)(2,1)S(1)}, bf16[2,1024,256]{2,1,0:T(8,128)(2,1)S(1)}, u32[]{:S(2)}, u32[]{:S(2)}) collective-permute-start(bf16[2,1024,256]{2,1,0:T(8,128)(2,1)S(1)} %get-tuple-element.62), channel_id=1, source_target_pairs={{0,1},{1,0},{2,3},{3,2},{4,5},{5,4},{6,7},{7,6},{8,9},{9,8},{10,11... | collective-permute-start | bytes 3145736 | tf_op jit(solution)/shard_map/ppermute | solution.py:454
  14.8 16.4 %collective-permute-start.4 = (bf16[2,4,256,128]{3,2,1,0:T(8,128)(2,1)S(1)}, bf16[2,4,256,128]{3,2,1,0:T(8,128)(2,1)S(1)}, u32[]{:S(2)}, u32[]{:S(2)}) collective-permute-start(bf16[2,4,256,128]{3,2,1,0:T(8,128)(2,1)S(1)} %pad_maximum_fusion), channel_id=1, source_target_pairs={{0,12},{1,13},{2,14},{3,15},{4,0},{5,1},{6,2},{7,3},{8,4},{9,5},{1... | collective-permute-start | bytes 1572872 | tf_op jit(solution)/shard_map/ppermute | solution.py:457
  18.9 23.5 %collective-permute-start.5 = (bf16[2,4,256,128]{3,2,1,0:T(8,128)(2,1)S(1)}, bf16[2,4,256,128]{3,2,1,0:T(8,128)(2,1)S(1)}, u32[]{:S(2)}, u32[]{:S(2)}) collective-permute-start(bf16[2,4,256,128]{3,2,1,0:T(8,128)(2,1)S(1)} %pad_maximum_fusion), channel_id=1, source_target_pairs={{0,4},{1,5},{2,6},{3,7},{4,8},{5,9},{6,10},{7,11},{8,12},{9,13},{1... | collective-permute-start | bytes 1572872 | tf_op jit(solution)/shard_map/ppermute | solution.py:457
  42.4 28.2 %collective-permute-start.12 = (bf16[2,1024,256]{2,1,0:T(8,128)(2,1)S(1)}, bf16[2,1024,256]{2,1,0:T(8,128)(2,1)S(1)}, u32[]{:S(2)}, u32[]{:S(2)}) collective-permute-start(bf16[2,1024,256]{2,1,0:T(8,128)(2,1)S(1)} %get-tuple-element.72), channel_id=1, source_target_pairs={{0,2},{1,3},{2,0},{3,1},{4,6},{5,7},{6,4},{7,5},{8,10},{9,11},{10,... | collective-permute-start | bytes 3145736 | tf_op jit(solution)/shard_map/ppermute | solution.py:454
  43.9 9.1 %collective-permute-start.7 = (bf16[1024,256]{1,0:T(8,128)(2,1)S(1)}, bf16[1024,256]{1,0:T(8,128)(2,1)S(1)}, u32[]{:S(2)}, u32[]{:S(2)}) collective-permute-start(bf16[1024,256]{1,0:T(8,128)(2,1)S(1)} %slice_bitcast_fusion.1), channel_id=1, source_target_pairs={{0,1},{1,0},{2,3},{3,2},{4,5},{5,4},{6,7},{7,6},{8,9},{9,8},{10,11... | collective-permute-start | bytes 1572872 | tf_op jit(solution)/shard_map/ppermute | solution.py:454
  44.1 9.0 %collective-permute-start.8 = (bf16[4,256,128]{2,1,0:T(8,128)(2,1)S(1)}, bf16[4,256,128]{2,1,0:T(8,128)(2,1)S(1)}, u32[]{:S(2)}, u32[]{:S(2)}) collective-permute-start(bf16[4,256,128]{2,1,0:T(8,128)(2,1)S(1)} %get-tuple-element.103.refs_0_), channel_id=1, source_target_pairs={{0,12},{1,13},{2,14},{3,15},{4,0},{5,1},{6,2},{7,3},{8,4},{9,5},{1... | collective-permute-start | bytes 786440 | tf_op jit(solution)/shard_map/ppermute | solution.py:457
  45.9 24.7 %collective-permute-start.13 = (bf16[4,256,128]{2,1,0:T(8,128)(2,1)S(1)}, bf16[4,256,128]{2,1,0:T(8,128)(2,1)S(1)}, u32[]{:S(2)}, u32[]{:S(2)}) collective-permute-start(bf16[4,256,128]{2,1,0:T(8,128)(2,1)S(1)} %get-tuple-element.76.refs_2_), channel_id=1, source_target_pairs={{0,4},{1,5},{2,6},{3,7},{4,8},{5,9},{6,10},{7,11},{8,12},{9,13},{1... | collective-permute-start | bytes 786440 | tf_op jit(solution)/shard_map/ppermute | solution.py:457
  64.6 13.0 %collective-permute-start.9 = (bf16[272,512]{1,0:T(8,128)(2,1)S(1)}, bf16[272,512]{1,0:T(8,128)(2,1)S(1)}, u32[]{:S(2)}, u32[]{:S(2)}) collective-permute-start(bf16[272,512]{1,0:T(8,128)(2,1)S(1)} %get-tuple-element.67), channel_id=1, source_target_pairs={{0,4},{1,5},{2,6},{3,7},{4,8},{5,9},{6,10},{7,11},{8,12},{9,13},{1... | collective-permute-start | bytes 835592 | tf_op jit(solution)/shard_map/ppermute | solution.py:457
  70.5 12.0 %collective-permute-start.10 = (bf16[272,512]{1,0:T(8,128)(2,1)S(1)}, bf16[272,512]{1,0:T(8,128)(2,1)S(1)}, u32[]{:S(2)}, u32[]{:S(2)}) collective-permute-start(bf16[272,512]{1,0:T(8,128)(2,1)S(1)} %get-tuple-element.68), channel_id=1, source_target_pairs={{0,12},{1,13},{2,14},{3,15},{4,0},{5,1},{6,2},{7,3},{8,4},{9,5},{1... | collective-permute-start | bytes 835592 | tf_op jit(solution)/shard_map/ppermute | solution.py:457
  70.6 16.9 %collective-permute-start.14 = (bf16[1024,256]{1,0:T(8,128)(2,1)S(1)}, bf16[1024,256]{1,0:T(8,128)(2,1)S(1)}, u32[]{:S(2)}, u32[]{:S(2)}) collective-permute-start(bf16[1024,256]{1,0:T(8,128)(2,1)S(1)} %slice_bitcast_fusion), channel_id=1, source_target_pairs={{0,1},{1,0},{2,3},{3,2},{4,5},{5,4},{6,7},{7,6},{8,9},{9,8},{10,11... | collective-permute-start | bytes 1572872 | tf_op jit(solution)/shard_map/ppermute | solution.py:454
  82.8 16.3 %collective-permute-start.11 = (bf16[272,512]{1,0:T(8,128)(2,1)S(1)}, bf16[272,512]{1,0:T(8,128)(2,1)S(1)}, u32[]{:S(2)}, u32[]{:S(2)}) collective-permute-start(bf16[272,512]{1,0:T(8,128)(2,1)S(1)} %merge.2), channel_id=1, source_target_pairs={{0,4},{1,5},{2,6},{3,7},{4,8},{5,9},{6,10},{7,11},{8,12},{9,13},{1... | collective-permute-start | bytes 835592 | tf_op jit(solution)/shard_map/ppermute | solution.py:457
  99.4 11.4 %collective-permute-start.18 = (bf16[272,512]{1,0:T(8,128)(2,1)S(1)}, bf16[272,512]{1,0:T(8,128)(2,1)S(1)}, u32[]{:S(2)}, u32[]{:S(2)}) collective-permute-start(bf16[272,512]{1,0:T(8,128)(2,1)S(1)} %get-tuple-element.91), channel_id=1, source_target_pairs={{0,12},{1,13},{2,14},{3,15},{4,0},{5,1},{6,2},{7,3},{8,4},{9,5},{1... | collective-permute-start | bytes 835592 | tf_op jit(solution)/shard_map/ppermute | solution.py:457
  103.7 12.3 %collective-permute-start.19 = (bf16[272,512]{1,0:T(8,128)(2,1)S(1)}, bf16[272,512]{1,0:T(8,128)(2,1)S(1)}, u32[]{:S(2)}, u32[]{:S(2)}) collective-permute-start(bf16[272,512]{1,0:T(8,128)(2,1)S(1)} %get-tuple-element.92), channel_id=1, source_target_pairs={{0,4},{1,5},{2,6},{3,7},{4,8},{5,9},{6,10},{7,11},{8,12},{9,13},{1... | collective-permute-start | bytes 835592 | tf_op jit(solution)/shard_map/ppermute | solution.py:457
  116.2 8.4 %collective-permute-start.20 = (bf16[272,512]{1,0:T(8,128)(2,1)S(1)}, bf16[272,512]{1,0:T(8,128)(2,1)S(1)}, u32[]{:S(2)}, u32[]{:S(2)}) collective-permute-start(bf16[272,512]{1,0:T(8,128)(2,1)S(1)} %merge.3), channel_id=1, source_target_pairs={{0,12},{1,13},{2,14},{3,15},{4,0},{5,1},{6,2},{7,3},{8,4},{9,5},{1... | collective-permute-start | bytes 835592 | tf_op jit(solution)/shard_map/ppermute | solution.py:457
  118.0 7.8 %collective-permute-start.15 = (bf16[320,128]{1,0:T(8,128)(2,1)S(1)}, bf16[320,128]{1,0:T(8,128)(2,1)S(1)}, u32[]{:S(2)}, u32[]{:S(2)}) collective-permute-start(bf16[320,128]{1,0:T(8,128)(2,1)S(1)} %get-tuple-element.83), channel_id=1, source_target_pairs={{0,1},{1,0},{2,3},{3,2},{4,5},{5,4},{6,7},{7,6},{8,9},{9,8},{10,11... | collective-permute-start | bytes 245768 | tf_op jit(solution)/shard_map/ppermute | solution.py:454
  122.7 5.3 %collective-permute-start.16 = (bf16[320,128]{1,0:T(8,128)(2,1)S(1)}, bf16[320,128]{1,0:T(8,128)(2,1)S(1)}, u32[]{:S(2)}, u32[]{:S(2)}) collective-permute-start(bf16[320,128]{1,0:T(8,128)(2,1)S(1)} %get-tuple-element.84), channel_id=1, source_target_pairs={{0,2},{1,3},{2,0},{3,1},{4,6},{5,7},{6,4},{7,5},{8,10},{9,11},{10,... | collective-permute-start | bytes 245768 | tf_op jit(solution)/shard_map/ppermute | solution.py:454
  123.3 5.7 %collective-permute-start.17 = (bf16[320,128]{1,0:T(8,128)(2,1)S(1)}, bf16[320,128]{1,0:T(8,128)(2,1)S(1)}, u32[]{:S(2)}, u32[]{:S(2)}) collective-permute-start(bf16[320,128]{1,0:T(8,128)(2,1)S(1)} %get-tuple-element.85), channel_id=1, source_target_pairs={{0,3},{1,2},{2,1},{3,0},{4,7},{5,6},{6,5},{7,4},{8,11},{9,10},{10,... | collective-permute-start | bytes 245768 | tf_op jit(solution)/shard_map/ppermute | solution.py:454
  124.9 4.0 %collective-permute-start.21 = (bf16[320,128]{1,0:T(8,128)(2,1)S(1)}, bf16[320,128]{1,0:T(8,128)(2,1)S(1)}, u32[]{:S(2)}, u32[]{:S(2)}) collective-permute-start(bf16[320,128]{1,0:T(8,128)(2,1)S(1)} %get-tuple-element.97), channel_id=1, source_target_pairs={{0,1},{1,0},{2,3},{3,2},{4,5},{5,4},{6,7},{7,6},{8,9},{9,8},{10,11... | collective-permute-start | bytes 245768 | tf_op jit(solution)/shard_map/ppermute | solution.py:454
  125.3 6.2 %collective-permute-start.22 = (bf16[320,128]{1,0:T(8,128)(2,1)S(1)}, bf16[320,128]{1,0:T(8,128)(2,1)S(1)}, u32[]{:S(2)}, u32[]{:S(2)}) collective-permute-start(bf16[320,128]{1,0:T(8,128)(2,1)S(1)} %get-tuple-element.98), channel_id=1, source_target_pairs={{0,2},{1,3},{2,0},{3,1},{4,6},{5,7},{6,4},{7,5},{8,10},{9,11},{10,... | collective-permute-start | bytes 245768 | tf_op jit(solution)/shard_map/ppermute | solution.py:454
  125.8 6.7 %collective-permute-start.23 = (bf16[320,128]{1,0:T(8,128)(2,1)S(1)}, bf16[320,128]{1,0:T(8,128)(2,1)S(1)}, u32[]{:S(2)}, u32[]{:S(2)}) collective-permute-start(bf16[320,128]{1,0:T(8,128)(2,1)S(1)} %get-tuple-element.99), channel_id=1, source_target_pairs={{0,3},{1,2},{2,1},{3,0},{4,7},{5,6},{6,5},{7,4},{8,11},{9,10},{10,... | collective-permute-start | bytes 245768 | tf_op jit(solution)/shard_map/ppermute | solution.py:454

commit v6 on v4

--- a/solution.py
+++ b/solution.py
@@ -135,7 +135,7 @@
     queries, refs = refs[:nq], refs[nq:]
     nout = 2 if steps else count
     outs, refs = refs[:nout], refs[nout:]
-    held, asked, fresh, state, acc, stage, sem = refs
+    held, asked, fresh, state, acc, stage, scores, weights, sem = refs
     nsample = lax.axis_size("sample")
     quads = nsample // QUAD
     index = lax.axis_index("sample")
@@ -203,20 +203,28 @@
         tokens = tiles * TILE
         query = asked[n, pl.ds(2 * pair, 2)].reshape(2 * size, HD)
         row = pl.multiple_of(low * BLK, BLK)
-        s = scores_of(flat[pl.ds(row, tokens), 0:HD], query)
-        last = s[tokens - TILE:]
-        token = lax.broadcasted_iota(jnp.int32, last.shape, 0)
-        last = jnp.where(token < (high - low) * BLK - (tokens - TILE), last, NEG)
-        s = last if tiles == 1 else jnp.concatenate([s[:tokens - TILE], last], axis=0)
-        m = jnp.max(s, axis=0, keepdims=True)
+        before = state[pair, 0:1] if steps else None
+        top = jnp.broadcast_to(before, (8, 2 * size)) if steps else None
+        for t in range(tiles):
+            s = scores_of(flat[pl.ds(row + t * TILE, TILE), 0:HD], query)
+            if t == tiles - 1:
+                token = lax.broadcasted_iota(jnp.int32, s.shape, 0)
+                s = jnp.where(token < (high - low - t * TILE_BLOCKS) * BLK, s, NEG)
+            scores[t * TILE:(t + 1) * TILE] = s
+            part = jnp.max(s.reshape(TILE // 8, 8, 2 * size), axis=0)
+            top = part if top is None else jnp.maximum(top, part)
+        m = jnp.max(top, axis=0, keepdims=True)
+        shift = m * EXP_SCALE
+        total = None
+        for b in range(tokens // BLK):
+            p = jnp.exp2(scores[b * BLK:(b + 1) * BLK] * EXP_SCALE - shift)
+            weights[b * BLK:(b + 1) * BLK] = p.astype(BF16)
+            part = jnp.sum(p.reshape(BLK // 8, 8, 2 * size), axis=0)
+            total = part if total is None else total + part
+        l = jnp.sum(total, axis=0, keepdims=True)
+        out = values_by(flat[pl.ds(row, tokens), HD:2 * HD], weights[0:tokens])
         if steps:
-            before = state[pair, 0:1]
-            m = jnp.maximum(m, before)
-        p = jnp.exp2((s - m) * EXP_SCALE)
-        l = jnp.sum(p, axis=0, keepdims=True)
-        out = values_by(flat[pl.ds(row, tokens), HD:2 * HD], p.astype(BF16))
-        if steps:
-            alpha = jnp.exp2((before - m) * EXP_SCALE)
+            alpha = jnp.exp2(before * EXP_SCALE - shift)
             l = l + alpha * state[pair, 1:2]
             out = out + alpha * acc[pair]
         state[pair, 0:1] = m
@@ -305,10 +313,12 @@
             pltpu.VMEM((2, 8, 2 * size), F32),
             pltpu.VMEM((2, HD, 2 * size), F32),
             pltpu.VMEM((1 if steps else count, 2 * HD + STAT_ROWS, 2 * size), BF16),
+            pltpu.VMEM((max_tiles * TILE, 2 * size), F32),
+            pltpu.VMEM((max_tiles * TILE, 2 * size), BF16),
             pltpu.SemaphoreType.DMA((2 * QUAD + 2 * count + 8,)),
         ],
         compiler_params=params(48),
-        cost_estimate=cost(0, 1024),
+        cost_estimate=cost(10**9 if steps else 10**10, 4 << 20),
         name="attend_own" if steps else "attend_others",
     )(counts, slots, kv3, *arrived, *queries)
 
@@ -452,58 +462,78 @@
     near, msgs = lax.optimization_barrier((near, msgs))
     near = across(near, 1).reshape(HPD, -1, BLK, 2 * HD)
 
-    def gather(h):
-        own = jnp.stack([m[h, :GROUP * rows] for m in msgs])
-        ahead = (quads - 1 + (1 - h % 2)) // 2
+    own = jnp.stack([jnp.stack([m[h, :GROUP * rows] for m in msgs]) for h in range(HPD)])
+    first_hop = {shift: along(own, shift) for shift in ((-1, 1) if quads > 2 else (-1,))}
+    asked = []
+    for h in range(HPD):
+        ahead = (quads - 1 + (1 - h % 2)) // 2 if quads > 2 else quads - 1
         held = {}
         for shift, hops in ((-1, ahead), (1, quads - 1 - ahead)):
-            block = own
             for s in range(1, hops + 1):
-                block = along(block, shift)
+                block = first_hop[shift][h] if s == 1 else block
+                if s == 2 and h:
+                    block, asked[h - 1] = lax.optimization_barrier((block, asked[h - 1]))
+                if s > 1:
+                    block = along(block, shift)
                 held[-shift * s % quads] = block
-        return held
-
-    asked = [gather(h) for h in range(HPD)]
+        asked.append(held)
     arrived, handed = [], []
     for h in range(HPD):
         source = far[h]
         if h:
-            source, arrived[-1], asked[h - 1], near = lax.optimization_barrier(
-                (source, arrived[-1], asked[h - 1], near)
+            source, arrived[-1], first_hop, near = lax.optimization_barrier(
+                (source, arrived[-1], first_hop, near)
             )
         arrived.append(across(source, 2))
         handed.append(arrived[h][1])
-    final = []
-    for h in range(HPD):
-        if h:
-            handed[h], asked[h] = lax.optimization_barrier((handed[h], asked[h]))
+
+    def others(h, gate):
+        if gate is not None:
+            handed[h], asked[h], _ = lax.optimization_barrier((handed[h], asked[h], gate))
         passed = across(handed[h], 1).reshape(-1, BLK, 2 * HD)
         blocks = [near, arrived[h].reshape(2, -1, BLK, 2 * HD), passed]
         offsets = tuple(sorted(asked[h]))
         partial = attend(
             h, offsets, 0, prompt_blocks, slot_prompt, kv3, blocks, [asked[h][o] for o in offsets]
         )
-        if h:
-            back, partial = lax.optimization_barrier((back, partial))
-            done = finish(steps, *mine, back)
-            final.append([done[0]] + [across(done[k], k) for k in range(1, QUAD)])
-            partial, _ = lax.optimization_barrier((partial, done[0]))
-        parts = dict(zip(offsets, partial))
+        return blocks, dict(zip(offsets, partial))
+
+    def chains(h):
         far_right = (quads - 1 + (1 - h % 2)) // 2
+        pair = ((1, far_right), (-1, quads - 1 - far_right))
+        return [c for c in sorted(pair, key=lambda x: x[1]) if c[1]]
+
+    def sent(h, parts):
+        return [along(parts[shift * hops % quads], shift) for shift, hops in chains(h)]
+
+    def summed(h, parts, moved, gate):
         back = []
-        for shift, hops in sorted(((1, far_right), (-1, quads - 1 - far_right)), key=lambda x: x[1]):
-            for s in range(hops, 0, -1):
-                block = parts[shift * s % quads]
-                if s < hops:
-                    if s == 1:
-                        moved, back = lax.optimization_barrier((moved, back))
-                    block = merge(block, moved)
-                moved = along(block, shift)
-            if hops:
-                back.append(moved)
-        mine = attend(h, (0,), steps, prompt_blocks, slot_prompt, kv3, blocks, msgs)
-    done = finish(steps, *mine, back)
-    final.append([done[0]] + [across(done[k], k) for k in range(1, QUAD)])
+        for (shift, hops), block in zip(chains(h), moved):
+            for s in range(hops - 1, 0, -1):
+                if s == hops - 1:
+                    block, back, _ = lax.optimization_barrier((block, back, gate))
+                block = along(merge(parts[shift * s % quads], block), shift)
+            back.append(block)
+        return back
+
+    def finished(h, mine, back):
+        done = finish(steps, *mine, back)
+        return [done[0]] + [across(done[k], k) for k in range(1, QUAD)]
+
+    final = []
+    waiting = None
+    gate = None
+    for h in range(HPD):
+        blocks, parts = others(h, gate)
+        if waiting is not None:
+            back = summed(*waiting[:3], parts)
+            final.append(finished(h - 1, waiting[3], back))
+        moved = sent(h, parts)
+        _, later_msgs = lax.optimization_barrier((parts, msgs))
+        mine = attend(h, (0,), steps, prompt_blocks, slot_prompt, kv3, blocks, later_msgs)
+        waiting = (h, parts, moved, mine)
+        gate = (mine[0], moved[-1]) if moved else (mine[0],)
+    final.append(finished(HPD - 1, mine, summed(*waiting[:3], moved)))
     return tuple(emit([m for per_head in final for m in per_head], queries.shape))
 
 

time: 116 us -> 114 us (0.983)
  starting transfers between devices: 35.8 us -> 27.5 us
  waiting for transfers between devices: 50 us -> 55.4 us
    ppermute x14, waiting for transfers between devices: 9.29 us -> 33.5 us  [across(): return lax.ppermute(array, 'sample', [(i, i ^ k) for i in range(nsample)])]
    ppermute x12 -> x10, waiting for transfers between devices: 40.7 us -> 21.9 us  [along(): lax.ppermute(array, 'sample', [(i, (i + shift * QUAD) % nsample) for i in...]
    ppermute x12 -> x10, starting transfers between devices: 24.8 us -> 16.7 us  [along(): lax.ppermute(array, 'sample', [(i, (i + shift * QUAD) % nsample) for i in...]
  transfers between devices with their start and end apart: 26 -> 24, of which waited for: 15 -> 14; matrix products, arithmetic and copies ran while one was open for 0% -> 0% of each run, Pallas kernels for 20% -> 21%
where the time goes in v6:
time: 114 us; the launch traced here: 113 us
  waiting for transfers between devices  55.4 us (49%)
  starting transfers between devices  27.5 us (24%)
  Pallas kernels  27.1 us (24%)
  local copies, waits for them, and re-layouts  2.38 us (2%)
    ppermute x14, waiting for transfers between devices, across(): return lax.ppermute(array, 'sample', [(i, i ^ k) for i in range(nsample)])  33.5 us
    ppermute x10, waiting for transfers between devices, along(): lax.ppermute(array, 'sample', [(i, (i + shift * QUAD) % nsample) for i in...  21.9 us
    pallas_call x4, Pallas kernels, attend(): pl.pallas_call(functools.partial(attend_kernel, h, offsets, steps, max_ti...  21.5 us
    ppermute x10, starting transfers between devices, along(): lax.ppermute(array, 'sample', [(i, (i + shift * QUAD) % nsample) for i in...  16.7 us
    ppermute x14, starting transfers between devices, across(): return lax.ppermute(array, 'sample', [(i, i ^ k) for i in range(nsample)])  10.8 us
  transfers between devices with their start and end apart: 24, of which 14 were waited for; matrix products, arithmetic and copies ran while one was open for 0% of the time, Pallas kernels for 21%

profile of v6, /device:TPU:0, one launch (start us, length us, event | category | flops | bytes accessed | tf_op | source)
XLA Modules:
  0.0 113.4 jit_solution(16007505906195909023)
XLA Ops:
  0.6 2.2 %pack_queries.1 = (bf16[2,320,128]{2,1,0:T(8,128)(2,1)}, bf16[2,320,128]{2,1,0:T(8,128)(2,1)}, bf16[2,320,128]{2,1,0:T(8,128)(2,1)}, bf16[2,320,128]{2,1,0:T(8,128)(2,1)}) custom-call(bf16[8,4,8192]{2,1,0:T(4,128)(2,1)} %q_hbm.1, bf16[8,4,2048]{2,1,0:T(4,128)(2,1)} %new_hbm.1), custom_call_target="tpu_custom_call" | custom-call | bytes 2097152 | tf_op jit(solution)/shard_map/pack_queries/pallas_call | solution.py:72
  3.4 2.6 %collective-permute-start.2 = (bf16[2,320,128]{2,1,0:T(8,128)(2,1)}, bf16[2,320,128]{2,1,0:T(8,128)(2,1)S(1)}, u32[]{:S(2)}, u32[]{:S(2)}) collective-permute-start(bf16[2,320,128]{2,1,0:T(8,128)(2,1)} %get-tuple-element.60), channel_id=1, source_target_pairs={{0,2},{1,3},{2,0},{3,1},{4,6},{5,7},{6,4},{7,5},{8,10},{9,11},{10,... | collective-permute-start | bytes 491528 | tf_op jit(solution)/shard_map/ppermute | solution.py:451
  6.1 2.2 %copy-done = bf16[32,1,32,2048]{3,2,1,0:T(8,128)(2,1)S(1)} copy-done((bf16[32,1,32,2048]{3,2,1,0:T(8,128)(2,1)S(1)}, bf16[32,1,32,2048]{3,2,1,0:T(8,128)(2,1)}, u32[]{:S(2)}) %copy-start) | copy-done | bytes 4194328
  8.3 1.0 pack_kv.1
  9.3 1.8 %collective-permute-start = (bf16[2,1024,256]{2,1,0:T(8,128)(2,1)S(1)}, bf16[2,1024,256]{2,1,0:T(8,128)(2,1)S(1)}, u32[]{:S(2)}, u32[]{:S(2)}) collective-permute-start(bf16[2,1024,256]{2,1,0:T(8,128)(2,1)S(1)} %get-tuple-element.56), channel_id=1, source_target_pairs={{0,2},{1,3},{2,0},{3,1},{4,6},{5,7},{6,4},{7,5},{8,10},{9,11},{10,... | collective-permute-start | bytes 3145736 | tf_op jit(solution)/shard_map/ppermute | solution.py:451
  11.3 3.1 %collective-permute-done.3.refs_3_ = bf16[2,320,128]{2,1,0:T(8,128)(2,1)S(1)} collective-permute-done((bf16[2,320,128]{2,1,0:T(8,128)(2,1)}, bf16[2,320,128]{2,1,0:T(8,128)(2,1)S(1)}, u32[]{:S(2)}, u32[]{:S(2)}) %collective-permute-start.3) | collective-permute-done | bytes 163872 | tf_op jit(solution)/shard_map/ppermute | solution.py:451
  14.8 4.1 %collective-permute-start.4 = (bf16[2,4,256,128]{3,2,1,0:T(8,128)(2,1)S(1)}, bf16[2,4,256,128]{3,2,1,0:T(8,128)(2,1)S(1)}, u32[]{:S(2)}, u32[]{:S(2)}) collective-permute-start(bf16[2,4,256,128]{3,2,1,0:T(8,128)(2,1)S(1)} %pad_maximum_fusion), channel_id=1, source_target_pairs={{0,12},{1,13},{2,14},{3,15},{4,0},{5,1},{6,2},{7,3},{8,4},{9,5},{1... | collective-permute-start | bytes 1572872 | tf_op jit(solution)/shard_map/ppermute | solution.py:454
  18.9 18.1 %collective-permute-done = bf16[2,1024,256]{2,1,0:T(8,128)(2,1)S(1)} collective-permute-done((bf16[2,1024,256]{2,1,0:T(8,128)(2,1)S(1)}, bf16[2,1024,256]{2,1,0:T(8,128)(2,1)S(1)}, u32[]{:S(2)}, u32[]{:S(2)}) %collective-permute-start) | collective-permute-done | bytes 1048608 | tf_op jit(solution)/shard_map/ppermute | solution.py:451
  37.1 3.9 %collective-permute-start.8 = (bf16[4,256,128]{2,1,0:T(8,128)(2,1)S(1)}, bf16[4,256,128]{2,1,0:T(8,128)(2,1)S(1)}, u32[]{:S(2)}, u32[]{:S(2)}) collective-permute-start(bf16[4,256,128]{2,1,0:T(8,128)(2,1)S(1)} %get-tuple-element.69.refs_0_), channel_id=1, source_target_pairs={{0,12},{1,13},{2,14},{3,15},{4,0},{5,1},{6,2},{7,3},{8,4},{9,5},{1... | collective-permute-start | bytes 786440 | tf_op jit(solution)/shard_map/ppermute | solution.py:454
  41.0 1.5 %collective-permute-done.5 = bf16[2,4,256,128]{3,2,1,0:T(8,128)(2,1)S(1)} collective-permute-done((bf16[2,4,256,128]{3,2,1,0:T(8,128)(2,1)S(1)}, bf16[2,4,256,128]{3,2,1,0:T(8,128)(2,1)S(1)}, u32[]{:S(2)}, u32[]{:S(2)}) %collective-permute-start.5) | collective-permute-done | bytes 524320 | tf_op jit(solution)/shard_map/ppermute | solution.py:454
  42.5 1.5 %collective-permute-start.11 = (bf16[2,1024,256]{2,1,0:T(8,128)(2,1)S(1)}, bf16[2,1024,256]{2,1,0:T(8,128)(2,1)S(1)}, u32[]{:S(2)}, u32[]{:S(2)}) collective-permute-start(bf16[2,1024,256]{2,1,0:T(8,128)(2,1)S(1)} %get-tuple-element.81), channel_id=1, source_target_pairs={{0,2},{1,3},{2,0},{3,1},{4,6},{5,7},{6,4},{7,5},{8,10},{9,11},{10,... | collective-permute-start | bytes 3145736 | tf_op jit(solution)/shard_map/ppermute | solution.py:451
  44.1 3.9 %collective-permute-done.8.refs_1_ = bf16[4,256,128]{2,1,0:T(8,128)(2,1)S(1)} collective-permute-done((bf16[4,256,128]{2,1,0:T(8,128)(2,1)S(1)}, bf16[4,256,128]{2,1,0:T(8,128)(2,1)S(1)}, u32[]{:S(2)}, u32[]{:S(2)}) %collective-permute-start.8) | collective-permute-done | bytes 262176 | tf_op jit(solution)/shard_map/ppermute | solution.py:454
  48.6 7.2 %attend_others.2 = (bf16[272,512]{1,0:T(8,128)(2,1)S(1)}, bf16[272,512]{1,0:T(8,128)(2,1)S(1)}, bf16[272,512]{1,0:T(8,128)(2,1)S(1)}) custom-call(s32[8]{0:T(128)S(1)} %copy-done.2, s32[16]{0:T(128)S(1)} %copy-done.3, bf16[32,32,2048]{2,1,0:T(8,128)(2,1)} %bitcast.23, bf16[2,32,32,256]{3,2,1,0:T(8,128)(2,1)S(1)} %bitcast.28, ...), custom_call_target="tpu_custom_call" | custom-call | flops 10000000000 | bytes 4194304 | tf_op jit(solution)/shard_map/attend_others/pallas_call | solution.py:304
  55.8 1.0 collective-permute-start.9
  56.8 3.6 %attend_own.2 = (f32[2,128,512]{2,1,0:T(8,128)S(1)}, f32[2,8,512]{2,1,0:T(8,128)S(1)}) custom-call(s32[8]{0:T(128)S(1)} %copy-done.2, s32[16]{0:T(128)S(1)} %copy-done.3, bf16[32,32,2048]{2,1,0:T(8,128)(2,1)} %bitcast.24, bf16[2,32,32,256]{3,2,1,0:T(8,128)(2,1)S(1)} %bitcast.29, bf16[2,32,32,256]{3,2,1,0:T(8,128)(2,1)S(1)} %bitcast.35, ...), custom_call_target="tpu_custom_call" | custom-call | flops 1000000000 | bytes 4194304 | tf_op jit(solution)/shard_map/attend_own/pallas_call | solution.py:304
  60.4 6.2 %collective-permute-done.11 = bf16[2,1024,256]{2,1,0:T(8,128)(2,1)S(1)} collective-permute-done((bf16[2,1024,256]{2,1,0:T(8,128)(2,1)S(1)}, bf16[2,1024,256]{2,1,0:T(8,128)(2,1)S(1)}, u32[]{:S(2)}, u32[]{:S(2)}) %collective-permute-start.11) | collective-permute-done | bytes 1048608 | tf_op jit(solution)/shard_map/ppermute | solution.py:451
  66.7 1.7 %collective-permute-start.10 = (bf16[272,512]{1,0:T(8,128)(2,1)S(1)}, bf16[272,512]{1,0:T(8,128)(2,1)S(1)}, u32[]{:S(2)}, u32[]{:S(2)}) collective-permute-start(bf16[272,512]{1,0:T(8,128)(2,1)S(1)} %get-tuple-element.74), channel_id=1, source_target_pairs={{0,12},{1,13},{2,14},{3,15},{4,0},{5,1},{6,2},{7,3},{8,4},{9,5},{1... | collective-permute-start | bytes 835592 | tf_op jit(solution)/shard_map/ppermute | solution.py:454
  68.6 7.2 %attend_others.3 = (bf16[272,512]{1,0:T(8,128)(2,1)S(1)}, bf16[272,512]{1,0:T(8,128)(2,1)S(1)}, bf16[272,512]{1,0:T(8,128)(2,1)S(1)}) custom-call(s32[8]{0:T(128)S(1)} %copy-done.2, s32[16]{0:T(128)S(1)} %copy-done.3, bf16[32,32,2048]{2,1,0:T(8,128)(2,1)} %bitcast.25, bf16[2,32,32,256]{3,2,1,0:T(8,128)(2,1)S(1)} %bitcast.30, ...), custom_call_target="tpu_custom_call" | custom-call | flops 10000000000 | bytes 4194304 | tf_op jit(solution)/shard_map/attend_others/pallas_call | solution.py:304
  75.8 1.1 collective-permute-start.18
  78.1 1.9 %collective-permute-start.14 = (bf16[272,512]{1,0:T(8,128)(2,1)S(1)}, bf16[272,512]{1,0:T(8,128)(2,1)S(1)}, u32[]{:S(2)}, u32[]{:S(2)}) collective-permute-start(bf16[272,512]{1,0:T(8,128)(2,1)S(1)} %merge.2), channel_id=1, source_target_pairs={{0,4},{1,5},{2,6},{3,7},{4,8},{5,9},{6,10},{7,11},{8,12},{9,13},{1... | collective-permute-start | bytes 835592 | tf_op jit(solution)/shard_map/ppermute | solution.py:454
  80.0 5.3 %collective-permute-done.18.two_ref = bf16[272,512]{1,0:T(8,128)(2,1)S(1)} collective-permute-done((bf16[272,512]{1,0:T(8,128)(2,1)S(1)}, bf16[272,512]{1,0:T(8,128)(2,1)S(1)}, u32[]{:S(2)}, u32[]{:S(2)}) %collective-permute-start.18) | collective-permute-done | bytes 278560 | tf_op jit(solution)/shard_map/ppermute | solution.py:454
  85.3 6.9 %collective-permute-done.19.refs_0_ = bf16[272,512]{1,0:T(8,128)(2,1)S(1)} collective-permute-done((bf16[272,512]{1,0:T(8,128)(2,1)S(1)}, bf16[272,512]{1,0:T(8,128)(2,1)S(1)}, u32[]{:S(2)}, u32[]{:S(2)}) %collective-permute-start.19) | collective-permute-done | bytes 278560 | tf_op jit(solution)/shard_map/ppermute | solution.py:454
  92.3 1.4 %collective-permute-start.20 = (bf16[272,512]{1,0:T(8,128)(2,1)S(1)}, bf16[272,512]{1,0:T(8,128)(2,1)S(1)}, u32[]{:S(2)}, u32[]{:S(2)}) collective-permute-start(bf16[272,512]{1,0:T(8,128)(2,1)S(1)} %merge.3), channel_id=1, source_target_pairs={{0,12},{1,13},{2,14},{3,15},{4,0},{5,1},{6,2},{7,3},{8,4},{9,5},{1... | collective-permute-start | bytes 835592 | tf_op jit(solution)/shard_map/ppermute | solution.py:454
  93.7 4.4 %collective-permute-done.14.refs_1_ = bf16[272,512]{1,0:T(8,128)(2,1)S(1)} collective-permute-done((bf16[272,512]{1,0:T(8,128)(2,1)S(1)}, bf16[272,512]{1,0:T(8,128)(2,1)S(1)}, u32[]{:S(2)}, u32[]{:S(2)}) %collective-permute-start.14) | collective-permute-done | bytes 278560 | tf_op jit(solution)/shard_map/ppermute | solution.py:454
  98.5 3.6 %attend_own.3 = (f32[2,128,512]{2,1,0:T(8,128)S(1)}, f32[2,8,512]{2,1,0:T(8,128)S(1)}) custom-call(s32[8]{0:T(128)S(1)} %copy-done.2, s32[16]{0:T(128)S(1)} %copy-done.3, bf16[32,32,2048]{2,1,0:T(8,128)(2,1)} %bitcast.26, bf16[2,32,32,256]{3,2,1,0:T(8,128)(2,1)S(1)} %bitcast.31, bf16[2,32,32,256]{3,2,1,0:T(8,128)(2,1)S(1)} %bitcast.33, ...), custom_call_target="tpu_custom_call" | custom-call | flops 1000000000 | bytes 4194304 | tf_op jit(solution)/shard_map/attend_own/pallas_call | solution.py:304
  102.1 1.6 %collective-permute-start.16 = (bf16[320,128]{1,0:T(8,128)(2,1)S(1)}, bf16[320,128]{1,0:T(8,128)(2,1)S(1)}, u32[]{:S(2)}, u32[]{:S(2)}) collective-permute-start(bf16[320,128]{1,0:T(8,128)(2,1)S(1)} %get-tuple-element.94), channel_id=1, source_target_pairs={{0,2},{1,3},{2,0},{3,1},{4,6},{5,7},{6,4},{7,5},{8,10},{9,11},{10,... | collective-permute-start | bytes 245768 | tf_op jit(solution)/shard_map/ppermute | solution.py:451
  104.7 1.5 %collective-permute-start.22 = (bf16[320,128]{1,0:T(8,128)(2,1)S(1)}, bf16[320,128]{1,0:T(8,128)(2,1)S(1)}, u32[]{:S(2)}, u32[]{:S(2)}) collective-permute-start(bf16[320,128]{1,0:T(8,128)(2,1)S(1)} %get-tuple-element.106), channel_id=1, source_target_pairs={{0,2},{1,3},{2,0},{3,1},{4,6},{5,7},{6,4},{7,5},{8,10},{9,11},{10,... | collective-permute-start | bytes 245768 | tf_op jit(solution)/shard_map/ppermute | solution.py:451
  106.3 1.0 collective-permute-done.16.refs_2_
  107.3 1.1 collective-permute-done.17.refs_3_
  108.4 2.4 %collective-permute-done.22.refs_6_ = bf16[320,128]{1,0:T(8,128)(2,1)S(1)} collective-permute-done((bf16[320,128]{1,0:T(8,128)(2,1)S(1)}, bf16[320,128]{1,0:T(8,128)(2,1)S(1)}, u32[]{:S(2)}, u32[]{:S(2)}) %collective-permute-start.22) | collective-permute-done | bytes 81952 | tf_op jit(solution)/shard_map/ppermute | solution.py:451
  110.8 1.1 collective-permute-done.23.refs_7_
  111.9 1.5 %emit.1 = (bf16[8,4,8192]{2,1,0:T(4,128)(2,1)}, bf16[8,4,8192]{2,1,0:T(4,128)(2,1)}) custom-call(bf16[320,128]{1,0:T(8,128)(2,1)S(1)} %get-tuple-element.92.refs_0_, bf16[320,128]{1,0:T(8,128)(2,1)S(1)} %collective-permute-done.15.refs_1_, bf16[320,128]{1,0:T(8,128)(2,1)S(1)} %collective-permute-done.16.refs_2_, ...), custom_call_target="tpu_custom_call" | custom-call | flops 1048576 | bytes 2097152 | tf_op jit(solution)/shard_map/emit/pallas_call | solution.py:433
  (44 shorter events, 5.0 us)
Async XLA Ops:
  2.9 8.2 %collective-permute-start.1 = (bf16[2,320,128]{2,1,0:T(8,128)(2,1)}, bf16[2,320,128]{2,1,0:T(8,128)(2,1)S(1)}, u32[]{:S(2)}, u32[]{:S(2)}) collective-permute-start(bf16[2,320,128]{2,1,0:T(8,128)(2,1)} %get-tuple-element.59), channel_id=1, source_target_pairs={{0,1},{1,0},{2,3},{3,2},{4,5},{5,4},{6,7},{7,6},{8,9},{9,8},{10,11... | collective-permute-start | bytes 491528 | tf_op jit(solution)/shard_map/ppermute | solution.py:451
  3.4 7.9 %collective-permute-start.2 = (bf16[2,320,128]{2,1,0:T(8,128)(2,1)}, bf16[2,320,128]{2,1,0:T(8,128)(2,1)S(1)}, u32[]{:S(2)}, u32[]{:S(2)}) collective-permute-start(bf16[2,320,128]{2,1,0:T(8,128)(2,1)} %get-tuple-element.60), channel_id=1, source_target_pairs={{0,2},{1,3},{2,0},{3,1},{4,6},{5,7},{6,4},{7,5},{8,10},{9,11},{10,... | collective-permute-start | bytes 491528 | tf_op jit(solution)/shard_map/ppermute | solution.py:451
  6.0 8.3 %collective-permute-start.3 = (bf16[2,320,128]{2,1,0:T(8,128)(2,1)}, bf16[2,320,128]{2,1,0:T(8,128)(2,1)S(1)}, u32[]{:S(2)}, u32[]{:S(2)}) collective-permute-start(bf16[2,320,128]{2,1,0:T(8,128)(2,1)} %get-tuple-element.61), channel_id=1, source_target_pairs={{0,3},{1,2},{2,1},{3,0},{4,7},{5,6},{6,5},{7,4},{8,11},{9,10},{10,... | collective-permute-start | bytes 491528 | tf_op jit(solution)/shard_map/ppermute | solution.py:451
  6.1 2.2 %copy-start = (bf16[32,1,32,2048]{3,2,1,0:T(8,128)(2,1)S(1)}, bf16[32,1,32,2048]{3,2,1,0:T(8,128)(2,1)}, u32[]{:S(2)}) copy-start(bf16[32,1,32,2048]{3,2,1,0:T(8,128)(2,1)} %param.5) | copy-start | bytes 12582916
  8.3 6.4 %copy-start.1 = (bf16[2,320,128]{2,1,0:T(8,128)(2,1)S(1)}, bf16[2,320,128]{2,1,0:T(8,128)(2,1)}, u32[]{:S(2)}) copy-start(bf16[2,320,128]{2,1,0:T(8,128)(2,1)} %get-tuple-element.96.refs_0_) | copy-start | bytes 491524
  9.2 39.3 %copy-start.2 = (s32[8]{0:T(128)S(1)}, s32[8]{0:T(128)}, u32[]{:S(2)}) copy-start(s32[8]{0:T(128)} %counts_ref.7) | copy-start | bytes 100
  9.3 39.3 %copy-start.3 = (s32[16]{0:T(128)S(1)}, s32[16]{0:T(128)}, u32[]{:S(2)}) copy-start(s32[16]{0:T(128)} %slots_ref.7) | copy-start | bytes 196
  9.3 27.7 %collective-permute-start = (bf16[2,1024,256]{2,1,0:T(8,128)(2,1)S(1)}, bf16[2,1024,256]{2,1,0:T(8,128)(2,1)S(1)}, u32[]{:S(2)}, u32[]{:S(2)}) collective-permute-start(bf16[2,1024,256]{2,1,0:T(8,128)(2,1)S(1)} %get-tuple-element.56), channel_id=1, source_target_pairs={{0,2},{1,3},{2,0},{3,1},{4,6},{5,7},{6,4},{7,5},{8,10},{9,11},{10,... | collective-permute-start | bytes 3145736 | tf_op jit(solution)/shard_map/ppermute | solution.py:451
  14.3 28.2 %collective-permute-start.6 = (bf16[2,1024,256]{2,1,0:T(8,128)(2,1)S(1)}, bf16[2,1024,256]{2,1,0:T(8,128)(2,1)S(1)}, u32[]{:S(2)}, u32[]{:S(2)}) collective-permute-start(bf16[2,1024,256]{2,1,0:T(8,128)(2,1)S(1)} %get-tuple-element.66), channel_id=1, source_target_pairs={{0,1},{1,0},{2,3},{3,2},{4,5},{5,4},{6,7},{7,6},{8,9},{9,8},{10,11... | collective-permute-start | bytes 3145736 | tf_op jit(solution)/shard_map/ppermute | solution.py:451
  14.8 22.3 %collective-permute-start.4 = (bf16[2,4,256,128]{3,2,1,0:T(8,128)(2,1)S(1)}, bf16[2,4,256,128]{3,2,1,0:T(8,128)(2,1)S(1)}, u32[]{:S(2)}, u32[]{:S(2)}) collective-permute-start(bf16[2,4,256,128]{3,2,1,0:T(8,128)(2,1)S(1)} %pad_maximum_fusion), channel_id=1, source_target_pairs={{0,12},{1,13},{2,14},{3,15},{4,0},{5,1},{6,2},{7,3},{8,4},{9,5},{1... | collective-permute-start | bytes 1572872 | tf_op jit(solution)/shard_map/ppermute | solution.py:454
  18.9 23.6 %collective-permute-start.5 = (bf16[2,4,256,128]{3,2,1,0:T(8,128)(2,1)S(1)}, bf16[2,4,256,128]{3,2,1,0:T(8,128)(2,1)S(1)}, u32[]{:S(2)}, u32[]{:S(2)}) collective-permute-start(bf16[2,4,256,128]{3,2,1,0:T(8,128)(2,1)S(1)} %pad_maximum_fusion), channel_id=1, source_target_pairs={{0,4},{1,5},{2,6},{3,7},{4,8},{5,9},{6,10},{7,11},{8,12},{9,13},{1... | collective-permute-start | bytes 1572872 | tf_op jit(solution)/shard_map/ppermute | solution.py:454
  37.0 11.5 %collective-permute-start.7 = (bf16[1024,256]{1,0:T(8,128)(2,1)S(1)}, bf16[1024,256]{1,0:T(8,128)(2,1)S(1)}, u32[]{:S(2)}, u32[]{:S(2)}) collective-permute-start(bf16[1024,256]{1,0:T(8,128)(2,1)S(1)} %slice_bitcast_fusion.1), channel_id=1, source_target_pairs={{0,1},{1,0},{2,3},{3,2},{4,5},{5,4},{6,7},{7,6},{8,9},{9,8},{10,11... | collective-permute-start | bytes 1572872 | tf_op jit(solution)/shard_map/ppermute | solution.py:451
  37.1 10.8 %collective-permute-start.8 = (bf16[4,256,128]{2,1,0:T(8,128)(2,1)S(1)}, bf16[4,256,128]{2,1,0:T(8,128)(2,1)S(1)}, u32[]{:S(2)}, u32[]{:S(2)}) collective-permute-start(bf16[4,256,128]{2,1,0:T(8,128)(2,1)S(1)} %get-tuple-element.69.refs_0_), channel_id=1, source_target_pairs={{0,12},{1,13},{2,14},{3,15},{4,0},{5,1},{6,2},{7,3},{8,4},{9,5},{1... | collective-permute-start | bytes 786440 | tf_op jit(solution)/shard_map/ppermute | solution.py:454
  42.5 24.1 %collective-permute-start.11 = (bf16[2,1024,256]{2,1,0:T(8,128)(2,1)S(1)}, bf16[2,1024,256]{2,1,0:T(8,128)(2,1)S(1)}, u32[]{:S(2)}, u32[]{:S(2)}) collective-permute-start(bf16[2,1024,256]{2,1,0:T(8,128)(2,1)S(1)} %get-tuple-element.81), channel_id=1, source_target_pairs={{0,2},{1,3},{2,0},{3,1},{4,6},{5,7},{6,4},{7,5},{8,10},{9,11},{10,... | collective-permute-start | bytes 3145736 | tf_op jit(solution)/shard_map/ppermute | solution.py:451
  48.0 18.6 %collective-permute-start.12 = (bf16[4,256,128]{2,1,0:T(8,128)(2,1)S(1)}, bf16[4,256,128]{2,1,0:T(8,128)(2,1)S(1)}, u32[]{:S(2)}, u32[]{:S(2)}) collective-permute-start(bf16[4,256,128]{2,1,0:T(8,128)(2,1)S(1)} %get-tuple-element.86.refs_2_), channel_id=1, source_target_pairs={{0,4},{1,5},{2,6},{3,7},{4,8},{5,9},{6,10},{7,11},{8,12},{9,13},{1... | collective-permute-start | bytes 786440 | tf_op jit(solution)/shard_map/ppermute | solution.py:454
  55.8 10.9 %collective-permute-start.9 = (bf16[272,512]{1,0:T(8,128)(2,1)S(1)}, bf16[272,512]{1,0:T(8,128)(2,1)S(1)}, u32[]{:S(2)}, u32[]{:S(2)}) collective-permute-start(bf16[272,512]{1,0:T(8,128)(2,1)S(1)} %get-tuple-element.73), channel_id=1, source_target_pairs={{0,4},{1,5},{2,6},{3,7},{4,8},{5,9},{6,10},{7,11},{8,12},{9,13},{1... | collective-permute-start | bytes 835592 | tf_op jit(solution)/shard_map/ppermute | solution.py:454
  66.6 2.0 %collective-permute-start.13 = (bf16[1024,256]{1,0:T(8,128)(2,1)S(1)}, bf16[1024,256]{1,0:T(8,128)(2,1)S(1)}, u32[]{:S(2)}, u32[]{:S(2)}) collective-permute-start(bf16[1024,256]{1,0:T(8,128)(2,1)S(1)} %slice_bitcast_fusion), channel_id=1, source_target_pairs={{0,1},{1,0},{2,3},{3,2},{4,5},{5,4},{6,7},{7,6},{8,9},{9,8},{10,11... | collective-permute-start | bytes 1572872 | tf_op jit(solution)/shard_map/ppermute | solution.py:451
  66.7 11.2 %collective-permute-start.10 = (bf16[272,512]{1,0:T(8,128)(2,1)S(1)}, bf16[272,512]{1,0:T(8,128)(2,1)S(1)}, u32[]{:S(2)}, u32[]{:S(2)}) collective-permute-start(bf16[272,512]{1,0:T(8,128)(2,1)S(1)} %get-tuple-element.74), channel_id=1, source_target_pairs={{0,12},{1,13},{2,14},{3,15},{4,0},{5,1},{6,2},{7,3},{8,4},{9,5},{1... | collective-permute-start | bytes 835592 | tf_op jit(solution)/shard_map/ppermute | solution.py:454
  75.8 9.5 %collective-permute-start.18 = (bf16[272,512]{1,0:T(8,128)(2,1)S(1)}, bf16[272,512]{1,0:T(8,128)(2,1)S(1)}, u32[]{:S(2)}, u32[]{:S(2)}) collective-permute-start(bf16[272,512]{1,0:T(8,128)(2,1)S(1)} %get-tuple-element.88), channel_id=1, source_target_pairs={{0,12},{1,13},{2,14},{3,15},{4,0},{5,1},{6,2},{7,3},{8,4},{9,5},{1... | collective-permute-start | bytes 835592 | tf_op jit(solution)/shard_map/ppermute | solution.py:454
  76.9 15.2 %collective-permute-start.19 = (bf16[272,512]{1,0:T(8,128)(2,1)S(1)}, bf16[272,512]{1,0:T(8,128)(2,1)S(1)}, u32[]{:S(2)}, u32[]{:S(2)}) collective-permute-start(bf16[272,512]{1,0:T(8,128)(2,1)S(1)} %get-tuple-element.87), channel_id=1, source_target_pairs={{0,4},{1,5},{2,6},{3,7},{4,8},{5,9},{6,10},{7,11},{8,12},{9,13},{1... | collective-permute-start | bytes 835592 | tf_op jit(solution)/shard_map/ppermute | solution.py:454
  78.1 20.0 %collective-permute-start.14 = (bf16[272,512]{1,0:T(8,128)(2,1)S(1)}, bf16[272,512]{1,0:T(8,128)(2,1)S(1)}, u32[]{:S(2)}, u32[]{:S(2)}) collective-permute-start(bf16[272,512]{1,0:T(8,128)(2,1)S(1)} %merge.2), channel_id=1, source_target_pairs={{0,4},{1,5},{2,6},{3,7},{4,8},{5,9},{6,10},{7,11},{8,12},{9,13},{1... | collective-permute-start | bytes 835592 | tf_op jit(solution)/shard_map/ppermute | solution.py:454
  92.3 11.7 %collective-permute-start.20 = (bf16[272,512]{1,0:T(8,128)(2,1)S(1)}, bf16[272,512]{1,0:T(8,128)(2,1)S(1)}, u32[]{:S(2)}, u32[]{:S(2)}) collective-permute-start(bf16[272,512]{1,0:T(8,128)(2,1)S(1)} %merge.3), channel_id=1, source_target_pairs={{0,12},{1,13},{2,14},{3,15},{4,0},{5,1},{6,2},{7,3},{8,4},{9,5},{1... | collective-permute-start | bytes 835592 | tf_op jit(solution)/shard_map/ppermute | solution.py:454
  98.4 7.8 %collective-permute-start.15 = (bf16[320,128]{1,0:T(8,128)(2,1)S(1)}, bf16[320,128]{1,0:T(8,128)(2,1)S(1)}, u32[]{:S(2)}, u32[]{:S(2)}) collective-permute-start(bf16[320,128]{1,0:T(8,128)(2,1)S(1)} %get-tuple-element.93), channel_id=1, source_target_pairs={{0,1},{1,0},{2,3},{3,2},{4,5},{5,4},{6,7},{7,6},{8,9},{9,8},{10,11... | collective-permute-start | bytes 245768 | tf_op jit(solution)/shard_map/ppermute | solution.py:451
  102.1 5.2 %collective-permute-start.16 = (bf16[320,128]{1,0:T(8,128)(2,1)S(1)}, bf16[320,128]{1,0:T(8,128)(2,1)S(1)}, u32[]{:S(2)}, u32[]{:S(2)}) collective-permute-start(bf16[320,128]{1,0:T(8,128)(2,1)S(1)} %get-tuple-element.94), channel_id=1, source_target_pairs={{0,2},{1,3},{2,0},{3,1},{4,6},{5,7},{6,4},{7,5},{8,10},{9,11},{10,... | collective-permute-start | bytes 245768 | tf_op jit(solution)/shard_map/ppermute | solution.py:451
  103.7 4.7 %collective-permute-start.17 = (bf16[320,128]{1,0:T(8,128)(2,1)S(1)}, bf16[320,128]{1,0:T(8,128)(2,1)S(1)}, u32[]{:S(2)}, u32[]{:S(2)}) collective-permute-start(bf16[320,128]{1,0:T(8,128)(2,1)S(1)} %get-tuple-element.95), channel_id=1, source_target_pairs={{0,3},{1,2},{2,1},{3,0},{4,7},{5,6},{6,5},{7,4},{8,11},{9,10},{10,... | collective-permute-start | bytes 245768 | tf_op jit(solution)/shard_map/ppermute | solution.py:451
  104.3 4.1 %collective-permute-start.21 = (bf16[320,128]{1,0:T(8,128)(2,1)S(1)}, bf16[320,128]{1,0:T(8,128)(2,1)S(1)}, u32[]{:S(2)}, u32[]{:S(2)}) collective-permute-start(bf16[320,128]{1,0:T(8,128)(2,1)S(1)} %get-tuple-element.105), channel_id=1, source_target_pairs={{0,1},{1,0},{2,3},{3,2},{4,5},{5,4},{6,7},{7,6},{8,9},{9,8},{10,11... | collective-permute-start | bytes 245768 | tf_op jit(solution)/shard_map/ppermute | solution.py:451
  104.7 6.1 %collective-permute-start.22 = (bf16[320,128]{1,0:T(8,128)(2,1)S(1)}, bf16[320,128]{1,0:T(8,128)(2,1)S(1)}, u32[]{:S(2)}, u32[]{:S(2)}) collective-permute-start(bf16[320,128]{1,0:T(8,128)(2,1)S(1)} %get-tuple-element.106), channel_id=1, source_target_pairs={{0,2},{1,3},{2,0},{3,1},{4,6},{5,7},{6,4},{7,5},{8,10},{9,11},{10,... | collective-permute-start | bytes 245768 | tf_op jit(solution)/shard_map/ppermute | solution.py:451
  106.2 5.7 %collective-permute-start.23 = (bf16[320,128]{1,0:T(8,128)(2,1)S(1)}, bf16[320,128]{1,0:T(8,128)(2,1)S(1)}, u32[]{:S(2)}, u32[]{:S(2)}) collective-permute-start(bf16[320,128]{1,0:T(8,128)(2,1)S(1)} %get-tuple-element.107), channel_id=1, source_target_pairs={{0,3},{1,2},{2,1},{3,0},{4,7},{5,6},{6,5},{7,4},{8,11},{9,10},{10,... | collective-permute-start | bytes 245768 | tf_op jit(solution)/shard_map/ppermute | solution.py:451

commit v7 on v6

--- a/solution.py
+++ b/solution.py
@@ -16,7 +16,7 @@
 QUAD = 4
 HPD = KVH // QUAD
 GROUP = HEADS // KVH
-TILE_BLOCKS = 8
+TILE_BLOCKS = 4
 TILE = TILE_BLOCKS * BLK
 STAT_ROWS = 16
 NEG = -1e30
@@ -205,13 +205,14 @@
         row = pl.multiple_of(low * BLK, BLK)
         before = state[pair, 0:1] if steps else None
         top = jnp.broadcast_to(before, (8, 2 * size)) if steps else None
+        s = scores_of(flat[pl.ds(row, tokens), 0:HD], query)
         for t in range(tiles):
-            s = scores_of(flat[pl.ds(row + t * TILE, TILE), 0:HD], query)
+            tile = s[t * TILE:(t + 1) * TILE]
             if t == tiles - 1:
-                token = lax.broadcasted_iota(jnp.int32, s.shape, 0)
-                s = jnp.where(token < (high - low - t * TILE_BLOCKS) * BLK, s, NEG)
-            scores[t * TILE:(t + 1) * TILE] = s
-            part = jnp.max(s.reshape(TILE // 8, 8, 2 * size), axis=0)
+                token = lax.broadcasted_iota(jnp.int32, tile.shape, 0)
+                tile = jnp.where(token < (high - low - t * TILE_BLOCKS) * BLK, tile, NEG)
+            scores[t * TILE:(t + 1) * TILE] = tile
+            part = jnp.max(tile.reshape(TILE // 8, 8, 2 * size), axis=0)
             top = part if top is None else jnp.maximum(top, part)
         m = jnp.max(top, axis=0, keepdims=True)
         shift = m * EXP_SCALE
@@ -318,7 +319,7 @@
             pltpu.SemaphoreType.DMA((2 * QUAD + 2 * count + 8,)),
         ],
         compiler_params=params(48),
-        cost_estimate=cost(10**9 if steps else 10**10, 4 << 20),
+        cost_estimate=cost(10**9 if steps else 5 * 10**9, 4 << 20),
         name="attend_own" if steps else "attend_others",
     )(counts, slots, kv3, *arrived, *queries)
 
@@ -457,11 +458,12 @@
 
     kv3 = prompt_kv.reshape(prompt_kv.shape[0], BLK, prompt_kv.shape[-1])
     msgs = pack_queries(queries, new_kv)
+    def tied(value, *others):
+        return lax.optimization_barrier((value, others))[0]
+
     near, *far = pack_kv(kv3.reshape(-1, kv3.shape[-1]))
     msgs = [msgs[0]] + [across(msgs[k], k) for k in range(1, QUAD)]
-    near, msgs = lax.optimization_barrier((near, msgs))
-    near = across(near, 1).reshape(HPD, -1, BLK, 2 * HD)
-
+    near = across(tied(near, msgs), 1).reshape(HPD, -1, BLK, 2 * HD)
     own = jnp.stack([jnp.stack([m[h, :GROUP * rows] for m in msgs]) for h in range(HPD)])
     first_hop = {shift: along(own, shift) for shift in ((-1, 1) if quads > 2 else (-1,))}
     asked = []
@@ -472,25 +474,19 @@
             for s in range(1, hops + 1):
                 block = first_hop[shift][h] if s == 1 else block
                 if s == 2 and h:
-                    block, asked[h - 1] = lax.optimization_barrier((block, asked[h - 1]))
+                    block = tied(block, asked[h - 1])
                 if s > 1:
                     block = along(block, shift)
                 held[-shift * s % quads] = block
         asked.append(held)
-    arrived, handed = [], []
+    arrived = []
     for h in range(HPD):
-        source = far[h]
-        if h:
-            source, arrived[-1], first_hop, near = lax.optimization_barrier(
-                (source, arrived[-1], first_hop, near)
-            )
+        source = tied(far[h], arrived[-1], first_hop, near) if h else far[h]
         arrived.append(across(source, 2))
-        handed.append(arrived[h][1])
 
     def others(h, gate):
-        if gate is not None:
-            handed[h], asked[h], _ = lax.optimization_barrier((handed[h], asked[h], gate))
-        passed = across(handed[h], 1).reshape(-1, BLK, 2 * HD)
+        handed = arrived[h][1] if gate is None else tied(arrived[h][1], gate, asked[h])
+        passed = across(handed, 1).reshape(-1, BLK, 2 * HD)
         blocks = [near, arrived[h].reshape(2, -1, BLK, 2 * HD), passed]
         offsets = tuple(sorted(asked[h]))
         partial = attend(
@@ -506,34 +502,35 @@
     def sent(h, parts):
         return [along(parts[shift * hops % quads], shift) for shift, hops in chains(h)]
 
-    def summed(h, parts, moved, gate):
-        back = []
+    def summed(h, parts, moved):
+        back, turned = [], parts[min(parts)] if parts else near
         for (shift, hops), block in zip(chains(h), moved):
             for s in range(hops - 1, 0, -1):
-                if s == hops - 1:
-                    block, back, _ = lax.optimization_barrier((block, back, gate))
-                block = along(merge(parts[shift * s % quads], block), shift)
+                block = merge(parts[shift * s % quads], block)
+                turned = block if s == hops - 1 else turned
+                block = along(block, shift)
             back.append(block)
-        return back
+        return back, turned
 
     def finished(h, mine, back):
         done = finish(steps, *mine, back)
         return [done[0]] + [across(done[k], k) for k in range(1, QUAD)]
 
-    final = []
-    waiting = None
-    gate = None
+    final, gate, before = [], None, None
     for h in range(HPD):
         blocks, parts = others(h, gate)
-        if waiting is not None:
-            back = summed(*waiting[:3], parts)
-            final.append(finished(h - 1, waiting[3], back))
-        moved = sent(h, parts)
-        _, later_msgs = lax.optimization_barrier((parts, msgs))
-        mine = attend(h, (0,), steps, prompt_blocks, slot_prompt, kv3, blocks, later_msgs)
-        waiting = (h, parts, moved, mine)
-        gate = (mine[0], moved[-1]) if moved else (mine[0],)
-    final.append(finished(HPD - 1, mine, summed(*waiting[:3], moved)))
+        ready = parts
+        if before is not None:
+            mine, back = before
+            final.append(finished(h - 1, mine, tied(back, parts)))
+            ready = tied(parts, final[-1][0])
+        moved = sent(h, ready)
+        late = tied(msgs, parts, asked[h + 1:h + 2])
+        mine = attend(h, (0,), steps, prompt_blocks, slot_prompt, kv3, blocks, late)
+        back, turned = summed(h, parts, moved)
+        before = mine, back
+        gate = mine[0], turned
+    final.append(finished(HPD - 1, *before))
     return tuple(emit([m for per_head in final for m in per_head], queries.shape))
 
 

time: 114 us -> 114 us (level)
    ppermute x14, waiting for transfers between devices: 33.5 us -> 25.6 us  [across(): return lax.ppermute(array, 'sample', [(i, i ^ k) for i in range(nsample)])]
    ppermute x10, waiting for transfers between devices: 21.9 us -> 29.1 us  [along(): lax.ppermute(array, 'sample', [(i, (i + shift * QUAD) % nsample) for i in...]
  transfers between devices with their start and end apart: 24 -> 24, of which waited for: 14 -> 11; matrix products, arithmetic and copies ran while one was open for 0% -> 0% of each run, Pallas kernels for 21% -> 21%
where the time goes in v7:
time: 114 us; the launch traced here: 113 us
  waiting for transfers between devices  54.7 us (48%)
  starting transfers between devices  27.9 us (24%)
  Pallas kernels  27.4 us (24%)
  local copies, waits for them, and re-layouts  2.38 us (2%)
    ppermute x10, waiting for transfers between devices, along(): lax.ppermute(array, 'sample', [(i, (i + shift * QUAD) % nsample) for i in...  29.1 us
    ppermute x14, waiting for transfers between devices, across(): return lax.ppermute(array, 'sample', [(i, i ^ k) for i in range(nsample)])  25.6 us
    pallas_call x4, Pallas kernels, attend(): pl.pallas_call(functools.partial(attend_kernel, h, offsets, steps, max_ti...  21.8 us
    ppermute x10, starting transfers between devices, along(): lax.ppermute(array, 'sample', [(i, (i + shift * QUAD) % nsample) for i in...  17.2 us
    ppermute x14, starting transfers between devices, across(): return lax.ppermute(array, 'sample', [(i, i ^ k) for i in range(nsample)])  10.7 us
  transfers between devices with their start and end apart: 24, of which 11 were waited for; matrix products, arithmetic and copies ran while one was open for 0% of the time, Pallas kernels for 21%

profile of v7, /device:TPU:0, one launch (start us, length us, event | category | flops | bytes accessed | tf_op | source)
XLA Modules:
  0.0 113.4 jit_solution(7437468985381590190)
XLA Ops:
  0.6 2.2 %pack_queries.1 = (bf16[2,320,128]{2,1,0:T(8,128)(2,1)}, bf16[2,320,128]{2,1,0:T(8,128)(2,1)}, bf16[2,320,128]{2,1,0:T(8,128)(2,1)}, bf16[2,320,128]{2,1,0:T(8,128)(2,1)}) custom-call(bf16[8,4,8192]{2,1,0:T(4,128)(2,1)} %q_hbm.1, bf16[8,4,2048]{2,1,0:T(4,128)(2,1)} %new_hbm.1), custom_call_target="tpu_custom_call" | custom-call | bytes 2097152 | tf_op jit(solution)/shard_map/pack_queries/pallas_call | solution.py:72
  3.4 2.6 %collective-permute-start.1 = (bf16[2,320,128]{2,1,0:T(8,128)(2,1)}, bf16[2,320,128]{2,1,0:T(8,128)(2,1)S(1)}, u32[]{:S(2)}, u32[]{:S(2)}) collective-permute-start(bf16[2,320,128]{2,1,0:T(8,128)(2,1)} %get-tuple-element.46), channel_id=1, source_target_pairs={{0,2},{1,3},{2,0},{3,1},{4,6},{5,7},{6,4},{7,5},{8,10},{9,11},{10,... | collective-permute-start | bytes 491528 | tf_op jit(solution)/shard_map/ppermute | solution.py:452
  6.1 2.2 %copy-done = bf16[32,1,32,2048]{3,2,1,0:T(8,128)(2,1)S(1)} copy-done((bf16[32,1,32,2048]{3,2,1,0:T(8,128)(2,1)S(1)}, bf16[32,1,32,2048]{3,2,1,0:T(8,128)(2,1)}, u32[]{:S(2)}) %copy-start) | copy-done | bytes 4194328
  8.3 1.0 pack_kv.1
  9.3 1.8 %collective-permute-start.4 = (bf16[2,1024,256]{2,1,0:T(8,128)(2,1)S(1)}, bf16[2,1024,256]{2,1,0:T(8,128)(2,1)S(1)}, u32[]{:S(2)}, u32[]{:S(2)}) collective-permute-start(bf16[2,1024,256]{2,1,0:T(8,128)(2,1)S(1)} %get-tuple-element.49), channel_id=1, source_target_pairs={{0,2},{1,3},{2,0},{3,1},{4,6},{5,7},{6,4},{7,5},{8,10},{9,11},{10,... | collective-permute-start | bytes 3145736 | tf_op jit(solution)/shard_map/ppermute | solution.py:452
  11.3 3.1 %collective-permute-done.2.refs_3_ = bf16[2,320,128]{2,1,0:T(8,128)(2,1)S(1)} collective-permute-done((bf16[2,320,128]{2,1,0:T(8,128)(2,1)}, bf16[2,320,128]{2,1,0:T(8,128)(2,1)S(1)}, u32[]{:S(2)}, u32[]{:S(2)}) %collective-permute-start.2) | collective-permute-done | bytes 163872 | tf_op jit(solution)/shard_map/ppermute | solution.py:452
  14.8 2.1 %collective-permute-start.8 = (bf16[2,4,256,128]{3,2,1,0:T(8,128)(2,1)S(1)}, bf16[2,4,256,128]{3,2,1,0:T(8,128)(2,1)S(1)}, u32[]{:S(2)}, u32[]{:S(2)}) collective-permute-start(bf16[2,4,256,128]{3,2,1,0:T(8,128)(2,1)S(1)} %pad_maximum_fusion), channel_id=1, source_target_pairs={{0,4},{1,5},{2,6},{3,7},{4,8},{5,9},{6,10},{7,11},{8,12},{9,13},{1... | collective-permute-start | bytes 1572872 | tf_op jit(solution)/shard_map/ppermute | solution.py:455
  16.8 2.1 %collective-permute-start.6 = (bf16[2,4,256,128]{3,2,1,0:T(8,128)(2,1)S(1)}, bf16[2,4,256,128]{3,2,1,0:T(8,128)(2,1)S(1)}, u32[]{:S(2)}, u32[]{:S(2)}) collective-permute-start(bf16[2,4,256,128]{3,2,1,0:T(8,128)(2,1)S(1)} %pad_maximum_fusion), channel_id=1, source_target_pairs={{0,12},{1,13},{2,14},{3,15},{4,0},{5,1},{6,2},{7,3},{8,4},{9,5},{1... | collective-permute-start | bytes 1572872 | tf_op jit(solution)/shard_map/ppermute | solution.py:455
  18.9 18.1 %collective-permute-done.4 = bf16[2,1024,256]{2,1,0:T(8,128)(2,1)S(1)} collective-permute-done((bf16[2,1024,256]{2,1,0:T(8,128)(2,1)S(1)}, bf16[2,1024,256]{2,1,0:T(8,128)(2,1)S(1)}, u32[]{:S(2)}, u32[]{:S(2)}) %collective-permute-start.4) | collective-permute-done | bytes 1048608 | tf_op jit(solution)/shard_map/ppermute | solution.py:452
  37.1 4.5 %collective-permute-done.6 = bf16[2,4,256,128]{3,2,1,0:T(8,128)(2,1)S(1)} collective-permute-done((bf16[2,4,256,128]{3,2,1,0:T(8,128)(2,1)S(1)}, bf16[2,4,256,128]{3,2,1,0:T(8,128)(2,1)S(1)}, u32[]{:S(2)}, u32[]{:S(2)}) %collective-permute-start.6) | collective-permute-done | bytes 524320 | tf_op jit(solution)/shard_map/ppermute | solution.py:455
  41.6 1.5 %collective-permute-start.13 = (bf16[2,1024,256]{2,1,0:T(8,128)(2,1)S(1)}, bf16[2,1024,256]{2,1,0:T(8,128)(2,1)S(1)}, u32[]{:S(2)}, u32[]{:S(2)}) collective-permute-start(bf16[2,1024,256]{2,1,0:T(8,128)(2,1)S(1)} %get-tuple-element.61), channel_id=1, source_target_pairs={{0,2},{1,3},{2,0},{3,1},{4,6},{5,7},{6,4},{7,5},{8,10},{9,11},{10,... | collective-permute-start | bytes 3145736 | tf_op jit(solution)/shard_map/ppermute | solution.py:452
  43.2 2.4 %collective-permute-start.7 = (bf16[4,256,128]{2,1,0:T(8,128)(2,1)S(1)}, bf16[4,256,128]{2,1,0:T(8,128)(2,1)S(1)}, u32[]{:S(2)}, u32[]{:S(2)}) collective-permute-start(bf16[4,256,128]{2,1,0:T(8,128)(2,1)S(1)} %get-tuple-element.87.refs_0_), channel_id=1, source_target_pairs={{0,12},{1,13},{2,14},{3,15},{4,0},{5,1},{6,2},{7,3},{8,4},{9,5},{1... | collective-permute-start | bytes 786440 | tf_op jit(solution)/shard_map/ppermute | solution.py:455
  45.6 5.0 %collective-permute-done.7.refs_1_ = bf16[4,256,128]{2,1,0:T(8,128)(2,1)S(1)} collective-permute-done((bf16[4,256,128]{2,1,0:T(8,128)(2,1)S(1)}, bf16[4,256,128]{2,1,0:T(8,128)(2,1)S(1)}, u32[]{:S(2)}, u32[]{:S(2)}) %collective-permute-start.7) | collective-permute-done | bytes 262176 | tf_op jit(solution)/shard_map/ppermute | solution.py:455
  50.6 1.7 %collective-permute-start.9 = (bf16[4,256,128]{2,1,0:T(8,128)(2,1)S(1)}, bf16[4,256,128]{2,1,0:T(8,128)(2,1)S(1)}, u32[]{:S(2)}, u32[]{:S(2)}) collective-permute-start(bf16[4,256,128]{2,1,0:T(8,128)(2,1)S(1)} %get-tuple-element.53.refs_2_), channel_id=1, source_target_pairs={{0,4},{1,5},{2,6},{3,7},{4,8},{5,9},{6,10},{7,11},{8,12},{9,13},{1... | collective-permute-start | bytes 786440 | tf_op jit(solution)/shard_map/ppermute | solution.py:455
  52.3 7.5 %attend_others.2 = (bf16[272,512]{1,0:T(8,128)(2,1)S(1)}, bf16[272,512]{1,0:T(8,128)(2,1)S(1)}, bf16[272,512]{1,0:T(8,128)(2,1)S(1)}) custom-call(s32[8]{0:T(128)S(1)} %copy-done.2, s32[16]{0:T(128)S(1)} %copy-done.3, bf16[32,32,2048]{2,1,0:T(8,128)(2,1)} %bitcast.23, bf16[2,32,32,256]{3,2,1,0:T(8,128)(2,1)S(1)} %bitcast.28, ...), custom_call_target="tpu_custom_call" | custom-call | flops 5000000000 | bytes 4194304 | tf_op jit(solution)/shard_map/attend_others/pallas_call | solution.py:305
  60.1 3.4 %attend_own.2 = (f32[2,128,512]{2,1,0:T(8,128)S(1)}, f32[2,8,512]{2,1,0:T(8,128)S(1)}) custom-call(s32[8]{0:T(128)S(1)} %copy-done.2, s32[16]{0:T(128)S(1)} %copy-done.3, bf16[32,32,2048]{2,1,0:T(8,128)(2,1)} %bitcast.24, bf16[2,32,32,256]{3,2,1,0:T(8,128)(2,1)S(1)} %bitcast.29, bf16[2,32,32,256]{3,2,1,0:T(8,128)(2,1)S(1)} %bitcast.35, ...), custom_call_target="tpu_custom_call" | custom-call | flops 1000000000 | bytes 4194304 | tf_op jit(solution)/shard_map/attend_own/pallas_call | solution.py:305
  63.5 5.5 %collective-permute-done.11.two_ref = bf16[272,512]{1,0:T(8,128)(2,1)S(1)} collective-permute-done((bf16[272,512]{1,0:T(8,128)(2,1)S(1)}, bf16[272,512]{1,0:T(8,128)(2,1)S(1)}, u32[]{:S(2)}, u32[]{:S(2)}) %collective-permute-start.11) | collective-permute-done | bytes 278560 | tf_op jit(solution)/shard_map/ppermute | solution.py:455
  69.4 2.0 %collective-permute-start.12 = (bf16[272,512]{1,0:T(8,128)(2,1)S(1)}, bf16[272,512]{1,0:T(8,128)(2,1)S(1)}, u32[]{:S(2)}, u32[]{:S(2)}) collective-permute-start(bf16[272,512]{1,0:T(8,128)(2,1)S(1)} %merge.2), channel_id=1, source_target_pairs={{0,4},{1,5},{2,6},{3,7},{4,8},{5,9},{6,10},{7,11},{8,12},{9,13},{1... | collective-permute-start | bytes 835592 | tf_op jit(solution)/shard_map/ppermute | solution.py:455
  71.4 7.5 %attend_others.3 = (bf16[272,512]{1,0:T(8,128)(2,1)S(1)}, bf16[272,512]{1,0:T(8,128)(2,1)S(1)}, bf16[272,512]{1,0:T(8,128)(2,1)S(1)}) custom-call(s32[8]{0:T(128)S(1)} %copy-done.2, s32[16]{0:T(128)S(1)} %copy-done.3, bf16[32,32,2048]{2,1,0:T(8,128)(2,1)} %bitcast.25, bf16[2,32,32,256]{3,2,1,0:T(8,128)(2,1)S(1)} %bitcast.30, ...), custom_call_target="tpu_custom_call" | custom-call | flops 5000000000 | bytes 4194304 | tf_op jit(solution)/shard_map/attend_others/pallas_call | solution.py:305
  78.9 5.4 %collective-permute-done.10.refs_0_ = bf16[272,512]{1,0:T(8,128)(2,1)S(1)} collective-permute-done((bf16[272,512]{1,0:T(8,128)(2,1)S(1)}, bf16[272,512]{1,0:T(8,128)(2,1)S(1)}, u32[]{:S(2)}, u32[]{:S(2)}) %collective-permute-start.10) | collective-permute-done | bytes 278560 | tf_op jit(solution)/shard_map/ppermute | solution.py:455
  84.7 1.3 %collective-permute-start.19 = (bf16[272,512]{1,0:T(8,128)(2,1)S(1)}, bf16[272,512]{1,0:T(8,128)(2,1)S(1)}, u32[]{:S(2)}, u32[]{:S(2)}) collective-permute-start(bf16[272,512]{1,0:T(8,128)(2,1)S(1)} %get-tuple-element.79), channel_id=1, source_target_pairs={{0,12},{1,13},{2,14},{3,15},{4,0},{5,1},{6,2},{7,3},{8,4},{9,5},{1... | collective-permute-start | bytes 835592 | tf_op jit(solution)/shard_map/ppermute | solution.py:455
  85.9 0.8 collective-permute-start.18
  86.7 6.4 %collective-permute-done.19.two_ref = bf16[272,512]{1,0:T(8,128)(2,1)S(1)} collective-permute-done((bf16[272,512]{1,0:T(8,128)(2,1)S(1)}, bf16[272,512]{1,0:T(8,128)(2,1)S(1)}, u32[]{:S(2)}, u32[]{:S(2)}) %collective-permute-start.19) | collective-permute-done | bytes 278560 | tf_op jit(solution)/shard_map/ppermute | solution.py:455
  93.3 4.6 %collective-permute-start.20 = (bf16[272,512]{1,0:T(8,128)(2,1)S(1)}, bf16[272,512]{1,0:T(8,128)(2,1)S(1)}, u32[]{:S(2)}, u32[]{:S(2)}) collective-permute-start(bf16[272,512]{1,0:T(8,128)(2,1)S(1)} %merge.3), channel_id=1, source_target_pairs={{0,12},{1,13},{2,14},{3,15},{4,0},{5,1},{6,2},{7,3},{8,4},{9,5},{1... | collective-permute-start | bytes 835592 | tf_op jit(solution)/shard_map/ppermute | solution.py:455
  98.3 1.4 %collective-permute-start.17 = (bf16[320,128]{1,0:T(8,128)(2,1)S(1)}, bf16[320,128]{1,0:T(8,128)(2,1)S(1)}, u32[]{:S(2)}, u32[]{:S(2)}) collective-permute-start(bf16[320,128]{1,0:T(8,128)(2,1)S(1)} %get-tuple-element.71), channel_id=1, source_target_pairs={{0,3},{1,2},{2,1},{3,0},{4,7},{5,6},{6,5},{7,4},{8,11},{9,10},{10,... | collective-permute-start | bytes 245768 | tf_op jit(solution)/shard_map/ppermute | solution.py:452
  99.7 3.4 %attend_own.3 = (f32[2,128,512]{2,1,0:T(8,128)S(1)}, f32[2,8,512]{2,1,0:T(8,128)S(1)}) custom-call(s32[8]{0:T(128)S(1)} %copy-done.2, s32[16]{0:T(128)S(1)} %copy-done.3, bf16[32,32,2048]{2,1,0:T(8,128)(2,1)} %bitcast.26, bf16[2,32,32,256]{3,2,1,0:T(8,128)(2,1)S(1)} %bitcast.31, bf16[2,32,32,256]{3,2,1,0:T(8,128)(2,1)S(1)} %bitcast.33, ...), custom_call_target="tpu_custom_call" | custom-call | flops 1000000000 | bytes 4194304 | tf_op jit(solution)/shard_map/attend_own/pallas_call | solution.py:305
  103.1 2.3 %collective-permute-done.20.refs_1_ = bf16[272,512]{1,0:T(8,128)(2,1)S(1)} collective-permute-done((bf16[272,512]{1,0:T(8,128)(2,1)S(1)}, bf16[272,512]{1,0:T(8,128)(2,1)S(1)}, u32[]{:S(2)}, u32[]{:S(2)}) %collective-permute-start.20) | collective-permute-done | bytes 278560 | tf_op jit(solution)/shard_map/ppermute | solution.py:455
  105.8 1.1 collective-permute-start.22
  106.9 0.8 collective-permute-start.23
  107.6 3.4 %collective-permute-done.22.refs_6_ = bf16[320,128]{1,0:T(8,128)(2,1)S(1)} collective-permute-done((bf16[320,128]{1,0:T(8,128)(2,1)S(1)}, bf16[320,128]{1,0:T(8,128)(2,1)S(1)}, u32[]{:S(2)}, u32[]{:S(2)}) %collective-permute-start.22) | collective-permute-done | bytes 81952 | tf_op jit(solution)/shard_map/ppermute | solution.py:452
  111.1 0.8 collective-permute-done.23.refs_7_
  111.9 1.5 %emit.1 = (bf16[8,4,8192]{2,1,0:T(4,128)(2,1)}, bf16[8,4,8192]{2,1,0:T(4,128)(2,1)}) custom-call(bf16[320,128]{1,0:T(8,128)(2,1)S(1)} %get-tuple-element.68.refs_0_, bf16[320,128]{1,0:T(8,128)(2,1)S(1)} %collective-permute-done.15.refs_1_, bf16[320,128]{1,0:T(8,128)(2,1)S(1)} %collective-permute-done.16.refs_2_, ...), custom_call_target="tpu_custom_call" | custom-call | flops 1048576 | bytes 2097152 | tf_op jit(solution)/shard_map/emit/pallas_call | solution.py:434
  (45 shorter events, 3.3 us)
Async XLA Ops:
  2.9 8.2 %collective-permute-start = (bf16[2,320,128]{2,1,0:T(8,128)(2,1)}, bf16[2,320,128]{2,1,0:T(8,128)(2,1)S(1)}, u32[]{:S(2)}, u32[]{:S(2)}) collective-permute-start(bf16[2,320,128]{2,1,0:T(8,128)(2,1)} %get-tuple-element.45), channel_id=1, source_target_pairs={{0,1},{1,0},{2,3},{3,2},{4,5},{5,4},{6,7},{7,6},{8,9},{9,8},{10,11... | collective-permute-start | bytes 491528 | tf_op jit(solution)/shard_map/ppermute | solution.py:452
  3.4 7.9 %collective-permute-start.1 = (bf16[2,320,128]{2,1,0:T(8,128)(2,1)}, bf16[2,320,128]{2,1,0:T(8,128)(2,1)S(1)}, u32[]{:S(2)}, u32[]{:S(2)}) collective-permute-start(bf16[2,320,128]{2,1,0:T(8,128)(2,1)} %get-tuple-element.46), channel_id=1, source_target_pairs={{0,2},{1,3},{2,0},{3,1},{4,6},{5,7},{6,4},{7,5},{8,10},{9,11},{10,... | collective-permute-start | bytes 491528 | tf_op jit(solution)/shard_map/ppermute | solution.py:452
  6.0 8.3 %collective-permute-start.2 = (bf16[2,320,128]{2,1,0:T(8,128)(2,1)}, bf16[2,320,128]{2,1,0:T(8,128)(2,1)S(1)}, u32[]{:S(2)}, u32[]{:S(2)}) collective-permute-start(bf16[2,320,128]{2,1,0:T(8,128)(2,1)} %get-tuple-element.47), channel_id=1, source_target_pairs={{0,3},{1,2},{2,1},{3,0},{4,7},{5,6},{6,5},{7,4},{8,11},{9,10},{10,... | collective-permute-start | bytes 491528 | tf_op jit(solution)/shard_map/ppermute | solution.py:452
  6.1 2.2 %copy-start = (bf16[32,1,32,2048]{3,2,1,0:T(8,128)(2,1)S(1)}, bf16[32,1,32,2048]{3,2,1,0:T(8,128)(2,1)}, u32[]{:S(2)}) copy-start(bf16[32,1,32,2048]{3,2,1,0:T(8,128)(2,1)} %param.5) | copy-start | bytes 12582916
  8.3 2.8 %copy-start.1 = (bf16[2,320,128]{2,1,0:T(8,128)(2,1)S(1)}, bf16[2,320,128]{2,1,0:T(8,128)(2,1)}, u32[]{:S(2)}) copy-start(bf16[2,320,128]{2,1,0:T(8,128)(2,1)} %get-tuple-element.72.refs_0_) | copy-start | bytes 491524
  9.3 43.1 %copy-start.2 = (s32[8]{0:T(128)S(1)}, s32[8]{0:T(128)}, u32[]{:S(2)}) copy-start(s32[8]{0:T(128)} %counts_ref.7) | copy-start | bytes 100
  9.3 43.1 %copy-start.3 = (s32[16]{0:T(128)S(1)}, s32[16]{0:T(128)}, u32[]{:S(2)}) copy-start(s32[16]{0:T(128)} %slots_ref.7) | copy-start | bytes 196
  9.3 27.7 %collective-permute-start.4 = (bf16[2,1024,256]{2,1,0:T(8,128)(2,1)S(1)}, bf16[2,1024,256]{2,1,0:T(8,128)(2,1)S(1)}, u32[]{:S(2)}, u32[]{:S(2)}) collective-permute-start(bf16[2,1024,256]{2,1,0:T(8,128)(2,1)S(1)} %get-tuple-element.49), channel_id=1, source_target_pairs={{0,2},{1,3},{2,0},{3,1},{4,6},{5,7},{6,4},{7,5},{8,10},{9,11},{10,... | collective-permute-start | bytes 3145736 | tf_op jit(solution)/shard_map/ppermute | solution.py:452
  14.3 27.3 %collective-permute-start.3 = (bf16[2,1024,256]{2,1,0:T(8,128)(2,1)S(1)}, bf16[2,1024,256]{2,1,0:T(8,128)(2,1)S(1)}, u32[]{:S(2)}, u32[]{:S(2)}) collective-permute-start(bf16[2,1024,256]{2,1,0:T(8,128)(2,1)S(1)} %get-tuple-element.48), channel_id=1, source_target_pairs={{0,1},{1,0},{2,3},{3,2},{4,5},{5,4},{6,7},{7,6},{8,9},{9,8},{10,11... | collective-permute-start | bytes 3145736 | tf_op jit(solution)/shard_map/ppermute | solution.py:452
  14.8 22.3 %collective-permute-start.8 = (bf16[2,4,256,128]{3,2,1,0:T(8,128)(2,1)S(1)}, bf16[2,4,256,128]{3,2,1,0:T(8,128)(2,1)S(1)}, u32[]{:S(2)}, u32[]{:S(2)}) collective-permute-start(bf16[2,4,256,128]{3,2,1,0:T(8,128)(2,1)S(1)} %pad_maximum_fusion), channel_id=1, source_target_pairs={{0,4},{1,5},{2,6},{3,7},{4,8},{5,9},{6,10},{7,11},{8,12},{9,13},{1... | collective-permute-start | bytes 1572872 | tf_op jit(solution)/shard_map/ppermute | solution.py:455
  16.8 24.8 %collective-permute-start.6 = (bf16[2,4,256,128]{3,2,1,0:T(8,128)(2,1)S(1)}, bf16[2,4,256,128]{3,2,1,0:T(8,128)(2,1)S(1)}, u32[]{:S(2)}, u32[]{:S(2)}) collective-permute-start(bf16[2,4,256,128]{3,2,1,0:T(8,128)(2,1)S(1)} %pad_maximum_fusion), channel_id=1, source_target_pairs={{0,12},{1,13},{2,14},{3,15},{4,0},{5,1},{6,2},{7,3},{8,4},{9,5},{1... | collective-permute-start | bytes 1572872 | tf_op jit(solution)/shard_map/ppermute | solution.py:455
  37.0 15.3 %collective-permute-start.5 = (bf16[1024,256]{1,0:T(8,128)(2,1)S(1)}, bf16[1024,256]{1,0:T(8,128)(2,1)S(1)}, u32[]{:S(2)}, u32[]{:S(2)}) collective-permute-start(bf16[1024,256]{1,0:T(8,128)(2,1)S(1)} %slice_bitcast_fusion.1), channel_id=1, source_target_pairs={{0,1},{1,0},{2,3},{3,2},{4,5},{5,4},{6,7},{7,6},{8,9},{9,8},{10,11... | collective-permute-start | bytes 1572872 | tf_op jit(solution)/shard_map/ppermute | solution.py:452
  41.6 27.6 %collective-permute-start.13 = (bf16[2,1024,256]{2,1,0:T(8,128)(2,1)S(1)}, bf16[2,1024,256]{2,1,0:T(8,128)(2,1)S(1)}, u32[]{:S(2)}, u32[]{:S(2)}) collective-permute-start(bf16[2,1024,256]{2,1,0:T(8,128)(2,1)S(1)} %get-tuple-element.61), channel_id=1, source_target_pairs={{0,2},{1,3},{2,0},{3,1},{4,6},{5,7},{6,4},{7,5},{8,10},{9,11},{10,... | collective-permute-start | bytes 3145736 | tf_op jit(solution)/shard_map/ppermute | solution.py:452
  43.2 7.4 %collective-permute-start.7 = (bf16[4,256,128]{2,1,0:T(8,128)(2,1)S(1)}, bf16[4,256,128]{2,1,0:T(8,128)(2,1)S(1)}, u32[]{:S(2)}, u32[]{:S(2)}) collective-permute-start(bf16[4,256,128]{2,1,0:T(8,128)(2,1)S(1)} %get-tuple-element.87.refs_0_), channel_id=1, source_target_pairs={{0,12},{1,13},{2,14},{3,15},{4,0},{5,1},{6,2},{7,3},{8,4},{9,5},{1... | collective-permute-start | bytes 786440 | tf_op jit(solution)/shard_map/ppermute | solution.py:455
  50.6 9.5 %collective-permute-start.9 = (bf16[4,256,128]{2,1,0:T(8,128)(2,1)S(1)}, bf16[4,256,128]{2,1,0:T(8,128)(2,1)S(1)}, u32[]{:S(2)}, u32[]{:S(2)}) collective-permute-start(bf16[4,256,128]{2,1,0:T(8,128)(2,1)S(1)} %get-tuple-element.53.refs_2_), channel_id=1, source_target_pairs={{0,4},{1,5},{2,6},{3,7},{4,8},{5,9},{6,10},{7,11},{8,12},{9,13},{1... | collective-permute-start | bytes 786440 | tf_op jit(solution)/shard_map/ppermute | solution.py:455
  59.9 9.1 %collective-permute-start.11 = (bf16[272,512]{1,0:T(8,128)(2,1)S(1)}, bf16[272,512]{1,0:T(8,128)(2,1)S(1)}, u32[]{:S(2)}, u32[]{:S(2)}) collective-permute-start(bf16[272,512]{1,0:T(8,128)(2,1)S(1)} %get-tuple-element.51), channel_id=1, source_target_pairs={{0,4},{1,5},{2,6},{3,7},{4,8},{5,9},{6,10},{7,11},{8,12},{9,13},{1... | collective-permute-start | bytes 835592 | tf_op jit(solution)/shard_map/ppermute | solution.py:455
  69.2 2.2 %collective-permute-start.14 = (bf16[1024,256]{1,0:T(8,128)(2,1)S(1)}, bf16[1024,256]{1,0:T(8,128)(2,1)S(1)}, u32[]{:S(2)}, u32[]{:S(2)}) collective-permute-start(bf16[1024,256]{1,0:T(8,128)(2,1)S(1)} %slice_bitcast_fusion), channel_id=1, source_target_pairs={{0,1},{1,0},{2,3},{3,2},{4,5},{5,4},{6,7},{7,6},{8,9},{9,8},{10,11... | collective-permute-start | bytes 1572872 | tf_op jit(solution)/shard_map/ppermute | solution.py:452
  69.3 15.0 %collective-permute-start.10 = (bf16[272,512]{1,0:T(8,128)(2,1)S(1)}, bf16[272,512]{1,0:T(8,128)(2,1)S(1)}, u32[]{:S(2)}, u32[]{:S(2)}) collective-permute-start(bf16[272,512]{1,0:T(8,128)(2,1)S(1)} %get-tuple-element.52), channel_id=1, source_target_pairs={{0,12},{1,13},{2,14},{3,15},{4,0},{5,1},{6,2},{7,3},{8,4},{9,5},{1... | collective-permute-start | bytes 835592 | tf_op jit(solution)/shard_map/ppermute | solution.py:455
  69.4 15.0 %collective-permute-start.12 = (bf16[272,512]{1,0:T(8,128)(2,1)S(1)}, bf16[272,512]{1,0:T(8,128)(2,1)S(1)}, u32[]{:S(2)}, u32[]{:S(2)}) collective-permute-start(bf16[272,512]{1,0:T(8,128)(2,1)S(1)} %merge.2), channel_id=1, source_target_pairs={{0,4},{1,5},{2,6},{3,7},{4,8},{5,9},{6,10},{7,11},{8,12},{9,13},{1... | collective-permute-start | bytes 835592 | tf_op jit(solution)/shard_map/ppermute | solution.py:455
  84.7 8.4 %collective-permute-start.19 = (bf16[272,512]{1,0:T(8,128)(2,1)S(1)}, bf16[272,512]{1,0:T(8,128)(2,1)S(1)}, u32[]{:S(2)}, u32[]{:S(2)}) collective-permute-start(bf16[272,512]{1,0:T(8,128)(2,1)S(1)} %get-tuple-element.79), channel_id=1, source_target_pairs={{0,12},{1,13},{2,14},{3,15},{4,0},{5,1},{6,2},{7,3},{8,4},{9,5},{1... | collective-permute-start | bytes 835592 | tf_op jit(solution)/shard_map/ppermute | solution.py:455
  85.9 17.1 %collective-permute-start.18 = (bf16[272,512]{1,0:T(8,128)(2,1)S(1)}, bf16[272,512]{1,0:T(8,128)(2,1)S(1)}, u32[]{:S(2)}, u32[]{:S(2)}) collective-permute-start(bf16[272,512]{1,0:T(8,128)(2,1)S(1)} %get-tuple-element.78), channel_id=1, source_target_pairs={{0,4},{1,5},{2,6},{3,7},{4,8},{5,9},{6,10},{7,11},{8,12},{9,13},{1... | collective-permute-start | bytes 835592 | tf_op jit(solution)/shard_map/ppermute | solution.py:455
  93.3 12.1 %collective-permute-start.20 = (bf16[272,512]{1,0:T(8,128)(2,1)S(1)}, bf16[272,512]{1,0:T(8,128)(2,1)S(1)}, u32[]{:S(2)}, u32[]{:S(2)}) collective-permute-start(bf16[272,512]{1,0:T(8,128)(2,1)S(1)} %merge.3), channel_id=1, source_target_pairs={{0,12},{1,13},{2,14},{3,15},{4,0},{5,1},{6,2},{7,3},{8,4},{9,5},{1... | collective-permute-start | bytes 835592 | tf_op jit(solution)/shard_map/ppermute | solution.py:455
  97.8 9.0 %collective-permute-start.15 = (bf16[320,128]{1,0:T(8,128)(2,1)S(1)}, bf16[320,128]{1,0:T(8,128)(2,1)S(1)}, u32[]{:S(2)}, u32[]{:S(2)}) collective-permute-start(bf16[320,128]{1,0:T(8,128)(2,1)S(1)} %get-tuple-element.69), channel_id=1, source_target_pairs={{0,1},{1,0},{2,3},{3,2},{4,5},{5,4},{6,7},{7,6},{8,9},{9,8},{10,11... | collective-permute-start | bytes 245768 | tf_op jit(solution)/shard_map/ppermute | solution.py:452
  97.8 9.8 %collective-permute-start.16 = (bf16[320,128]{1,0:T(8,128)(2,1)S(1)}, bf16[320,128]{1,0:T(8,128)(2,1)S(1)}, u32[]{:S(2)}, u32[]{:S(2)}) collective-permute-start(bf16[320,128]{1,0:T(8,128)(2,1)S(1)} %get-tuple-element.70), channel_id=1, source_target_pairs={{0,2},{1,3},{2,0},{3,1},{4,6},{5,7},{6,4},{7,5},{8,10},{9,11},{10,... | collective-permute-start | bytes 245768 | tf_op jit(solution)/shard_map/ppermute | solution.py:452
  98.3 9.3 %collective-permute-start.17 = (bf16[320,128]{1,0:T(8,128)(2,1)S(1)}, bf16[320,128]{1,0:T(8,128)(2,1)S(1)}, u32[]{:S(2)}, u32[]{:S(2)}) collective-permute-start(bf16[320,128]{1,0:T(8,128)(2,1)S(1)} %get-tuple-element.71), channel_id=1, source_target_pairs={{0,3},{1,2},{2,1},{3,0},{4,7},{5,6},{6,5},{7,4},{8,11},{9,10},{10,... | collective-permute-start | bytes 245768 | tf_op jit(solution)/shard_map/ppermute | solution.py:452
  105.7 2.0 %collective-permute-start.21 = (bf16[320,128]{1,0:T(8,128)(2,1)S(1)}, bf16[320,128]{1,0:T(8,128)(2,1)S(1)}, u32[]{:S(2)}, u32[]{:S(2)}) collective-permute-start(bf16[320,128]{1,0:T(8,128)(2,1)S(1)} %get-tuple-element.81), channel_id=1, source_target_pairs={{0,1},{1,0},{2,3},{3,2},{4,5},{5,4},{6,7},{7,6},{8,9},{9,8},{10,11... | collective-permute-start | bytes 245768 | tf_op jit(solution)/shard_map/ppermute | solution.py:452
  105.8 5.3 %collective-permute-start.22 = (bf16[320,128]{1,0:T(8,128)(2,1)S(1)}, bf16[320,128]{1,0:T(8,128)(2,1)S(1)}, u32[]{:S(2)}, u32[]{:S(2)}) collective-permute-start(bf16[320,128]{1,0:T(8,128)(2,1)S(1)} %get-tuple-element.82), channel_id=1, source_target_pairs={{0,2},{1,3},{2,0},{3,1},{4,6},{5,7},{6,4},{7,5},{8,10},{9,11},{10,... | collective-permute-start | bytes 245768 | tf_op jit(solution)/shard_map/ppermute | solution.py:452
  106.9 5.1 %collective-permute-start.23 = (bf16[320,128]{1,0:T(8,128)(2,1)S(1)}, bf16[320,128]{1,0:T(8,128)(2,1)S(1)}, u32[]{:S(2)}, u32[]{:S(2)}) collective-permute-start(bf16[320,128]{1,0:T(8,128)(2,1)S(1)} %get-tuple-element.83), channel_id=1, source_target_pairs={{0,3},{1,2},{2,1},{3,0},{4,7},{5,6},{6,5},{7,4},{8,11},{9,10},{10,... | collective-permute-start | bytes 245768 | tf_op jit(solution)/shard_map/ppermute | solution.py:452

commit v8 on v7

--- a/solution.py
+++ b/solution.py
@@ -92,7 +92,7 @@
     for h in range(HPD):
         for k in range(1, QUAD):
             head = jnp.bitwise_xor(mine, k) * HPD + h
-            out = near.at[h] if k == 1 else far[h].at[k - 2]
+            out = near.at[h] if k == 1 else far[h * (QUAD - 2) + k - 2]
             for part in range(2):
                 copies.append(
                     pltpu.make_async_copy(
@@ -108,12 +108,13 @@
 
 
 def pack_kv(kv2):
-    shape = jax.ShapeDtypeStruct((2, kv2.shape[0], 2 * HD), BF16)
+    tokens, count = kv2.shape[0], HPD * (QUAD - 2)
     return pl.pallas_call(
         pack_kv_kernel,
-        out_shape=[shape] * (1 + HPD),
+        out_shape=[jax.ShapeDtypeStruct((HPD, tokens, 2 * HD), BF16)]
+        + [jax.ShapeDtypeStruct((tokens, 2 * HD), BF16)] * count,
         in_specs=[ANY],
-        out_specs=[ANY] * (1 + HPD),
+        out_specs=[ANY] * (1 + count),
         scratch_shapes=[pltpu.SemaphoreType.DMA((2 * HPD * (QUAD - 1),))],
         compiler_params=params(16),
         cost_estimate=cost(0, 6 << 20),
@@ -129,7 +130,8 @@
     return lax.dot_general(values, weights, (((0,), (0,)), ((), ())), preferred_element_type=F32)
 
 
-def attend_kernel(h, offsets, steps, max_tiles, counts_ref, slots_ref, kv_ref, near, same, passed, *refs):
+def attend_kernel(h, offsets, steps, max_tiles, counts_ref, slots_ref, kv_ref, near, *refs):
+    far, refs = refs[:QUAD - 2], refs[QUAD - 2:]
     count = len(offsets)
     nq = QUAD if steps else count
     queries, refs = refs[:nq], refs[nq:]
@@ -162,7 +164,8 @@
             kv_ref.at[:, :, lanes((part * KVH + mine * HPD + h) * HD, HD)],
             held.at[0:blocks, mine, :, part * HD:(part + 1) * HD],
         )
-    for k, source in ((1, near.at[h]), (2, same.at[0]), (3, passed)):
+    for k in range(1, QUAD):
+        source = near.at[h] if k == 1 else far[k - 2]
         copied(later, source, held.at[0:blocks, jnp.bitwise_xor(mine, k)])
     held[blocks:] = jnp.zeros_like(held[blocks:])
     for copy in first_copies:
@@ -481,13 +484,14 @@
         asked.append(held)
     arrived = []
     for h in range(HPD):
-        source = tied(far[h], arrived[-1], first_hop, near) if h else far[h]
-        arrived.append(across(source, 2))
+        sources = far[h * (QUAD - 2):(h + 1) * (QUAD - 2)]
+        if h:
+            sources = tied(sources, arrived[-1], first_hop, near)
+        arrived.append([across(block, 2 + i) for i, block in enumerate(sources)])
 
     def others(h, gate):
-        handed = arrived[h][1] if gate is None else tied(arrived[h][1], gate, asked[h])
-        passed = across(handed, 1).reshape(-1, BLK, 2 * HD)
-        blocks = [near, arrived[h].reshape(2, -1, BLK, 2 * HD), passed]
+        received = arrived[h] if gate is None else tied(arrived[h], gate, asked[h])
+        blocks = [near] + [block.reshape(-1, BLK, 2 * HD) for block in received]
         offsets = tuple(sorted(asked[h]))
         partial = attend(
             h, offsets, 0, prompt_blocks, slot_prompt, kv3, blocks, [asked[h][o] for o in offsets]
@@ -506,6 +510,8 @@
         back, turned = [], parts[min(parts)] if parts else near
         for (shift, hops), block in zip(chains(h), moved):
             for s in range(hops - 1, 0, -1):
+                if h + 1 < HPD and s == hops - 1:
+                    block = tied(block, moved)
                 block = merge(parts[shift * s % quads], block)
                 turned = block if s == hops - 1 else turned
                 block = along(block, shift)

time: 114 us -> 116 us (1.018)
  waiting for transfers between devices: 54.7 us -> 58.8 us
  starting transfers between devices: 27.9 us -> 26.7 us
    ppermute x10, waiting for transfers between devices: 29.1 us -> 48.3 us  [along(): lax.ppermute(array, 'sample', [(i, (i + shift * QUAD) % nsample) for i in...]
    ppermute x14, waiting for transfers between devices: 25.6 us -> 10.4 us  [across(): return lax.ppermute(array, 'sample', [(i, i ^ k) for i in range(nsample)])]
    ppermute x10, starting transfers between devices: 17.2 us -> 15.1 us  [along(): lax.ppermute(array, 'sample', [(i, (i + shift * QUAD) % nsample) for i in...]
  transfers between devices with their start and end apart: 24 -> 24, of which waited for: 11 -> 13; matrix products, arithmetic and copies ran while one was open for 0% -> 0% of each run, Pallas kernels for 21% -> 20%
where the time goes in v8:
time: 116 us
  waiting for transfers between devices  58.8 us (51%)
  Pallas kernels  27.5 us (24%)
  starting transfers between devices  26.7 us (23%)
  local copies, waits for them, and re-layouts  2.31 us (2%)
    ppermute x10, waiting for transfers between devices, along(): lax.ppermute(array, 'sample', [(i, (i + shift * QUAD) % nsample) for i in...  48.3 us
    pallas_call x4, Pallas kernels, attend(): pl.pallas_call(functools.partial(attend_kernel, h, offsets, steps, max_ti...  21.9 us
    ppermute x10, starting transfers between devices, along(): lax.ppermute(array, 'sample', [(i, (i + shift * QUAD) % nsample) for i in...  15.1 us
    ppermute x14, starting transfers between devices, across(): return lax.ppermute(array, 'sample', [(i, i ^ k) for i in range(nsample)])  11.6 us
    ppermute x14, waiting for transfers between devices, across(): return lax.ppermute(array, 'sample', [(i, i ^ k) for i in range(nsample)])  10.4 us
  transfers between devices with their start and end apart: 24, of which 13 were waited for; matrix products, arithmetic and copies ran while one was open for 0% of the time, Pallas kernels for 20%

profile of v8, /device:TPU:0, one launch (start us, length us, event | category | flops | bytes accessed | tf_op | source)
XLA Modules:
  0.0 116.2 jit_solution(16254968668616399416)
XLA Ops:
  0.6 2.2 %pack_queries.1 = (bf16[2,320,128]{2,1,0:T(8,128)(2,1)}, bf16[2,320,128]{2,1,0:T(8,128)(2,1)}, bf16[2,320,128]{2,1,0:T(8,128)(2,1)}, bf16[2,320,128]{2,1,0:T(8,128)(2,1)}) custom-call(bf16[8,4,8192]{2,1,0:T(4,128)(2,1)} %q_hbm.1, bf16[8,4,2048]{2,1,0:T(4,128)(2,1)} %new_hbm.1), custom_call_target="tpu_custom_call" | custom-call | bytes 2097152 | tf_op jit(solution)/shard_map/pack_queries/pallas_call | solution.py:72
  3.4 2.6 %collective-permute-start.1 = (bf16[2,320,128]{2,1,0:T(8,128)(2,1)}, bf16[2,320,128]{2,1,0:T(8,128)(2,1)S(1)}, u32[]{:S(2)}, u32[]{:S(2)}) collective-permute-start(bf16[2,320,128]{2,1,0:T(8,128)(2,1)} %get-tuple-element.51), channel_id=1, source_target_pairs={{0,2},{1,3},{2,0},{3,1},{4,6},{5,7},{6,4},{7,5},{8,10},{9,11},{10,... | collective-permute-start | bytes 491528 | tf_op jit(solution)/shard_map/ppermute | solution.py:455
  6.1 2.2 %copy-done = bf16[32,1,32,2048]{3,2,1,0:T(8,128)(2,1)S(1)} copy-done((bf16[32,1,32,2048]{3,2,1,0:T(8,128)(2,1)S(1)}, bf16[32,1,32,2048]{3,2,1,0:T(8,128)(2,1)}, u32[]{:S(2)}) %copy-start) | copy-done | bytes 4194328
  8.3 1.0 pack_kv.1
  9.3 2.0 %collective-permute-done.1.refs_4_ = bf16[2,320,128]{2,1,0:T(8,128)(2,1)S(1)} collective-permute-done((bf16[2,320,128]{2,1,0:T(8,128)(2,1)}, bf16[2,320,128]{2,1,0:T(8,128)(2,1)S(1)}, u32[]{:S(2)}, u32[]{:S(2)}) %collective-permute-start.1) | collective-permute-done | bytes 163872 | tf_op jit(solution)/shard_map/ppermute | solution.py:455
  11.3 3.0 %collective-permute-done.2.refs_5_ = bf16[2,320,128]{2,1,0:T(8,128)(2,1)S(1)} collective-permute-done((bf16[2,320,128]{2,1,0:T(8,128)(2,1)}, bf16[2,320,128]{2,1,0:T(8,128)(2,1)S(1)}, u32[]{:S(2)}, u32[]{:S(2)}) %collective-permute-start.2) | collective-permute-done | bytes 163872 | tf_op jit(solution)/shard_map/ppermute | solution.py:455
  14.5 3.9 %collective-permute-start.6 = (bf16[2,4,256,128]{3,2,1,0:T(8,128)(2,1)S(1)}, bf16[2,4,256,128]{3,2,1,0:T(8,128)(2,1)S(1)}, u32[]{:S(2)}, u32[]{:S(2)}) collective-permute-start(bf16[2,4,256,128]{3,2,1,0:T(8,128)(2,1)S(1)} %pad_maximum_fusion), channel_id=1, source_target_pairs={{0,12},{1,13},{2,14},{3,15},{4,0},{5,1},{6,2},{7,3},{8,4},{9,5},{1... | collective-permute-start | bytes 1572872 | tf_op jit(solution)/shard_map/ppermute | solution.py:458
  18.4 1.5 %collective-permute-start.4 = (bf16[1024,256]{1,0:T(8,128)(2,1)S(1)}, bf16[1024,256]{1,0:T(8,128)(2,1)S(1)}, u32[]{:S(2)}, u32[]{:S(2)}) collective-permute-start(bf16[1024,256]{1,0:T(8,128)(2,1)S(1)} %get-tuple-element.54), channel_id=1, source_target_pairs={{0,2},{1,3},{2,0},{3,1},{4,6},{5,7},{6,4},{7,5},{8,10},{9,11},{10,... | collective-permute-start | bytes 1572872 | tf_op jit(solution)/shard_map/ppermute | solution.py:455
  19.9 10.8 %collective-permute-done.6 = bf16[2,4,256,128]{3,2,1,0:T(8,128)(2,1)S(1)} collective-permute-done((bf16[2,4,256,128]{3,2,1,0:T(8,128)(2,1)S(1)}, bf16[2,4,256,128]{3,2,1,0:T(8,128)(2,1)S(1)}, u32[]{:S(2)}, u32[]{:S(2)}) %collective-permute-start.6) | collective-permute-done | bytes 524320 | tf_op jit(solution)/shard_map/ppermute | solution.py:458
  30.8 4.3 %collective-permute-start.7 = (bf16[4,256,128]{2,1,0:T(8,128)(2,1)S(1)}, bf16[4,256,128]{2,1,0:T(8,128)(2,1)S(1)}, u32[]{:S(2)}, u32[]{:S(2)}) collective-permute-start(bf16[4,256,128]{2,1,0:T(8,128)(2,1)S(1)} %get-tuple-element.97.refs_2_), channel_id=1, source_target_pairs={{0,12},{1,13},{2,14},{3,15},{4,0},{5,1},{6,2},{7,3},{8,4},{9,5},{1... | collective-permute-start | bytes 786440 | tf_op jit(solution)/shard_map/ppermute | solution.py:458
  35.1 7.8 %collective-permute-done.8 = bf16[2,4,256,128]{3,2,1,0:T(8,128)(2,1)S(1)} collective-permute-done((bf16[2,4,256,128]{3,2,1,0:T(8,128)(2,1)S(1)}, bf16[2,4,256,128]{3,2,1,0:T(8,128)(2,1)S(1)}, u32[]{:S(2)}, u32[]{:S(2)}) %collective-permute-start.8) | collective-permute-done | bytes 524320 | tf_op jit(solution)/shard_map/ppermute | solution.py:458
  42.9 4.8 %collective-permute-done.7.refs_3_ = bf16[4,256,128]{2,1,0:T(8,128)(2,1)S(1)} collective-permute-done((bf16[4,256,128]{2,1,0:T(8,128)(2,1)S(1)}, bf16[4,256,128]{2,1,0:T(8,128)(2,1)S(1)}, u32[]{:S(2)}, u32[]{:S(2)}) %collective-permute-start.7) | collective-permute-done | bytes 262176 | tf_op jit(solution)/shard_map/ppermute | solution.py:458
  47.8 0.6 collective-permute-start.9
  48.3 1.6 %collective-permute-start.13 = (bf16[1024,256]{1,0:T(8,128)(2,1)S(1)}, bf16[1024,256]{1,0:T(8,128)(2,1)S(1)}, u32[]{:S(2)}, u32[]{:S(2)}) collective-permute-start(bf16[1024,256]{1,0:T(8,128)(2,1)S(1)} %get-tuple-element.69), channel_id=1, source_target_pairs={{0,2},{1,3},{2,0},{3,1},{4,6},{5,7},{6,4},{7,5},{8,10},{9,11},{10,... | collective-permute-start | bytes 1572872 | tf_op jit(solution)/shard_map/ppermute | solution.py:455
  49.9 6.7 %attend_others.2 = (bf16[272,512]{1,0:T(8,128)(2,1)S(1)}, bf16[272,512]{1,0:T(8,128)(2,1)S(1)}, bf16[272,512]{1,0:T(8,128)(2,1)S(1)}) custom-call(s32[8]{0:T(128)S(1)} %copy-done.2, s32[16]{0:T(128)S(1)} %copy-done.3, bf16[32,32,2048]{2,1,0:T(8,128)(2,1)} %bitcast.19, bf16[2,32,32,256]{3,2,1,0:T(8,128)(2,1)S(1)} %bitcast.24, ...), custom_call_target="tpu_custom_call" | custom-call | flops 5000000000 | bytes 4194304 | tf_op jit(solution)/shard_map/attend_others/pallas_call | solution.py:308
  56.6 3.6 %collective-permute-start.10 = (bf16[272,512]{1,0:T(8,128)(2,1)S(1)}, bf16[272,512]{1,0:T(8,128)(2,1)S(1)}, u32[]{:S(2)}, u32[]{:S(2)}) collective-permute-start(bf16[272,512]{1,0:T(8,128)(2,1)S(1)} %get-tuple-element.58), channel_id=1, source_target_pairs={{0,12},{1,13},{2,14},{3,15},{4,0},{5,1},{6,2},{7,3},{8,4},{9,5},{1... | collective-permute-start | bytes 835592 | tf_op jit(solution)/shard_map/ppermute | solution.py:458
  60.2 4.3 %attend_own.2 = (f32[2,128,512]{2,1,0:T(8,128)S(1)}, f32[2,8,512]{2,1,0:T(8,128)S(1)}) custom-call(s32[8]{0:T(128)S(1)} %copy-done.2, s32[16]{0:T(128)S(1)} %copy-done.3, bf16[32,32,2048]{2,1,0:T(8,128)(2,1)} %bitcast.20, bf16[2,32,32,256]{3,2,1,0:T(8,128)(2,1)S(1)} %bitcast.25, bf16[32,32,256]{2,1,0:T(8,128)(2,1)S(1)} %bitcast.33, ...), custom_call_target="tpu_custom_call" | custom-call | flops 1000000000 | bytes 4194304 | tf_op jit(solution)/shard_map/attend_own/pallas_call | solution.py:308
  64.5 2.7 %collective-permute-done.10.refs_0_ = bf16[272,512]{1,0:T(8,128)(2,1)S(1)} collective-permute-done((bf16[272,512]{1,0:T(8,128)(2,1)S(1)}, bf16[272,512]{1,0:T(8,128)(2,1)S(1)}, u32[]{:S(2)}, u32[]{:S(2)}) %collective-permute-start.10) | collective-permute-done | bytes 278560 | tf_op jit(solution)/shard_map/ppermute | solution.py:458
  67.2 7.9 %collective-permute-done.11.two_ref = bf16[272,512]{1,0:T(8,128)(2,1)S(1)} collective-permute-done((bf16[272,512]{1,0:T(8,128)(2,1)S(1)}, bf16[272,512]{1,0:T(8,128)(2,1)S(1)}, u32[]{:S(2)}, u32[]{:S(2)}) %collective-permute-start.11) | collective-permute-done | bytes 278560 | tf_op jit(solution)/shard_map/ppermute | solution.py:458
  75.6 6.7 %attend_others.3 = (bf16[272,512]{1,0:T(8,128)(2,1)S(1)}, bf16[272,512]{1,0:T(8,128)(2,1)S(1)}, bf16[272,512]{1,0:T(8,128)(2,1)S(1)}) custom-call(s32[8]{0:T(128)S(1)} %copy-done.2, s32[16]{0:T(128)S(1)} %copy-done.3, bf16[32,32,2048]{2,1,0:T(8,128)(2,1)} %bitcast.21, bf16[2,32,32,256]{3,2,1,0:T(8,128)(2,1)S(1)} %bitcast.26, ...), custom_call_target="tpu_custom_call" | custom-call | flops 5000000000 | bytes 4194304 | tf_op jit(solution)/shard_map/attend_others/pallas_call | solution.py:308
  82.3 3.2 %collective-permute-done.12.refs_1_ = bf16[272,512]{1,0:T(8,128)(2,1)S(1)} collective-permute-done((bf16[272,512]{1,0:T(8,128)(2,1)S(1)}, bf16[272,512]{1,0:T(8,128)(2,1)S(1)}, u32[]{:S(2)}, u32[]{:S(2)}) %collective-permute-start.12) | collective-permute-done | bytes 278560 | tf_op jit(solution)/shard_map/ppermute | solution.py:458
  85.8 0.7 collective-permute-start.19
  86.5 1.4 %collective-permute-start.18 = (bf16[272,512]{1,0:T(8,128)(2,1)S(1)}, bf16[272,512]{1,0:T(8,128)(2,1)S(1)}, u32[]{:S(2)}, u32[]{:S(2)}) collective-permute-start(bf16[272,512]{1,0:T(8,128)(2,1)S(1)} %get-tuple-element.88), channel_id=1, source_target_pairs={{0,4},{1,5},{2,6},{3,7},{4,8},{5,9},{6,10},{7,11},{8,12},{9,13},{1... | collective-permute-start | bytes 835592 | tf_op jit(solution)/shard_map/ppermute | solution.py:458
  87.9 11.2 %collective-permute-done.19.two_ref = bf16[272,512]{1,0:T(8,128)(2,1)S(1)} collective-permute-done((bf16[272,512]{1,0:T(8,128)(2,1)S(1)}, bf16[272,512]{1,0:T(8,128)(2,1)S(1)}, u32[]{:S(2)}, u32[]{:S(2)}) %collective-permute-start.19) | collective-permute-done | bytes 278560 | tf_op jit(solution)/shard_map/ppermute | solution.py:458
  99.6 4.3 %attend_own.3 = (f32[2,128,512]{2,1,0:T(8,128)S(1)}, f32[2,8,512]{2,1,0:T(8,128)S(1)}) custom-call(s32[8]{0:T(128)S(1)} %copy-done.2, s32[16]{0:T(128)S(1)} %copy-done.3, bf16[32,32,2048]{2,1,0:T(8,128)(2,1)} %bitcast.22, bf16[2,32,32,256]{3,2,1,0:T(8,128)(2,1)S(1)} %bitcast.27, bf16[32,32,256]{2,1,0:T(8,128)(2,1)S(1)} %bitcast.29, ...), custom_call_target="tpu_custom_call" | custom-call | flops 1000000000 | bytes 4194304 | tf_op jit(solution)/shard_map/attend_own/pallas_call | solution.py:308
  103.9 2.8 %collective-permute-start.16 = (bf16[320,128]{1,0:T(8,128)(2,1)S(1)}, bf16[320,128]{1,0:T(8,128)(2,1)S(1)}, u32[]{:S(2)}, u32[]{:S(2)}) collective-permute-start(bf16[320,128]{1,0:T(8,128)(2,1)S(1)} %get-tuple-element.80), channel_id=1, source_target_pairs={{0,2},{1,3},{2,0},{3,1},{4,6},{5,7},{6,4},{7,5},{8,10},{9,11},{10,... | collective-permute-start | bytes 245768 | tf_op jit(solution)/shard_map/ppermute | solution.py:455
  107.3 1.9 %collective-permute-start.22 = (bf16[320,128]{1,0:T(8,128)(2,1)S(1)}, bf16[320,128]{1,0:T(8,128)(2,1)S(1)}, u32[]{:S(2)}, u32[]{:S(2)}) collective-permute-start(bf16[320,128]{1,0:T(8,128)(2,1)S(1)} %get-tuple-element.92), channel_id=1, source_target_pairs={{0,2},{1,3},{2,0},{3,1},{4,6},{5,7},{6,4},{7,5},{8,10},{9,11},{10,... | collective-permute-start | bytes 245768 | tf_op jit(solution)/shard_map/ppermute | solution.py:455
  109.3 0.5 collective-permute-done.16.refs_2_
  109.8 1.4 %collective-permute-done.17.refs_3_ = bf16[320,128]{1,0:T(8,128)(2,1)S(1)} collective-permute-done((bf16[320,128]{1,0:T(8,128)(2,1)S(1)}, bf16[320,128]{1,0:T(8,128)(2,1)S(1)}, u32[]{:S(2)}, u32[]{:S(2)}) %collective-permute-start.17) | collective-permute-done | bytes 81952 | tf_op jit(solution)/shard_map/ppermute | solution.py:455
  111.3 2.3 %collective-permute-done.22.refs_6_ = bf16[320,128]{1,0:T(8,128)(2,1)S(1)} collective-permute-done((bf16[320,128]{1,0:T(8,128)(2,1)S(1)}, bf16[320,128]{1,0:T(8,128)(2,1)S(1)}, u32[]{:S(2)}, u32[]{:S(2)}) %collective-permute-start.22) | collective-permute-done | bytes 81952 | tf_op jit(solution)/shard_map/ppermute | solution.py:455
  113.6 1.2 %collective-permute-done.23.refs_7_ = bf16[320,128]{1,0:T(8,128)(2,1)S(1)} collective-permute-done((bf16[320,128]{1,0:T(8,128)(2,1)S(1)}, bf16[320,128]{1,0:T(8,128)(2,1)S(1)}, u32[]{:S(2)}, u32[]{:S(2)}) %collective-permute-start.23) | collective-permute-done | bytes 81952 | tf_op jit(solution)/shard_map/ppermute | solution.py:455
  114.8 1.5 %emit.1 = (bf16[8,4,8192]{2,1,0:T(4,128)(2,1)}, bf16[8,4,8192]{2,1,0:T(4,128)(2,1)}) custom-call(bf16[320,128]{1,0:T(8,128)(2,1)S(1)} %get-tuple-element.78.refs_0_, bf16[320,128]{1,0:T(8,128)(2,1)S(1)} %collective-permute-done.15.refs_1_, bf16[320,128]{1,0:T(8,128)(2,1)S(1)} %collective-permute-done.16.refs_2_, ...), custom_call_target="tpu_custom_call" | custom-call | flops 1048576 | bytes 2097152 | tf_op jit(solution)/shard_map/emit/pallas_call | solution.py:437
  (43 shorter events, 3.0 us)
Async XLA Ops:
  2.9 6.4 %collective-permute-start = (bf16[2,320,128]{2,1,0:T(8,128)(2,1)}, bf16[2,320,128]{2,1,0:T(8,128)(2,1)S(1)}, u32[]{:S(2)}, u32[]{:S(2)}) collective-permute-start(bf16[2,320,128]{2,1,0:T(8,128)(2,1)} %get-tuple-element.50), channel_id=1, source_target_pairs={{0,1},{1,0},{2,3},{3,2},{4,5},{5,4},{6,7},{7,6},{8,9},{9,8},{10,11... | collective-permute-start | bytes 491528 | tf_op jit(solution)/shard_map/ppermute | solution.py:455
  3.4 7.9 %collective-permute-start.1 = (bf16[2,320,128]{2,1,0:T(8,128)(2,1)}, bf16[2,320,128]{2,1,0:T(8,128)(2,1)S(1)}, u32[]{:S(2)}, u32[]{:S(2)}) collective-permute-start(bf16[2,320,128]{2,1,0:T(8,128)(2,1)} %get-tuple-element.51), channel_id=1, source_target_pairs={{0,2},{1,3},{2,0},{3,1},{4,6},{5,7},{6,4},{7,5},{8,10},{9,11},{10,... | collective-permute-start | bytes 491528 | tf_op jit(solution)/shard_map/ppermute | solution.py:455
  6.0 8.3 %collective-permute-start.2 = (bf16[2,320,128]{2,1,0:T(8,128)(2,1)}, bf16[2,320,128]{2,1,0:T(8,128)(2,1)S(1)}, u32[]{:S(2)}, u32[]{:S(2)}) collective-permute-start(bf16[2,320,128]{2,1,0:T(8,128)(2,1)} %get-tuple-element.52), channel_id=1, source_target_pairs={{0,3},{1,2},{2,1},{3,0},{4,7},{5,6},{6,5},{7,4},{8,11},{9,10},{10,... | collective-permute-start | bytes 491528 | tf_op jit(solution)/shard_map/ppermute | solution.py:455
  6.1 2.2 %copy-start = (bf16[32,1,32,2048]{3,2,1,0:T(8,128)(2,1)S(1)}, bf16[32,1,32,2048]{3,2,1,0:T(8,128)(2,1)}, u32[]{:S(2)}) copy-start(bf16[32,1,32,2048]{3,2,1,0:T(8,128)(2,1)} %param.5) | copy-start | bytes 12582916
  8.3 1.0 copy-start.1
  8.3 41.7 %copy-start.2 = (s32[8]{0:T(128)S(1)}, s32[8]{0:T(128)}, u32[]{:S(2)}) copy-start(s32[8]{0:T(128)} %counts_ref.7) | copy-start | bytes 100
  8.3 41.7 %copy-start.3 = (s32[16]{0:T(128)S(1)}, s32[16]{0:T(128)}, u32[]{:S(2)}) copy-start(s32[16]{0:T(128)} %slots_ref.7) | copy-start | bytes 196
  14.2 34.1 %collective-permute-start.3 = (bf16[2,1024,256]{2,1,0:T(8,128)(2,1)S(1)}, bf16[2,1024,256]{2,1,0:T(8,128)(2,1)S(1)}, u32[]{:S(2)}, u32[]{:S(2)}) collective-permute-start(bf16[2,1024,256]{2,1,0:T(8,128)(2,1)S(1)} %get-tuple-element.53), channel_id=1, source_target_pairs={{0,1},{1,0},{2,3},{3,2},{4,5},{5,4},{6,7},{7,6},{8,9},{9,8},{10,11... | collective-permute-start | bytes 3145736 | tf_op jit(solution)/shard_map/ppermute | solution.py:455
  14.5 16.2 %collective-permute-start.6 = (bf16[2,4,256,128]{3,2,1,0:T(8,128)(2,1)S(1)}, bf16[2,4,256,128]{3,2,1,0:T(8,128)(2,1)S(1)}, u32[]{:S(2)}, u32[]{:S(2)}) collective-permute-start(bf16[2,4,256,128]{3,2,1,0:T(8,128)(2,1)S(1)} %pad_maximum_fusion), channel_id=1, source_target_pairs={{0,12},{1,13},{2,14},{3,15},{4,0},{5,1},{6,2},{7,3},{8,4},{9,5},{1... | collective-permute-start | bytes 1572872 | tf_op jit(solution)/shard_map/ppermute | solution.py:458
  18.4 24.5 %collective-permute-start.8 = (bf16[2,4,256,128]{3,2,1,0:T(8,128)(2,1)S(1)}, bf16[2,4,256,128]{3,2,1,0:T(8,128)(2,1)S(1)}, u32[]{:S(2)}, u32[]{:S(2)}) collective-permute-start(bf16[2,4,256,128]{3,2,1,0:T(8,128)(2,1)S(1)} %pad_maximum_fusion), channel_id=1, source_target_pairs={{0,4},{1,5},{2,6},{3,7},{4,8},{5,9},{6,10},{7,11},{8,12},{9,13},{1... | collective-permute-start | bytes 1572872 | tf_op jit(solution)/shard_map/ppermute | solution.py:458
  18.4 29.9 %collective-permute-start.4 = (bf16[1024,256]{1,0:T(8,128)(2,1)S(1)}, bf16[1024,256]{1,0:T(8,128)(2,1)S(1)}, u32[]{:S(2)}, u32[]{:S(2)}) collective-permute-start(bf16[1024,256]{1,0:T(8,128)(2,1)S(1)} %get-tuple-element.54), channel_id=1, source_target_pairs={{0,2},{1,3},{2,0},{3,1},{4,6},{5,7},{6,4},{7,5},{8,10},{9,11},{10,... | collective-permute-start | bytes 1572872 | tf_op jit(solution)/shard_map/ppermute | solution.py:455
  19.9 28.4 %collective-permute-start.5 = (bf16[1024,256]{1,0:T(8,128)(2,1)S(1)}, bf16[1024,256]{1,0:T(8,128)(2,1)S(1)}, u32[]{:S(2)}, u32[]{:S(2)}) collective-permute-start(bf16[1024,256]{1,0:T(8,128)(2,1)S(1)} %get-tuple-element.55), channel_id=1, source_target_pairs={{0,3},{1,2},{2,1},{3,0},{4,7},{5,6},{6,5},{7,4},{8,11},{9,10},{10,... | collective-permute-start | bytes 1572872 | tf_op jit(solution)/shard_map/ppermute | solution.py:455
  30.8 17.0 %collective-permute-start.7 = (bf16[4,256,128]{2,1,0:T(8,128)(2,1)S(1)}, bf16[4,256,128]{2,1,0:T(8,128)(2,1)S(1)}, u32[]{:S(2)}, u32[]{:S(2)}) collective-permute-start(bf16[4,256,128]{2,1,0:T(8,128)(2,1)S(1)} %get-tuple-element.97.refs_2_), channel_id=1, source_target_pairs={{0,12},{1,13},{2,14},{3,15},{4,0},{5,1},{6,2},{7,3},{8,4},{9,5},{1... | collective-permute-start | bytes 786440 | tf_op jit(solution)/shard_map/ppermute | solution.py:458
  47.8 12.5 %collective-permute-start.9 = (bf16[4,256,128]{2,1,0:T(8,128)(2,1)S(1)}, bf16[4,256,128]{2,1,0:T(8,128)(2,1)S(1)}, u32[]{:S(2)}, u32[]{:S(2)}) collective-permute-start(bf16[4,256,128]{2,1,0:T(8,128)(2,1)S(1)} %get-tuple-element.59.refs_4_), channel_id=1, source_target_pairs={{0,4},{1,5},{2,6},{3,7},{4,8},{5,9},{6,10},{7,11},{8,12},{9,13},{1... | collective-permute-start | bytes 786440 | tf_op jit(solution)/shard_map/ppermute | solution.py:458
  48.3 27.3 %collective-permute-start.13 = (bf16[1024,256]{1,0:T(8,128)(2,1)S(1)}, bf16[1024,256]{1,0:T(8,128)(2,1)S(1)}, u32[]{:S(2)}, u32[]{:S(2)}) collective-permute-start(bf16[1024,256]{1,0:T(8,128)(2,1)S(1)} %get-tuple-element.69), channel_id=1, source_target_pairs={{0,2},{1,3},{2,0},{3,1},{4,6},{5,7},{6,4},{7,5},{8,10},{9,11},{10,... | collective-permute-start | bytes 1572872 | tf_op jit(solution)/shard_map/ppermute | solution.py:455
  49.9 25.7 %collective-permute-start.14 = (bf16[1024,256]{1,0:T(8,128)(2,1)S(1)}, bf16[1024,256]{1,0:T(8,128)(2,1)S(1)}, u32[]{:S(2)}, u32[]{:S(2)}) collective-permute-start(bf16[1024,256]{1,0:T(8,128)(2,1)S(1)} %get-tuple-element.70), channel_id=1, source_target_pairs={{0,3},{1,2},{2,1},{3,0},{4,7},{5,6},{6,5},{7,4},{8,11},{9,10},{10,... | collective-permute-start | bytes 1572872 | tf_op jit(solution)/shard_map/ppermute | solution.py:455
  56.6 10.6 %collective-permute-start.10 = (bf16[272,512]{1,0:T(8,128)(2,1)S(1)}, bf16[272,512]{1,0:T(8,128)(2,1)S(1)}, u32[]{:S(2)}, u32[]{:S(2)}) collective-permute-start(bf16[272,512]{1,0:T(8,128)(2,1)S(1)} %get-tuple-element.58), channel_id=1, source_target_pairs={{0,12},{1,13},{2,14},{3,15},{4,0},{5,1},{6,2},{7,3},{8,4},{9,5},{1... | collective-permute-start | bytes 835592 | tf_op jit(solution)/shard_map/ppermute | solution.py:458
  60.2 14.9 %collective-permute-start.11 = (bf16[272,512]{1,0:T(8,128)(2,1)S(1)}, bf16[272,512]{1,0:T(8,128)(2,1)S(1)}, u32[]{:S(2)}, u32[]{:S(2)}) collective-permute-start(bf16[272,512]{1,0:T(8,128)(2,1)S(1)} %get-tuple-element.57), channel_id=1, source_target_pairs={{0,4},{1,5},{2,6},{3,7},{4,8},{5,9},{6,10},{7,11},{8,12},{9,13},{1... | collective-permute-start | bytes 835592 | tf_op jit(solution)/shard_map/ppermute | solution.py:458
  75.3 10.2 %collective-permute-start.12 = (bf16[272,512]{1,0:T(8,128)(2,1)S(1)}, bf16[272,512]{1,0:T(8,128)(2,1)S(1)}, u32[]{:S(2)}, u32[]{:S(2)}) collective-permute-start(bf16[272,512]{1,0:T(8,128)(2,1)S(1)} %merge.2), channel_id=1, source_target_pairs={{0,4},{1,5},{2,6},{3,7},{4,8},{5,9},{6,10},{7,11},{8,12},{9,13},{1... | collective-permute-start | bytes 835592 | tf_op jit(solution)/shard_map/ppermute | solution.py:458
  85.8 13.2 %collective-permute-start.19 = (bf16[272,512]{1,0:T(8,128)(2,1)S(1)}, bf16[272,512]{1,0:T(8,128)(2,1)S(1)}, u32[]{:S(2)}, u32[]{:S(2)}) collective-permute-start(bf16[272,512]{1,0:T(8,128)(2,1)S(1)} %get-tuple-element.89), channel_id=1, source_target_pairs={{0,12},{1,13},{2,14},{3,15},{4,0},{5,1},{6,2},{7,3},{8,4},{9,5},{1... | collective-permute-start | bytes 835592 | tf_op jit(solution)/shard_map/ppermute | solution.py:458
  86.5 20.4 %collective-permute-start.18 = (bf16[272,512]{1,0:T(8,128)(2,1)S(1)}, bf16[272,512]{1,0:T(8,128)(2,1)S(1)}, u32[]{:S(2)}, u32[]{:S(2)}) collective-permute-start(bf16[272,512]{1,0:T(8,128)(2,1)S(1)} %get-tuple-element.88), channel_id=1, source_target_pairs={{0,4},{1,5},{2,6},{3,7},{4,8},{5,9},{6,10},{7,11},{8,12},{9,13},{1... | collective-permute-start | bytes 835592 | tf_op jit(solution)/shard_map/ppermute | solution.py:458
  99.2 7.7 %collective-permute-start.20 = (bf16[272,512]{1,0:T(8,128)(2,1)S(1)}, bf16[272,512]{1,0:T(8,128)(2,1)S(1)}, u32[]{:S(2)}, u32[]{:S(2)}) collective-permute-start(bf16[272,512]{1,0:T(8,128)(2,1)S(1)} %merge.3), channel_id=1, source_target_pairs={{0,12},{1,13},{2,14},{3,15},{4,0},{5,1},{6,2},{7,3},{8,4},{9,5},{1... | collective-permute-start | bytes 835592 | tf_op jit(solution)/shard_map/ppermute | solution.py:458
  99.5 9.7 %collective-permute-start.15 = (bf16[320,128]{1,0:T(8,128)(2,1)S(1)}, bf16[320,128]{1,0:T(8,128)(2,1)S(1)}, u32[]{:S(2)}, u32[]{:S(2)}) collective-permute-start(bf16[320,128]{1,0:T(8,128)(2,1)S(1)} %get-tuple-element.79), channel_id=1, source_target_pairs={{0,1},{1,0},{2,3},{3,2},{4,5},{5,4},{6,7},{7,6},{8,9},{9,8},{10,11... | collective-permute-start | bytes 245768 | tf_op jit(solution)/shard_map/ppermute | solution.py:455
  103.9 6.0 %collective-permute-start.16 = (bf16[320,128]{1,0:T(8,128)(2,1)S(1)}, bf16[320,128]{1,0:T(8,128)(2,1)S(1)}, u32[]{:S(2)}, u32[]{:S(2)}) collective-permute-start(bf16[320,128]{1,0:T(8,128)(2,1)S(1)} %get-tuple-element.80), channel_id=1, source_target_pairs={{0,2},{1,3},{2,0},{3,1},{4,6},{5,7},{6,4},{7,5},{8,10},{9,11},{10,... | collective-permute-start | bytes 245768 | tf_op jit(solution)/shard_map/ppermute | solution.py:455
  106.7 4.6 %collective-permute-start.17 = (bf16[320,128]{1,0:T(8,128)(2,1)S(1)}, bf16[320,128]{1,0:T(8,128)(2,1)S(1)}, u32[]{:S(2)}, u32[]{:S(2)}) collective-permute-start(bf16[320,128]{1,0:T(8,128)(2,1)S(1)} %get-tuple-element.81), channel_id=1, source_target_pairs={{0,3},{1,2},{2,1},{3,0},{4,7},{5,6},{6,5},{7,4},{8,11},{9,10},{10,... | collective-permute-start | bytes 245768 | tf_op jit(solution)/shard_map/ppermute | solution.py:455
  107.2 4.1 %collective-permute-start.21 = (bf16[320,128]{1,0:T(8,128)(2,1)S(1)}, bf16[320,128]{1,0:T(8,128)(2,1)S(1)}, u32[]{:S(2)}, u32[]{:S(2)}) collective-permute-start(bf16[320,128]{1,0:T(8,128)(2,1)S(1)} %get-tuple-element.91), channel_id=1, source_target_pairs={{0,1},{1,0},{2,3},{3,2},{4,5},{5,4},{6,7},{7,6},{8,9},{9,8},{10,11... | collective-permute-start | bytes 245768 | tf_op jit(solution)/shard_map/ppermute | solution.py:455
  107.3 6.3 %collective-permute-start.22 = (bf16[320,128]{1,0:T(8,128)(2,1)S(1)}, bf16[320,128]{1,0:T(8,128)(2,1)S(1)}, u32[]{:S(2)}, u32[]{:S(2)}) collective-permute-start(bf16[320,128]{1,0:T(8,128)(2,1)S(1)} %get-tuple-element.92), channel_id=1, source_target_pairs={{0,2},{1,3},{2,0},{3,1},{4,6},{5,7},{6,4},{7,5},{8,10},{9,11},{10,... | collective-permute-start | bytes 245768 | tf_op jit(solution)/shard_map/ppermute | solution.py:455
  109.2 5.5 %collective-permute-start.23 = (bf16[320,128]{1,0:T(8,128)(2,1)S(1)}, bf16[320,128]{1,0:T(8,128)(2,1)S(1)}, u32[]{:S(2)}, u32[]{:S(2)}) collective-permute-start(bf16[320,128]{1,0:T(8,128)(2,1)S(1)} %get-tuple-element.93), channel_id=1, source_target_pairs={{0,3},{1,2},{2,1},{3,0},{4,7},{5,6},{6,5},{7,4},{8,11},{9,10},{10,... | collective-permute-start | bytes 245768 | tf_op jit(solution)/shard_map/ppermute | solution.py:455

commit v9 on v8

--- a/solution.py
+++ b/solution.py
@@ -204,36 +204,42 @@
 
     def one_pass(n, pair, low, high, tiles):
         tokens = tiles * TILE
-        query = asked[n, pl.ds(2 * pair, 2)].reshape(2 * size, HD)
         row = pl.multiple_of(low * BLK, BLK)
-        before = state[pair, 0:1] if steps else None
-        top = jnp.broadcast_to(before, (8, 2 * size)) if steps else None
-        s = scores_of(flat[pl.ds(row, tokens), 0:HD], query)
-        for t in range(tiles):
-            tile = s[t * TILE:(t + 1) * TILE]
-            if t == tiles - 1:
-                token = lax.broadcasted_iota(jnp.int32, tile.shape, 0)
-                tile = jnp.where(token < (high - low - t * TILE_BLOCKS) * BLK, tile, NEG)
-            scores[t * TILE:(t + 1) * TILE] = tile
-            part = jnp.max(tile.reshape(TILE // 8, 8, 2 * size), axis=0)
-            top = part if top is None else jnp.maximum(top, part)
-        m = jnp.max(top, axis=0, keepdims=True)
-        shift = m * EXP_SCALE
-        total = None
-        for b in range(tokens // BLK):
-            p = jnp.exp2(scores[b * BLK:(b + 1) * BLK] * EXP_SCALE - shift)
-            weights[b * BLK:(b + 1) * BLK] = p.astype(BF16)
-            part = jnp.sum(p.reshape(BLK // 8, 8, 2 * size), axis=0)
-            total = part if total is None else total + part
-        l = jnp.sum(total, axis=0, keepdims=True)
-        out = values_by(flat[pl.ds(row, tokens), HD:2 * HD], weights[0:tokens])
-        if steps:
-            alpha = jnp.exp2(before * EXP_SCALE - shift)
-            l = l + alpha * state[pair, 1:2]
-            out = out + alpha * acc[pair]
-        state[pair, 0:1] = m
-        state[pair, 1:2] = l
-        acc[pair] = out
+        halves = [slice(half * size, (half + 1) * size) for half in range(2)]
+        tops = []
+        for half, cols in enumerate(halves):
+            top = None
+            s = scores_of(flat[pl.ds(row, tokens), 0:HD], asked[n, 2 * pair + half])
+            for t in range(tiles):
+                tile = s[t * TILE:(t + 1) * TILE]
+                if t == tiles - 1:
+                    token = lax.broadcasted_iota(jnp.int32, tile.shape, 0)
+                    tile = jnp.where(token < (high - low - t * TILE_BLOCKS) * BLK, tile, NEG)
+                scores[t * TILE:(t + 1) * TILE, cols] = tile
+                part = jnp.max(tile.reshape(TILE // 8, 8, size), axis=0)
+                top = part if top is None else jnp.maximum(top, part)
+            tops.append(top)
+        for half, cols in enumerate(halves):
+            m = jnp.max(tops[half], axis=0, keepdims=True)
+            if steps:
+                before = state[pair, 0:1, cols]
+                m = jnp.maximum(m, before)
+            shift = m * EXP_SCALE
+            total = None
+            for b in range(tokens // BLK):
+                p = jnp.exp2(scores[b * BLK:(b + 1) * BLK, cols] * EXP_SCALE - shift)
+                weights[b * BLK:(b + 1) * BLK, cols] = p.astype(BF16)
+                part = jnp.sum(p.reshape(BLK // 8, 8, size), axis=0)
+                total = part if total is None else total + part
+            l = jnp.sum(total, axis=0, keepdims=True)
+            out = values_by(flat[pl.ds(row, tokens), HD:2 * HD], weights[0:tokens, cols])
+            if steps:
+                alpha = jnp.exp2(before * EXP_SCALE - shift)
+                l = l + alpha * state[pair, 1:2, cols]
+                out = out + alpha * acc[pair, :, cols]
+            state[pair, 0:1, cols] = m
+            state[pair, 1:2, cols] = l
+            acc[pair, :, cols] = out
 
     def chunk(n, _):
         offset = jnp.int32(0) if steps else offset_of(n)
@@ -322,7 +328,7 @@
             pltpu.SemaphoreType.DMA((2 * QUAD + 2 * count + 8,)),
         ],
         compiler_params=params(48),
-        cost_estimate=cost(10**9 if steps else 5 * 10**9, 4 << 20),
+        cost_estimate=cost(5 * 10**8 if steps else (10**10 if h else 2 * 10**9), 4 << 20),
         name="attend_own" if steps else "attend_others",
     )(counts, slots, kv3, *arrived, *queries)
 
@@ -489,31 +495,36 @@
             sources = tied(sources, arrived[-1], first_hop, near)
         arrived.append([across(block, 2 + i) for i, block in enumerate(sources)])
 
-    def others(h, gate):
-        received = arrived[h] if gate is None else tied(arrived[h], gate, asked[h])
-        blocks = [near] + [block.reshape(-1, BLK, 2 * HD) for block in received]
-        offsets = tuple(sorted(asked[h]))
-        partial = attend(
-            h, offsets, 0, prompt_blocks, slot_prompt, kv3, blocks, [asked[h][o] for o in offsets]
-        )
-        return blocks, dict(zip(offsets, partial))
-
     def chains(h):
         far_right = (quads - 1 + (1 - h % 2)) // 2
         pair = ((1, far_right), (-1, quads - 1 - far_right))
         return [c for c in sorted(pair, key=lambda x: x[1]) if c[1]]
 
-    def sent(h, parts):
-        return [along(parts[shift * hops % quads], shift) for shift, hops in chains(h)]
-
-    def summed(h, parts, moved):
-        back, turned = [], parts[min(parts)] if parts else near
-        for (shift, hops), block in zip(chains(h), moved):
+    def others(h, gate):
+        received = arrived[h] if gate is None else tied(arrived[h], gate, asked[h])
+        blocks = [near] + [block.reshape(-1, BLK, 2 * HD) for block in received]
+
+        def some(offsets, inputs):
+            partial = attend(h, offsets, 0, prompt_blocks, slot_prompt, kv3, blocks, inputs)
+            return dict(zip(offsets, partial))
+
+        shift, hops = chains(h)[-1]
+        lead = shift * hops % quads
+        parts = some((lead,), [asked[h][lead]])
+        ahead = along(parts[lead], shift)
+        rest = tuple(o for o in sorted(asked[h]) if o != lead)
+        if rest:
+            parts.update(some(rest, tied([asked[h][o] for o in rest], parts[lead])))
+        return blocks, parts, ahead
+
+    def summed(h, parts, ahead):
+        back, turned = [], ahead
+        for shift, hops in chains(h)[::-1]:
+            block = ahead if not back else along(parts[shift * hops % quads], shift)
             for s in range(hops - 1, 0, -1):
-                if h + 1 < HPD and s == hops - 1:
-                    block = tied(block, moved)
                 block = merge(parts[shift * s % quads], block)
-                turned = block if s == hops - 1 else turned
+                if s == hops - 1 and not back:
+                    turned = block
                 block = along(block, shift)
             back.append(block)
         return back, turned
@@ -524,16 +535,13 @@
 
     final, gate, before = [], None, None
     for h in range(HPD):
-        blocks, parts = others(h, gate)
-        ready = parts
+        blocks, parts, ahead = others(h, gate)
         if before is not None:
             mine, back = before
             final.append(finished(h - 1, mine, tied(back, parts)))
-            ready = tied(parts, final[-1][0])
-        moved = sent(h, ready)
-        late = tied(msgs, parts, asked[h + 1:h + 2])
+        late = tied(msgs, parts, asked[h + 1:h + 2], final[-1:])
         mine = attend(h, (0,), steps, prompt_blocks, slot_prompt, kv3, blocks, late)
-        back, turned = summed(h, parts, moved)
+        back, turned = summed(h, parts, ahead)
         before = mine, back
         gate = mine[0], turned
     final.append(finished(HPD - 1, *before))

time: 116 us -> 104 us (0.90)
  waiting for transfers between devices: 58.8 us -> 38.4 us
  starting transfers between devices: 26.7 us -> 32.1 us
  Pallas kernels: 27.5 us -> 30.4 us
    ppermute x10, waiting for transfers between devices: 48.3 us -> 16.3 us  [along(): lax.ppermute(array, 'sample', [(i, (i + shift * QUAD) % nsample) for i in...]
    ppermute x14, waiting for transfers between devices: 10.4 us -> 22.1 us  [across(): return lax.ppermute(array, 'sample', [(i, i ^ k) for i in range(nsample)])]
    ppermute x10, starting transfers between devices: 15.1 us -> 21.2 us  [along(): lax.ppermute(array, 'sample', [(i, (i + shift * QUAD) % nsample) for i in...]
    pallas_call x4 -> x6, Pallas kernels: 21.9 us -> 24.7 us  [attend(): pl.pallas_call(functools.partial(attend_kernel, h, offsets, steps, max_ti...]
  transfers between devices with their start and end apart: 24 -> 24, of which waited for: 13 -> 12; matrix products, arithmetic and copies ran while one was open for 0% -> 0% of each run, Pallas kernels for 20% -> 25%
where the time goes in v9:
time: 104 us
  waiting for transfers between devices  38.4 us (37%)
  starting transfers between devices  32.1 us (31%)
  Pallas kernels  30.4 us (29%)
  local copies, waits for them, and re-layouts  2.31 us (2%)
    pallas_call x6, Pallas kernels, attend(): pl.pallas_call(functools.partial(attend_kernel, h, offsets, steps, max_ti...  24.7 us
    ppermute x14, waiting for transfers between devices, across(): return lax.ppermute(array, 'sample', [(i, i ^ k) for i in range(nsample)])  22.1 us
    ppermute x10, starting transfers between devices, along(): lax.ppermute(array, 'sample', [(i, (i + shift * QUAD) % nsample) for i in...  21.2 us
    ppermute x10, waiting for transfers between devices, along(): lax.ppermute(array, 'sample', [(i, (i + shift * QUAD) % nsample) for i in...  16.3 us
    ppermute x14, starting transfers between devices, across(): return lax.ppermute(array, 'sample', [(i, i ^ k) for i in range(nsample)])  10.9 us
    pallas_call x1, Pallas kernels, pack_queries(): pl.pallas_call(pack_queries_kernel, out_shape=[jax.ShapeDtypeStruct((HPD,...  2.25 us
    unnamed x8, local copies, waits for them, and re-layouts  2.2 us
  transfers between devices with their start and end apart: 24, of which 12 were waited for; matrix products, arithmetic and copies ran while one was open for 0% of the time, Pallas kernels for 25%

profile of v9, /device:TPU:0, one launch (start us, length us, event | category | flops | bytes accessed | tf_op | source)
XLA Modules:
  0.0 104.1 jit_solution(9558290256215951878)
XLA Ops:
  0.6 2.2 %pack_queries.1 = (bf16[2,320,128]{2,1,0:T(8,128)(2,1)}, bf16[2,320,128]{2,1,0:T(8,128)(2,1)}, bf16[2,320,128]{2,1,0:T(8,128)(2,1)}, bf16[2,320,128]{2,1,0:T(8,128)(2,1)}) custom-call(bf16[8,4,8192]{2,1,0:T(4,128)(2,1)} %q_hbm.1, bf16[8,4,2048]{2,1,0:T(4,128)(2,1)} %new_hbm.1), custom_call_target="tpu_custom_call" | custom-call | bytes 2097152 | tf_op jit(solution)/shard_map/pack_queries/pallas_call | solution.py:72
  2.9 3.0 %collective-permute-start.1 = (bf16[2,320,128]{2,1,0:T(8,128)(2,1)}, bf16[2,320,128]{2,1,0:T(8,128)(2,1)S(1)}, u32[]{:S(2)}, u32[]{:S(2)}) collective-permute-start(bf16[2,320,128]{2,1,0:T(8,128)(2,1)} %get-tuple-element.50), channel_id=1, source_target_pairs={{0,2},{1,3},{2,0},{3,1},{4,6},{5,7},{6,4},{7,5},{8,10},{9,11},{10,... | collective-permute-start | bytes 491528 | tf_op jit(solution)/shard_map/ppermute | solution.py:461
  6.1 2.2 %copy-done = bf16[32,1,32,2048]{3,2,1,0:T(8,128)(2,1)S(1)} copy-done((bf16[32,1,32,2048]{3,2,1,0:T(8,128)(2,1)S(1)}, bf16[32,1,32,2048]{3,2,1,0:T(8,128)(2,1)}, u32[]{:S(2)}) %copy-start) | copy-done | bytes 4194328
  8.3 1.0 pack_kv.1
  9.3 1.8 %collective-permute-done.1.refs_4_ = bf16[2,320,128]{2,1,0:T(8,128)(2,1)S(1)} collective-permute-done((bf16[2,320,128]{2,1,0:T(8,128)(2,1)}, bf16[2,320,128]{2,1,0:T(8,128)(2,1)S(1)}, u32[]{:S(2)}, u32[]{:S(2)}) %collective-permute-start.1) | collective-permute-done | bytes 163872 | tf_op jit(solution)/shard_map/ppermute | solution.py:461
  11.2 2.0 %collective-permute-done.2.refs_5_ = bf16[2,320,128]{2,1,0:T(8,128)(2,1)S(1)} collective-permute-done((bf16[2,320,128]{2,1,0:T(8,128)(2,1)}, bf16[2,320,128]{2,1,0:T(8,128)(2,1)S(1)}, u32[]{:S(2)}, u32[]{:S(2)}) %collective-permute-start.2) | collective-permute-done | bytes 163872 | tf_op jit(solution)/shard_map/ppermute | solution.py:461
  13.8 3.9 %collective-permute-start.6 = (bf16[2,4,256,128]{3,2,1,0:T(8,128)(2,1)S(1)}, bf16[2,4,256,128]{3,2,1,0:T(8,128)(2,1)S(1)}, u32[]{:S(2)}, u32[]{:S(2)}) collective-permute-start(bf16[2,4,256,128]{3,2,1,0:T(8,128)(2,1)S(1)} %pad_maximum_fusion), channel_id=1, source_target_pairs={{0,12},{1,13},{2,14},{3,15},{4,0},{5,1},{6,2},{7,3},{8,4},{9,5},{1... | collective-permute-start | bytes 1572872 | tf_op jit(solution)/shard_map/ppermute | solution.py:464
  17.7 1.5 %collective-permute-start.4 = (bf16[1024,256]{1,0:T(8,128)(2,1)S(1)}, bf16[1024,256]{1,0:T(8,128)(2,1)S(1)}, u32[]{:S(2)}, u32[]{:S(2)}) collective-permute-start(bf16[1024,256]{1,0:T(8,128)(2,1)S(1)} %get-tuple-element.53), channel_id=1, source_target_pairs={{0,2},{1,3},{2,0},{3,1},{4,6},{5,7},{6,4},{7,5},{8,10},{9,11},{10,... | collective-permute-start | bytes 1572872 | tf_op jit(solution)/shard_map/ppermute | solution.py:461
  19.3 10.8 %collective-permute-done.6 = bf16[2,4,256,128]{3,2,1,0:T(8,128)(2,1)S(1)} collective-permute-done((bf16[2,4,256,128]{3,2,1,0:T(8,128)(2,1)S(1)}, bf16[2,4,256,128]{3,2,1,0:T(8,128)(2,1)S(1)}, u32[]{:S(2)}, u32[]{:S(2)}) %collective-permute-start.6) | collective-permute-done | bytes 524320 | tf_op jit(solution)/shard_map/ppermute | solution.py:464
  30.1 4.3 %collective-permute-start.8 = (bf16[4,256,128]{2,1,0:T(8,128)(2,1)S(1)}, bf16[4,256,128]{2,1,0:T(8,128)(2,1)S(1)}, u32[]{:S(2)}, u32[]{:S(2)}) collective-permute-start(bf16[4,256,128]{2,1,0:T(8,128)(2,1)S(1)} %get-tuple-element.55.refs_2_), channel_id=1, source_target_pairs={{0,12},{1,13},{2,14},{3,15},{4,0},{5,1},{6,2},{7,3},{8,4},{9,5},{1... | collective-permute-start | bytes 786440 | tf_op jit(solution)/shard_map/ppermute | solution.py:464
  34.5 7.1 %collective-permute-done.5 = bf16[1024,256]{1,0:T(8,128)(2,1)S(1)} collective-permute-done((bf16[1024,256]{1,0:T(8,128)(2,1)S(1)}, bf16[1024,256]{1,0:T(8,128)(2,1)S(1)}, u32[]{:S(2)}, u32[]{:S(2)}) %collective-permute-start.5) | collective-permute-done | bytes 524320 | tf_op jit(solution)/shard_map/ppermute | solution.py:461
  42.3 1.5 %collective-permute-start.13 = (bf16[1024,256]{1,0:T(8,128)(2,1)S(1)}, bf16[1024,256]{1,0:T(8,128)(2,1)S(1)}, u32[]{:S(2)}, u32[]{:S(2)}) collective-permute-start(bf16[1024,256]{1,0:T(8,128)(2,1)S(1)} %get-tuple-element.68), channel_id=1, source_target_pairs={{0,2},{1,3},{2,0},{3,1},{4,6},{5,7},{6,4},{7,5},{8,10},{9,11},{10,... | collective-permute-start | bytes 1572872 | tf_op jit(solution)/shard_map/ppermute | solution.py:461
  44.0 2.8 %collective-permute-done.8.refs_2_ = bf16[4,256,128]{2,1,0:T(8,128)(2,1)S(1)} collective-permute-done((bf16[4,256,128]{2,1,0:T(8,128)(2,1)S(1)}, bf16[4,256,128]{2,1,0:T(8,128)(2,1)S(1)}, u32[]{:S(2)}, u32[]{:S(2)}) %collective-permute-start.8) | collective-permute-done | bytes 262176 | tf_op jit(solution)/shard_map/ppermute | solution.py:464
  47.3 3.7 %attend_others.4 = bf16[272,512]{1,0:T(8,128)(2,1)S(1)} custom-call(s32[8]{0:T(128)S(1)} %copy-done.2, s32[16]{0:T(128)S(1)} %copy-done.3, bf16[32,32,2048]{2,1,0:T(8,128)(2,1)} %bitcast.19, bf16[2,32,32,256]{3,2,1,0:T(8,128)(2,1)S(1)} %bitcast.26, bf16[32,32,256]{2,1,0:T(8,128)(2,1)S(1)} %bitcast.38, bf16[32,32,256]{2,1,0:T(8,128)(2,1)S(1)} %bitcast.41, ...), custom_call_target="tpu_custom_call" | custom-call | flops 2000000000 | bytes 4194304 | tf_op jit(solution)/shard_map/attend_others/pallas_call | solution.py:314
  51.5 4.7 %attend_others.5 = (bf16[272,512]{1,0:T(8,128)(2,1)S(1)}, bf16[272,512]{1,0:T(8,128)(2,1)S(1)}) custom-call(s32[8]{0:T(128)S(1)} %copy-done.2, s32[16]{0:T(128)S(1)} %copy-done.3, bf16[32,32,2048]{2,1,0:T(8,128)(2,1)} %bitcast.20, bf16[2,32,32,256]{3,2,1,0:T(8,128)(2,1)S(1)} %bitcast.27, bf16[32,32,256]{2,1,0:T(8,128)(2,1)S(1)} %bitcast.39, ...), custom_call_target="tpu_custom_call" | custom-call | flops 2000000000 | bytes 4194304 | tf_op jit(solution)/shard_map/attend_others/pallas_call | solution.py:314
  56.2 4.7 %collective-permute-start.12 = (bf16[272,512]{1,0:T(8,128)(2,1)S(1)}, bf16[272,512]{1,0:T(8,128)(2,1)S(1)}, u32[]{:S(2)}, u32[]{:S(2)}) collective-permute-start(bf16[272,512]{1,0:T(8,128)(2,1)S(1)} %get-tuple-element.58), channel_id=1, source_target_pairs={{0,12},{1,13},{2,14},{3,15},{4,0},{5,1},{6,2},{7,3},{8,4},{9,5},{1... | collective-permute-start | bytes 835592 | tf_op jit(solution)/shard_map/ppermute | solution.py:464
  61.0 3.9 %attend_own.2 = (f32[2,128,512]{2,1,0:T(8,128)S(1)}, f32[2,8,512]{2,1,0:T(8,128)S(1)}) custom-call(s32[8]{0:T(128)S(1)} %copy-done.2, s32[16]{0:T(128)S(1)} %copy-done.3, bf16[32,32,2048]{2,1,0:T(8,128)(2,1)} %bitcast.21, bf16[2,32,32,256]{3,2,1,0:T(8,128)(2,1)S(1)} %bitcast.28, bf16[32,32,256]{2,1,0:T(8,128)(2,1)S(1)} %bitcast.40, ...), custom_call_target="tpu_custom_call" | custom-call | flops 500000000 | bytes 4194304 | tf_op jit(solution)/shard_map/attend_own/pallas_call | solution.py:314
  65.3 1.8 %collective-permute-done.14 = bf16[1024,256]{1,0:T(8,128)(2,1)S(1)} collective-permute-done((bf16[1024,256]{1,0:T(8,128)(2,1)S(1)}, bf16[1024,256]{1,0:T(8,128)(2,1)S(1)}, u32[]{:S(2)}, u32[]{:S(2)}) %collective-permute-start.14) | collective-permute-done | bytes 524320 | tf_op jit(solution)/shard_map/ppermute | solution.py:461
  67.1 3.7 %attend_others.6 = bf16[272,512]{1,0:T(8,128)(2,1)S(1)} custom-call(s32[8]{0:T(128)S(1)} %copy-done.2, s32[16]{0:T(128)S(1)} %copy-done.3, bf16[32,32,2048]{2,1,0:T(8,128)(2,1)} %bitcast.22, bf16[2,32,32,256]{3,2,1,0:T(8,128)(2,1)S(1)} %bitcast.29, bf16[32,32,256]{2,1,0:T(8,128)(2,1)S(1)} %bitcast.32, bf16[32,32,256]{2,1,0:T(8,128)(2,1)S(1)} %bitcast.35, ...), custom_call_target="tpu_custom_call" | custom-call | flops 10000000000 | bytes 4194304 | tf_op jit(solution)/shard_map/attend_others/pallas_call | solution.py:314
  70.9 2.1 %collective-permute-start.18 = (bf16[272,512]{1,0:T(8,128)(2,1)S(1)}, bf16[272,512]{1,0:T(8,128)(2,1)S(1)}, u32[]{:S(2)}, u32[]{:S(2)}) collective-permute-start(bf16[272,512]{1,0:T(8,128)(2,1)S(1)} %attend_others.6), channel_id=1, source_target_pairs={{0,12},{1,13},{2,14},{3,15},{4,0},{5,1},{6,2},{7,3},{8,4},{9,5},{1... | collective-permute-start | bytes 835592 | tf_op jit(solution)/shard_map/ppermute | solution.py:464
  73.0 4.8 %attend_others.7 = (bf16[272,512]{1,0:T(8,128)(2,1)S(1)}, bf16[272,512]{1,0:T(8,128)(2,1)S(1)}) custom-call(s32[8]{0:T(128)S(1)} %copy-done.2, s32[16]{0:T(128)S(1)} %copy-done.3, bf16[32,32,2048]{2,1,0:T(8,128)(2,1)} %bitcast.23, bf16[2,32,32,256]{3,2,1,0:T(8,128)(2,1)S(1)} %bitcast.30, bf16[32,32,256]{2,1,0:T(8,128)(2,1)S(1)} %bitcast.33, ...), custom_call_target="tpu_custom_call" | custom-call | flops 10000000000 | bytes 4194304 | tf_op jit(solution)/shard_map/attend_others/pallas_call | solution.py:314
  77.8 1.0 collective-permute-start.20
  78.8 1.9 %collective-permute-done.18.two_ref = bf16[272,512]{1,0:T(8,128)(2,1)S(1)} collective-permute-done((bf16[272,512]{1,0:T(8,128)(2,1)S(1)}, bf16[272,512]{1,0:T(8,128)(2,1)S(1)}, u32[]{:S(2)}, u32[]{:S(2)}) %collective-permute-start.18) | collective-permute-done | bytes 278560 | tf_op jit(solution)/shard_map/ppermute | solution.py:464
  80.9 4.0 %collective-permute-start.19 = (bf16[272,512]{1,0:T(8,128)(2,1)S(1)}, bf16[272,512]{1,0:T(8,128)(2,1)S(1)}, u32[]{:S(2)}, u32[]{:S(2)}) collective-permute-start(bf16[272,512]{1,0:T(8,128)(2,1)S(1)} %merge.3), channel_id=1, source_target_pairs={{0,12},{1,13},{2,14},{3,15},{4,0},{5,1},{6,2},{7,3},{8,4},{9,5},{1... | collective-permute-start | bytes 835592 | tf_op jit(solution)/shard_map/ppermute | solution.py:464
  85.3 1.7 %collective-permute-start.16 = (bf16[320,128]{1,0:T(8,128)(2,1)S(1)}, bf16[320,128]{1,0:T(8,128)(2,1)S(1)}, u32[]{:S(2)}, u32[]{:S(2)}) collective-permute-start(bf16[320,128]{1,0:T(8,128)(2,1)S(1)} %get-tuple-element.80), channel_id=1, source_target_pairs={{0,2},{1,3},{2,0},{3,1},{4,6},{5,7},{6,4},{7,5},{8,10},{9,11},{10,... | collective-permute-start | bytes 245768 | tf_op jit(solution)/shard_map/ppermute | solution.py:461
  87.2 3.1 %collective-permute-done.16.refs_2_ = bf16[320,128]{1,0:T(8,128)(2,1)S(1)} collective-permute-done((bf16[320,128]{1,0:T(8,128)(2,1)S(1)}, bf16[320,128]{1,0:T(8,128)(2,1)S(1)}, u32[]{:S(2)}, u32[]{:S(2)}) %collective-permute-start.16) | collective-permute-done | bytes 81952 | tf_op jit(solution)/shard_map/ppermute | solution.py:461
  90.3 1.4 %collective-permute-done.17.refs_3_ = bf16[320,128]{1,0:T(8,128)(2,1)S(1)} collective-permute-done((bf16[320,128]{1,0:T(8,128)(2,1)S(1)}, bf16[320,128]{1,0:T(8,128)(2,1)S(1)}, u32[]{:S(2)}, u32[]{:S(2)}) %collective-permute-start.17) | collective-permute-done | bytes 81952 | tf_op jit(solution)/shard_map/ppermute | solution.py:461
  91.7 3.9 %attend_own.3 = (f32[2,128,512]{2,1,0:T(8,128)S(1)}, f32[2,8,512]{2,1,0:T(8,128)S(1)}) custom-call(s32[8]{0:T(128)S(1)} %copy-done.2, s32[16]{0:T(128)S(1)} %copy-done.3, bf16[32,32,2048]{2,1,0:T(8,128)(2,1)} %bitcast.24, bf16[2,32,32,256]{3,2,1,0:T(8,128)(2,1)S(1)} %bitcast.31, bf16[32,32,256]{2,1,0:T(8,128)(2,1)S(1)} %bitcast.34, ...), custom_call_target="tpu_custom_call" | custom-call | flops 500000000 | bytes 4194304 | tf_op jit(solution)/shard_map/attend_own/pallas_call | solution.py:314
  96.3 1.7 %collective-permute-start.22 = (bf16[320,128]{1,0:T(8,128)(2,1)S(1)}, bf16[320,128]{1,0:T(8,128)(2,1)S(1)}, u32[]{:S(2)}, u32[]{:S(2)}) collective-permute-start(bf16[320,128]{1,0:T(8,128)(2,1)S(1)} %get-tuple-element.90), channel_id=1, source_target_pairs={{0,2},{1,3},{2,0},{3,1},{4,6},{5,7},{6,4},{7,5},{8,10},{9,11},{10,... | collective-permute-start | bytes 245768 | tf_op jit(solution)/shard_map/ppermute | solution.py:461
  98.0 2.9 %collective-permute-done.22.refs_6_ = bf16[320,128]{1,0:T(8,128)(2,1)S(1)} collective-permute-done((bf16[320,128]{1,0:T(8,128)(2,1)S(1)}, bf16[320,128]{1,0:T(8,128)(2,1)S(1)}, u32[]{:S(2)}, u32[]{:S(2)}) %collective-permute-start.22) | collective-permute-done | bytes 81952 | tf_op jit(solution)/shard_map/ppermute | solution.py:461
  100.8 1.9 %collective-permute-done.23.refs_7_ = bf16[320,128]{1,0:T(8,128)(2,1)S(1)} collective-permute-done((bf16[320,128]{1,0:T(8,128)(2,1)S(1)}, bf16[320,128]{1,0:T(8,128)(2,1)S(1)}, u32[]{:S(2)}, u32[]{:S(2)}) %collective-permute-start.23) | collective-permute-done | bytes 81952 | tf_op jit(solution)/shard_map/ppermute | solution.py:461
  102.7 1.5 %emit.1 = (bf16[8,4,8192]{2,1,0:T(4,128)(2,1)}, bf16[8,4,8192]{2,1,0:T(4,128)(2,1)}) custom-call(bf16[320,128]{1,0:T(8,128)(2,1)S(1)} %get-tuple-element.78.refs_0_, bf16[320,128]{1,0:T(8,128)(2,1)S(1)} %collective-permute-done.15.refs_1_, bf16[320,128]{1,0:T(8,128)(2,1)S(1)} %collective-permute-done.16.refs_2_, ...), custom_call_target="tpu_custom_call" | custom-call | flops 1048576 | bytes 2097152 | tf_op jit(solution)/shard_map/emit/pallas_call | solution.py:443
  (45 shorter events, 4.5 us)
Async XLA Ops:
  2.9 8.3 %collective-permute-start.1 = (bf16[2,320,128]{2,1,0:T(8,128)(2,1)}, bf16[2,320,128]{2,1,0:T(8,128)(2,1)S(1)}, u32[]{:S(2)}, u32[]{:S(2)}) collective-permute-start(bf16[2,320,128]{2,1,0:T(8,128)(2,1)} %get-tuple-element.50), channel_id=1, source_target_pairs={{0,2},{1,3},{2,0},{3,1},{4,6},{5,7},{6,4},{7,5},{8,10},{9,11},{10,... | collective-permute-start | bytes 491528 | tf_op jit(solution)/shard_map/ppermute | solution.py:461
  5.9 7.3 %collective-permute-start.2 = (bf16[2,320,128]{2,1,0:T(8,128)(2,1)}, bf16[2,320,128]{2,1,0:T(8,128)(2,1)S(1)}, u32[]{:S(2)}, u32[]{:S(2)}) collective-permute-start(bf16[2,320,128]{2,1,0:T(8,128)(2,1)} %get-tuple-element.51), channel_id=1, source_target_pairs={{0,3},{1,2},{2,1},{3,0},{4,7},{5,6},{6,5},{7,4},{8,11},{9,10},{10,... | collective-permute-start | bytes 491528 | tf_op jit(solution)/shard_map/ppermute | solution.py:461
  5.9 7.3 %collective-permute-start = (bf16[2,320,128]{2,1,0:T(8,128)(2,1)}, bf16[2,320,128]{2,1,0:T(8,128)(2,1)S(1)}, u32[]{:S(2)}, u32[]{:S(2)}) collective-permute-start(bf16[2,320,128]{2,1,0:T(8,128)(2,1)} %get-tuple-element.49), channel_id=1, source_target_pairs={{0,1},{1,0},{2,3},{3,2},{4,5},{5,4},{6,7},{7,6},{8,9},{9,8},{10,11... | collective-permute-start | bytes 491528 | tf_op jit(solution)/shard_map/ppermute | solution.py:461
  6.1 2.2 %copy-start = (bf16[32,1,32,2048]{3,2,1,0:T(8,128)(2,1)S(1)}, bf16[32,1,32,2048]{3,2,1,0:T(8,128)(2,1)}, u32[]{:S(2)}) copy-start(bf16[32,1,32,2048]{3,2,1,0:T(8,128)(2,1)} %param.5) | copy-start | bytes 12582916
  8.3 1.0 copy-start.1
  8.3 39.0 %copy-start.2 = (s32[8]{0:T(128)S(1)}, s32[8]{0:T(128)}, u32[]{:S(2)}) copy-start(s32[8]{0:T(128)} %counts_ref.11) | copy-start | bytes 100
  8.3 39.0 %copy-start.3 = (s32[16]{0:T(128)S(1)}, s32[16]{0:T(128)}, u32[]{:S(2)}) copy-start(s32[16]{0:T(128)} %slots_ref.11) | copy-start | bytes 196
  13.2 29.1 %collective-permute-start.3 = (bf16[2,1024,256]{2,1,0:T(8,128)(2,1)S(1)}, bf16[2,1024,256]{2,1,0:T(8,128)(2,1)S(1)}, u32[]{:S(2)}, u32[]{:S(2)}) collective-permute-start(bf16[2,1024,256]{2,1,0:T(8,128)(2,1)S(1)} %get-tuple-element.52), channel_id=1, source_target_pairs={{0,1},{1,0},{2,3},{3,2},{4,5},{5,4},{6,7},{7,6},{8,9},{9,8},{10,11... | collective-permute-start | bytes 3145736 | tf_op jit(solution)/shard_map/ppermute | solution.py:461
  13.8 16.2 %collective-permute-start.6 = (bf16[2,4,256,128]{3,2,1,0:T(8,128)(2,1)S(1)}, bf16[2,4,256,128]{3,2,1,0:T(8,128)(2,1)S(1)}, u32[]{:S(2)}, u32[]{:S(2)}) collective-permute-start(bf16[2,4,256,128]{3,2,1,0:T(8,128)(2,1)S(1)} %pad_maximum_fusion), channel_id=1, source_target_pairs={{0,12},{1,13},{2,14},{3,15},{4,0},{5,1},{6,2},{7,3},{8,4},{9,5},{1... | collective-permute-start | bytes 1572872 | tf_op jit(solution)/shard_map/ppermute | solution.py:464
  17.7 16.7 %collective-permute-start.4 = (bf16[1024,256]{1,0:T(8,128)(2,1)S(1)}, bf16[1024,256]{1,0:T(8,128)(2,1)S(1)}, u32[]{:S(2)}, u32[]{:S(2)}) collective-permute-start(bf16[1024,256]{1,0:T(8,128)(2,1)S(1)} %get-tuple-element.53), channel_id=1, source_target_pairs={{0,2},{1,3},{2,0},{3,1},{4,6},{5,7},{6,4},{7,5},{8,10},{9,11},{10,... | collective-permute-start | bytes 1572872 | tf_op jit(solution)/shard_map/ppermute | solution.py:461
  19.2 22.3 %collective-permute-start.5 = (bf16[1024,256]{1,0:T(8,128)(2,1)S(1)}, bf16[1024,256]{1,0:T(8,128)(2,1)S(1)}, u32[]{:S(2)}, u32[]{:S(2)}) collective-permute-start(bf16[1024,256]{1,0:T(8,128)(2,1)S(1)} %get-tuple-element.54), channel_id=1, source_target_pairs={{0,3},{1,2},{2,1},{3,0},{4,7},{5,6},{6,5},{7,4},{8,11},{9,10},{10,... | collective-permute-start | bytes 1572872 | tf_op jit(solution)/shard_map/ppermute | solution.py:461
  19.2 23.0 %collective-permute-start.7 = (bf16[2,4,256,128]{3,2,1,0:T(8,128)(2,1)S(1)}, bf16[2,4,256,128]{3,2,1,0:T(8,128)(2,1)S(1)}, u32[]{:S(2)}, u32[]{:S(2)}) collective-permute-start(bf16[2,4,256,128]{3,2,1,0:T(8,128)(2,1)S(1)} %pad_maximum_fusion), channel_id=1, source_target_pairs={{0,4},{1,5},{2,6},{3,7},{4,8},{5,9},{6,10},{7,11},{8,12},{9,13},{1... | collective-permute-start | bytes 1572872 | tf_op jit(solution)/shard_map/ppermute | solution.py:464
  30.1 16.7 %collective-permute-start.8 = (bf16[4,256,128]{2,1,0:T(8,128)(2,1)S(1)}, bf16[4,256,128]{2,1,0:T(8,128)(2,1)S(1)}, u32[]{:S(2)}, u32[]{:S(2)}) collective-permute-start(bf16[4,256,128]{2,1,0:T(8,128)(2,1)S(1)} %get-tuple-element.55.refs_2_), channel_id=1, source_target_pairs={{0,12},{1,13},{2,14},{3,15},{4,0},{5,1},{6,2},{7,3},{8,4},{9,5},{1... | collective-permute-start | bytes 786440 | tf_op jit(solution)/shard_map/ppermute | solution.py:464
  42.3 23.0 %collective-permute-start.13 = (bf16[1024,256]{1,0:T(8,128)(2,1)S(1)}, bf16[1024,256]{1,0:T(8,128)(2,1)S(1)}, u32[]{:S(2)}, u32[]{:S(2)}) collective-permute-start(bf16[1024,256]{1,0:T(8,128)(2,1)S(1)} %get-tuple-element.68), channel_id=1, source_target_pairs={{0,2},{1,3},{2,0},{3,1},{4,6},{5,7},{6,4},{7,5},{8,10},{9,11},{10,... | collective-permute-start | bytes 1572872 | tf_op jit(solution)/shard_map/ppermute | solution.py:461
  43.8 23.3 %collective-permute-start.14 = (bf16[1024,256]{1,0:T(8,128)(2,1)S(1)}, bf16[1024,256]{1,0:T(8,128)(2,1)S(1)}, u32[]{:S(2)}, u32[]{:S(2)}) collective-permute-start(bf16[1024,256]{1,0:T(8,128)(2,1)S(1)} %get-tuple-element.69), channel_id=1, source_target_pairs={{0,3},{1,2},{2,1},{3,0},{4,7},{5,6},{6,5},{7,4},{8,11},{9,10},{10,... | collective-permute-start | bytes 1572872 | tf_op jit(solution)/shard_map/ppermute | solution.py:461
  46.8 14.1 %collective-permute-start.9 = (bf16[4,256,128]{2,1,0:T(8,128)(2,1)S(1)}, bf16[4,256,128]{2,1,0:T(8,128)(2,1)S(1)}, u32[]{:S(2)}, u32[]{:S(2)}) collective-permute-start(bf16[4,256,128]{2,1,0:T(8,128)(2,1)S(1)} %get-tuple-element.73.refs_3_), channel_id=1, source_target_pairs={{0,4},{1,5},{2,6},{3,7},{4,8},{5,9},{6,10},{7,11},{8,12},{9,13},{1... | collective-permute-start | bytes 786440 | tf_op jit(solution)/shard_map/ppermute | solution.py:464
  51.1 13.7 %collective-permute-start.10 = (bf16[272,512]{1,0:T(8,128)(2,1)S(1)}, bf16[272,512]{1,0:T(8,128)(2,1)S(1)}, u32[]{:S(2)}, u32[]{:S(2)}) collective-permute-start(bf16[272,512]{1,0:T(8,128)(2,1)S(1)} %attend_others.4), channel_id=1, source_target_pairs={{0,4},{1,5},{2,6},{3,7},{4,8},{5,9},{6,10},{7,11},{8,12},{9,13},{1... | collective-permute-start | bytes 835592 | tf_op jit(solution)/shard_map/ppermute | solution.py:464
  56.2 28.7 %collective-permute-start.12 = (bf16[272,512]{1,0:T(8,128)(2,1)S(1)}, bf16[272,512]{1,0:T(8,128)(2,1)S(1)}, u32[]{:S(2)}, u32[]{:S(2)}) collective-permute-start(bf16[272,512]{1,0:T(8,128)(2,1)S(1)} %get-tuple-element.58), channel_id=1, source_target_pairs={{0,12},{1,13},{2,14},{3,15},{4,0},{5,1},{6,2},{7,3},{8,4},{9,5},{1... | collective-permute-start | bytes 835592 | tf_op jit(solution)/shard_map/ppermute | solution.py:464
  65.0 19.9 %collective-permute-start.11 = (bf16[272,512]{1,0:T(8,128)(2,1)S(1)}, bf16[272,512]{1,0:T(8,128)(2,1)S(1)}, u32[]{:S(2)}, u32[]{:S(2)}) collective-permute-start(bf16[272,512]{1,0:T(8,128)(2,1)S(1)} %merge.2), channel_id=1, source_target_pairs={{0,4},{1,5},{2,6},{3,7},{4,8},{5,9},{6,10},{7,11},{8,12},{9,13},{1... | collective-permute-start | bytes 835592 | tf_op jit(solution)/shard_map/ppermute | solution.py:464
  70.9 9.8 %collective-permute-start.18 = (bf16[272,512]{1,0:T(8,128)(2,1)S(1)}, bf16[272,512]{1,0:T(8,128)(2,1)S(1)}, u32[]{:S(2)}, u32[]{:S(2)}) collective-permute-start(bf16[272,512]{1,0:T(8,128)(2,1)S(1)} %attend_others.6), channel_id=1, source_target_pairs={{0,12},{1,13},{2,14},{3,15},{4,0},{5,1},{6,2},{7,3},{8,4},{9,5},{1... | collective-permute-start | bytes 835592 | tf_op jit(solution)/shard_map/ppermute | solution.py:464
  77.8 17.8 %collective-permute-start.20 = (bf16[272,512]{1,0:T(8,128)(2,1)S(1)}, bf16[272,512]{1,0:T(8,128)(2,1)S(1)}, u32[]{:S(2)}, u32[]{:S(2)}) collective-permute-start(bf16[272,512]{1,0:T(8,128)(2,1)S(1)} %get-tuple-element.74), channel_id=1, source_target_pairs={{0,4},{1,5},{2,6},{3,7},{4,8},{5,9},{6,10},{7,11},{8,12},{9,13},{1... | collective-permute-start | bytes 835592 | tf_op jit(solution)/shard_map/ppermute | solution.py:464
  80.9 14.7 %collective-permute-start.19 = (bf16[272,512]{1,0:T(8,128)(2,1)S(1)}, bf16[272,512]{1,0:T(8,128)(2,1)S(1)}, u32[]{:S(2)}, u32[]{:S(2)}) collective-permute-start(bf16[272,512]{1,0:T(8,128)(2,1)S(1)} %merge.3), channel_id=1, source_target_pairs={{0,12},{1,13},{2,14},{3,15},{4,0},{5,1},{6,2},{7,3},{8,4},{9,5},{1... | collective-permute-start | bytes 835592 | tf_op jit(solution)/shard_map/ppermute | solution.py:464
  85.2 1.9 %collective-permute-start.15 = (bf16[320,128]{1,0:T(8,128)(2,1)S(1)}, bf16[320,128]{1,0:T(8,128)(2,1)S(1)}, u32[]{:S(2)}, u32[]{:S(2)}) collective-permute-start(bf16[320,128]{1,0:T(8,128)(2,1)S(1)} %get-tuple-element.79), channel_id=1, source_target_pairs={{0,1},{1,0},{2,3},{3,2},{4,5},{5,4},{6,7},{7,6},{8,9},{9,8},{10,11... | collective-permute-start | bytes 245768 | tf_op jit(solution)/shard_map/ppermute | solution.py:461
  85.3 5.0 %collective-permute-start.16 = (bf16[320,128]{1,0:T(8,128)(2,1)S(1)}, bf16[320,128]{1,0:T(8,128)(2,1)S(1)}, u32[]{:S(2)}, u32[]{:S(2)}) collective-permute-start(bf16[320,128]{1,0:T(8,128)(2,1)S(1)} %get-tuple-element.80), channel_id=1, source_target_pairs={{0,2},{1,3},{2,0},{3,1},{4,6},{5,7},{6,4},{7,5},{8,10},{9,11},{10,... | collective-permute-start | bytes 245768 | tf_op jit(solution)/shard_map/ppermute | solution.py:461
  87.0 4.7 %collective-permute-start.17 = (bf16[320,128]{1,0:T(8,128)(2,1)S(1)}, bf16[320,128]{1,0:T(8,128)(2,1)S(1)}, u32[]{:S(2)}, u32[]{:S(2)}) collective-permute-start(bf16[320,128]{1,0:T(8,128)(2,1)S(1)} %get-tuple-element.81), channel_id=1, source_target_pairs={{0,3},{1,2},{2,1},{3,0},{4,7},{5,6},{6,5},{7,4},{8,11},{9,10},{10,... | collective-permute-start | bytes 245768 | tf_op jit(solution)/shard_map/ppermute | solution.py:461
  95.9 2.1 %collective-permute-start.21 = (bf16[320,128]{1,0:T(8,128)(2,1)S(1)}, bf16[320,128]{1,0:T(8,128)(2,1)S(1)}, u32[]{:S(2)}, u32[]{:S(2)}) collective-permute-start(bf16[320,128]{1,0:T(8,128)(2,1)S(1)} %get-tuple-element.89), channel_id=1, source_target_pairs={{0,1},{1,0},{2,3},{3,2},{4,5},{5,4},{6,7},{7,6},{8,9},{9,8},{10,11... | collective-permute-start | bytes 245768 | tf_op jit(solution)/shard_map/ppermute | solution.py:461
  96.3 4.5 %collective-permute-start.22 = (bf16[320,128]{1,0:T(8,128)(2,1)S(1)}, bf16[320,128]{1,0:T(8,128)(2,1)S(1)}, u32[]{:S(2)}, u32[]{:S(2)}) collective-permute-start(bf16[320,128]{1,0:T(8,128)(2,1)S(1)} %get-tuple-element.90), channel_id=1, source_target_pairs={{0,2},{1,3},{2,0},{3,1},{4,6},{5,7},{6,4},{7,5},{8,10},{9,11},{10,... | collective-permute-start | bytes 245768 | tf_op jit(solution)/shard_map/ppermute | solution.py:461
  98.0 4.7 %collective-permute-start.23 = (bf16[320,128]{1,0:T(8,128)(2,1)S(1)}, bf16[320,128]{1,0:T(8,128)(2,1)S(1)}, u32[]{:S(2)}, u32[]{:S(2)}) collective-permute-start(bf16[320,128]{1,0:T(8,128)(2,1)S(1)} %get-tuple-element.91), channel_id=1, source_target_pairs={{0,3},{1,2},{2,1},{3,0},{4,7},{5,6},{6,5},{7,4},{8,11},{9,10},{10,... | collective-permute-start | bytes 245768 | tf_op jit(solution)/shard_map/ppermute | solution.py:461

commit v10 on v9

--- a/solution.py
+++ b/solution.py
@@ -328,7 +328,7 @@
             pltpu.SemaphoreType.DMA((2 * QUAD + 2 * count + 8,)),
         ],
         compiler_params=params(48),
-        cost_estimate=cost(5 * 10**8 if steps else (10**10 if h else 2 * 10**9), 4 << 20),
+        cost_estimate=cost((10**10 if h else 5 * 10**8) if steps else (10**10 if h else 2 * 10**9), 4 << 20),
         name="attend_own" if steps else "attend_others",
     )(counts, slots, kv3, *arrived, *queries)
 
@@ -531,6 +531,8 @@
 
     def finished(h, mine, back):
         done = finish(steps, *mine, back)
+        if final:
+            done = tied(done, final[-1])
         return [done[0]] + [across(done[k], k) for k in range(1, QUAD)]
 
     final, gate, before = [], None, None
@@ -539,7 +541,7 @@
         if before is not None:
             mine, back = before
             final.append(finished(h - 1, mine, tied(back, parts)))
-        late = tied(msgs, parts, asked[h + 1:h + 2], final[-1:])
+        late = tied(msgs, parts, asked[h + 1:h + 2])
         mine = attend(h, (0,), steps, prompt_blocks, slot_prompt, kv3, blocks, late)
         back, turned = summed(h, parts, ahead)
         before = mine, back

time: 104 us -> 105 us (level)
  starting transfers between devices: 32.1 us -> 30.5 us
  waiting for transfers between devices: 38.4 us -> 39.8 us
    ppermute x10, waiting for transfers between devices: 16.3 us -> 20.6 us  [along(): lax.ppermute(array, 'sample', [(i, (i + shift * QUAD) % nsample) for i in...]
    ppermute x14, waiting for transfers between devices: 22.1 us -> 19.2 us  [across(): return lax.ppermute(array, 'sample', [(i, i ^ k) for i in range(nsample)])]
    ppermute x10, starting transfers between devices: 21.2 us -> 19.7 us  [along(): lax.ppermute(array, 'sample', [(i, (i + shift * QUAD) % nsample) for i in...]
  transfers between devices with their start and end apart: 24 -> 24, of which waited for: 12 -> 11; matrix products, arithmetic and copies ran while one was open for 0% -> 0% of each run, Pallas kernels for 25% -> 26%
where the time goes in v10:
time: 105 us; the launch traced here: 104 us
  waiting for transfers between devices  39.8 us (38%)
  Pallas kernels  30.7 us (29%)
  starting transfers between devices  30.5 us (29%)
  local copies, waits for them, and re-layouts  2.31 us (2%)
    pallas_call x6, Pallas kernels, attend(): pl.pallas_call(functools.partial(attend_kernel, h, offsets, steps, max_ti...  25 us
    ppermute x10, waiting for transfers between devices, along(): lax.ppermute(array, 'sample', [(i, (i + shift * QUAD) % nsample) for i in...  20.6 us
    ppermute x10, starting transfers between devices, along(): lax.ppermute(array, 'sample', [(i, (i + shift * QUAD) % nsample) for i in...  19.7 us
    ppermute x14, waiting for transfers between devices, across(): return lax.ppermute(array, 'sample', [(i, i ^ k) for i in range(nsample)])  19.2 us
    ppermute x14, starting transfers between devices, across(): return lax.ppermute(array, 'sample', [(i, i ^ k) for i in range(nsample)])  10.8 us
    pallas_call x1, Pallas kernels, pack_queries(): pl.pallas_call(pack_queries_kernel, out_shape=[jax.ShapeDtypeStruct((HPD,...  2.25 us
    unnamed x8, local copies, waits for them, and re-layouts  2.2 us
  transfers between devices with their start and end apart: 24, of which 11 were waited for; matrix products, arithmetic and copies ran while one was open for 0% of the time, Pallas kernels for 26%

profile of v10, /device:TPU:0, one launch (start us, length us, event | category | flops | bytes accessed | tf_op | source)
XLA Modules:
  0.0 104.2 jit_solution(15069407454597370543)
XLA Ops:
  0.6 2.2 %pack_queries.1 = (bf16[2,320,128]{2,1,0:T(8,128)(2,1)}, bf16[2,320,128]{2,1,0:T(8,128)(2,1)}, bf16[2,320,128]{2,1,0:T(8,128)(2,1)}, bf16[2,320,128]{2,1,0:T(8,128)(2,1)}) custom-call(bf16[8,4,8192]{2,1,0:T(4,128)(2,1)} %q_hbm.1, bf16[8,4,2048]{2,1,0:T(4,128)(2,1)} %new_hbm.1), custom_call_target="tpu_custom_call" | custom-call | bytes 2097152 | tf_op jit(solution)/shard_map/pack_queries/pallas_call | solution.py:72
  3.4 2.6 %collective-permute-start.1 = (bf16[2,320,128]{2,1,0:T(8,128)(2,1)}, bf16[2,320,128]{2,1,0:T(8,128)(2,1)S(1)}, u32[]{:S(2)}, u32[]{:S(2)}) collective-permute-start(bf16[2,320,128]{2,1,0:T(8,128)(2,1)} %get-tuple-element.54), channel_id=1, source_target_pairs={{0,2},{1,3},{2,0},{3,1},{4,6},{5,7},{6,4},{7,5},{8,10},{9,11},{10,... | collective-permute-start | bytes 491528 | tf_op jit(solution)/shard_map/ppermute | solution.py:461
  6.1 2.2 %copy-done = bf16[32,1,32,2048]{3,2,1,0:T(8,128)(2,1)S(1)} copy-done((bf16[32,1,32,2048]{3,2,1,0:T(8,128)(2,1)S(1)}, bf16[32,1,32,2048]{3,2,1,0:T(8,128)(2,1)}, u32[]{:S(2)}) %copy-start) | copy-done | bytes 4194328
  8.3 1.0 pack_kv.1
  9.3 2.0 %collective-permute-done.1.refs_4_ = bf16[2,320,128]{2,1,0:T(8,128)(2,1)S(1)} collective-permute-done((bf16[2,320,128]{2,1,0:T(8,128)(2,1)}, bf16[2,320,128]{2,1,0:T(8,128)(2,1)S(1)}, u32[]{:S(2)}, u32[]{:S(2)}) %collective-permute-start.1) | collective-permute-done | bytes 163872 | tf_op jit(solution)/shard_map/ppermute | solution.py:461
  11.3 3.0 %collective-permute-done.2.refs_5_ = bf16[2,320,128]{2,1,0:T(8,128)(2,1)S(1)} collective-permute-done((bf16[2,320,128]{2,1,0:T(8,128)(2,1)}, bf16[2,320,128]{2,1,0:T(8,128)(2,1)S(1)}, u32[]{:S(2)}, u32[]{:S(2)}) %collective-permute-start.2) | collective-permute-done | bytes 163872 | tf_op jit(solution)/shard_map/ppermute | solution.py:461
  14.5 3.9 %collective-permute-start.6 = (bf16[2,4,256,128]{3,2,1,0:T(8,128)(2,1)S(1)}, bf16[2,4,256,128]{3,2,1,0:T(8,128)(2,1)S(1)}, u32[]{:S(2)}, u32[]{:S(2)}) collective-permute-start(bf16[2,4,256,128]{3,2,1,0:T(8,128)(2,1)S(1)} %pad_maximum_fusion), channel_id=1, source_target_pairs={{0,12},{1,13},{2,14},{3,15},{4,0},{5,1},{6,2},{7,3},{8,4},{9,5},{1... | collective-permute-start | bytes 1572872 | tf_op jit(solution)/shard_map/ppermute | solution.py:464
  18.4 1.5 %collective-permute-start.4 = (bf16[1024,256]{1,0:T(8,128)(2,1)S(1)}, bf16[1024,256]{1,0:T(8,128)(2,1)S(1)}, u32[]{:S(2)}, u32[]{:S(2)}) collective-permute-start(bf16[1024,256]{1,0:T(8,128)(2,1)S(1)} %get-tuple-element.57), channel_id=1, source_target_pairs={{0,2},{1,3},{2,0},{3,1},{4,6},{5,7},{6,4},{7,5},{8,10},{9,11},{10,... | collective-permute-start | bytes 1572872 | tf_op jit(solution)/shard_map/ppermute | solution.py:461
  19.9 10.8 %collective-permute-done.6 = bf16[2,4,256,128]{3,2,1,0:T(8,128)(2,1)S(1)} collective-permute-done((bf16[2,4,256,128]{3,2,1,0:T(8,128)(2,1)S(1)}, bf16[2,4,256,128]{3,2,1,0:T(8,128)(2,1)S(1)}, u32[]{:S(2)}, u32[]{:S(2)}) %collective-permute-start.6) | collective-permute-done | bytes 524320 | tf_op jit(solution)/shard_map/ppermute | solution.py:464
  30.8 4.3 %collective-permute-start.8 = (bf16[4,256,128]{2,1,0:T(8,128)(2,1)S(1)}, bf16[4,256,128]{2,1,0:T(8,128)(2,1)S(1)}, u32[]{:S(2)}, u32[]{:S(2)}) collective-permute-start(bf16[4,256,128]{2,1,0:T(8,128)(2,1)S(1)} %get-tuple-element.59.refs_2_), channel_id=1, source_target_pairs={{0,12},{1,13},{2,14},{3,15},{4,0},{5,1},{6,2},{7,3},{8,4},{9,5},{1... | collective-permute-start | bytes 786440 | tf_op jit(solution)/shard_map/ppermute | solution.py:464
  35.1 7.4 %collective-permute-done.5 = bf16[1024,256]{1,0:T(8,128)(2,1)S(1)} collective-permute-done((bf16[1024,256]{1,0:T(8,128)(2,1)S(1)}, bf16[1024,256]{1,0:T(8,128)(2,1)S(1)}, u32[]{:S(2)}, u32[]{:S(2)}) %collective-permute-start.5) | collective-permute-done | bytes 524320 | tf_op jit(solution)/shard_map/ppermute | solution.py:461
  42.9 1.5 %collective-permute-start.13 = (bf16[1024,256]{1,0:T(8,128)(2,1)S(1)}, bf16[1024,256]{1,0:T(8,128)(2,1)S(1)}, u32[]{:S(2)}, u32[]{:S(2)}) collective-permute-start(bf16[1024,256]{1,0:T(8,128)(2,1)S(1)} %get-tuple-element.72), channel_id=1, source_target_pairs={{0,2},{1,3},{2,0},{3,1},{4,6},{5,7},{6,4},{7,5},{8,10},{9,11},{10,... | collective-permute-start | bytes 1572872 | tf_op jit(solution)/shard_map/ppermute | solution.py:461
  45.0 2.8 %collective-permute-done.8.refs_2_ = bf16[4,256,128]{2,1,0:T(8,128)(2,1)S(1)} collective-permute-done((bf16[4,256,128]{2,1,0:T(8,128)(2,1)S(1)}, bf16[4,256,128]{2,1,0:T(8,128)(2,1)S(1)}, u32[]{:S(2)}, u32[]{:S(2)}) %collective-permute-start.8) | collective-permute-done | bytes 262176 | tf_op jit(solution)/shard_map/ppermute | solution.py:464
  47.8 0.6 collective-permute-start.9
  48.3 4.0 %attend_others.4 = bf16[272,512]{1,0:T(8,128)(2,1)S(1)} custom-call(s32[8]{0:T(128)S(1)} %copy-done.2, s32[16]{0:T(128)S(1)} %copy-done.3, bf16[32,32,2048]{2,1,0:T(8,128)(2,1)} %bitcast.19, bf16[2,32,32,256]{3,2,1,0:T(8,128)(2,1)S(1)} %bitcast.26, bf16[32,32,256]{2,1,0:T(8,128)(2,1)S(1)} %bitcast.32, bf16[32,32,256]{2,1,0:T(8,128)(2,1)S(1)} %bitcast.35, ...), custom_call_target="tpu_custom_call" | custom-call | flops 2000000000 | bytes 4194304 | tf_op jit(solution)/shard_map/attend_others/pallas_call | solution.py:314
  52.5 4.9 %attend_others.5 = (bf16[272,512]{1,0:T(8,128)(2,1)S(1)}, bf16[272,512]{1,0:T(8,128)(2,1)S(1)}) custom-call(s32[8]{0:T(128)S(1)} %copy-done.2, s32[16]{0:T(128)S(1)} %copy-done.3, bf16[32,32,2048]{2,1,0:T(8,128)(2,1)} %bitcast.20, bf16[2,32,32,256]{3,2,1,0:T(8,128)(2,1)S(1)} %bitcast.27, bf16[32,32,256]{2,1,0:T(8,128)(2,1)S(1)} %bitcast.33, ...), custom_call_target="tpu_custom_call" | custom-call | flops 2000000000 | bytes 4194304 | tf_op jit(solution)/shard_map/attend_others/pallas_call | solution.py:314
  57.4 4.4 %collective-permute-start.12 = (bf16[272,512]{1,0:T(8,128)(2,1)S(1)}, bf16[272,512]{1,0:T(8,128)(2,1)S(1)}, u32[]{:S(2)}, u32[]{:S(2)}) collective-permute-start(bf16[272,512]{1,0:T(8,128)(2,1)S(1)} %get-tuple-element.62), channel_id=1, source_target_pairs={{0,12},{1,13},{2,14},{3,15},{4,0},{5,1},{6,2},{7,3},{8,4},{9,5},{1... | collective-permute-start | bytes 835592 | tf_op jit(solution)/shard_map/ppermute | solution.py:464
  61.8 3.7 %attend_own.2 = (f32[2,128,512]{2,1,0:T(8,128)S(1)}, f32[2,8,512]{2,1,0:T(8,128)S(1)}) custom-call(s32[8]{0:T(128)S(1)} %copy-done.2, s32[16]{0:T(128)S(1)} %copy-done.3, bf16[32,32,2048]{2,1,0:T(8,128)(2,1)} %bitcast.21, bf16[2,32,32,256]{3,2,1,0:T(8,128)(2,1)S(1)} %bitcast.28, bf16[32,32,256]{2,1,0:T(8,128)(2,1)S(1)} %bitcast.34, ...), custom_call_target="tpu_custom_call" | custom-call | flops 500000000 | bytes 4194304 | tf_op jit(solution)/shard_map/attend_own/pallas_call | solution.py:314
  66.0 2.3 %collective-permute-done.14 = bf16[1024,256]{1,0:T(8,128)(2,1)S(1)} collective-permute-done((bf16[1024,256]{1,0:T(8,128)(2,1)S(1)}, bf16[1024,256]{1,0:T(8,128)(2,1)S(1)}, u32[]{:S(2)}, u32[]{:S(2)}) %collective-permute-start.14) | collective-permute-done | bytes 524320 | tf_op jit(solution)/shard_map/ppermute | solution.py:461
  68.3 4.0 %attend_others.6 = bf16[272,512]{1,0:T(8,128)(2,1)S(1)} custom-call(s32[8]{0:T(128)S(1)} %copy-done.2, s32[16]{0:T(128)S(1)} %copy-done.3, bf16[32,32,2048]{2,1,0:T(8,128)(2,1)} %bitcast.22, bf16[2,32,32,256]{3,2,1,0:T(8,128)(2,1)S(1)} %bitcast.29, bf16[32,32,256]{2,1,0:T(8,128)(2,1)S(1)} %bitcast.38, bf16[32,32,256]{2,1,0:T(8,128)(2,1)S(1)} %bitcast.41, ...), custom_call_target="tpu_custom_call" | custom-call | flops 10000000000 | bytes 4194304 | tf_op jit(solution)/shard_map/attend_others/pallas_call | solution.py:314
  72.3 1.5 %collective-permute-start.18 = (bf16[272,512]{1,0:T(8,128)(2,1)S(1)}, bf16[272,512]{1,0:T(8,128)(2,1)S(1)}, u32[]{:S(2)}, u32[]{:S(2)}) collective-permute-start(bf16[272,512]{1,0:T(8,128)(2,1)S(1)} %attend_others.6), channel_id=1, source_target_pairs={{0,12},{1,13},{2,14},{3,15},{4,0},{5,1},{6,2},{7,3},{8,4},{9,5},{1... | collective-permute-start | bytes 835592 | tf_op jit(solution)/shard_map/ppermute | solution.py:464
  73.8 4.9 %attend_others.7 = (bf16[272,512]{1,0:T(8,128)(2,1)S(1)}, bf16[272,512]{1,0:T(8,128)(2,1)S(1)}) custom-call(s32[8]{0:T(128)S(1)} %copy-done.2, s32[16]{0:T(128)S(1)} %copy-done.3, bf16[32,32,2048]{2,1,0:T(8,128)(2,1)} %bitcast.23, bf16[2,32,32,256]{3,2,1,0:T(8,128)(2,1)S(1)} %bitcast.30, bf16[32,32,256]{2,1,0:T(8,128)(2,1)S(1)} %bitcast.39, ...), custom_call_target="tpu_custom_call" | custom-call | flops 10000000000 | bytes 4194304 | tf_op jit(solution)/shard_map/attend_others/pallas_call | solution.py:314
  78.7 1.5 %collective-permute-start.20 = (bf16[272,512]{1,0:T(8,128)(2,1)S(1)}, bf16[272,512]{1,0:T(8,128)(2,1)S(1)}, u32[]{:S(2)}, u32[]{:S(2)}) collective-permute-start(bf16[272,512]{1,0:T(8,128)(2,1)S(1)} %get-tuple-element.78), channel_id=1, source_target_pairs={{0,4},{1,5},{2,6},{3,7},{4,8},{5,9},{6,10},{7,11},{8,12},{9,13},{1... | collective-permute-start | bytes 835592 | tf_op jit(solution)/shard_map/ppermute | solution.py:464
  80.6 1.6 %collective-permute-start.16 = (bf16[320,128]{1,0:T(8,128)(2,1)S(1)}, bf16[320,128]{1,0:T(8,128)(2,1)S(1)}, u32[]{:S(2)}, u32[]{:S(2)}) collective-permute-start(bf16[320,128]{1,0:T(8,128)(2,1)S(1)} %get-tuple-element.84), channel_id=1, source_target_pairs={{0,2},{1,3},{2,0},{3,1},{4,6},{5,7},{6,4},{7,5},{8,10},{9,11},{10,... | collective-permute-start | bytes 245768 | tf_op jit(solution)/shard_map/ppermute | solution.py:461
  82.6 3.0 %collective-permute-start.19 = (bf16[272,512]{1,0:T(8,128)(2,1)S(1)}, bf16[272,512]{1,0:T(8,128)(2,1)S(1)}, u32[]{:S(2)}, u32[]{:S(2)}) collective-permute-start(bf16[272,512]{1,0:T(8,128)(2,1)S(1)} %merge.3), channel_id=1, source_target_pairs={{0,12},{1,13},{2,14},{3,15},{4,0},{5,1},{6,2},{7,3},{8,4},{9,5},{1... | collective-permute-start | bytes 835592 | tf_op jit(solution)/shard_map/ppermute | solution.py:464
  85.7 3.7 %attend_own.3 = (f32[2,128,512]{2,1,0:T(8,128)S(1)}, f32[2,8,512]{2,1,0:T(8,128)S(1)}) custom-call(s32[8]{0:T(128)S(1)} %copy-done.2, s32[16]{0:T(128)S(1)} %copy-done.3, bf16[32,32,2048]{2,1,0:T(8,128)(2,1)} %bitcast.24, bf16[2,32,32,256]{3,2,1,0:T(8,128)(2,1)S(1)} %bitcast.31, bf16[32,32,256]{2,1,0:T(8,128)(2,1)S(1)} %bitcast.40, ...), custom_call_target="tpu_custom_call" | custom-call | flops 10000000000 | bytes 4194304 | tf_op jit(solution)/shard_map/attend_own/pallas_call | solution.py:314
  89.3 0.8 collective-permute-done.20.refs_1_
  90.1 5.8 %collective-permute-done.19.refs_0_ = bf16[272,512]{1,0:T(8,128)(2,1)S(1)} collective-permute-done((bf16[272,512]{1,0:T(8,128)(2,1)S(1)}, bf16[272,512]{1,0:T(8,128)(2,1)S(1)}, u32[]{:S(2)}, u32[]{:S(2)}) %collective-permute-start.19) | collective-permute-done | bytes 278560 | tf_op jit(solution)/shard_map/ppermute | solution.py:464
  96.4 1.6 %collective-permute-start.22 = (bf16[320,128]{1,0:T(8,128)(2,1)S(1)}, bf16[320,128]{1,0:T(8,128)(2,1)S(1)}, u32[]{:S(2)}, u32[]{:S(2)}) collective-permute-start(bf16[320,128]{1,0:T(8,128)(2,1)S(1)} %get-tuple-element.98), channel_id=1, source_target_pairs={{0,2},{1,3},{2,0},{3,1},{4,6},{5,7},{6,4},{7,5},{8,10},{9,11},{10,... | collective-permute-start | bytes 245768 | tf_op jit(solution)/shard_map/ppermute | solution.py:461
  98.2 3.2 %collective-permute-done.22.refs_6_ = bf16[320,128]{1,0:T(8,128)(2,1)S(1)} collective-permute-done((bf16[320,128]{1,0:T(8,128)(2,1)S(1)}, bf16[320,128]{1,0:T(8,128)(2,1)S(1)}, u32[]{:S(2)}, u32[]{:S(2)}) %collective-permute-start.22) | collective-permute-done | bytes 81952 | tf_op jit(solution)/shard_map/ppermute | solution.py:461
  101.5 1.3 %collective-permute-done.23.refs_7_ = bf16[320,128]{1,0:T(8,128)(2,1)S(1)} collective-permute-done((bf16[320,128]{1,0:T(8,128)(2,1)S(1)}, bf16[320,128]{1,0:T(8,128)(2,1)S(1)}, u32[]{:S(2)}, u32[]{:S(2)}) %collective-permute-start.23) | collective-permute-done | bytes 81952 | tf_op jit(solution)/shard_map/ppermute | solution.py:461
  102.7 1.5 %emit.1 = (bf16[8,4,8192]{2,1,0:T(4,128)(2,1)}, bf16[8,4,8192]{2,1,0:T(4,128)(2,1)}) custom-call(bf16[320,128]{1,0:T(8,128)(2,1)S(1)} %get-tuple-element.82.refs_0_, bf16[320,128]{1,0:T(8,128)(2,1)S(1)} %collective-permute-done.15.refs_1_, bf16[320,128]{1,0:T(8,128)(2,1)S(1)} %collective-permute-done.16.refs_2_, ...), custom_call_target="tpu_custom_call" | custom-call | flops 1048576 | bytes 2097152 | tf_op jit(solution)/shard_map/emit/pallas_call | solution.py:443
  (45 shorter events, 4.2 us)
Async XLA Ops:
  2.9 6.4 %collective-permute-start = (bf16[2,320,128]{2,1,0:T(8,128)(2,1)}, bf16[2,320,128]{2,1,0:T(8,128)(2,1)S(1)}, u32[]{:S(2)}, u32[]{:S(2)}) collective-permute-start(bf16[2,320,128]{2,1,0:T(8,128)(2,1)} %get-tuple-element.53), channel_id=1, source_target_pairs={{0,1},{1,0},{2,3},{3,2},{4,5},{5,4},{6,7},{7,6},{8,9},{9,8},{10,11... | collective-permute-start | bytes 491528 | tf_op jit(solution)/shard_map/ppermute | solution.py:461
  3.4 7.9 %collective-permute-start.1 = (bf16[2,320,128]{2,1,0:T(8,128)(2,1)}, bf16[2,320,128]{2,1,0:T(8,128)(2,1)S(1)}, u32[]{:S(2)}, u32[]{:S(2)}) collective-permute-start(bf16[2,320,128]{2,1,0:T(8,128)(2,1)} %get-tuple-element.54), channel_id=1, source_target_pairs={{0,2},{1,3},{2,0},{3,1},{4,6},{5,7},{6,4},{7,5},{8,10},{9,11},{10,... | collective-permute-start | bytes 491528 | tf_op jit(solution)/shard_map/ppermute | solution.py:461
  6.0 8.3 %collective-permute-start.2 = (bf16[2,320,128]{2,1,0:T(8,128)(2,1)}, bf16[2,320,128]{2,1,0:T(8,128)(2,1)S(1)}, u32[]{:S(2)}, u32[]{:S(2)}) collective-permute-start(bf16[2,320,128]{2,1,0:T(8,128)(2,1)} %get-tuple-element.55), channel_id=1, source_target_pairs={{0,3},{1,2},{2,1},{3,0},{4,7},{5,6},{6,5},{7,4},{8,11},{9,10},{10,... | collective-permute-start | bytes 491528 | tf_op jit(solution)/shard_map/ppermute | solution.py:461
  6.1 2.2 %copy-start = (bf16[32,1,32,2048]{3,2,1,0:T(8,128)(2,1)S(1)}, bf16[32,1,32,2048]{3,2,1,0:T(8,128)(2,1)}, u32[]{:S(2)}) copy-start(bf16[32,1,32,2048]{3,2,1,0:T(8,128)(2,1)} %param.5) | copy-start | bytes 12582916
  8.3 1.0 copy-start.1
  8.3 40.1 %copy-start.2 = (s32[8]{0:T(128)S(1)}, s32[8]{0:T(128)}, u32[]{:S(2)}) copy-start(s32[8]{0:T(128)} %counts_ref.11) | copy-start | bytes 100
  8.3 40.1 %copy-start.3 = (s32[16]{0:T(128)S(1)}, s32[16]{0:T(128)}, u32[]{:S(2)}) copy-start(s32[16]{0:T(128)} %slots_ref.11) | copy-start | bytes 196
  14.2 28.6 %collective-permute-start.3 = (bf16[2,1024,256]{2,1,0:T(8,128)(2,1)S(1)}, bf16[2,1024,256]{2,1,0:T(8,128)(2,1)S(1)}, u32[]{:S(2)}, u32[]{:S(2)}) collective-permute-start(bf16[2,1024,256]{2,1,0:T(8,128)(2,1)S(1)} %get-tuple-element.56), channel_id=1, source_target_pairs={{0,1},{1,0},{2,3},{3,2},{4,5},{5,4},{6,7},{7,6},{8,9},{9,8},{10,11... | collective-permute-start | bytes 3145736 | tf_op jit(solution)/shard_map/ppermute | solution.py:461
  14.5 16.2 %collective-permute-start.6 = (bf16[2,4,256,128]{3,2,1,0:T(8,128)(2,1)S(1)}, bf16[2,4,256,128]{3,2,1,0:T(8,128)(2,1)S(1)}, u32[]{:S(2)}, u32[]{:S(2)}) collective-permute-start(bf16[2,4,256,128]{3,2,1,0:T(8,128)(2,1)S(1)} %pad_maximum_fusion), channel_id=1, source_target_pairs={{0,12},{1,13},{2,14},{3,15},{4,0},{5,1},{6,2},{7,3},{8,4},{9,5},{1... | collective-permute-start | bytes 1572872 | tf_op jit(solution)/shard_map/ppermute | solution.py:464
  18.4 16.7 %collective-permute-start.4 = (bf16[1024,256]{1,0:T(8,128)(2,1)S(1)}, bf16[1024,256]{1,0:T(8,128)(2,1)S(1)}, u32[]{:S(2)}, u32[]{:S(2)}) collective-permute-start(bf16[1024,256]{1,0:T(8,128)(2,1)S(1)} %get-tuple-element.57), channel_id=1, source_target_pairs={{0,2},{1,3},{2,0},{3,1},{4,6},{5,7},{6,4},{7,5},{8,10},{9,11},{10,... | collective-permute-start | bytes 1572872 | tf_op jit(solution)/shard_map/ppermute | solution.py:461
  19.9 22.5 %collective-permute-start.5 = (bf16[1024,256]{1,0:T(8,128)(2,1)S(1)}, bf16[1024,256]{1,0:T(8,128)(2,1)S(1)}, u32[]{:S(2)}, u32[]{:S(2)}) collective-permute-start(bf16[1024,256]{1,0:T(8,128)(2,1)S(1)} %get-tuple-element.58), channel_id=1, source_target_pairs={{0,3},{1,2},{2,1},{3,0},{4,7},{5,6},{6,5},{7,4},{8,11},{9,10},{10,... | collective-permute-start | bytes 1572872 | tf_op jit(solution)/shard_map/ppermute | solution.py:461
  19.9 22.9 %collective-permute-start.7 = (bf16[2,4,256,128]{3,2,1,0:T(8,128)(2,1)S(1)}, bf16[2,4,256,128]{3,2,1,0:T(8,128)(2,1)S(1)}, u32[]{:S(2)}, u32[]{:S(2)}) collective-permute-start(bf16[2,4,256,128]{3,2,1,0:T(8,128)(2,1)S(1)} %pad_maximum_fusion), channel_id=1, source_target_pairs={{0,4},{1,5},{2,6},{3,7},{4,8},{5,9},{6,10},{7,11},{8,12},{9,13},{1... | collective-permute-start | bytes 1572872 | tf_op jit(solution)/shard_map/ppermute | solution.py:464
  30.8 17.0 %collective-permute-start.8 = (bf16[4,256,128]{2,1,0:T(8,128)(2,1)S(1)}, bf16[4,256,128]{2,1,0:T(8,128)(2,1)S(1)}, u32[]{:S(2)}, u32[]{:S(2)}) collective-permute-start(bf16[4,256,128]{2,1,0:T(8,128)(2,1)S(1)} %get-tuple-element.59.refs_2_), channel_id=1, source_target_pairs={{0,12},{1,13},{2,14},{3,15},{4,0},{5,1},{6,2},{7,3},{8,4},{9,5},{1... | collective-permute-start | bytes 786440 | tf_op jit(solution)/shard_map/ppermute | solution.py:464
  42.9 23.1 %collective-permute-start.13 = (bf16[1024,256]{1,0:T(8,128)(2,1)S(1)}, bf16[1024,256]{1,0:T(8,128)(2,1)S(1)}, u32[]{:S(2)}, u32[]{:S(2)}) collective-permute-start(bf16[1024,256]{1,0:T(8,128)(2,1)S(1)} %get-tuple-element.72), channel_id=1, source_target_pairs={{0,2},{1,3},{2,0},{3,1},{4,6},{5,7},{6,4},{7,5},{8,10},{9,11},{10,... | collective-permute-start | bytes 1572872 | tf_op jit(solution)/shard_map/ppermute | solution.py:461
  44.4 23.9 %collective-permute-start.14 = (bf16[1024,256]{1,0:T(8,128)(2,1)S(1)}, bf16[1024,256]{1,0:T(8,128)(2,1)S(1)}, u32[]{:S(2)}, u32[]{:S(2)}) collective-permute-start(bf16[1024,256]{1,0:T(8,128)(2,1)S(1)} %get-tuple-element.73), channel_id=1, source_target_pairs={{0,3},{1,2},{2,1},{3,0},{4,7},{5,6},{6,5},{7,4},{8,11},{9,10},{10,... | collective-permute-start | bytes 1572872 | tf_op jit(solution)/shard_map/ppermute | solution.py:461
  47.8 14.1 %collective-permute-start.9 = (bf16[4,256,128]{2,1,0:T(8,128)(2,1)S(1)}, bf16[4,256,128]{2,1,0:T(8,128)(2,1)S(1)}, u32[]{:S(2)}, u32[]{:S(2)}) collective-permute-start(bf16[4,256,128]{2,1,0:T(8,128)(2,1)S(1)} %get-tuple-element.77.refs_3_), channel_id=1, source_target_pairs={{0,4},{1,5},{2,6},{3,7},{4,8},{5,9},{6,10},{7,11},{8,12},{9,13},{1... | collective-permute-start | bytes 786440 | tf_op jit(solution)/shard_map/ppermute | solution.py:464
  52.3 13.2 %collective-permute-start.10 = (bf16[272,512]{1,0:T(8,128)(2,1)S(1)}, bf16[272,512]{1,0:T(8,128)(2,1)S(1)}, u32[]{:S(2)}, u32[]{:S(2)}) collective-permute-start(bf16[272,512]{1,0:T(8,128)(2,1)S(1)} %attend_others.4), channel_id=1, source_target_pairs={{0,4},{1,5},{2,6},{3,7},{4,8},{5,9},{6,10},{7,11},{8,12},{9,13},{1... | collective-permute-start | bytes 835592 | tf_op jit(solution)/shard_map/ppermute | solution.py:464
  57.4 22.8 %collective-permute-start.12 = (bf16[272,512]{1,0:T(8,128)(2,1)S(1)}, bf16[272,512]{1,0:T(8,128)(2,1)S(1)}, u32[]{:S(2)}, u32[]{:S(2)}) collective-permute-start(bf16[272,512]{1,0:T(8,128)(2,1)S(1)} %get-tuple-element.62), channel_id=1, source_target_pairs={{0,12},{1,13},{2,14},{3,15},{4,0},{5,1},{6,2},{7,3},{8,4},{9,5},{1... | collective-permute-start | bytes 835592 | tf_op jit(solution)/shard_map/ppermute | solution.py:464
  65.7 14.5 %collective-permute-start.11 = (bf16[272,512]{1,0:T(8,128)(2,1)S(1)}, bf16[272,512]{1,0:T(8,128)(2,1)S(1)}, u32[]{:S(2)}, u32[]{:S(2)}) collective-permute-start(bf16[272,512]{1,0:T(8,128)(2,1)S(1)} %merge.2), channel_id=1, source_target_pairs={{0,4},{1,5},{2,6},{3,7},{4,8},{5,9},{6,10},{7,11},{8,12},{9,13},{1... | collective-permute-start | bytes 835592 | tf_op jit(solution)/shard_map/ppermute | solution.py:464
  72.3 10.2 %collective-permute-start.18 = (bf16[272,512]{1,0:T(8,128)(2,1)S(1)}, bf16[272,512]{1,0:T(8,128)(2,1)S(1)}, u32[]{:S(2)}, u32[]{:S(2)}) collective-permute-start(bf16[272,512]{1,0:T(8,128)(2,1)S(1)} %attend_others.6), channel_id=1, source_target_pairs={{0,12},{1,13},{2,14},{3,15},{4,0},{5,1},{6,2},{7,3},{8,4},{9,5},{1... | collective-permute-start | bytes 835592 | tf_op jit(solution)/shard_map/ppermute | solution.py:464
  78.7 11.4 %collective-permute-start.20 = (bf16[272,512]{1,0:T(8,128)(2,1)S(1)}, bf16[272,512]{1,0:T(8,128)(2,1)S(1)}, u32[]{:S(2)}, u32[]{:S(2)}) collective-permute-start(bf16[272,512]{1,0:T(8,128)(2,1)S(1)} %get-tuple-element.78), channel_id=1, source_target_pairs={{0,4},{1,5},{2,6},{3,7},{4,8},{5,9},{6,10},{7,11},{8,12},{9,13},{1... | collective-permute-start | bytes 835592 | tf_op jit(solution)/shard_map/ppermute | solution.py:464
  80.5 15.7 %collective-permute-start.15 = (bf16[320,128]{1,0:T(8,128)(2,1)S(1)}, bf16[320,128]{1,0:T(8,128)(2,1)S(1)}, u32[]{:S(2)}, u32[]{:S(2)}) collective-permute-start(bf16[320,128]{1,0:T(8,128)(2,1)S(1)} %get-tuple-element.83), channel_id=1, source_target_pairs={{0,1},{1,0},{2,3},{3,2},{4,5},{5,4},{6,7},{7,6},{8,9},{9,8},{10,11... | collective-permute-start | bytes 245768 | tf_op jit(solution)/shard_map/ppermute | solution.py:461
  80.6 15.7 %collective-permute-start.16 = (bf16[320,128]{1,0:T(8,128)(2,1)S(1)}, bf16[320,128]{1,0:T(8,128)(2,1)S(1)}, u32[]{:S(2)}, u32[]{:S(2)}) collective-permute-start(bf16[320,128]{1,0:T(8,128)(2,1)S(1)} %get-tuple-element.84), channel_id=1, source_target_pairs={{0,2},{1,3},{2,0},{3,1},{4,6},{5,7},{6,4},{7,5},{8,10},{9,11},{10,... | collective-permute-start | bytes 245768 | tf_op jit(solution)/shard_map/ppermute | solution.py:461
  82.2 14.1 %collective-permute-start.17 = (bf16[320,128]{1,0:T(8,128)(2,1)S(1)}, bf16[320,128]{1,0:T(8,128)(2,1)S(1)}, u32[]{:S(2)}, u32[]{:S(2)}) collective-permute-start(bf16[320,128]{1,0:T(8,128)(2,1)S(1)} %get-tuple-element.85), channel_id=1, source_target_pairs={{0,3},{1,2},{2,1},{3,0},{4,7},{5,6},{6,5},{7,4},{8,11},{9,10},{10,... | collective-permute-start | bytes 245768 | tf_op jit(solution)/shard_map/ppermute | solution.py:461
  82.6 13.3 %collective-permute-start.19 = (bf16[272,512]{1,0:T(8,128)(2,1)S(1)}, bf16[272,512]{1,0:T(8,128)(2,1)S(1)}, u32[]{:S(2)}, u32[]{:S(2)}) collective-permute-start(bf16[272,512]{1,0:T(8,128)(2,1)S(1)} %merge.3), channel_id=1, source_target_pairs={{0,12},{1,13},{2,14},{3,15},{4,0},{5,1},{6,2},{7,3},{8,4},{9,5},{1... | collective-permute-start | bytes 835592 | tf_op jit(solution)/shard_map/ppermute | solution.py:464
  96.3 1.9 %collective-permute-start.21 = (bf16[320,128]{1,0:T(8,128)(2,1)S(1)}, bf16[320,128]{1,0:T(8,128)(2,1)S(1)}, u32[]{:S(2)}, u32[]{:S(2)}) collective-permute-start(bf16[320,128]{1,0:T(8,128)(2,1)S(1)} %get-tuple-element.97), channel_id=1, source_target_pairs={{0,1},{1,0},{2,3},{3,2},{4,5},{5,4},{6,7},{7,6},{8,9},{9,8},{10,11... | collective-permute-start | bytes 245768 | tf_op jit(solution)/shard_map/ppermute | solution.py:461
  96.4 5.0 %collective-permute-start.22 = (bf16[320,128]{1,0:T(8,128)(2,1)S(1)}, bf16[320,128]{1,0:T(8,128)(2,1)S(1)}, u32[]{:S(2)}, u32[]{:S(2)}) collective-permute-start(bf16[320,128]{1,0:T(8,128)(2,1)S(1)} %get-tuple-element.98), channel_id=1, source_target_pairs={{0,2},{1,3},{2,0},{3,1},{4,6},{5,7},{6,4},{7,5},{8,10},{9,11},{10,... | collective-permute-start | bytes 245768 | tf_op jit(solution)/shard_map/ppermute | solution.py:461
  98.0 4.7 %collective-permute-start.23 = (bf16[320,128]{1,0:T(8,128)(2,1)S(1)}, bf16[320,128]{1,0:T(8,128)(2,1)S(1)}, u32[]{:S(2)}, u32[]{:S(2)}) collective-permute-start(bf16[320,128]{1,0:T(8,128)(2,1)S(1)} %get-tuple-element.99), channel_id=1, source_target_pairs={{0,3},{1,2},{2,1},{3,0},{4,7},{5,6},{6,5},{7,4},{8,11},{9,10},{10,... | collective-permute-start | bytes 245768 | tf_op jit(solution)/shard_map/ppermute | solution.py:461

commit v11 on v10

--- a/solution.py
+++ b/solution.py
@@ -538,12 +538,12 @@
     final, gate, before = [], None, None
     for h in range(HPD):
         blocks, parts, ahead = others(h, gate)
+        back, turned = summed(h, parts, ahead)
         if before is not None:
-            mine, back = before
-            final.append(finished(h - 1, mine, tied(back, parts)))
+            mine, earlier = before
+            final.append(finished(h - 1, mine, tied(earlier, parts, turned)))
         late = tied(msgs, parts, asked[h + 1:h + 2])
         mine = attend(h, (0,), steps, prompt_blocks, slot_prompt, kv3, blocks, late)
-        back, turned = summed(h, parts, ahead)
         before = mine, back
         gate = mine[0], turned
     final.append(finished(HPD - 1, *before))

time: 105 us -> 104 us (level)
  Pallas kernels: 30.7 us -> 29.5 us
    pallas_call x6, Pallas kernels: 25 us -> 23.9 us  [attend(): pl.pallas_call(functools.partial(attend_kernel, h, offsets, steps, max_ti...]
  transfers between devices with their start and end apart: 24 -> 24, of which waited for: 11 -> 11; matrix products, arithmetic and copies ran while one was open for 0% -> 0% of each run, Pallas kernels for 26% -> 25%
where the time goes in v11:
time: 104 us; the launch traced here: 103 us
  waiting for transfers between devices  39.8 us (38%)
  starting transfers between devices  30.6 us (29%)
  Pallas kernels  29.5 us (28%)
  local copies, waits for them, and re-layouts  2.31 us (2%)
    pallas_call x6, Pallas kernels, attend(): pl.pallas_call(functools.partial(attend_kernel, h, offsets, steps, max_ti...  23.9 us
    ppermute x10, waiting for transfers between devices, along(): lax.ppermute(array, 'sample', [(i, (i + shift * QUAD) % nsample) for i in...  20.5 us
    ppermute x10, starting transfers between devices, along(): lax.ppermute(array, 'sample', [(i, (i + shift * QUAD) % nsample) for i in...  19.9 us
    ppermute x14, waiting for transfers between devices, across(): return lax.ppermute(array, 'sample', [(i, i ^ k) for i in range(nsample)])  19.4 us
    ppermute x14, starting transfers between devices, across(): return lax.ppermute(array, 'sample', [(i, i ^ k) for i in range(nsample)])  10.8 us
    pallas_call x1, Pallas kernels, pack_queries(): pl.pallas_call(pack_queries_kernel, out_shape=[jax.ShapeDtypeStruct((HPD,...  2.25 us
    unnamed x8, local copies, waits for them, and re-layouts  2.2 us
  transfers between devices with their start and end apart: 24, of which 11 were waited for; matrix products, arithmetic and copies ran while one was open for 0% of the time, Pallas kernels for 25%

profile of v11, /device:TPU:0, one launch (start us, length us, event | category | flops | bytes accessed | tf_op | source)
XLA Modules:
  0.0 103.3 jit_solution(17118896608018249557)
XLA Ops:
  0.6 2.2 %pack_queries.1 = (bf16[2,320,128]{2,1,0:T(8,128)(2,1)}, bf16[2,320,128]{2,1,0:T(8,128)(2,1)}, bf16[2,320,128]{2,1,0:T(8,128)(2,1)}, bf16[2,320,128]{2,1,0:T(8,128)(2,1)}) custom-call(bf16[8,4,8192]{2,1,0:T(4,128)(2,1)} %q_hbm.1, bf16[8,4,2048]{2,1,0:T(4,128)(2,1)} %new_hbm.1), custom_call_target="tpu_custom_call" | custom-call | bytes 2097152 | tf_op jit(solution)/shard_map/pack_queries/pallas_call | solution.py:72
  3.4 2.6 %collective-permute-start.1 = (bf16[2,320,128]{2,1,0:T(8,128)(2,1)}, bf16[2,320,128]{2,1,0:T(8,128)(2,1)S(1)}, u32[]{:S(2)}, u32[]{:S(2)}) collective-permute-start(bf16[2,320,128]{2,1,0:T(8,128)(2,1)} %get-tuple-element.54), channel_id=1, source_target_pairs={{0,2},{1,3},{2,0},{3,1},{4,6},{5,7},{6,4},{7,5},{8,10},{9,11},{10,... | collective-permute-start | bytes 491528 | tf_op jit(solution)/shard_map/ppermute | solution.py:461
  6.1 2.2 %copy-done = bf16[32,1,32,2048]{3,2,1,0:T(8,128)(2,1)S(1)} copy-done((bf16[32,1,32,2048]{3,2,1,0:T(8,128)(2,1)S(1)}, bf16[32,1,32,2048]{3,2,1,0:T(8,128)(2,1)}, u32[]{:S(2)}) %copy-start) | copy-done | bytes 4194328
  8.3 1.0 pack_kv.1
  9.3 2.0 %collective-permute-done.1.refs_4_ = bf16[2,320,128]{2,1,0:T(8,128)(2,1)S(1)} collective-permute-done((bf16[2,320,128]{2,1,0:T(8,128)(2,1)}, bf16[2,320,128]{2,1,0:T(8,128)(2,1)S(1)}, u32[]{:S(2)}, u32[]{:S(2)}) %collective-permute-start.1) | collective-permute-done | bytes 163872 | tf_op jit(solution)/shard_map/ppermute | solution.py:461
  11.3 3.0 %collective-permute-done.2.refs_5_ = bf16[2,320,128]{2,1,0:T(8,128)(2,1)S(1)} collective-permute-done((bf16[2,320,128]{2,1,0:T(8,128)(2,1)}, bf16[2,320,128]{2,1,0:T(8,128)(2,1)S(1)}, u32[]{:S(2)}, u32[]{:S(2)}) %collective-permute-start.2) | collective-permute-done | bytes 163872 | tf_op jit(solution)/shard_map/ppermute | solution.py:461
  14.5 3.9 %collective-permute-start.6 = (bf16[2,4,256,128]{3,2,1,0:T(8,128)(2,1)S(1)}, bf16[2,4,256,128]{3,2,1,0:T(8,128)(2,1)S(1)}, u32[]{:S(2)}, u32[]{:S(2)}) collective-permute-start(bf16[2,4,256,128]{3,2,1,0:T(8,128)(2,1)S(1)} %pad_maximum_fusion), channel_id=1, source_target_pairs={{0,12},{1,13},{2,14},{3,15},{4,0},{5,1},{6,2},{7,3},{8,4},{9,5},{1... | collective-permute-start | bytes 1572872 | tf_op jit(solution)/shard_map/ppermute | solution.py:464
  18.4 1.5 %collective-permute-start.4 = (bf16[1024,256]{1,0:T(8,128)(2,1)S(1)}, bf16[1024,256]{1,0:T(8,128)(2,1)S(1)}, u32[]{:S(2)}, u32[]{:S(2)}) collective-permute-start(bf16[1024,256]{1,0:T(8,128)(2,1)S(1)} %get-tuple-element.57), channel_id=1, source_target_pairs={{0,2},{1,3},{2,0},{3,1},{4,6},{5,7},{6,4},{7,5},{8,10},{9,11},{10,... | collective-permute-start | bytes 1572872 | tf_op jit(solution)/shard_map/ppermute | solution.py:461
  19.9 10.8 %collective-permute-done.6 = bf16[2,4,256,128]{3,2,1,0:T(8,128)(2,1)S(1)} collective-permute-done((bf16[2,4,256,128]{3,2,1,0:T(8,128)(2,1)S(1)}, bf16[2,4,256,128]{3,2,1,0:T(8,128)(2,1)S(1)}, u32[]{:S(2)}, u32[]{:S(2)}) %collective-permute-start.6) | collective-permute-done | bytes 524320 | tf_op jit(solution)/shard_map/ppermute | solution.py:464
  30.8 4.3 %collective-permute-start.8 = (bf16[4,256,128]{2,1,0:T(8,128)(2,1)S(1)}, bf16[4,256,128]{2,1,0:T(8,128)(2,1)S(1)}, u32[]{:S(2)}, u32[]{:S(2)}) collective-permute-start(bf16[4,256,128]{2,1,0:T(8,128)(2,1)S(1)} %get-tuple-element.59.refs_2_), channel_id=1, source_target_pairs={{0,12},{1,13},{2,14},{3,15},{4,0},{5,1},{6,2},{7,3},{8,4},{9,5},{1... | collective-permute-start | bytes 786440 | tf_op jit(solution)/shard_map/ppermute | solution.py:464
  35.1 7.4 %collective-permute-done.5 = bf16[1024,256]{1,0:T(8,128)(2,1)S(1)} collective-permute-done((bf16[1024,256]{1,0:T(8,128)(2,1)S(1)}, bf16[1024,256]{1,0:T(8,128)(2,1)S(1)}, u32[]{:S(2)}, u32[]{:S(2)}) %collective-permute-start.5) | collective-permute-done | bytes 524320 | tf_op jit(solution)/shard_map/ppermute | solution.py:461
  42.9 1.5 %collective-permute-start.13 = (bf16[1024,256]{1,0:T(8,128)(2,1)S(1)}, bf16[1024,256]{1,0:T(8,128)(2,1)S(1)}, u32[]{:S(2)}, u32[]{:S(2)}) collective-permute-start(bf16[1024,256]{1,0:T(8,128)(2,1)S(1)} %get-tuple-element.72), channel_id=1, source_target_pairs={{0,2},{1,3},{2,0},{3,1},{4,6},{5,7},{6,4},{7,5},{8,10},{9,11},{10,... | collective-permute-start | bytes 1572872 | tf_op jit(solution)/shard_map/ppermute | solution.py:461
  45.0 2.8 %collective-permute-done.8.refs_2_ = bf16[4,256,128]{2,1,0:T(8,128)(2,1)S(1)} collective-permute-done((bf16[4,256,128]{2,1,0:T(8,128)(2,1)S(1)}, bf16[4,256,128]{2,1,0:T(8,128)(2,1)S(1)}, u32[]{:S(2)}, u32[]{:S(2)}) %collective-permute-start.8) | collective-permute-done | bytes 262176 | tf_op jit(solution)/shard_map/ppermute | solution.py:464
  48.3 3.1 %attend_others.4 = bf16[272,512]{1,0:T(8,128)(2,1)S(1)} custom-call(s32[8]{0:T(128)S(1)} %copy-done.2, s32[16]{0:T(128)S(1)} %copy-done.3, bf16[32,32,2048]{2,1,0:T(8,128)(2,1)} %bitcast.19, bf16[2,32,32,256]{3,2,1,0:T(8,128)(2,1)S(1)} %bitcast.26, bf16[32,32,256]{2,1,0:T(8,128)(2,1)S(1)} %bitcast.32, bf16[32,32,256]{2,1,0:T(8,128)(2,1)S(1)} %bitcast.35, ...), custom_call_target="tpu_custom_call" | custom-call | flops 2000000000 | bytes 4194304 | tf_op jit(solution)/shard_map/attend_others/pallas_call | solution.py:314
  51.4 1.6 %collective-permute-start.10 = (bf16[272,512]{1,0:T(8,128)(2,1)S(1)}, bf16[272,512]{1,0:T(8,128)(2,1)S(1)}, u32[]{:S(2)}, u32[]{:S(2)}) collective-permute-start(bf16[272,512]{1,0:T(8,128)(2,1)S(1)} %attend_others.4), channel_id=1, source_target_pairs={{0,4},{1,5},{2,6},{3,7},{4,8},{5,9},{6,10},{7,11},{8,12},{9,13},{1... | collective-permute-start | bytes 835592 | tf_op jit(solution)/shard_map/ppermute | solution.py:464
  53.0 4.7 %attend_others.5 = (bf16[272,512]{1,0:T(8,128)(2,1)S(1)}, bf16[272,512]{1,0:T(8,128)(2,1)S(1)}) custom-call(s32[8]{0:T(128)S(1)} %copy-done.2, s32[16]{0:T(128)S(1)} %copy-done.3, bf16[32,32,2048]{2,1,0:T(8,128)(2,1)} %bitcast.20, bf16[2,32,32,256]{3,2,1,0:T(8,128)(2,1)S(1)} %bitcast.27, bf16[32,32,256]{2,1,0:T(8,128)(2,1)S(1)} %bitcast.33, ...), custom_call_target="tpu_custom_call" | custom-call | flops 2000000000 | bytes 4194304 | tf_op jit(solution)/shard_map/attend_others/pallas_call | solution.py:314
  57.8 3.4 %collective-permute-start.12 = (bf16[272,512]{1,0:T(8,128)(2,1)S(1)}, bf16[272,512]{1,0:T(8,128)(2,1)S(1)}, u32[]{:S(2)}, u32[]{:S(2)}) collective-permute-start(bf16[272,512]{1,0:T(8,128)(2,1)S(1)} %get-tuple-element.62), channel_id=1, source_target_pairs={{0,12},{1,13},{2,14},{3,15},{4,0},{5,1},{6,2},{7,3},{8,4},{9,5},{1... | collective-permute-start | bytes 835592 | tf_op jit(solution)/shard_map/ppermute | solution.py:464
  61.2 4.1 %attend_own.2 = (f32[2,128,512]{2,1,0:T(8,128)S(1)}, f32[2,8,512]{2,1,0:T(8,128)S(1)}) custom-call(s32[8]{0:T(128)S(1)} %copy-done.2, s32[16]{0:T(128)S(1)} %copy-done.3, bf16[32,32,2048]{2,1,0:T(8,128)(2,1)} %bitcast.21, bf16[2,32,32,256]{3,2,1,0:T(8,128)(2,1)S(1)} %bitcast.28, bf16[32,32,256]{2,1,0:T(8,128)(2,1)S(1)} %bitcast.34, ...), custom_call_target="tpu_custom_call" | custom-call | flops 500000000 | bytes 4194304 | tf_op jit(solution)/shard_map/attend_own/pallas_call | solution.py:314
  65.8 2.5 %collective-permute-done.14 = bf16[1024,256]{1,0:T(8,128)(2,1)S(1)} collective-permute-done((bf16[1024,256]{1,0:T(8,128)(2,1)S(1)}, bf16[1024,256]{1,0:T(8,128)(2,1)S(1)}, u32[]{:S(2)}, u32[]{:S(2)}) %collective-permute-start.14) | collective-permute-done | bytes 524320 | tf_op jit(solution)/shard_map/ppermute | solution.py:461
  68.3 3.1 %attend_others.6 = bf16[272,512]{1,0:T(8,128)(2,1)S(1)} custom-call(s32[8]{0:T(128)S(1)} %copy-done.2, s32[16]{0:T(128)S(1)} %copy-done.3, bf16[32,32,2048]{2,1,0:T(8,128)(2,1)} %bitcast.22, bf16[2,32,32,256]{3,2,1,0:T(8,128)(2,1)S(1)} %bitcast.29, bf16[32,32,256]{2,1,0:T(8,128)(2,1)S(1)} %bitcast.38, bf16[32,32,256]{2,1,0:T(8,128)(2,1)S(1)} %bitcast.41, ...), custom_call_target="tpu_custom_call" | custom-call | flops 10000000000 | bytes 4194304 | tf_op jit(solution)/shard_map/attend_others/pallas_call | solution.py:314
  71.4 1.7 %collective-permute-start.15 = (bf16[272,512]{1,0:T(8,128)(2,1)S(1)}, bf16[272,512]{1,0:T(8,128)(2,1)S(1)}, u32[]{:S(2)}, u32[]{:S(2)}) collective-permute-start(bf16[272,512]{1,0:T(8,128)(2,1)S(1)} %attend_others.6), channel_id=1, source_target_pairs={{0,12},{1,13},{2,14},{3,15},{4,0},{5,1},{6,2},{7,3},{8,4},{9,5},{1... | collective-permute-start | bytes 835592 | tf_op jit(solution)/shard_map/ppermute | solution.py:464
  73.2 4.7 %attend_others.7 = (bf16[272,512]{1,0:T(8,128)(2,1)S(1)}, bf16[272,512]{1,0:T(8,128)(2,1)S(1)}) custom-call(s32[8]{0:T(128)S(1)} %copy-done.2, s32[16]{0:T(128)S(1)} %copy-done.3, bf16[32,32,2048]{2,1,0:T(8,128)(2,1)} %bitcast.23, bf16[2,32,32,256]{3,2,1,0:T(8,128)(2,1)S(1)} %bitcast.30, bf16[32,32,256]{2,1,0:T(8,128)(2,1)S(1)} %bitcast.39, ...), custom_call_target="tpu_custom_call" | custom-call | flops 10000000000 | bytes 4194304 | tf_op jit(solution)/shard_map/attend_others/pallas_call | solution.py:314
  77.9 0.8 collective-permute-start.20
  78.7 2.9 %collective-permute-done.15.two_ref = bf16[272,512]{1,0:T(8,128)(2,1)S(1)} collective-permute-done((bf16[272,512]{1,0:T(8,128)(2,1)S(1)}, bf16[272,512]{1,0:T(8,128)(2,1)S(1)}, u32[]{:S(2)}, u32[]{:S(2)}) %collective-permute-start.15) | collective-permute-done | bytes 278560 | tf_op jit(solution)/shard_map/ppermute | solution.py:464
  81.8 3.2 %collective-permute-start.19 = (bf16[272,512]{1,0:T(8,128)(2,1)S(1)}, bf16[272,512]{1,0:T(8,128)(2,1)S(1)}, u32[]{:S(2)}, u32[]{:S(2)}) collective-permute-start(bf16[272,512]{1,0:T(8,128)(2,1)S(1)} %merge.3), channel_id=1, source_target_pairs={{0,12},{1,13},{2,14},{3,15},{4,0},{5,1},{6,2},{7,3},{8,4},{9,5},{1... | collective-permute-start | bytes 835592 | tf_op jit(solution)/shard_map/ppermute | solution.py:464
  85.4 1.4 %collective-permute-start.17 = (bf16[320,128]{1,0:T(8,128)(2,1)S(1)}, bf16[320,128]{1,0:T(8,128)(2,1)S(1)}, u32[]{:S(2)}, u32[]{:S(2)}) collective-permute-start(bf16[320,128]{1,0:T(8,128)(2,1)S(1)} %get-tuple-element.84), channel_id=1, source_target_pairs={{0,2},{1,3},{2,0},{3,1},{4,6},{5,7},{6,4},{7,5},{8,10},{9,11},{10,... | collective-permute-start | bytes 245768 | tf_op jit(solution)/shard_map/ppermute | solution.py:461
  87.3 4.2 %attend_own.3 = (f32[2,128,512]{2,1,0:T(8,128)S(1)}, f32[2,8,512]{2,1,0:T(8,128)S(1)}) custom-call(s32[8]{0:T(128)S(1)} %copy-done.2, s32[16]{0:T(128)S(1)} %copy-done.3, bf16[32,32,2048]{2,1,0:T(8,128)(2,1)} %bitcast.24, bf16[2,32,32,256]{3,2,1,0:T(8,128)(2,1)S(1)} %bitcast.31, bf16[32,32,256]{2,1,0:T(8,128)(2,1)S(1)} %bitcast.40, ...), custom_call_target="tpu_custom_call" | custom-call | flops 10000000000 | bytes 4194304 | tf_op jit(solution)/shard_map/attend_own/pallas_call | solution.py:314
  91.5 3.6 %collective-permute-done.19.refs_0_ = bf16[272,512]{1,0:T(8,128)(2,1)S(1)} collective-permute-done((bf16[272,512]{1,0:T(8,128)(2,1)S(1)}, bf16[272,512]{1,0:T(8,128)(2,1)S(1)}, u32[]{:S(2)}, u32[]{:S(2)}) %collective-permute-start.19) | collective-permute-done | bytes 278560 | tf_op jit(solution)/shard_map/ppermute | solution.py:464
  95.5 1.6 %collective-permute-start.22 = (bf16[320,128]{1,0:T(8,128)(2,1)S(1)}, bf16[320,128]{1,0:T(8,128)(2,1)S(1)}, u32[]{:S(2)}, u32[]{:S(2)}) collective-permute-start(bf16[320,128]{1,0:T(8,128)(2,1)S(1)} %get-tuple-element.98), channel_id=1, source_target_pairs={{0,2},{1,3},{2,0},{3,1},{4,6},{5,7},{6,4},{7,5},{8,10},{9,11},{10,... | collective-permute-start | bytes 245768 | tf_op jit(solution)/shard_map/ppermute | solution.py:461
  97.3 3.3 %collective-permute-done.22.refs_6_ = bf16[320,128]{1,0:T(8,128)(2,1)S(1)} collective-permute-done((bf16[320,128]{1,0:T(8,128)(2,1)S(1)}, bf16[320,128]{1,0:T(8,128)(2,1)S(1)}, u32[]{:S(2)}, u32[]{:S(2)}) %collective-permute-start.22) | collective-permute-done | bytes 81952 | tf_op jit(solution)/shard_map/ppermute | solution.py:461
  100.6 1.2 %collective-permute-done.23.refs_7_ = bf16[320,128]{1,0:T(8,128)(2,1)S(1)} collective-permute-done((bf16[320,128]{1,0:T(8,128)(2,1)S(1)}, bf16[320,128]{1,0:T(8,128)(2,1)S(1)}, u32[]{:S(2)}, u32[]{:S(2)}) %collective-permute-start.23) | collective-permute-done | bytes 81952 | tf_op jit(solution)/shard_map/ppermute | solution.py:461
  101.8 1.5 %emit.1 = (bf16[8,4,8192]{2,1,0:T(4,128)(2,1)}, bf16[8,4,8192]{2,1,0:T(4,128)(2,1)}) custom-call(bf16[320,128]{1,0:T(8,128)(2,1)S(1)} %get-tuple-element.82.refs_0_, bf16[320,128]{1,0:T(8,128)(2,1)S(1)} %collective-permute-done.16.refs_1_, bf16[320,128]{1,0:T(8,128)(2,1)S(1)} %collective-permute-done.17.refs_2_, ...), custom_call_target="tpu_custom_call" | custom-call | flops 1048576 | bytes 2097152 | tf_op jit(solution)/shard_map/emit/pallas_call | solution.py:443
  (45 shorter events, 4.6 us)
Async XLA Ops:
  2.9 6.4 %collective-permute-start = (bf16[2,320,128]{2,1,0:T(8,128)(2,1)}, bf16[2,320,128]{2,1,0:T(8,128)(2,1)S(1)}, u32[]{:S(2)}, u32[]{:S(2)}) collective-permute-start(bf16[2,320,128]{2,1,0:T(8,128)(2,1)} %get-tuple-element.53), channel_id=1, source_target_pairs={{0,1},{1,0},{2,3},{3,2},{4,5},{5,4},{6,7},{7,6},{8,9},{9,8},{10,11... | collective-permute-start | bytes 491528 | tf_op jit(solution)/shard_map/ppermute | solution.py:461
  3.4 7.9 %collective-permute-start.1 = (bf16[2,320,128]{2,1,0:T(8,128)(2,1)}, bf16[2,320,128]{2,1,0:T(8,128)(2,1)S(1)}, u32[]{:S(2)}, u32[]{:S(2)}) collective-permute-start(bf16[2,320,128]{2,1,0:T(8,128)(2,1)} %get-tuple-element.54), channel_id=1, source_target_pairs={{0,2},{1,3},{2,0},{3,1},{4,6},{5,7},{6,4},{7,5},{8,10},{9,11},{10,... | collective-permute-start | bytes 491528 | tf_op jit(solution)/shard_map/ppermute | solution.py:461
  6.0 8.3 %collective-permute-start.2 = (bf16[2,320,128]{2,1,0:T(8,128)(2,1)}, bf16[2,320,128]{2,1,0:T(8,128)(2,1)S(1)}, u32[]{:S(2)}, u32[]{:S(2)}) collective-permute-start(bf16[2,320,128]{2,1,0:T(8,128)(2,1)} %get-tuple-element.55), channel_id=1, source_target_pairs={{0,3},{1,2},{2,1},{3,0},{4,7},{5,6},{6,5},{7,4},{8,11},{9,10},{10,... | collective-permute-start | bytes 491528 | tf_op jit(solution)/shard_map/ppermute | solution.py:461
  6.1 2.2 %copy-start = (bf16[32,1,32,2048]{3,2,1,0:T(8,128)(2,1)S(1)}, bf16[32,1,32,2048]{3,2,1,0:T(8,128)(2,1)}, u32[]{:S(2)}) copy-start(bf16[32,1,32,2048]{3,2,1,0:T(8,128)(2,1)} %param.5) | copy-start | bytes 12582916
  8.3 1.0 copy-start.1
  8.3 40.1 %copy-start.2 = (s32[8]{0:T(128)S(1)}, s32[8]{0:T(128)}, u32[]{:S(2)}) copy-start(s32[8]{0:T(128)} %counts_ref.11) | copy-start | bytes 100
  8.3 40.1 %copy-start.3 = (s32[16]{0:T(128)S(1)}, s32[16]{0:T(128)}, u32[]{:S(2)}) copy-start(s32[16]{0:T(128)} %slots_ref.11) | copy-start | bytes 196
  14.2 28.6 %collective-permute-start.3 = (bf16[2,1024,256]{2,1,0:T(8,128)(2,1)S(1)}, bf16[2,1024,256]{2,1,0:T(8,128)(2,1)S(1)}, u32[]{:S(2)}, u32[]{:S(2)}) collective-permute-start(bf16[2,1024,256]{2,1,0:T(8,128)(2,1)S(1)} %get-tuple-element.56), channel_id=1, source_target_pairs={{0,1},{1,0},{2,3},{3,2},{4,5},{5,4},{6,7},{7,6},{8,9},{9,8},{10,11... | collective-permute-start | bytes 3145736 | tf_op jit(solution)/shard_map/ppermute | solution.py:461
  14.5 16.2 %collective-permute-start.6 = (bf16[2,4,256,128]{3,2,1,0:T(8,128)(2,1)S(1)}, bf16[2,4,256,128]{3,2,1,0:T(8,128)(2,1)S(1)}, u32[]{:S(2)}, u32[]{:S(2)}) collective-permute-start(bf16[2,4,256,128]{3,2,1,0:T(8,128)(2,1)S(1)} %pad_maximum_fusion), channel_id=1, source_target_pairs={{0,12},{1,13},{2,14},{3,15},{4,0},{5,1},{6,2},{7,3},{8,4},{9,5},{1... | collective-permute-start | bytes 1572872 | tf_op jit(solution)/shard_map/ppermute | solution.py:464
  18.4 16.7 %collective-permute-start.4 = (bf16[1024,256]{1,0:T(8,128)(2,1)S(1)}, bf16[1024,256]{1,0:T(8,128)(2,1)S(1)}, u32[]{:S(2)}, u32[]{:S(2)}) collective-permute-start(bf16[1024,256]{1,0:T(8,128)(2,1)S(1)} %get-tuple-element.57), channel_id=1, source_target_pairs={{0,2},{1,3},{2,0},{3,1},{4,6},{5,7},{6,4},{7,5},{8,10},{9,11},{10,... | collective-permute-start | bytes 1572872 | tf_op jit(solution)/shard_map/ppermute | solution.py:461
  19.9 22.5 %collective-permute-start.5 = (bf16[1024,256]{1,0:T(8,128)(2,1)S(1)}, bf16[1024,256]{1,0:T(8,128)(2,1)S(1)}, u32[]{:S(2)}, u32[]{:S(2)}) collective-permute-start(bf16[1024,256]{1,0:T(8,128)(2,1)S(1)} %get-tuple-element.58), channel_id=1, source_target_pairs={{0,3},{1,2},{2,1},{3,0},{4,7},{5,6},{6,5},{7,4},{8,11},{9,10},{10,... | collective-permute-start | bytes 1572872 | tf_op jit(solution)/shard_map/ppermute | solution.py:461
  19.9 22.9 %collective-permute-start.7 = (bf16[2,4,256,128]{3,2,1,0:T(8,128)(2,1)S(1)}, bf16[2,4,256,128]{3,2,1,0:T(8,128)(2,1)S(1)}, u32[]{:S(2)}, u32[]{:S(2)}) collective-permute-start(bf16[2,4,256,128]{3,2,1,0:T(8,128)(2,1)S(1)} %pad_maximum_fusion), channel_id=1, source_target_pairs={{0,4},{1,5},{2,6},{3,7},{4,8},{5,9},{6,10},{7,11},{8,12},{9,13},{1... | collective-permute-start | bytes 1572872 | tf_op jit(solution)/shard_map/ppermute | solution.py:464
  30.8 17.0 %collective-permute-start.8 = (bf16[4,256,128]{2,1,0:T(8,128)(2,1)S(1)}, bf16[4,256,128]{2,1,0:T(8,128)(2,1)S(1)}, u32[]{:S(2)}, u32[]{:S(2)}) collective-permute-start(bf16[4,256,128]{2,1,0:T(8,128)(2,1)S(1)} %get-tuple-element.59.refs_2_), channel_id=1, source_target_pairs={{0,12},{1,13},{2,14},{3,15},{4,0},{5,1},{6,2},{7,3},{8,4},{9,5},{1... | collective-permute-start | bytes 786440 | tf_op jit(solution)/shard_map/ppermute | solution.py:464
  42.9 22.9 %collective-permute-start.13 = (bf16[1024,256]{1,0:T(8,128)(2,1)S(1)}, bf16[1024,256]{1,0:T(8,128)(2,1)S(1)}, u32[]{:S(2)}, u32[]{:S(2)}) collective-permute-start(bf16[1024,256]{1,0:T(8,128)(2,1)S(1)} %get-tuple-element.72), channel_id=1, source_target_pairs={{0,2},{1,3},{2,0},{3,1},{4,6},{5,7},{6,4},{7,5},{8,10},{9,11},{10,... | collective-permute-start | bytes 1572872 | tf_op jit(solution)/shard_map/ppermute | solution.py:461
  44.4 23.9 %collective-permute-start.14 = (bf16[1024,256]{1,0:T(8,128)(2,1)S(1)}, bf16[1024,256]{1,0:T(8,128)(2,1)S(1)}, u32[]{:S(2)}, u32[]{:S(2)}) collective-permute-start(bf16[1024,256]{1,0:T(8,128)(2,1)S(1)} %get-tuple-element.73), channel_id=1, source_target_pairs={{0,3},{1,2},{2,1},{3,0},{4,7},{5,6},{6,5},{7,4},{8,11},{9,10},{10,... | collective-permute-start | bytes 1572872 | tf_op jit(solution)/shard_map/ppermute | solution.py:461
  47.8 13.4 %collective-permute-start.9 = (bf16[4,256,128]{2,1,0:T(8,128)(2,1)S(1)}, bf16[4,256,128]{2,1,0:T(8,128)(2,1)S(1)}, u32[]{:S(2)}, u32[]{:S(2)}) collective-permute-start(bf16[4,256,128]{2,1,0:T(8,128)(2,1)S(1)} %get-tuple-element.77.refs_3_), channel_id=1, source_target_pairs={{0,4},{1,5},{2,6},{3,7},{4,8},{5,9},{6,10},{7,11},{8,12},{9,13},{1... | collective-permute-start | bytes 786440 | tf_op jit(solution)/shard_map/ppermute | solution.py:464
  51.4 13.9 %collective-permute-start.10 = (bf16[272,512]{1,0:T(8,128)(2,1)S(1)}, bf16[272,512]{1,0:T(8,128)(2,1)S(1)}, u32[]{:S(2)}, u32[]{:S(2)}) collective-permute-start(bf16[272,512]{1,0:T(8,128)(2,1)S(1)} %attend_others.4), channel_id=1, source_target_pairs={{0,4},{1,5},{2,6},{3,7},{4,8},{5,9},{6,10},{7,11},{8,12},{9,13},{1... | collective-permute-start | bytes 835592 | tf_op jit(solution)/shard_map/ppermute | solution.py:464
  57.8 27.3 %collective-permute-start.12 = (bf16[272,512]{1,0:T(8,128)(2,1)S(1)}, bf16[272,512]{1,0:T(8,128)(2,1)S(1)}, u32[]{:S(2)}, u32[]{:S(2)}) collective-permute-start(bf16[272,512]{1,0:T(8,128)(2,1)S(1)} %get-tuple-element.62), channel_id=1, source_target_pairs={{0,12},{1,13},{2,14},{3,15},{4,0},{5,1},{6,2},{7,3},{8,4},{9,5},{1... | collective-permute-start | bytes 835592 | tf_op jit(solution)/shard_map/ppermute | solution.py:464
  65.5 19.6 %collective-permute-start.11 = (bf16[272,512]{1,0:T(8,128)(2,1)S(1)}, bf16[272,512]{1,0:T(8,128)(2,1)S(1)}, u32[]{:S(2)}, u32[]{:S(2)}) collective-permute-start(bf16[272,512]{1,0:T(8,128)(2,1)S(1)} %merge.2), channel_id=1, source_target_pairs={{0,4},{1,5},{2,6},{3,7},{4,8},{5,9},{6,10},{7,11},{8,12},{9,13},{1... | collective-permute-start | bytes 835592 | tf_op jit(solution)/shard_map/ppermute | solution.py:464
  71.4 10.2 %collective-permute-start.15 = (bf16[272,512]{1,0:T(8,128)(2,1)S(1)}, bf16[272,512]{1,0:T(8,128)(2,1)S(1)}, u32[]{:S(2)}, u32[]{:S(2)}) collective-permute-start(bf16[272,512]{1,0:T(8,128)(2,1)S(1)} %attend_others.6), channel_id=1, source_target_pairs={{0,12},{1,13},{2,14},{3,15},{4,0},{5,1},{6,2},{7,3},{8,4},{9,5},{1... | collective-permute-start | bytes 835592 | tf_op jit(solution)/shard_map/ppermute | solution.py:464
  77.9 13.6 %collective-permute-start.20 = (bf16[272,512]{1,0:T(8,128)(2,1)S(1)}, bf16[272,512]{1,0:T(8,128)(2,1)S(1)}, u32[]{:S(2)}, u32[]{:S(2)}) collective-permute-start(bf16[272,512]{1,0:T(8,128)(2,1)S(1)} %get-tuple-element.78), channel_id=1, source_target_pairs={{0,4},{1,5},{2,6},{3,7},{4,8},{5,9},{6,10},{7,11},{8,12},{9,13},{1... | collective-permute-start | bytes 835592 | tf_op jit(solution)/shard_map/ppermute | solution.py:464
  81.8 13.3 %collective-permute-start.19 = (bf16[272,512]{1,0:T(8,128)(2,1)S(1)}, bf16[272,512]{1,0:T(8,128)(2,1)S(1)}, u32[]{:S(2)}, u32[]{:S(2)}) collective-permute-start(bf16[272,512]{1,0:T(8,128)(2,1)S(1)} %merge.3), channel_id=1, source_target_pairs={{0,12},{1,13},{2,14},{3,15},{4,0},{5,1},{6,2},{7,3},{8,4},{9,5},{1... | collective-permute-start | bytes 835592 | tf_op jit(solution)/shard_map/ppermute | solution.py:464
  85.4 10.0 %collective-permute-start.16 = (bf16[320,128]{1,0:T(8,128)(2,1)S(1)}, bf16[320,128]{1,0:T(8,128)(2,1)S(1)}, u32[]{:S(2)}, u32[]{:S(2)}) collective-permute-start(bf16[320,128]{1,0:T(8,128)(2,1)S(1)} %get-tuple-element.83), channel_id=1, source_target_pairs={{0,1},{1,0},{2,3},{3,2},{4,5},{5,4},{6,7},{7,6},{8,9},{9,8},{10,11... | collective-permute-start | bytes 245768 | tf_op jit(solution)/shard_map/ppermute | solution.py:461
  85.4 10.0 %collective-permute-start.17 = (bf16[320,128]{1,0:T(8,128)(2,1)S(1)}, bf16[320,128]{1,0:T(8,128)(2,1)S(1)}, u32[]{:S(2)}, u32[]{:S(2)}) collective-permute-start(bf16[320,128]{1,0:T(8,128)(2,1)S(1)} %get-tuple-element.84), channel_id=1, source_target_pairs={{0,2},{1,3},{2,0},{3,1},{4,6},{5,7},{6,4},{7,5},{8,10},{9,11},{10,... | collective-permute-start | bytes 245768 | tf_op jit(solution)/shard_map/ppermute | solution.py:461
  86.8 8.6 %collective-permute-start.18 = (bf16[320,128]{1,0:T(8,128)(2,1)S(1)}, bf16[320,128]{1,0:T(8,128)(2,1)S(1)}, u32[]{:S(2)}, u32[]{:S(2)}) collective-permute-start(bf16[320,128]{1,0:T(8,128)(2,1)S(1)} %get-tuple-element.85), channel_id=1, source_target_pairs={{0,3},{1,2},{2,1},{3,0},{4,7},{5,6},{6,5},{7,4},{8,11},{9,10},{10,... | collective-permute-start | bytes 245768 | tf_op jit(solution)/shard_map/ppermute | solution.py:461
  95.4 1.9 %collective-permute-start.21 = (bf16[320,128]{1,0:T(8,128)(2,1)S(1)}, bf16[320,128]{1,0:T(8,128)(2,1)S(1)}, u32[]{:S(2)}, u32[]{:S(2)}) collective-permute-start(bf16[320,128]{1,0:T(8,128)(2,1)S(1)} %get-tuple-element.97), channel_id=1, source_target_pairs={{0,1},{1,0},{2,3},{3,2},{4,5},{5,4},{6,7},{7,6},{8,9},{9,8},{10,11... | collective-permute-start | bytes 245768 | tf_op jit(solution)/shard_map/ppermute | solution.py:461
  95.5 5.1 %collective-permute-start.22 = (bf16[320,128]{1,0:T(8,128)(2,1)S(1)}, bf16[320,128]{1,0:T(8,128)(2,1)S(1)}, u32[]{:S(2)}, u32[]{:S(2)}) collective-permute-start(bf16[320,128]{1,0:T(8,128)(2,1)S(1)} %get-tuple-element.98), channel_id=1, source_target_pairs={{0,2},{1,3},{2,0},{3,1},{4,6},{5,7},{6,4},{7,5},{8,10},{9,11},{10,... | collective-permute-start | bytes 245768 | tf_op jit(solution)/shard_map/ppermute | solution.py:461
  97.1 4.7 %collective-permute-start.23 = (bf16[320,128]{1,0:T(8,128)(2,1)S(1)}, bf16[320,128]{1,0:T(8,128)(2,1)S(1)}, u32[]{:S(2)}, u32[]{:S(2)}) collective-permute-start(bf16[320,128]{1,0:T(8,128)(2,1)S(1)} %get-tuple-element.99), channel_id=1, source_target_pairs={{0,3},{1,2},{2,1},{3,0},{4,7},{5,6},{6,5},{7,4},{8,11},{9,10},{10,... | collective-permute-start | bytes 245768 | tf_op jit(solution)/shard_map/ppermute | solution.py:461

commit v12 on v9

--- a/solution.py
+++ b/solution.py
@@ -492,7 +492,7 @@
     for h in range(HPD):
         sources = far[h * (QUAD - 2):(h + 1) * (QUAD - 2)]
         if h:
-            sources = tied(sources, arrived[-1], first_hop, near)
+            sources = tied(sources, first_hop[-1], near)
         arrived.append([across(block, 2 + i) for i, block in enumerate(sources)])
 
     def chains(h):

time: 104 us -> 104 us (level); the launches traced: 104 us -> 103 us
  starting transfers between devices: 32.1 us -> 29.2 us
  waiting for transfers between devices: 38.4 us -> 39.9 us
    ppermute x10, waiting for transfers between devices: 16.3 us -> 25.7 us  [along(): lax.ppermute(array, 'sample', [(i, (i + shift * QUAD) % nsample) for i in...]
    ppermute x14, waiting for transfers between devices: 22.1 us -> 14.2 us  [across(): return lax.ppermute(array, 'sample', [(i, i ^ k) for i in range(nsample)])]
    ppermute x10, starting transfers between devices: 21.2 us -> 19 us  [along(): lax.ppermute(array, 'sample', [(i, (i + shift * QUAD) % nsample) for i in...]
  transfers between devices with their start and end apart: 24 -> 24, of which waited for: 12 -> 10; matrix products, arithmetic and copies ran while one was open for 0% -> 0% of each run, Pallas kernels for 25% -> 26%
where the time goes in v12:
time: 104 us; the launch traced here: 103 us
  waiting for transfers between devices  39.9 us (38%)
  Pallas kernels  30.6 us (29%)
  starting transfers between devices  29.2 us (28%)
  local copies, waits for them, and re-layouts  2.31 us (2%)
    ppermute x10, waiting for transfers between devices, along(): lax.ppermute(array, 'sample', [(i, (i + shift * QUAD) % nsample) for i in...  25.7 us
    pallas_call x6, Pallas kernels, attend(): pl.pallas_call(functools.partial(attend_kernel, h, offsets, steps, max_ti...  25 us
    ppermute x10, starting transfers between devices, along(): lax.ppermute(array, 'sample', [(i, (i + shift * QUAD) % nsample) for i in...  19 us
    ppermute x14, waiting for transfers between devices, across(): return lax.ppermute(array, 'sample', [(i, i ^ k) for i in range(nsample)])  14.2 us
    ppermute x14, starting transfers between devices, across(): return lax.ppermute(array, 'sample', [(i, i ^ k) for i in range(nsample)])  10.3 us
    pallas_call x1, Pallas kernels, pack_queries(): pl.pallas_call(pack_queries_kernel, out_shape=[jax.ShapeDtypeStruct((HPD,...  2.25 us
    unnamed x8, local copies, waits for them, and re-layouts  2.2 us
  transfers between devices with their start and end apart: 24, of which 10 were waited for; matrix products, arithmetic and copies ran while one was open for 0% of the time, Pallas kernels for 26%

profile of v12, /device:TPU:0, one launch (start us, length us, event | category | flops | bytes accessed | tf_op | source)
XLA Modules:
  0.0 103.1 jit_solution(9504685169479025013)
XLA Ops:
  0.6 2.2 %pack_queries.1 = (bf16[2,320,128]{2,1,0:T(8,128)(2,1)}, bf16[2,320,128]{2,1,0:T(8,128)(2,1)}, bf16[2,320,128]{2,1,0:T(8,128)(2,1)}, bf16[2,320,128]{2,1,0:T(8,128)(2,1)}) custom-call(bf16[8,4,8192]{2,1,0:T(4,128)(2,1)} %q_hbm.1, bf16[8,4,2048]{2,1,0:T(4,128)(2,1)} %new_hbm.1), custom_call_target="tpu_custom_call" | custom-call | bytes 2097152 | tf_op jit(solution)/shard_map/pack_queries/pallas_call | solution.py:72
  3.4 2.6 %collective-permute-start.1 = (bf16[2,320,128]{2,1,0:T(8,128)(2,1)}, bf16[2,320,128]{2,1,0:T(8,128)(2,1)S(1)}, u32[]{:S(2)}, u32[]{:S(2)}) collective-permute-start(bf16[2,320,128]{2,1,0:T(8,128)(2,1)} %get-tuple-element.50), channel_id=1, source_target_pairs={{0,2},{1,3},{2,0},{3,1},{4,6},{5,7},{6,4},{7,5},{8,10},{9,11},{10,... | collective-permute-start | bytes 491528 | tf_op jit(solution)/shard_map/ppermute | solution.py:461
  6.1 2.2 %copy-done = bf16[32,1,32,2048]{3,2,1,0:T(8,128)(2,1)S(1)} copy-done((bf16[32,1,32,2048]{3,2,1,0:T(8,128)(2,1)S(1)}, bf16[32,1,32,2048]{3,2,1,0:T(8,128)(2,1)}, u32[]{:S(2)}) %copy-start) | copy-done | bytes 4194328
  8.3 1.0 pack_kv.1
  9.3 2.0 %collective-permute-done.1.refs_4_ = bf16[2,320,128]{2,1,0:T(8,128)(2,1)S(1)} collective-permute-done((bf16[2,320,128]{2,1,0:T(8,128)(2,1)}, bf16[2,320,128]{2,1,0:T(8,128)(2,1)S(1)}, u32[]{:S(2)}, u32[]{:S(2)}) %collective-permute-start.1) | collective-permute-done | bytes 163872 | tf_op jit(solution)/shard_map/ppermute | solution.py:461
  11.3 3.0 %collective-permute-done.2.refs_5_ = bf16[2,320,128]{2,1,0:T(8,128)(2,1)S(1)} collective-permute-done((bf16[2,320,128]{2,1,0:T(8,128)(2,1)}, bf16[2,320,128]{2,1,0:T(8,128)(2,1)S(1)}, u32[]{:S(2)}, u32[]{:S(2)}) %collective-permute-start.2) | collective-permute-done | bytes 163872 | tf_op jit(solution)/shard_map/ppermute | solution.py:461
  14.5 3.9 %collective-permute-start.6 = (bf16[2,4,256,128]{3,2,1,0:T(8,128)(2,1)S(1)}, bf16[2,4,256,128]{3,2,1,0:T(8,128)(2,1)S(1)}, u32[]{:S(2)}, u32[]{:S(2)}) collective-permute-start(bf16[2,4,256,128]{3,2,1,0:T(8,128)(2,1)S(1)} %pad_maximum_fusion), channel_id=1, source_target_pairs={{0,12},{1,13},{2,14},{3,15},{4,0},{5,1},{6,2},{7,3},{8,4},{9,5},{1... | collective-permute-start | bytes 1572872 | tf_op jit(solution)/shard_map/ppermute | solution.py:464
  18.4 1.5 %collective-permute-start.4 = (bf16[1024,256]{1,0:T(8,128)(2,1)S(1)}, bf16[1024,256]{1,0:T(8,128)(2,1)S(1)}, u32[]{:S(2)}, u32[]{:S(2)}) collective-permute-start(bf16[1024,256]{1,0:T(8,128)(2,1)S(1)} %get-tuple-element.53), channel_id=1, source_target_pairs={{0,2},{1,3},{2,0},{3,1},{4,6},{5,7},{6,4},{7,5},{8,10},{9,11},{10,... | collective-permute-start | bytes 1572872 | tf_op jit(solution)/shard_map/ppermute | solution.py:461
  19.9 10.8 %collective-permute-done.6 = bf16[2,4,256,128]{3,2,1,0:T(8,128)(2,1)S(1)} collective-permute-done((bf16[2,4,256,128]{3,2,1,0:T(8,128)(2,1)S(1)}, bf16[2,4,256,128]{3,2,1,0:T(8,128)(2,1)S(1)}, u32[]{:S(2)}, u32[]{:S(2)}) %collective-permute-start.6) | collective-permute-done | bytes 524320 | tf_op jit(solution)/shard_map/ppermute | solution.py:464
  30.8 4.3 %collective-permute-start.8 = (bf16[4,256,128]{2,1,0:T(8,128)(2,1)S(1)}, bf16[4,256,128]{2,1,0:T(8,128)(2,1)S(1)}, u32[]{:S(2)}, u32[]{:S(2)}) collective-permute-start(bf16[4,256,128]{2,1,0:T(8,128)(2,1)S(1)} %get-tuple-element.55.refs_2_), channel_id=1, source_target_pairs={{0,12},{1,13},{2,14},{3,15},{4,0},{5,1},{6,2},{7,3},{8,4},{9,5},{1... | collective-permute-start | bytes 786440 | tf_op jit(solution)/shard_map/ppermute | solution.py:464
  35.1 1.5 %collective-permute-start.13 = (bf16[1024,256]{1,0:T(8,128)(2,1)S(1)}, bf16[1024,256]{1,0:T(8,128)(2,1)S(1)}, u32[]{:S(2)}, u32[]{:S(2)}) collective-permute-start(bf16[1024,256]{1,0:T(8,128)(2,1)S(1)} %get-tuple-element.68), channel_id=1, source_target_pairs={{0,2},{1,3},{2,0},{3,1},{4,6},{5,7},{6,4},{7,5},{8,10},{9,11},{10,... | collective-permute-start | bytes 1572872 | tf_op jit(solution)/shard_map/ppermute | solution.py:461
  36.6 6.2 %collective-permute-done.7 = bf16[2,4,256,128]{3,2,1,0:T(8,128)(2,1)S(1)} collective-permute-done((bf16[2,4,256,128]{3,2,1,0:T(8,128)(2,1)S(1)}, bf16[2,4,256,128]{3,2,1,0:T(8,128)(2,1)S(1)}, u32[]{:S(2)}, u32[]{:S(2)}) %collective-permute-start.7) | collective-permute-done | bytes 524320 | tf_op jit(solution)/shard_map/ppermute | solution.py:464
  42.9 4.8 %collective-permute-done.8.refs_2_ = bf16[4,256,128]{2,1,0:T(8,128)(2,1)S(1)} collective-permute-done((bf16[4,256,128]{2,1,0:T(8,128)(2,1)S(1)}, bf16[4,256,128]{2,1,0:T(8,128)(2,1)S(1)}, u32[]{:S(2)}, u32[]{:S(2)}) %collective-permute-start.8) | collective-permute-done | bytes 262176 | tf_op jit(solution)/shard_map/ppermute | solution.py:464
  47.8 0.6 collective-permute-start.9
  48.3 3.7 %attend_others.4 = bf16[272,512]{1,0:T(8,128)(2,1)S(1)} custom-call(s32[8]{0:T(128)S(1)} %copy-done.2, s32[16]{0:T(128)S(1)} %copy-done.3, bf16[32,32,2048]{2,1,0:T(8,128)(2,1)} %bitcast.19, bf16[2,32,32,256]{3,2,1,0:T(8,128)(2,1)S(1)} %bitcast.26, bf16[32,32,256]{2,1,0:T(8,128)(2,1)S(1)} %bitcast.38, bf16[32,32,256]{2,1,0:T(8,128)(2,1)S(1)} %bitcast.41, ...), custom_call_target="tpu_custom_call" | custom-call | flops 2000000000 | bytes 4194304 | tf_op jit(solution)/shard_map/attend_others/pallas_call | solution.py:314
  52.0 1.0 collective-permute-start.10
  53.0 5.3 %attend_others.5 = (bf16[272,512]{1,0:T(8,128)(2,1)S(1)}, bf16[272,512]{1,0:T(8,128)(2,1)S(1)}) custom-call(s32[8]{0:T(128)S(1)} %copy-done.2, s32[16]{0:T(128)S(1)} %copy-done.3, bf16[32,32,2048]{2,1,0:T(8,128)(2,1)} %bitcast.20, bf16[2,32,32,256]{3,2,1,0:T(8,128)(2,1)S(1)} %bitcast.27, bf16[32,32,256]{2,1,0:T(8,128)(2,1)S(1)} %bitcast.39, ...), custom_call_target="tpu_custom_call" | custom-call | flops 2000000000 | bytes 4194304 | tf_op jit(solution)/shard_map/attend_others/pallas_call | solution.py:314
  58.3 3.1 %collective-permute-start.12 = (bf16[272,512]{1,0:T(8,128)(2,1)S(1)}, bf16[272,512]{1,0:T(8,128)(2,1)S(1)}, u32[]{:S(2)}, u32[]{:S(2)}) collective-permute-start(bf16[272,512]{1,0:T(8,128)(2,1)S(1)} %get-tuple-element.58), channel_id=1, source_target_pairs={{0,12},{1,13},{2,14},{3,15},{4,0},{5,1},{6,2},{7,3},{8,4},{9,5},{1... | collective-permute-start | bytes 835592 | tf_op jit(solution)/shard_map/ppermute | solution.py:464
  61.4 3.5 %attend_own.2 = (f32[2,128,512]{2,1,0:T(8,128)S(1)}, f32[2,8,512]{2,1,0:T(8,128)S(1)}) custom-call(s32[8]{0:T(128)S(1)} %copy-done.2, s32[16]{0:T(128)S(1)} %copy-done.3, bf16[32,32,2048]{2,1,0:T(8,128)(2,1)} %bitcast.21, bf16[2,32,32,256]{3,2,1,0:T(8,128)(2,1)S(1)} %bitcast.28, bf16[32,32,256]{2,1,0:T(8,128)(2,1)S(1)} %bitcast.40, ...), custom_call_target="tpu_custom_call" | custom-call | flops 500000000 | bytes 4194304 | tf_op jit(solution)/shard_map/attend_own/pallas_call | solution.py:314
  65.5 3.7 %attend_others.6 = bf16[272,512]{1,0:T(8,128)(2,1)S(1)} custom-call(s32[8]{0:T(128)S(1)} %copy-done.2, s32[16]{0:T(128)S(1)} %copy-done.3, bf16[32,32,2048]{2,1,0:T(8,128)(2,1)} %bitcast.22, bf16[2,32,32,256]{3,2,1,0:T(8,128)(2,1)S(1)} %bitcast.29, bf16[32,32,256]{2,1,0:T(8,128)(2,1)S(1)} %bitcast.32, bf16[32,32,256]{2,1,0:T(8,128)(2,1)S(1)} %bitcast.35, ...), custom_call_target="tpu_custom_call" | custom-call | flops 10000000000 | bytes 4194304 | tf_op jit(solution)/shard_map/attend_others/pallas_call | solution.py:314
  69.1 3.3 %collective-permute-start.18 = (bf16[272,512]{1,0:T(8,128)(2,1)S(1)}, bf16[272,512]{1,0:T(8,128)(2,1)S(1)}, u32[]{:S(2)}, u32[]{:S(2)}) collective-permute-start(bf16[272,512]{1,0:T(8,128)(2,1)S(1)} %attend_others.6), channel_id=1, source_target_pairs={{0,12},{1,13},{2,14},{3,15},{4,0},{5,1},{6,2},{7,3},{8,4},{9,5},{1... | collective-permute-start | bytes 835592 | tf_op jit(solution)/shard_map/ppermute | solution.py:464
  72.5 5.3 %attend_others.7 = (bf16[272,512]{1,0:T(8,128)(2,1)S(1)}, bf16[272,512]{1,0:T(8,128)(2,1)S(1)}) custom-call(s32[8]{0:T(128)S(1)} %copy-done.2, s32[16]{0:T(128)S(1)} %copy-done.3, bf16[32,32,2048]{2,1,0:T(8,128)(2,1)} %bitcast.23, bf16[2,32,32,256]{3,2,1,0:T(8,128)(2,1)S(1)} %bitcast.30, bf16[32,32,256]{2,1,0:T(8,128)(2,1)S(1)} %bitcast.33, ...), custom_call_target="tpu_custom_call" | custom-call | flops 10000000000 | bytes 4194304 | tf_op jit(solution)/shard_map/attend_others/pallas_call | solution.py:314
  77.8 3.8 %collective-permute-done.18.two_ref = bf16[272,512]{1,0:T(8,128)(2,1)S(1)} collective-permute-done((bf16[272,512]{1,0:T(8,128)(2,1)S(1)}, bf16[272,512]{1,0:T(8,128)(2,1)S(1)}, u32[]{:S(2)}, u32[]{:S(2)}) %collective-permute-start.18) | collective-permute-done | bytes 278560 | tf_op jit(solution)/shard_map/ppermute | solution.py:464
  81.8 2.4 %collective-permute-start.19 = (bf16[272,512]{1,0:T(8,128)(2,1)S(1)}, bf16[272,512]{1,0:T(8,128)(2,1)S(1)}, u32[]{:S(2)}, u32[]{:S(2)}) collective-permute-start(bf16[272,512]{1,0:T(8,128)(2,1)S(1)} %merge.3), channel_id=1, source_target_pairs={{0,12},{1,13},{2,14},{3,15},{4,0},{5,1},{6,2},{7,3},{8,4},{9,5},{1... | collective-permute-start | bytes 835592 | tf_op jit(solution)/shard_map/ppermute | solution.py:464
  84.7 1.6 %collective-permute-start.16 = (bf16[320,128]{1,0:T(8,128)(2,1)S(1)}, bf16[320,128]{1,0:T(8,128)(2,1)S(1)}, u32[]{:S(2)}, u32[]{:S(2)}) collective-permute-start(bf16[320,128]{1,0:T(8,128)(2,1)S(1)} %get-tuple-element.80), channel_id=1, source_target_pairs={{0,2},{1,3},{2,0},{3,1},{4,6},{5,7},{6,4},{7,5},{8,10},{9,11},{10,... | collective-permute-start | bytes 245768 | tf_op jit(solution)/shard_map/ppermute | solution.py:461
  86.5 3.3 %collective-permute-done.16.refs_2_ = bf16[320,128]{1,0:T(8,128)(2,1)S(1)} collective-permute-done((bf16[320,128]{1,0:T(8,128)(2,1)S(1)}, bf16[320,128]{1,0:T(8,128)(2,1)S(1)}, u32[]{:S(2)}, u32[]{:S(2)}) %collective-permute-start.16) | collective-permute-done | bytes 81952 | tf_op jit(solution)/shard_map/ppermute | solution.py:461
  89.8 1.2 %collective-permute-done.17.refs_3_ = bf16[320,128]{1,0:T(8,128)(2,1)S(1)} collective-permute-done((bf16[320,128]{1,0:T(8,128)(2,1)S(1)}, bf16[320,128]{1,0:T(8,128)(2,1)S(1)}, u32[]{:S(2)}, u32[]{:S(2)}) %collective-permute-start.17) | collective-permute-done | bytes 81952 | tf_op jit(solution)/shard_map/ppermute | solution.py:461
  91.0 3.5 %attend_own.3 = (f32[2,128,512]{2,1,0:T(8,128)S(1)}, f32[2,8,512]{2,1,0:T(8,128)S(1)}) custom-call(s32[8]{0:T(128)S(1)} %copy-done.2, s32[16]{0:T(128)S(1)} %copy-done.3, bf16[32,32,2048]{2,1,0:T(8,128)(2,1)} %bitcast.24, bf16[2,32,32,256]{3,2,1,0:T(8,128)(2,1)S(1)} %bitcast.31, bf16[32,32,256]{2,1,0:T(8,128)(2,1)S(1)} %bitcast.34, ...), custom_call_target="tpu_custom_call" | custom-call | flops 500000000 | bytes 4194304 | tf_op jit(solution)/shard_map/attend_own/pallas_call | solution.py:314
  95.3 1.5 %collective-permute-start.22 = (bf16[320,128]{1,0:T(8,128)(2,1)S(1)}, bf16[320,128]{1,0:T(8,128)(2,1)S(1)}, u32[]{:S(2)}, u32[]{:S(2)}) collective-permute-start(bf16[320,128]{1,0:T(8,128)(2,1)S(1)} %get-tuple-element.90), channel_id=1, source_target_pairs={{0,2},{1,3},{2,0},{3,1},{4,6},{5,7},{6,4},{7,5},{8,10},{9,11},{10,... | collective-permute-start | bytes 245768 | tf_op jit(solution)/shard_map/ppermute | solution.py:461
  96.9 2.9 %collective-permute-done.22.refs_6_ = bf16[320,128]{1,0:T(8,128)(2,1)S(1)} collective-permute-done((bf16[320,128]{1,0:T(8,128)(2,1)S(1)}, bf16[320,128]{1,0:T(8,128)(2,1)S(1)}, u32[]{:S(2)}, u32[]{:S(2)}) %collective-permute-start.22) | collective-permute-done | bytes 81952 | tf_op jit(solution)/shard_map/ppermute | solution.py:461
  99.8 1.8 %collective-permute-done.23.refs_7_ = bf16[320,128]{1,0:T(8,128)(2,1)S(1)} collective-permute-done((bf16[320,128]{1,0:T(8,128)(2,1)S(1)}, bf16[320,128]{1,0:T(8,128)(2,1)S(1)}, u32[]{:S(2)}, u32[]{:S(2)}) %collective-permute-start.23) | collective-permute-done | bytes 81952 | tf_op jit(solution)/shard_map/ppermute | solution.py:461
  101.6 1.5 %emit.1 = (bf16[8,4,8192]{2,1,0:T(4,128)(2,1)}, bf16[8,4,8192]{2,1,0:T(4,128)(2,1)}) custom-call(bf16[320,128]{1,0:T(8,128)(2,1)S(1)} %get-tuple-element.78.refs_0_, bf16[320,128]{1,0:T(8,128)(2,1)S(1)} %collective-permute-done.15.refs_1_, bf16[320,128]{1,0:T(8,128)(2,1)S(1)} %collective-permute-done.16.refs_2_, ...), custom_call_target="tpu_custom_call" | custom-call | flops 1048576 | bytes 2097152 | tf_op jit(solution)/shard_map/emit/pallas_call | solution.py:443
  (45 shorter events, 3.0 us)
Async XLA Ops:
  2.9 6.4 %collective-permute-start = (bf16[2,320,128]{2,1,0:T(8,128)(2,1)}, bf16[2,320,128]{2,1,0:T(8,128)(2,1)S(1)}, u32[]{:S(2)}, u32[]{:S(2)}) collective-permute-start(bf16[2,320,128]{2,1,0:T(8,128)(2,1)} %get-tuple-element.49), channel_id=1, source_target_pairs={{0,1},{1,0},{2,3},{3,2},{4,5},{5,4},{6,7},{7,6},{8,9},{9,8},{10,11... | collective-permute-start | bytes 491528 | tf_op jit(solution)/shard_map/ppermute | solution.py:461
  3.4 7.9 %collective-permute-start.1 = (bf16[2,320,128]{2,1,0:T(8,128)(2,1)}, bf16[2,320,128]{2,1,0:T(8,128)(2,1)S(1)}, u32[]{:S(2)}, u32[]{:S(2)}) collective-permute-start(bf16[2,320,128]{2,1,0:T(8,128)(2,1)} %get-tuple-element.50), channel_id=1, source_target_pairs={{0,2},{1,3},{2,0},{3,1},{4,6},{5,7},{6,4},{7,5},{8,10},{9,11},{10,... | collective-permute-start | bytes 491528 | tf_op jit(solution)/shard_map/ppermute | solution.py:461
  6.0 8.3 %collective-permute-start.2 = (bf16[2,320,128]{2,1,0:T(8,128)(2,1)}, bf16[2,320,128]{2,1,0:T(8,128)(2,1)S(1)}, u32[]{:S(2)}, u32[]{:S(2)}) collective-permute-start(bf16[2,320,128]{2,1,0:T(8,128)(2,1)} %get-tuple-element.51), channel_id=1, source_target_pairs={{0,3},{1,2},{2,1},{3,0},{4,7},{5,6},{6,5},{7,4},{8,11},{9,10},{10,... | collective-permute-start | bytes 491528 | tf_op jit(solution)/shard_map/ppermute | solution.py:461
  6.1 2.2 %copy-start = (bf16[32,1,32,2048]{3,2,1,0:T(8,128)(2,1)S(1)}, bf16[32,1,32,2048]{3,2,1,0:T(8,128)(2,1)}, u32[]{:S(2)}) copy-start(bf16[32,1,32,2048]{3,2,1,0:T(8,128)(2,1)} %param.5) | copy-start | bytes 12582916
  8.3 1.0 copy-start.1
  8.3 40.1 %copy-start.2 = (s32[8]{0:T(128)S(1)}, s32[8]{0:T(128)}, u32[]{:S(2)}) copy-start(s32[8]{0:T(128)} %counts_ref.11) | copy-start | bytes 100
  8.3 40.1 %copy-start.3 = (s32[16]{0:T(128)S(1)}, s32[16]{0:T(128)}, u32[]{:S(2)}) copy-start(s32[16]{0:T(128)} %slots_ref.11) | copy-start | bytes 196
  14.2 20.9 %collective-permute-start.3 = (bf16[2,1024,256]{2,1,0:T(8,128)(2,1)S(1)}, bf16[2,1024,256]{2,1,0:T(8,128)(2,1)S(1)}, u32[]{:S(2)}, u32[]{:S(2)}) collective-permute-start(bf16[2,1024,256]{2,1,0:T(8,128)(2,1)S(1)} %get-tuple-element.52), channel_id=1, source_target_pairs={{0,1},{1,0},{2,3},{3,2},{4,5},{5,4},{6,7},{7,6},{8,9},{9,8},{10,11... | collective-permute-start | bytes 3145736 | tf_op jit(solution)/shard_map/ppermute | solution.py:461
  14.5 16.2 %collective-permute-start.6 = (bf16[2,4,256,128]{3,2,1,0:T(8,128)(2,1)S(1)}, bf16[2,4,256,128]{3,2,1,0:T(8,128)(2,1)S(1)}, u32[]{:S(2)}, u32[]{:S(2)}) collective-permute-start(bf16[2,4,256,128]{3,2,1,0:T(8,128)(2,1)S(1)} %pad_maximum_fusion), channel_id=1, source_target_pairs={{0,12},{1,13},{2,14},{3,15},{4,0},{5,1},{6,2},{7,3},{8,4},{9,5},{1... | collective-permute-start | bytes 1572872 | tf_op jit(solution)/shard_map/ppermute | solution.py:464
  18.4 24.5 %collective-permute-start.7 = (bf16[2,4,256,128]{3,2,1,0:T(8,128)(2,1)S(1)}, bf16[2,4,256,128]{3,2,1,0:T(8,128)(2,1)S(1)}, u32[]{:S(2)}, u32[]{:S(2)}) collective-permute-start(bf16[2,4,256,128]{3,2,1,0:T(8,128)(2,1)S(1)} %pad_maximum_fusion), channel_id=1, source_target_pairs={{0,4},{1,5},{2,6},{3,7},{4,8},{5,9},{6,10},{7,11},{8,12},{9,13},{1... | collective-permute-start | bytes 1572872 | tf_op jit(solution)/shard_map/ppermute | solution.py:464
  18.4 29.9 %collective-permute-start.4 = (bf16[1024,256]{1,0:T(8,128)(2,1)S(1)}, bf16[1024,256]{1,0:T(8,128)(2,1)S(1)}, u32[]{:S(2)}, u32[]{:S(2)}) collective-permute-start(bf16[1024,256]{1,0:T(8,128)(2,1)S(1)} %get-tuple-element.53), channel_id=1, source_target_pairs={{0,2},{1,3},{2,0},{3,1},{4,6},{5,7},{6,4},{7,5},{8,10},{9,11},{10,... | collective-permute-start | bytes 1572872 | tf_op jit(solution)/shard_map/ppermute | solution.py:461
  19.9 28.4 %collective-permute-start.5 = (bf16[1024,256]{1,0:T(8,128)(2,1)S(1)}, bf16[1024,256]{1,0:T(8,128)(2,1)S(1)}, u32[]{:S(2)}, u32[]{:S(2)}) collective-permute-start(bf16[1024,256]{1,0:T(8,128)(2,1)S(1)} %get-tuple-element.54), channel_id=1, source_target_pairs={{0,3},{1,2},{2,1},{3,0},{4,7},{5,6},{6,5},{7,4},{8,11},{9,10},{10,... | collective-permute-start | bytes 1572872 | tf_op jit(solution)/shard_map/ppermute | solution.py:461
  30.8 17.0 %collective-permute-start.8 = (bf16[4,256,128]{2,1,0:T(8,128)(2,1)S(1)}, bf16[4,256,128]{2,1,0:T(8,128)(2,1)S(1)}, u32[]{:S(2)}, u32[]{:S(2)}) collective-permute-start(bf16[4,256,128]{2,1,0:T(8,128)(2,1)S(1)} %get-tuple-element.55.refs_2_), channel_id=1, source_target_pairs={{0,12},{1,13},{2,14},{3,15},{4,0},{5,1},{6,2},{7,3},{8,4},{9,5},{1... | collective-permute-start | bytes 786440 | tf_op jit(solution)/shard_map/ppermute | solution.py:464
  35.1 30.3 %collective-permute-start.13 = (bf16[1024,256]{1,0:T(8,128)(2,1)S(1)}, bf16[1024,256]{1,0:T(8,128)(2,1)S(1)}, u32[]{:S(2)}, u32[]{:S(2)}) collective-permute-start(bf16[1024,256]{1,0:T(8,128)(2,1)S(1)} %get-tuple-element.68), channel_id=1, source_target_pairs={{0,2},{1,3},{2,0},{3,1},{4,6},{5,7},{6,4},{7,5},{8,10},{9,11},{10,... | collective-permute-start | bytes 1572872 | tf_op jit(solution)/shard_map/ppermute | solution.py:461
  42.9 22.6 %collective-permute-start.14 = (bf16[1024,256]{1,0:T(8,128)(2,1)S(1)}, bf16[1024,256]{1,0:T(8,128)(2,1)S(1)}, u32[]{:S(2)}, u32[]{:S(2)}) collective-permute-start(bf16[1024,256]{1,0:T(8,128)(2,1)S(1)} %get-tuple-element.69), channel_id=1, source_target_pairs={{0,3},{1,2},{2,1},{3,0},{4,7},{5,6},{6,5},{7,4},{8,11},{9,10},{10,... | collective-permute-start | bytes 1572872 | tf_op jit(solution)/shard_map/ppermute | solution.py:461
  47.8 13.7 %collective-permute-start.9 = (bf16[4,256,128]{2,1,0:T(8,128)(2,1)S(1)}, bf16[4,256,128]{2,1,0:T(8,128)(2,1)S(1)}, u32[]{:S(2)}, u32[]{:S(2)}) collective-permute-start(bf16[4,256,128]{2,1,0:T(8,128)(2,1)S(1)} %get-tuple-element.73.refs_3_), channel_id=1, source_target_pairs={{0,4},{1,5},{2,6},{3,7},{4,8},{5,9},{6,10},{7,11},{8,12},{9,13},{1... | collective-permute-start | bytes 786440 | tf_op jit(solution)/shard_map/ppermute | solution.py:464
  52.0 13.0 %collective-permute-start.10 = (bf16[272,512]{1,0:T(8,128)(2,1)S(1)}, bf16[272,512]{1,0:T(8,128)(2,1)S(1)}, u32[]{:S(2)}, u32[]{:S(2)}) collective-permute-start(bf16[272,512]{1,0:T(8,128)(2,1)S(1)} %attend_others.4), channel_id=1, source_target_pairs={{0,4},{1,5},{2,6},{3,7},{4,8},{5,9},{6,10},{7,11},{8,12},{9,13},{1... | collective-permute-start | bytes 835592 | tf_op jit(solution)/shard_map/ppermute | solution.py:464
  58.3 25.9 %collective-permute-start.12 = (bf16[272,512]{1,0:T(8,128)(2,1)S(1)}, bf16[272,512]{1,0:T(8,128)(2,1)S(1)}, u32[]{:S(2)}, u32[]{:S(2)}) collective-permute-start(bf16[272,512]{1,0:T(8,128)(2,1)S(1)} %get-tuple-element.58), channel_id=1, source_target_pairs={{0,12},{1,13},{2,14},{3,15},{4,0},{5,1},{6,2},{7,3},{8,4},{9,5},{1... | collective-permute-start | bytes 835592 | tf_op jit(solution)/shard_map/ppermute | solution.py:464
  65.2 19.1 %collective-permute-start.11 = (bf16[272,512]{1,0:T(8,128)(2,1)S(1)}, bf16[272,512]{1,0:T(8,128)(2,1)S(1)}, u32[]{:S(2)}, u32[]{:S(2)}) collective-permute-start(bf16[272,512]{1,0:T(8,128)(2,1)S(1)} %merge.2), channel_id=1, source_target_pairs={{0,4},{1,5},{2,6},{3,7},{4,8},{5,9},{6,10},{7,11},{8,12},{9,13},{1... | collective-permute-start | bytes 835592 | tf_op jit(solution)/shard_map/ppermute | solution.py:464
  69.1 12.5 %collective-permute-start.18 = (bf16[272,512]{1,0:T(8,128)(2,1)S(1)}, bf16[272,512]{1,0:T(8,128)(2,1)S(1)}, u32[]{:S(2)}, u32[]{:S(2)}) collective-permute-start(bf16[272,512]{1,0:T(8,128)(2,1)S(1)} %attend_others.6), channel_id=1, source_target_pairs={{0,12},{1,13},{2,14},{3,15},{4,0},{5,1},{6,2},{7,3},{8,4},{9,5},{1... | collective-permute-start | bytes 835592 | tf_op jit(solution)/shard_map/ppermute | solution.py:464
  77.8 16.8 %collective-permute-start.20 = (bf16[272,512]{1,0:T(8,128)(2,1)S(1)}, bf16[272,512]{1,0:T(8,128)(2,1)S(1)}, u32[]{:S(2)}, u32[]{:S(2)}) collective-permute-start(bf16[272,512]{1,0:T(8,128)(2,1)S(1)} %get-tuple-element.74), channel_id=1, source_target_pairs={{0,4},{1,5},{2,6},{3,7},{4,8},{5,9},{6,10},{7,11},{8,12},{9,13},{1... | collective-permute-start | bytes 835592 | tf_op jit(solution)/shard_map/ppermute | solution.py:464
  81.8 12.7 %collective-permute-start.19 = (bf16[272,512]{1,0:T(8,128)(2,1)S(1)}, bf16[272,512]{1,0:T(8,128)(2,1)S(1)}, u32[]{:S(2)}, u32[]{:S(2)}) collective-permute-start(bf16[272,512]{1,0:T(8,128)(2,1)S(1)} %merge.3), channel_id=1, source_target_pairs={{0,12},{1,13},{2,14},{3,15},{4,0},{5,1},{6,2},{7,3},{8,4},{9,5},{1... | collective-permute-start | bytes 835592 | tf_op jit(solution)/shard_map/ppermute | solution.py:464
  84.6 1.9 %collective-permute-start.15 = (bf16[320,128]{1,0:T(8,128)(2,1)S(1)}, bf16[320,128]{1,0:T(8,128)(2,1)S(1)}, u32[]{:S(2)}, u32[]{:S(2)}) collective-permute-start(bf16[320,128]{1,0:T(8,128)(2,1)S(1)} %get-tuple-element.79), channel_id=1, source_target_pairs={{0,1},{1,0},{2,3},{3,2},{4,5},{5,4},{6,7},{7,6},{8,9},{9,8},{10,11... | collective-permute-start | bytes 245768 | tf_op jit(solution)/shard_map/ppermute | solution.py:461
  84.7 5.1 %collective-permute-start.16 = (bf16[320,128]{1,0:T(8,128)(2,1)S(1)}, bf16[320,128]{1,0:T(8,128)(2,1)S(1)}, u32[]{:S(2)}, u32[]{:S(2)}) collective-permute-start(bf16[320,128]{1,0:T(8,128)(2,1)S(1)} %get-tuple-element.80), channel_id=1, source_target_pairs={{0,2},{1,3},{2,0},{3,1},{4,6},{5,7},{6,4},{7,5},{8,10},{9,11},{10,... | collective-permute-start | bytes 245768 | tf_op jit(solution)/shard_map/ppermute | solution.py:461
  86.3 4.7 %collective-permute-start.17 = (bf16[320,128]{1,0:T(8,128)(2,1)S(1)}, bf16[320,128]{1,0:T(8,128)(2,1)S(1)}, u32[]{:S(2)}, u32[]{:S(2)}) collective-permute-start(bf16[320,128]{1,0:T(8,128)(2,1)S(1)} %get-tuple-element.81), channel_id=1, source_target_pairs={{0,3},{1,2},{2,1},{3,0},{4,7},{5,6},{6,5},{7,4},{8,11},{9,10},{10,... | collective-permute-start | bytes 245768 | tf_op jit(solution)/shard_map/ppermute | solution.py:461
  94.9 2.0 %collective-permute-start.21 = (bf16[320,128]{1,0:T(8,128)(2,1)S(1)}, bf16[320,128]{1,0:T(8,128)(2,1)S(1)}, u32[]{:S(2)}, u32[]{:S(2)}) collective-permute-start(bf16[320,128]{1,0:T(8,128)(2,1)S(1)} %get-tuple-element.89), channel_id=1, source_target_pairs={{0,1},{1,0},{2,3},{3,2},{4,5},{5,4},{6,7},{7,6},{8,9},{9,8},{10,11... | collective-permute-start | bytes 245768 | tf_op jit(solution)/shard_map/ppermute | solution.py:461
  95.3 4.5 %collective-permute-start.22 = (bf16[320,128]{1,0:T(8,128)(2,1)S(1)}, bf16[320,128]{1,0:T(8,128)(2,1)S(1)}, u32[]{:S(2)}, u32[]{:S(2)}) collective-permute-start(bf16[320,128]{1,0:T(8,128)(2,1)S(1)} %get-tuple-element.90), channel_id=1, source_target_pairs={{0,2},{1,3},{2,0},{3,1},{4,6},{5,7},{6,4},{7,5},{8,10},{9,11},{10,... | collective-permute-start | bytes 245768 | tf_op jit(solution)/shard_map/ppermute | solution.py:461
  96.9 4.7 %collective-permute-start.23 = (bf16[320,128]{1,0:T(8,128)(2,1)S(1)}, bf16[320,128]{1,0:T(8,128)(2,1)S(1)}, u32[]{:S(2)}, u32[]{:S(2)}) collective-permute-start(bf16[320,128]{1,0:T(8,128)(2,1)S(1)} %get-tuple-element.91), channel_id=1, source_target_pairs={{0,3},{1,2},{2,1},{3,0},{4,7},{5,6},{6,5},{7,4},{8,11},{9,10},{10,... | collective-permute-start | bytes 245768 | tf_op jit(solution)/shard_map/ppermute | solution.py:461
